TPU v7x, 256 devices: a whole 4x4x8 slice. The times are simulated.
256 devices in a mesh: row: 32 (over x, z), col: 8 (over y, core).
Axes of the slice: x: 4, y: 4, z: 8, core: 2. Of those that a mesh axis runs over, the one named last changes fastest.
Arguments:
- affinity: bfloat16 [131072, 8192], P('row', 'col'), may hold values from -250 to 250
- seed_values: int32 [16], replicated, may hold values from 0 to 1073741823
- sku_ids: int32 [8192], P('col'), may hold values from 0 to 8191, each once
Outputs:
- range_basis: float32 [16, 131072], P(None, ('row', 'col'))
- range_factor: float32 [16, 16], replicated
All inputs are finite; a program needn't handle non-finite values.
Results may differ from a plain program's by a relative error of at most 0.0046.
Values may be sent and summed in bfloat16 or wider, within the bound.
No kernel may reach another device: no remote copies, remote signals or barrier semaphores. Data moves between devices by JAX's collectives and lax.ppermute only.
A program may use at most 64 MiB of HBM per device.

v0:
```python
import math

import jax
import jax.numpy as jnp
from jax import lax
from jax.sharding import PartitionSpec as P

ITERS = 2


mix_first = -2048144789
mix_second = -1028477387
golden = -1640531535
salt_value = 1540483477


def shifted(value, amount):
    return lax.shift_right_logical(value, jnp.full(value.shape, amount, jnp.int32))


def scramble(value):
    value = jnp.bitwise_xor(value, shifted(value, 16))
    value = value * jnp.int32(mix_first)
    value = jnp.bitwise_xor(value, shifted(value, 13))
    value = value * jnp.int32(mix_second)
    return jnp.bitwise_xor(value, shifted(value, 16))


def test_matrix(seed_values, sku_ids, total_columns):
    first = scramble(jnp.bitwise_xor(seed_values[:, None], sku_ids[None, :] * jnp.int32(golden)))
    second = scramble(jnp.bitwise_xor(first, jnp.int32(salt_value)))
    uniform_a = (shifted(first, 9) + 1).astype(jnp.float32) / 8388608.0
    uniform_b = (shifted(second, 9) + 1).astype(jnp.float32) / 8388608.0
    gauss = jnp.sqrt(-2.0 * jnp.log(uniform_a)) * jnp.cos(6.283185307179586 * uniform_b)
    return (gauss / math.sqrt(total_columns)).astype(jnp.bfloat16)


def lower_solve(lower, right):
    return lax.linalg.triangular_solve(lower, right, left_side=True, lower=True)


def body(affinity, seed_values, sku_ids):
    col_count = lax.axis_size("col")
    total_columns = sku_ids.shape[0] * col_count
    local_rows = affinity.shape[0]
    piece_rows = local_rows // col_count
    total_rows = local_rows * lax.axis_size("row")
    inv_root = 1.0 / math.sqrt(total_columns)

    def project(left):
        return lax.dot_general(
            left, affinity, (((1,), (1,)), ((), ())), preferred_element_type=jnp.float32
        )

    omega = test_matrix(seed_values, sku_ids, total_columns)
    partial_sketch = project(omega)
    for repeat in range(ITERS + 1):
        sketch = lax.psum(partial_sketch, "col")
        gram = lax.psum(
            jnp.dot(
                sketch,
                sketch.T,
                precision=lax.Precision.HIGHEST,
                preferred_element_type=jnp.float32,
            ),
            "row",
        )
        lower = jnp.linalg.cholesky(gram)
        ortho = lower_solve(lower, sketch)
        if repeat < ITERS:
            back_part = jnp.dot(
                ortho.astype(jnp.bfloat16), affinity, preferred_element_type=jnp.float32
            )
        else:
            start_row = lax.axis_index("col") * piece_rows
            ortho = lax.dynamic_slice_in_dim(ortho, start_row, piece_rows, 1)
        if repeat < ITERS:
            back = lax.psum(back_part, "row")
            partial_sketch = project(back.astype(jnp.bfloat16)) * inv_root
    scale = math.sqrt(total_rows)
    return (ortho * scale, lower.T / scale)


def solution(mesh):
    placed = (P("row", "col"), P(), P("col"))
    return jax.shard_map(
        body, mesh=mesh, in_specs=placed, out_specs=(P(None, ("row", "col")), P()), check_vma=False
    )
```

profile of v0, /device:TPU:1, one launch (start us, length us, event | category | flops | bytes accessed | tf_op | source)
XLA Modules:
  0.0 734.2 jit_solution(8240218755186192134)
XLA Ops:
  7.2 0.0 all-reduce.4.cloned.1.call-start
  7.2 0.7 broadcast_multiply_fusion
  7.9 6.7 fusion.12
  14.6 0.0 all-reduce.4.cloned.1.call-update
  14.6 0.0 all-reduce.6.cloned.1.call-start
  14.7 66.9 %all-reduce.4.cloned.1.call-done = f32[16,4096]{1,0:T(8,128)} async-done(((f32[16,4096]{1,0:T(8,128)}), f32[16,4096]{1,0:T(8,128)}) %all-reduce.4.cloned.1.call-update) | async-done | bytes 262160 | tf_op jit(solution)/shard_map/psum | solution.py:58
  81.5 1.5 fusion.54
  83.0 62.0 %psum.57 = f32[16,16]{0,1:T(8,128)S(1)} all-reduce(f32[16,16]{0,1:T(8,128)S(1)} %fusion.54), channel_id=1, replica_groups=mesh['row'=32,'col'=8] {'row'}, use_global_device_ids=true, to_apply=%region_1.0 | all-reduce | flops 256 | bytes 2048 | tf_op jit(solution)/shard_map/psum | solution.py:59
  145.0 0.1 copy.6
  145.1 1.5 cholesky.59
  146.6 0.6 compare_reduce_fusion.2
  147.2 0.6 fusion.29
  147.9 1.2 custom-call.7
  149.1 1.4 convolution_convert_fusion.1
  150.5 4.6 fusion.55
  155.1 109.9 %psum.58 = bf16[16,1024]{1,0:T(8,128)(2,1)S(1)} all-reduce(f32[16,1024]{1,0:T(8,128)S(1)} %fusion.55), channel_id=1, replica_groups=mesh['row'=32,'col'=8] {'row'}, use_global_device_ids=true, to_apply=%region_4.7 | all-reduce | flops 16384 | bytes 98304 | tf_op jit(solution)/shard_map/psum | solution.py:78
  265.0 6.4 convolution_multiply_fusion.1
  271.4 0.0 all-reduce.6.cloned.1.call-update
  271.4 0.0 all-reduce.8.cloned.1.call-start
  271.4 98.0 %all-reduce.6.cloned.1.call-done = f32[16,4096]{1,0:T(8,128)} async-done(((f32[16,4096]{1,0:T(8,128)}), f32[16,4096]{1,0:T(8,128)}) %all-reduce.6.cloned.1.call-update) | async-done | bytes 262160 | tf_op jit(solution)/shard_map/psum | solution.py:58
  369.5 1.5 fusion.56
  370.9 62.0 %psum.60 = f32[16,16]{0,1:T(8,128)S(1)} all-reduce(f32[16,16]{0,1:T(8,128)S(1)} %fusion.56), channel_id=1, replica_groups=mesh['row'=32,'col'=8] {'row'}, use_global_device_ids=true, to_apply=%region_6.9 | all-reduce | flops 256 | bytes 2048 | tf_op jit(solution)/shard_map/psum | solution.py:59
  433.0 0.1 copy.8
  433.0 1.5 cholesky.70
  434.5 0.6 compare_reduce_fusion.1
  435.2 0.6 fusion.30
  435.8 1.2 custom-call.8
  437.1 1.4 convolution_convert_fusion
  438.4 4.6 fusion.57
  443.0 109.9 %psum.61 = bf16[16,1024]{1,0:T(8,128)(2,1)S(1)} all-reduce(f32[16,1024]{1,0:T(8,128)S(1)} %fusion.57), channel_id=1, replica_groups=mesh['row'=32,'col'=8] {'row'}, use_global_device_ids=true, to_apply=%region_7.10 | all-reduce | flops 16384 | bytes 98304 | tf_op jit(solution)/shard_map/psum | solution.py:78
  552.9 6.4 convolution_multiply_fusion
  559.3 0.0 all-reduce.8.cloned.1.call-update
  559.3 98.1 %all-reduce.8.cloned.1.call-done = f32[16,4096]{1,0:T(8,128)} async-done(((f32[16,4096]{1,0:T(8,128)}), f32[16,4096]{1,0:T(8,128)}) %all-reduce.8.cloned.1.call-update) | async-done | bytes 262160 | tf_op jit(solution)/shard_map/psum | solution.py:58
  657.4 1.5 fusion.58
  658.9 62.0 %psum.63 = f32[16,16]{0,1:T(8,128)S(1)} all-reduce(f32[16,16]{0,1:T(8,128)S(1)} %fusion.58), channel_id=1, replica_groups=mesh['row'=32,'col'=8] {'row'}, use_global_device_ids=true, to_apply=%region_9.12 | all-reduce | flops 256 | bytes 2048 | tf_op jit(solution)/shard_map/psum | solution.py:59
  720.9 0.1 copy.10
  721.0 1.5 cholesky.81
  722.5 0.6 compare_reduce_fusion
  723.1 0.7 multiply_bitcast_fusion
  723.8 1.2 custom-call.9
  725.0 0.7 copy.11
  725.7 1.4 fusion.31
  727.1 0.6 dynamic-slice_multiply_fusion
  (6 shorter events, 0.1 us)
Async XLA Ops:
  7.2 74.3 %all-reduce.4.cloned.1.call-start = ((), (), s32[]{:S(2)}) async-start(), calls=%async_computation | async-start | bytes 524288 | tf_op jit(solution)/shard_map/psum | solution.py:58
  14.6 354.9 %all-reduce.6.cloned.1.call-start = ((), (), s32[]{:S(2)}) async-start(), calls=%async_computation.1 | async-start | bytes 524288 | tf_op jit(solution)/shard_map/psum | solution.py:58
  271.4 386.1 %all-reduce.8.cloned.1.call-start = ((), (), s32[]{:S(2)}) async-start(), calls=%async_computation.2 | async-start | bytes 524288 | tf_op jit(solution)/shard_map/psum | solution.py:58
Sparse Core Ops, SparseCore 0:
  14.7 66.7 all-reduce.3
  271.5 97.9 all-reduce.5
  559.4 97.9 all-reduce.7
where the time goes:
time: 748 us; the launch traced here: 734 us
  blocking collectives  406 us (54%)
  waiting for transfers between devices  263 us (35%)
  matrix products  37.1 us (5%)
  between operations  13.8 us (2%)
  other arithmetic  13.4 us (2%)
    psum x3, waiting for transfers between devices, body(): sketch = lax.psum(partial_sketch, 'col')  263 us
    psum x2, blocking collectives, body(): back = lax.psum(back_part, 'row')  220 us
    psum x3, blocking collectives, body(): lax.psum(jnp.dot(sketch, sketch.T, precision=lax.Precision.HIGHEST, prefe...  186 us
    dot_general x3, matrix products, project(): lax.dot_general(left, affinity, (((1,), (1,)), ((), ())), preferred_eleme...  19.4 us
  transfers between devices with their start and end apart: 3, of which 3 were waited for; matrix products, arithmetic and copies ran while one was open for 0% of the time, Pallas kernels for 0%

commit v1 on v0

v1 whole, which is shorter than its diff:
```python
import math

import jax
import jax.numpy as jnp
from jax import lax
from jax.sharding import Mesh, PartitionSpec as P

ITERS = 2
K = 16


mix_first = -2048144789
mix_second = -1028477387
golden = -1640531535
salt_value = 1540483477


def shifted(value, amount):
    return lax.shift_right_logical(value, jnp.full(value.shape, amount, jnp.int32))


def scramble(value):
    value = jnp.bitwise_xor(value, shifted(value, 16))
    value = value * jnp.int32(mix_first)
    value = jnp.bitwise_xor(value, shifted(value, 13))
    value = value * jnp.int32(mix_second)
    return jnp.bitwise_xor(value, shifted(value, 16))


def test_matrix(seed_values, sku_ids, total_columns):
    first = scramble(jnp.bitwise_xor(seed_values[:, None], sku_ids[None, :] * jnp.int32(golden)))
    second = scramble(jnp.bitwise_xor(first, jnp.int32(salt_value)))
    uniform_a = (shifted(first, 9) + 1).astype(jnp.float32) / 8388608.0
    uniform_b = (shifted(second, 9) + 1).astype(jnp.float32) / 8388608.0
    gauss = jnp.sqrt(-2.0 * jnp.log(uniform_a)) * jnp.cos(6.283185307179586 * uniform_b)
    return (gauss / math.sqrt(total_columns)).astype(jnp.bfloat16)


def lower_solve(lower, right):
    return lax.linalg.triangular_solve(lower, right, left_side=True, lower=True)


def swap(value, axis, count, offset):
    return lax.ppermute(value, axis, [(i, i ^ offset) for i in range(count)])


def sum_four(value, axis):
    one, two, three = (swap(value, axis, 4, k) for k in (1, 2, 3))
    return (value + two) + (one + three)


def exact_gram(left):
    return lax.dot_general(
        left,
        left,
        (((1,), (1,)), ((), ())),
        precision=lax.Precision.HIGHEST,
        preferred_element_type=jnp.float32,
    )


def body(affinity, seed_values, sku_ids):
    total_columns = sku_ids.shape[0] * 8
    local_rows = affinity.shape[0]
    total_rows = local_rows * 32
    inv_root = 1.0 / math.sqrt(total_columns)
    core = lax.axis_index("core")
    on_first = core == 0

    def project(left):
        return lax.dot_general(
            left, affinity, (((1,), (1,)), ((), ())), preferred_element_type=jnp.float32
        )

    def halves(partial):
        pieces = partial.reshape(K, 4, 2, local_rows // 8)
        first, second = pieces[:, :, 0], pieces[:, :, 1]
        return jnp.where(on_first, first, second), jnp.where(on_first, second, first)

    omega = test_matrix(seed_values, sku_ids, total_columns)
    partial_sketch = project(omega)
    for repeat in range(ITERS + 1):
        own, other = halves(partial_sketch)
        half = own + swap(other, "core", 2, 1)
        half = sum_four(half, "y")
        if repeat < ITERS:
            sibling = swap(half, "core", 2, 1)
            sketch = jnp.stack(
                [jnp.where(on_first, half, sibling), jnp.where(on_first, sibling, half)], axis=2
            ).reshape(K, local_rows)
            gram = exact_gram(sketch)
            high = sketch.astype(jnp.bfloat16)
            low = (sketch - high.astype(jnp.float32)).astype(jnp.bfloat16)
            both = jnp.dot(
                jnp.concatenate([high, low], axis=0), affinity, preferred_element_type=jnp.float32
            )
            back = both[:K] + both[K:]
            packed = jnp.concatenate([back, gram, jnp.zeros((K, 128 - K), jnp.float32)], axis=1)
            packed = sum_four(packed, "x")
            spread = jnp.broadcast_to(packed[None], (8,) + packed.shape)
            packed = jnp.sum(lax.all_to_all(spread, "z", 0, 0), axis=0)
            gram = packed[:, back.shape[1] : back.shape[1] + K]
            lower = jnp.linalg.cholesky(gram)
            back = lower_solve(lower, packed[:, : back.shape[1]])
            partial_sketch = project(back.astype(jnp.bfloat16)) * inv_root
        else:
            gram = exact_gram(half.reshape(K, local_rows // 2))
            gram = gram + swap(gram, "core", 2, 1)
            gram = jnp.pad(gram, ((0, 0), (0, 128 - K)))
            spread = jnp.broadcast_to(gram[None], (32,) + gram.shape)
            gram = jnp.sum(lax.all_to_all(spread, ("x", "z"), 0, 0), axis=0)[:, :K]
            lower = jnp.linalg.cholesky(gram)
            piece = lax.dynamic_index_in_dim(half, lax.axis_index("y"), 1, keepdims=False)
            ortho = lower_solve(lower, piece)
    scale = math.sqrt(total_rows)
    return (ortho * scale, lower.T / scale)


def solution(mesh):
    split = Mesh(mesh.devices.reshape(4, 8, 4, 2), ("x", "z", "y", "core"))
    row, col = ("x", "z"), ("y", "core")
    return jax.shard_map(
        body,
        mesh=split,
        in_specs=(P(row, col), P(), P(col)),
        out_specs=(P(None, row + col), P()),
        check_vma=False,
    )
```

time: 748 us -> 171 us (0.23); the launches traced: 734 us -> 169 us
  blocking collectives: 406 us -> 41.9 us
  waiting for transfers between devices: 263 us -> 39.6 us
  starting transfers between devices: 0.12 us -> 39 us
  between operations: 13.8 us -> 0.95 us
    psum x5 -> x0, blocking collectives: 406 us -> none  [the longest x2 220 us: body(): back = lax.psum(back_part, 'row')]
    psum x3 -> x0, waiting for transfers between devices: 263 us -> none  [body(): sketch = lax.psum(partial_sketch, 'col')]
    all_to_all x0 -> x2, blocking collectives: none -> 41.9 us  [body(): packed = jnp.sum(lax.all_to_all(spread, 'z', 0, 0), axis=0)]
    ppermute x0 -> x21, starting transfers between devices: none -> 35.1 us  [swap(): return lax.ppermute(value, axis, [(i, i ^ offset) for i in range(count)])]
    ppermute x0 -> x21, waiting for transfers between devices: none -> 29.3 us  [swap(): return lax.ppermute(value, axis, [(i, i ^ offset) for i in range(count)])]
    all_to_all x0 -> x1, waiting for transfers between devices: none -> 10.3 us  [body(): gram = jnp.sum(lax.all_to_all(spread, ('x', 'z'), 0, 0), axis=0)[:, :K]]
  transfers between devices with their start and end apart: 3 -> 22, of which waited for: 3 -> 20; matrix products, arithmetic and copies ran while one was open for 0% -> 0% of each run, Pallas kernels for 0% -> 0%
where the time goes in v1:
time: 171 us; the launch traced here: 169 us
  blocking collectives  41.9 us (25%)
  waiting for transfers between devices  39.6 us (23%)
  starting transfers between devices  39 us (23%)
  matrix products  29.7 us (17%)
  other arithmetic  13.7 us (8%)
  local copies, waits for them, and re-layouts  4.05 us (2%)
    all_to_all x2, blocking collectives, body(): packed = jnp.sum(lax.all_to_all(spread, 'z', 0, 0), axis=0)  41.9 us
    ppermute x21, starting transfers between devices, swap(): return lax.ppermute(value, axis, [(i, i ^ offset) for i in range(count)])  35.1 us
    ppermute x21, waiting for transfers between devices, swap(): return lax.ppermute(value, axis, [(i, i ^ offset) for i in range(count)])  29.3 us
    dot_general x3, matrix products, project(): lax.dot_general(left, affinity, (((1,), (1,)), ((), ())), preferred_eleme...  17.3 us
    all_to_all x1, waiting for transfers between devices, body(): gram = jnp.sum(lax.all_to_all(spread, ('x', 'z'), 0, 0), axis=0)[:, :K]  10.3 us
    dot_general x2, matrix products, body(): jnp.dot(jnp.concatenate([high, low], axis=0), affinity, preferred_element...  9.87 us
    another operation x9, other arithmetic, body(): lower = jnp.linalg.cholesky(gram)  6.39 us
    another operation x5, other arithmetic, lower_solve(): return lax.linalg.triangular_solve(lower, right, left_side=True, lower=True)  4.98 us
  transfers between devices with their start and end apart: 22, of which 20 were waited for; matrix products, arithmetic and copies ran while one was open for 0% of the time, Pallas kernels for 0%

profile of v1, /device:TPU:1, one launch (start us, length us, event | category | flops | bytes accessed | tf_op | source)
XLA Modules:
  0.0 168.8 jit_solution(921812750268577194)
XLA Ops:
  1.3 6.0 %fusion.23 = f32[16,4096]{1,0:T(8,128)S(1)} fusion(bf16[4096,1024]{1,0:T(8,128)(2,1)} %param.6, s32[1024]{0:T(1024)S(1)} %broadcast_multiply_fusion, s32[16]{0:T(128)} %param.7), kind=kOutput, calls=%fused_computation.58 | convolution fusion | flops 134709248 | bytes 8654912 | tf_op jit(solution)/shard_map/dot_general | solution.py:71
  7.8 3.3 %collective-permute-start = (f32[16,4,512]{2,0,1:T(8,128)S(1)}, f32[16,4,512]{2,0,1:T(8,128)S(1)}, u32[]{:S(2)}, u32[]{:S(2)}) collective-permute-start(f32[16,4,512]{2,0,1:T(8,128)S(1)} %select_bitcast_fusion.6), channel_id=1, source_target_pairs={{0,1},{1,0},{2,3},{3,2},{4,5},{5,4},{6,7},{7,6},{8,9},{9,8},{10,11... | collective-permute-start | bytes 393224 | tf_op jit(solution)/shard_map/ppermute | solution.py:44
  11.2 1.0 collective-permute-done
  12.3 1.1 collective-permute-start.3
  13.4 2.9 %collective-permute-start.1 = (f32[16,4,512]{2,0,1:T(8,128)S(1)}, f32[16,4,512]{2,0,1:T(8,128)S(1)}, u32[]{:S(2)}, u32[]{:S(2)}) collective-permute-start(f32[16,4,512]{2,0,1:T(8,128)S(1)} %bitcast_add_fusion.2), channel_id=1, source_target_pairs={{0,4},{2,6},{4,0},{6,2},{1,5},{3,7},{5,1},{7,3},{8,12},{10,14},{12... | collective-permute-start | bytes 393224 | tf_op jit(solution)/shard_map/ppermute | solution.py:44
  16.2 2.1 %collective-permute-done.3 = f32[16,4,512]{2,0,1:T(8,128)S(1)} collective-permute-done((f32[16,4,512]{2,0,1:T(8,128)S(1)}, f32[16,4,512]{2,0,1:T(8,128)S(1)}, u32[]{:S(2)}, u32[]{:S(2)}) %collective-permute-start.3) | collective-permute-done | bytes 131104 | tf_op jit(solution)/shard_map/ppermute | solution.py:44
  18.3 3.7 %collective-permute-done.1 = f32[16,4,512]{2,0,1:T(8,128)S(1)} collective-permute-done((f32[16,4,512]{2,0,1:T(8,128)S(1)}, f32[16,4,512]{2,0,1:T(8,128)S(1)}, u32[]{:S(2)}, u32[]{:S(2)}) %collective-permute-start.1) | collective-permute-done | bytes 131104 | tf_op jit(solution)/shard_map/ppermute | solution.py:44
  22.0 1.6 collective-permute-start.4
  23.6 1.0 collective-permute-done.4
  25.6 4.9 %fusion = f32[32,1024]{1,0:T(8,128)S(1)} fusion(bf16[4096,1024]{1,0:T(8,128)(2,1)} %param.6, bf16[16,4096]{1,0:T(8,128)(2,1)S(1)} %get-tuple-element.12, bf16[16,4096]{1,0:T(8,128)(2,1)S(1)} %get-tuple-element.13), kind=kOutput, calls=%fused_computation.9 | convolution fusion | flops 268959744 | bytes 8781824 | tf_op jit(solution)/shard_map/dot_general | solution.py:94
  30.6 0.9 collective-permute-start.7
  31.6 3.0 %collective-permute-start.5 = (f32[16,1152]{1,0:T(8,128)S(1)}, f32[16,1152]{1,0:T(8,128)S(1)}, u32[]{:S(2)}, u32[]{:S(2)}) collective-permute-start(f32[16,1152]{1,0:T(8,128)S(1)} %concatenate.13), channel_id=1, source_target_pairs={{0,128},{64,192},{128,0},{192,64},{1,129},{65,193},{129,1},{193,65... | collective-permute-start | bytes 221192 | tf_op jit(solution)/shard_map/ppermute | solution.py:44
  35.1 2.4 %collective-permute-done.5 = f32[16,1152]{1,0:T(8,128)S(1)} collective-permute-done((f32[16,1152]{1,0:T(8,128)S(1)}, f32[16,1152]{1,0:T(8,128)S(1)}, u32[]{:S(2)}, u32[]{:S(2)}) %collective-permute-start.5) | collective-permute-done | bytes 73760 | tf_op jit(solution)/shard_map/ppermute | solution.py:44
  37.6 22.7 %all_to_all.15 = f32[8,16,1152]{2,1,0:T(8,128)S(1)} all-to-all(f32[8,16,1152]{2,1,0:T(8,128)S(1)} %broadcast_in_dim.6), channel_id=1, replica_groups=mesh['x'=4,'z'=8,'y'=4,'core'=2] {'z'}, dimensions={0} | all-to-all | bytes 1179648 | tf_op jit(solution)/shard_map/all_to_all | solution.py:101
  60.4 1.5 cholesky.59
  63.2 1.2 custom-call.10
  64.7 5.7 %convolution_multiply_fusion.1 = f32[16,4096]{1,0:T(8,128)S(1)} fusion(bf16[16,1024]{1,0:T(8,128)(2,1)S(1)} %convolution_convert_fusion.1, bf16[4096,1024]{1,0:T(8,128)(2,1)} %param.6), kind=kOutput, calls=%fused_computation.1 | convolution fusion | flops 134283264 | bytes 8683520 | tf_op jit(solution)/shard_map/dot_general | solution.py:71
  70.9 4.2 %collective-permute-start.8 = (f32[16,4,512]{2,0,1:T(8,128)S(1)}, f32[16,4,512]{2,0,1:T(8,128)S(1)}, u32[]{:S(2)}, u32[]{:S(2)}) collective-permute-start(f32[16,4,512]{2,0,1:T(8,128)S(1)} %select_bitcast_fusion.3), channel_id=1, source_target_pairs={{0,1},{1,0},{2,3},{3,2},{4,5},{5,4},{6,7},{7,6},{8,9},{9,8},{10,11... | collective-permute-start | bytes 393224 | tf_op jit(solution)/shard_map/ppermute | solution.py:44
  75.2 1.0 collective-permute-done.8
  76.3 2.7 %collective-permute-start.11 = (f32[16,4,512]{2,0,1:T(8,128)S(1)}, f32[16,4,512]{2,0,1:T(8,128)S(1)}, u32[]{:S(2)}, u32[]{:S(2)}) collective-permute-start(f32[16,4,512]{2,0,1:T(8,128)S(1)} %bitcast_add_fusion.1), channel_id=1, source_target_pairs={{0,6},{2,4},{4,2},{6,0},{1,7},{3,5},{5,3},{7,1},{8,14},{10,12},{12... | collective-permute-start | bytes 393224 | tf_op jit(solution)/shard_map/ppermute | solution.py:44
  78.9 1.3 collective-permute-start.9
  80.2 2.1 %collective-permute-done.11 = f32[16,4,512]{2,0,1:T(8,128)S(1)} collective-permute-done((f32[16,4,512]{2,0,1:T(8,128)S(1)}, f32[16,4,512]{2,0,1:T(8,128)S(1)}, u32[]{:S(2)}, u32[]{:S(2)}) %collective-permute-start.11) | collective-permute-done | bytes 131104 | tf_op jit(solution)/shard_map/ppermute | solution.py:44
  82.3 1.0 collective-permute-done.10
  83.3 2.6 %collective-permute-done.9 = f32[16,4,512]{2,0,1:T(8,128)S(1)} collective-permute-done((f32[16,4,512]{2,0,1:T(8,128)S(1)}, f32[16,4,512]{2,0,1:T(8,128)S(1)}, u32[]{:S(2)}, u32[]{:S(2)}) %collective-permute-start.9) | collective-permute-done | bytes 131104 | tf_op jit(solution)/shard_map/ppermute | solution.py:44
  86.0 1.6 collective-permute-start.12
  87.6 1.0 collective-permute-done.12
  89.6 4.9 %fusion.4 = f32[32,1024]{1,0:T(8,128)S(1)} fusion(bf16[4096,1024]{1,0:T(8,128)(2,1)} %param.6, bf16[16,4096]{1,0:T(8,128)(2,1)S(1)} %get-tuple-element.10, bf16[16,4096]{1,0:T(8,128)(2,1)S(1)} %get-tuple-element.11), kind=kOutput, calls=%fused_computation.14 | convolution fusion | flops 268959744 | bytes 8781824 | tf_op jit(solution)/shard_map/dot_general | solution.py:94
  94.6 1.9 %collective-permute-start.15 = (f32[16,1152]{1,0:T(8,128)S(1)}, f32[16,1152]{1,0:T(8,128)S(1)}, u32[]{:S(2)}, u32[]{:S(2)}) collective-permute-start(f32[16,1152]{1,0:T(8,128)S(1)} %concatenate.15), channel_id=1, source_target_pairs={{0,192},{64,128},{128,64},{192,0},{1,193},{65,129},{129,65},{193,1... | collective-permute-start | bytes 221192 | tf_op jit(solution)/shard_map/ppermute | solution.py:44
  96.5 2.0 %collective-permute-start.13 = (f32[16,1152]{1,0:T(8,128)S(1)}, f32[16,1152]{1,0:T(8,128)S(1)}, u32[]{:S(2)}, u32[]{:S(2)}) collective-permute-start(f32[16,1152]{1,0:T(8,128)S(1)} %concatenate.15), channel_id=1, source_target_pairs={{0,128},{64,192},{128,0},{192,64},{1,129},{65,193},{129,1},{193,65... | collective-permute-start | bytes 221192 | tf_op jit(solution)/shard_map/ppermute | solution.py:44
  99.1 0.9 collective-permute-done.14
  100.0 1.8 %collective-permute-done.13 = f32[16,1152]{1,0:T(8,128)S(1)} collective-permute-done((f32[16,1152]{1,0:T(8,128)S(1)}, f32[16,1152]{1,0:T(8,128)S(1)}, u32[]{:S(2)}, u32[]{:S(2)}) %collective-permute-start.13) | collective-permute-done | bytes 73760 | tf_op jit(solution)/shard_map/ppermute | solution.py:44
  101.9 19.2 %all_to_all.16 = f32[8,16,1152]{2,1,0:T(8,128)S(1)} all-to-all(f32[8,16,1152]{2,1,0:T(8,128)S(1)} %broadcast_in_dim.8), channel_id=1, replica_groups=mesh['x'=4,'z'=8,'y'=4,'core'=2] {'z'}, dimensions={0} | all-to-all | bytes 1179648 | tf_op jit(solution)/shard_map/all_to_all | solution.py:101
  121.2 1.5 cholesky.70
  124.0 1.2 custom-call.11
  125.5 5.7 %convolution_multiply_fusion = f32[16,4096]{1,0:T(8,128)S(1)} fusion(bf16[16,1024]{1,0:T(8,128)(2,1)S(1)} %convolution_convert_fusion, bf16[4096,1024]{1,0:T(8,128)(2,1)} %param.6), kind=kOutput, calls=%fused_computation | convolution fusion | flops 134283264 | bytes 8683520 | tf_op jit(solution)/shard_map/dot_general | solution.py:71
  131.7 3.2 %collective-permute-start.16 = (f32[16,4,512]{2,0,1:T(8,128)S(1)}, f32[16,4,512]{2,0,1:T(8,128)S(1)}, u32[]{:S(2)}, u32[]{:S(2)}) collective-permute-start(f32[16,4,512]{2,0,1:T(8,128)S(1)} %select_bitcast_fusion), channel_id=1, source_target_pairs={{0,1},{1,0},{2,3},{3,2},{4,5},{5,4},{6,7},{7,6},{8,9},{9,8},{10,11... | collective-permute-start | bytes 393224 | tf_op jit(solution)/shard_map/ppermute | solution.py:44
  134.8 1.0 collective-permute-done.16
  135.9 2.7 %collective-permute-start.19 = (f32[16,4,512]{2,0,1:T(8,128)S(1)}, f32[16,4,512]{2,0,1:T(8,128)S(1)}, u32[]{:S(2)}, u32[]{:S(2)}) collective-permute-start(f32[16,4,512]{2,0,1:T(8,128)S(1)} %bitcast_add_fusion), channel_id=1, source_target_pairs={{0,6},{2,4},{4,2},{6,0},{1,7},{3,5},{5,3},{7,1},{8,14},{10,12},{12... | collective-permute-start | bytes 393224 | tf_op jit(solution)/shard_map/ppermute | solution.py:44
  138.6 1.3 collective-permute-start.17
  139.9 2.1 %collective-permute-done.19 = f32[16,4,512]{2,0,1:T(8,128)S(1)} collective-permute-done((f32[16,4,512]{2,0,1:T(8,128)S(1)}, f32[16,4,512]{2,0,1:T(8,128)S(1)}, u32[]{:S(2)}, u32[]{:S(2)}) %collective-permute-start.19) | collective-permute-done | bytes 131104 | tf_op jit(solution)/shard_map/ppermute | solution.py:44
  141.9 1.1 collective-permute-done.18
  143.0 2.6 %collective-permute-done.17 = f32[16,4,512]{2,0,1:T(8,128)S(1)} collective-permute-done((f32[16,4,512]{2,0,1:T(8,128)S(1)}, f32[16,4,512]{2,0,1:T(8,128)S(1)}, u32[]{:S(2)}, u32[]{:S(2)}) %collective-permute-start.17) | collective-permute-done | bytes 131104 | tf_op jit(solution)/shard_map/ppermute | solution.py:44
  145.9 1.6 collective-permute-start.20
  149.0 3.9 %all-to-all-start.2 = ((f32[32,16,128]{2,1,0:T(8,128)}), f32[32,16,128]{2,1,0:T(8,128)S(1)}, u32[]{:S(2)}, u32[]{:S(2)}) async-start(f32[32,16,128]{2,1,0:T(8,128)} %broadcast_in_dim.9), calls=%async_computation.2 | async-start | bytes 524288 | tf_op jit(solution)/shard_map/all_to_all | solution.py:111
  152.9 10.3 %all-to-all-done.2 = f32[32,16,128]{2,1,0:T(8,128)S(1)} async-done(((f32[32,16,128]{2,1,0:T(8,128)}), f32[32,16,128]{2,1,0:T(8,128)S(1)}, u32[]{:S(2)}, u32[]{:S(2)}) %all-to-all-start.2) | async-done | bytes 262176 | tf_op jit(solution)/shard_map/all_to_all | solution.py:111
  163.3 1.5 cholesky.81
  166.7 1.2 custom-call.8
  168.0 0.9 convolution_multiply_fusion.2
  (74 shorter events, 13.3 us)
Async XLA Ops:
  7.8 4.3 %collective-permute-start = (f32[16,4,512]{2,0,1:T(8,128)S(1)}, f32[16,4,512]{2,0,1:T(8,128)S(1)}, u32[]{:S(2)}, u32[]{:S(2)}) collective-permute-start(f32[16,4,512]{2,0,1:T(8,128)S(1)} %select_bitcast_fusion.6), channel_id=1, source_target_pairs={{0,1},{1,0},{2,3},{3,2},{4,5},{5,4},{6,7},{7,6},{8,9},{9,8},{10,11... | collective-permute-start | bytes 393224 | tf_op jit(solution)/shard_map/ppermute | solution.py:44
  12.3 6.0 %collective-permute-start.3 = (f32[16,4,512]{2,0,1:T(8,128)S(1)}, f32[16,4,512]{2,0,1:T(8,128)S(1)}, u32[]{:S(2)}, u32[]{:S(2)}) collective-permute-start(f32[16,4,512]{2,0,1:T(8,128)S(1)} %bitcast_add_fusion.2), channel_id=1, source_target_pairs={{0,6},{2,4},{4,2},{6,0},{1,7},{3,5},{5,3},{7,1},{8,14},{10,12},{12... | collective-permute-start | bytes 393224 | tf_op jit(solution)/shard_map/ppermute | solution.py:44
  13.3 4.9 %collective-permute-start.2 = (f32[16,4,512]{2,0,1:T(8,128)S(1)}, f32[16,4,512]{2,0,1:T(8,128)S(1)}, u32[]{:S(2)}, u32[]{:S(2)}) collective-permute-start(f32[16,4,512]{2,0,1:T(8,128)S(1)} %bitcast_add_fusion.2), channel_id=1, source_target_pairs={{0,2},{2,0},{4,6},{6,4},{1,3},{3,1},{5,7},{7,5},{8,10},{10,8},{12,... | collective-permute-start | bytes 393224 | tf_op jit(solution)/shard_map/ppermute | solution.py:44
  13.4 8.6 %collective-permute-start.1 = (f32[16,4,512]{2,0,1:T(8,128)S(1)}, f32[16,4,512]{2,0,1:T(8,128)S(1)}, u32[]{:S(2)}, u32[]{:S(2)}) collective-permute-start(f32[16,4,512]{2,0,1:T(8,128)S(1)} %bitcast_add_fusion.2), channel_id=1, source_target_pairs={{0,4},{2,6},{4,0},{6,2},{1,5},{3,7},{5,1},{7,3},{8,12},{10,14},{12... | collective-permute-start | bytes 393224 | tf_op jit(solution)/shard_map/ppermute | solution.py:44
  22.0 2.6 %collective-permute-start.4 = (f32[16,4,512]{2,0,1:T(8,128)S(1)}, f32[16,4,512]{2,0,1:T(8,128)S(1)}, u32[]{:S(2)}, u32[]{:S(2)}) collective-permute-start(f32[16,4,512]{2,0,1:T(8,128)S(1)} %add_add_fusion.2), channel_id=1, source_target_pairs={{0,1},{1,0},{2,3},{3,2},{4,5},{5,4},{6,7},{7,6},{8,9},{9,8},{10,11... | collective-permute-start | bytes 393224 | tf_op jit(solution)/shard_map/ppermute | solution.py:44
  30.6 4.4 %collective-permute-start.7 = (f32[16,1152]{1,0:T(8,128)S(1)}, f32[16,1152]{1,0:T(8,128)S(1)}, u32[]{:S(2)}, u32[]{:S(2)}) collective-permute-start(f32[16,1152]{1,0:T(8,128)S(1)} %concatenate.13), channel_id=1, source_target_pairs={{0,192},{64,128},{128,64},{192,0},{1,193},{65,129},{129,65},{193,1... | collective-permute-start | bytes 221192 | tf_op jit(solution)/shard_map/ppermute | solution.py:44
  31.6 3.5 %collective-permute-start.6 = (f32[16,1152]{1,0:T(8,128)S(1)}, f32[16,1152]{1,0:T(8,128)S(1)}, u32[]{:S(2)}, u32[]{:S(2)}) collective-permute-start(f32[16,1152]{1,0:T(8,128)S(1)} %concatenate.13), channel_id=1, source_target_pairs={{0,64},{64,0},{128,192},{192,128},{1,65},{65,1},{129,193},{193,129... | collective-permute-start | bytes 221192 | tf_op jit(solution)/shard_map/ppermute | solution.py:44
  31.6 5.9 %collective-permute-start.5 = (f32[16,1152]{1,0:T(8,128)S(1)}, f32[16,1152]{1,0:T(8,128)S(1)}, u32[]{:S(2)}, u32[]{:S(2)}) collective-permute-start(f32[16,1152]{1,0:T(8,128)S(1)} %concatenate.13), channel_id=1, source_target_pairs={{0,128},{64,192},{128,0},{192,64},{1,129},{65,193},{129,1},{193,65... | collective-permute-start | bytes 221192 | tf_op jit(solution)/shard_map/ppermute | solution.py:44
  70.9 5.2 %collective-permute-start.8 = (f32[16,4,512]{2,0,1:T(8,128)S(1)}, f32[16,4,512]{2,0,1:T(8,128)S(1)}, u32[]{:S(2)}, u32[]{:S(2)}) collective-permute-start(f32[16,4,512]{2,0,1:T(8,128)S(1)} %select_bitcast_fusion.3), channel_id=1, source_target_pairs={{0,1},{1,0},{2,3},{3,2},{4,5},{5,4},{6,7},{7,6},{8,9},{9,8},{10,11... | collective-permute-start | bytes 393224 | tf_op jit(solution)/shard_map/ppermute | solution.py:44
  76.3 6.0 %collective-permute-start.11 = (f32[16,4,512]{2,0,1:T(8,128)S(1)}, f32[16,4,512]{2,0,1:T(8,128)S(1)}, u32[]{:S(2)}, u32[]{:S(2)}) collective-permute-start(f32[16,4,512]{2,0,1:T(8,128)S(1)} %bitcast_add_fusion.1), channel_id=1, source_target_pairs={{0,6},{2,4},{4,2},{6,0},{1,7},{3,5},{5,3},{7,1},{8,14},{10,12},{12... | collective-permute-start | bytes 393224 | tf_op jit(solution)/shard_map/ppermute | solution.py:44
  78.9 4.4 %collective-permute-start.10 = (f32[16,4,512]{2,0,1:T(8,128)S(1)}, f32[16,4,512]{2,0,1:T(8,128)S(1)}, u32[]{:S(2)}, u32[]{:S(2)}) collective-permute-start(f32[16,4,512]{2,0,1:T(8,128)S(1)} %bitcast_add_fusion.1), channel_id=1, source_target_pairs={{0,2},{2,0},{4,6},{6,4},{1,3},{3,1},{5,7},{7,5},{8,10},{10,8},{12,... | collective-permute-start | bytes 393224 | tf_op jit(solution)/shard_map/ppermute | solution.py:44
  78.9 7.0 %collective-permute-start.9 = (f32[16,4,512]{2,0,1:T(8,128)S(1)}, f32[16,4,512]{2,0,1:T(8,128)S(1)}, u32[]{:S(2)}, u32[]{:S(2)}) collective-permute-start(f32[16,4,512]{2,0,1:T(8,128)S(1)} %bitcast_add_fusion.1), channel_id=1, source_target_pairs={{0,4},{2,6},{4,0},{6,2},{1,5},{3,7},{5,1},{7,3},{8,12},{10,14},{12... | collective-permute-start | bytes 393224 | tf_op jit(solution)/shard_map/ppermute | solution.py:44
  86.0 2.6 %collective-permute-start.12 = (f32[16,4,512]{2,0,1:T(8,128)S(1)}, f32[16,4,512]{2,0,1:T(8,128)S(1)}, u32[]{:S(2)}, u32[]{:S(2)}) collective-permute-start(f32[16,4,512]{2,0,1:T(8,128)S(1)} %add_add_fusion.1), channel_id=1, source_target_pairs={{0,1},{1,0},{2,3},{3,2},{4,5},{5,4},{6,7},{7,6},{8,9},{9,8},{10,11... | collective-permute-start | bytes 393224 | tf_op jit(solution)/shard_map/ppermute | solution.py:44
  94.6 4.4 %collective-permute-start.15 = (f32[16,1152]{1,0:T(8,128)S(1)}, f32[16,1152]{1,0:T(8,128)S(1)}, u32[]{:S(2)}, u32[]{:S(2)}) collective-permute-start(f32[16,1152]{1,0:T(8,128)S(1)} %concatenate.15), channel_id=1, source_target_pairs={{0,192},{64,128},{128,64},{192,0},{1,193},{65,129},{129,65},{193,1... | collective-permute-start | bytes 221192 | tf_op jit(solution)/shard_map/ppermute | solution.py:44
  96.5 3.5 %collective-permute-start.14 = (f32[16,1152]{1,0:T(8,128)S(1)}, f32[16,1152]{1,0:T(8,128)S(1)}, u32[]{:S(2)}, u32[]{:S(2)}) collective-permute-start(f32[16,1152]{1,0:T(8,128)S(1)} %concatenate.15), channel_id=1, source_target_pairs={{0,64},{64,0},{128,192},{192,128},{1,65},{65,1},{129,193},{193,129... | collective-permute-start | bytes 221192 | tf_op jit(solution)/shard_map/ppermute | solution.py:44
  96.5 5.3 %collective-permute-start.13 = (f32[16,1152]{1,0:T(8,128)S(1)}, f32[16,1152]{1,0:T(8,128)S(1)}, u32[]{:S(2)}, u32[]{:S(2)}) collective-permute-start(f32[16,1152]{1,0:T(8,128)S(1)} %concatenate.15), channel_id=1, source_target_pairs={{0,128},{64,192},{128,0},{192,64},{1,129},{65,193},{129,1},{193,65... | collective-permute-start | bytes 221192 | tf_op jit(solution)/shard_map/ppermute | solution.py:44
  131.7 4.1 %collective-permute-start.16 = (f32[16,4,512]{2,0,1:T(8,128)S(1)}, f32[16,4,512]{2,0,1:T(8,128)S(1)}, u32[]{:S(2)}, u32[]{:S(2)}) collective-permute-start(f32[16,4,512]{2,0,1:T(8,128)S(1)} %select_bitcast_fusion), channel_id=1, source_target_pairs={{0,1},{1,0},{2,3},{3,2},{4,5},{5,4},{6,7},{7,6},{8,9},{9,8},{10,11... | collective-permute-start | bytes 393224 | tf_op jit(solution)/shard_map/ppermute | solution.py:44
  135.9 6.0 %collective-permute-start.19 = (f32[16,4,512]{2,0,1:T(8,128)S(1)}, f32[16,4,512]{2,0,1:T(8,128)S(1)}, u32[]{:S(2)}, u32[]{:S(2)}) collective-permute-start(f32[16,4,512]{2,0,1:T(8,128)S(1)} %bitcast_add_fusion), channel_id=1, source_target_pairs={{0,6},{2,4},{4,2},{6,0},{1,7},{3,5},{5,3},{7,1},{8,14},{10,12},{12... | collective-permute-start | bytes 393224 | tf_op jit(solution)/shard_map/ppermute | solution.py:44
  138.6 4.4 %collective-permute-start.18 = (f32[16,4,512]{2,0,1:T(8,128)S(1)}, f32[16,4,512]{2,0,1:T(8,128)S(1)}, u32[]{:S(2)}, u32[]{:S(2)}) collective-permute-start(f32[16,4,512]{2,0,1:T(8,128)S(1)} %bitcast_add_fusion), channel_id=1, source_target_pairs={{0,2},{2,0},{4,6},{6,4},{1,3},{3,1},{5,7},{7,5},{8,10},{10,8},{12,... | collective-permute-start | bytes 393224 | tf_op jit(solution)/shard_map/ppermute | solution.py:44
  138.6 7.0 %collective-permute-start.17 = (f32[16,4,512]{2,0,1:T(8,128)S(1)}, f32[16,4,512]{2,0,1:T(8,128)S(1)}, u32[]{:S(2)}, u32[]{:S(2)}) collective-permute-start(f32[16,4,512]{2,0,1:T(8,128)S(1)} %bitcast_add_fusion), channel_id=1, source_target_pairs={{0,4},{2,6},{4,0},{6,2},{1,5},{3,7},{5,1},{7,3},{8,12},{10,14},{12... | collective-permute-start | bytes 393224 | tf_op jit(solution)/shard_map/ppermute | solution.py:44
  145.9 2.4 %collective-permute-start.20 = (f32[16,16]{1,0:T(8,128)S(1)}, f32[16,16]{1,0:T(8,128)S(1)}, u32[]{:S(2)}, u32[]{:S(2)}) collective-permute-start(f32[16,16]{1,0:T(8,128)S(1)} %convolution_bitcast_fusion), channel_id=1, source_target_pairs={{0,1},{1,0},{2,3},{3,2},{4,5},{5,4},{6,7},{7,6},{8,9},{9,8},{10,11... | collective-permute-start | bytes 3080 | tf_op jit(solution)/shard_map/ppermute | solution.py:44
  149.0 14.1 %all-to-all-start.2 = ((f32[32,16,128]{2,1,0:T(8,128)}), f32[32,16,128]{2,1,0:T(8,128)S(1)}, u32[]{:S(2)}, u32[]{:S(2)}) async-start(f32[32,16,128]{2,1,0:T(8,128)} %broadcast_in_dim.9), calls=%async_computation.2 | async-start | bytes 524288 | tf_op jit(solution)/shard_map/all_to_all | solution.py:111

commit v2 on v1

v2 whole, which is shorter than its diff:
```python
import functools
import math

import jax
import jax.numpy as jnp
from jax import lax
from jax.experimental import pallas as pl
from jax.experimental.pallas import tpu as pltpu
from jax.sharding import Mesh, PartitionSpec as P

ITERS = 2
K = 16
PIECE = 512


mix_first = -2048144789
mix_second = -1028477387
golden = -1640531535
salt_value = 1540483477


def shifted(value, amount):
    return lax.shift_right_logical(value, jnp.full(value.shape, amount, jnp.int32))


def scramble(value):
    value = jnp.bitwise_xor(value, shifted(value, 16))
    value = value * jnp.int32(mix_first)
    value = jnp.bitwise_xor(value, shifted(value, 13))
    value = value * jnp.int32(mix_second)
    return jnp.bitwise_xor(value, shifted(value, 16))


def test_matrix(seed_values, sku_ids, total_columns):
    first = scramble(jnp.bitwise_xor(seed_values[:, None], sku_ids[None, :] * jnp.int32(golden)))
    second = scramble(jnp.bitwise_xor(first, jnp.int32(salt_value)))
    uniform_a = (shifted(first, 9) + 1).astype(jnp.float32) / 8388608.0
    uniform_b = (shifted(second, 9) + 1).astype(jnp.float32) / 8388608.0
    gauss = jnp.sqrt(-2.0 * jnp.log(uniform_a)) * jnp.cos(6.283185307179586 * uniform_b)
    return (gauss / math.sqrt(total_columns)).astype(jnp.bfloat16)


def swap(value, axis, count, offset):
    return lax.ppermute(value, axis, [(i, i ^ offset) for i in range(count)])


def sum_four(value, axis, count):
    one, two, three = (swap(value, axis, count, k) for k in (1, 2, 3))
    return (value + two) + (one + three)


def block_rows(piece, core):
    return pl.ds(pl.multiple_of((2 * piece + core) * PIECE, PIECE), PIECE)


def project_into(left, affinity, own, other, scale):
    core = lax.axis_index("core")
    for target, side in ((other, 1 - core), (own, core)):
        for step in range(4):
            part = lax.dot_general(
                left,
                affinity[block_rows(step, side), :],
                (((1,), (1,)), ((), ())),
                preferred_element_type=jnp.float32,
            )
            if scale is not None:
                part = part * scale
            target[:, step * PIECE : (step + 1) * PIECE] = part


def eliminate(gram, right):
    row = lax.broadcasted_iota(jnp.int32, (K, 128), 0)
    lane = lax.broadcasted_iota(jnp.int32, (K, 128), 1)
    columns = [jnp.broadcast_to(gram[:, k : k + 1], (K, 128)) for k in range(K)]
    lower = jnp.zeros((K, 128), jnp.float32)
    pivots = jnp.ones((K, 128), jnp.float32)
    for k in range(K):
        column = columns[k]
        pivot = jnp.broadcast_to(column[k : k + 1, :], (K, 128))
        factor = column * (1.0 / pivot)
        lower = jnp.where((lane == k) & (row >= k), column / jnp.sqrt(pivot), lower)
        pivots = jnp.where(row == k, pivot, pivots)
        factor = jnp.where(row > k, factor, 0.0)
        for j in range(k + 1, K):
            columns[j] = columns[j] - factor * jnp.broadcast_to(column[j : j + 1, :], (K, 128))
        wide = jnp.tile(factor, (1, right.shape[1] // 128))
        right = right - wide * right[k : k + 1, :]
    root = jnp.sqrt(pivots)
    return lower, right / jnp.tile(root, (1, right.shape[1] // 128))


def first_kernel(omega, affinity, own, other):
    project_into(omega[...], affinity, own, other, None)


def back_kernel(own, sibling, affinity, packed):
    core = lax.axis_index("core")
    both = jnp.zeros((2 * K, affinity.shape[1]), jnp.float32)
    gram = jnp.zeros((3 * K, 3 * K), jnp.float32)
    for source, side in ((own, core), (sibling, 1 - core)):
        for step in range(4):
            value = source[:, step * PIECE : (step + 1) * PIECE]
            high = value.astype(jnp.bfloat16)
            rest = value - high.astype(jnp.float32)
            low = rest.astype(jnp.bfloat16)
            last = (rest - low.astype(jnp.float32)).astype(jnp.bfloat16)
            pair = jnp.concatenate([high, low], axis=0)
            triple = jnp.concatenate([pair, last], axis=0)
            both += jnp.dot(
                pair, affinity[block_rows(step, side), :], preferred_element_type=jnp.float32
            )
            gram += lax.dot_general(
                triple, triple, (((1,), (1,)), ((), ())), preferred_element_type=jnp.float32
            )
    wide = affinity.shape[1]
    packed[:, :wide] = both[:K] + both[K:]
    rows = (gram[2 * K :] + gram[K : 2 * K]) + gram[:K]
    packed[:, wide:] = jnp.zeros((K, 128), jnp.float32)
    packed[:, wide : wide + K] = (rows[:, 2 * K :] + rows[:, K : 2 * K]) + rows[:, :K]


def solve_kernel(mine, theirs, affinity, own, other, *, scale):
    wide = affinity.shape[1]
    total = mine[...] + theirs[...]
    _, back = eliminate(total[:, wide:], total[:, :wide])
    project_into(back.astype(jnp.bfloat16), affinity, own, other, scale)


def last_kernel(grams, half, basis, factor, *, scale):
    gram = jnp.sum(grams[...], axis=0)
    place = pl.multiple_of(lax.axis_index("y") * PIECE, PIECE)
    lower, ortho = eliminate(gram, half[:, pl.ds(place, PIECE)])
    basis[...] = ortho * scale
    factor[...] = lower.T[:K, :] / scale


def call(kernel, outs, *args):
    whole = pl.BlockSpec(memory_space=pltpu.VMEM)
    return pl.pallas_call(
        kernel,
        in_specs=[whole] * len(args),
        out_specs=[whole] * len(outs),
        out_shape=[jax.ShapeDtypeStruct(shape, jnp.float32) for shape in outs],
        compiler_params=pltpu.CompilerParams(vmem_limit_bytes=32 * 1024 * 1024),
    )(*args)


def body(affinity, seed_values, sku_ids):
    local_rows, local_columns = affinity.shape
    total_columns = local_columns * 8
    total_rows = local_rows * 32
    half_shape = (K, local_rows // 2)
    packed_shape = (K, local_columns + 128)

    omega = test_matrix(seed_values, sku_ids, total_columns)
    own, other = call(first_kernel, [half_shape] * 2, omega, affinity)
    for repeat in range(ITERS + 1):
        half = sum_four(own + swap(other, "core", 2, 1), "y", 4)
        if repeat < ITERS:
            sibling = swap(half, "core", 2, 1)
            (packed,) = call(back_kernel, [packed_shape], half, sibling, affinity)
            packed = sum_four(packed, "x", 4)
            packed = sum_four(packed, "z", 8)
            own, other = call(
                functools.partial(solve_kernel, scale=1.0 / math.sqrt(total_columns)),
                [half_shape] * 2,
                packed,
                swap(packed, "z", 8, 6),
                affinity,
            )
        else:
            gram = lax.dot_general(
                half,
                half,
                (((1,), (1,)), ((), ())),
                precision=lax.Precision.HIGHEST,
                preferred_element_type=jnp.float32,
            )
            gram = gram + swap(gram, "core", 2, 1)
            gram = jnp.pad(gram, ((0, 0), (0, 128 - K)))
            spread = jnp.broadcast_to(gram[None], (32,) + gram.shape)
            grams = lax.all_to_all(spread, ("x", "z"), 0, 0)
            basis, factor = call(
                functools.partial(last_kernel, scale=math.sqrt(total_rows)),
                [(K, PIECE), (K, K)],
                grams,
                half,
            )
    return basis, factor


def solution(mesh):
    split = Mesh(mesh.devices.reshape(4, 8, 4, 2), ("x", "z", "y", "core"))
    row, col = ("x", "z"), ("y", "core")
    return jax.shard_map(
        body,
        mesh=split,
        in_specs=(P(row, col), P(), P(col)),
        out_specs=(P(None, row + col), P()),
        check_vma=False,
    )
```

time: 171 us -> 130 us (0.76)
  matrix products: 29.7 us -> 0.22 us
  blocking collectives: 41.9 us -> 16.7 us
  other arithmetic: 13.7 us -> 1.96 us
  Pallas kernels: 0 us -> 11.3 us
  starting transfers between devices: 39 us -> 48.9 us
  waiting for transfers between devices: 39.6 us -> 44.2 us
    dot_general x8 -> x1, matrix products: 28.3 us -> 0.22 us  [body(): lax.dot_general(half, half, (((1,), (1,)), ((), ())), precision=lax.Preci...]
    all_to_all x2 -> x1, blocking collectives: 41.9 us -> 16.7 us  [body(): grams = lax.all_to_all(spread, ('x', 'z'), 0, 0)]
    ppermute x21 -> x29, waiting for transfers between devices: 29.3 us -> 44.2 us  [swap(): return lax.ppermute(value, axis, [(i, i ^ offset) for i in range(count)])]
    ppermute x21 -> x29, starting transfers between devices: 35.1 us -> 48.9 us  [swap(): return lax.ppermute(value, axis, [(i, i ^ offset) for i in range(count)])]
    another operation x18 -> x0, other arithmetic: 11.5 us -> none  [the longest x9 6.39 us: body(): lower = jnp.linalg.cholesky(gram)]
    pallas_call x0 -> x6, Pallas kernels: none -> 11.3 us  [call(): pl.pallas_call(kernel, in_specs=[whole] * len(args), out_specs=[whole] *...]
    all_to_all x1 -> x0, waiting for transfers between devices: 10.3 us -> none  [body(): gram = jnp.sum(lax.all_to_all(spread, ('x', 'z'), 0, 0), axis=0)[:, :K]]
    all_to_all x1 -> x0, starting transfers between devices: 3.87 us -> none  [body(): gram = jnp.sum(lax.all_to_all(spread, ('x', 'z'), 0, 0), axis=0)[:, :K]]
  transfers between devices with their start and end apart: 22 -> 29, of which waited for: 20 -> 27; matrix products, arithmetic and copies ran while one was open for 0% -> 0% of each run, Pallas kernels for 0% -> 0%
where the time goes in v2:
time: 130 us; the launch traced here: 127 us
  starting transfers between devices  48.9 us (38%)
  waiting for transfers between devices  44.2 us (34%)
  blocking collectives  16.7 us (13%)
  Pallas kernels  11.3 us (9%)
  local copies, waits for them, and re-layouts  3.41 us (3%)
  other arithmetic  1.96 us (2%)
    ppermute x29, starting transfers between devices, swap(): return lax.ppermute(value, axis, [(i, i ^ offset) for i in range(count)])  48.9 us
    ppermute x29, waiting for transfers between devices, swap(): return lax.ppermute(value, axis, [(i, i ^ offset) for i in range(count)])  44.2 us
    all_to_all x1, blocking collectives, body(): grams = lax.all_to_all(spread, ('x', 'z'), 0, 0)  16.7 us
    pallas_call x6, Pallas kernels, call(): pl.pallas_call(kernel, in_specs=[whole] * len(args), out_specs=[whole] *...  11.3 us
    unnamed x4, local copies, waits for them, and re-layouts  3.38 us
  transfers between devices with their start and end apart: 29, of which 27 were waited for; matrix products, arithmetic and copies ran while one was open for 0% of the time, Pallas kernels for 0%

profile of v2, /device:TPU:1, one launch (start us, length us, event | category | flops | bytes accessed | tf_op | source)
XLA Modules:
  0.0 127.4 jit_solution(17246782159539417102)
XLA Ops:
  1.3 1.0 fusion.11.omega
  2.4 3.4 %copy-done = bf16[4096,1024]{1,0:T(8,128)(2,1)S(1)} copy-done((bf16[4096,1024]{1,0:T(8,128)(2,1)S(1)}, bf16[4096,1024]{1,0:T(8,128)(2,1)}, u32[]{:S(2)}) %copy-start) | copy-done | bytes 8388632
  5.7 2.3 %shard_map.50 = (f32[16,2048]{1,0:T(8,128)S(1)}, f32[16,2048]{1,0:T(8,128)S(1)}) custom-call(bf16[16,1024]{1,0:T(8,128)(2,1)S(1)} %fusion.11.omega, bf16[4096,1024]{1,0:T(8,128)(2,1)S(1)} %copy-done), custom_call_target="tpu_custom_call" | custom-call | tf_op jit(solution)/shard_map/pallas_call | solution.py:139
  8.0 3.3 %collective-permute-start = (f32[16,2048]{1,0:T(8,128)S(1)}, f32[16,2048]{1,0:T(8,128)S(1)}, u32[]{:S(2)}, u32[]{:S(2)}) collective-permute-start(f32[16,2048]{1,0:T(8,128)S(1)} %get-tuple-element.9), channel_id=1, source_target_pairs={{0,1},{1,0},{2,3},{3,2},{4,5},{5,4},{6,7},{7,6},{8,9},{9,8},{10,11... | collective-permute-start | bytes 393224 | tf_op jit(solution)/shard_map/ppermute | solution.py:44
  12.3 1.1 collective-permute-start.3
  13.4 2.9 %collective-permute-start.1 = (f32[16,2048]{1,0:T(8,128)S(1)}, f32[16,2048]{1,0:T(8,128)S(1)}, u32[]{:S(2)}, u32[]{:S(2)}) collective-permute-start(f32[16,2048]{1,0:T(8,128)S(1)} %add.85), channel_id=1, source_target_pairs={{0,4},{2,6},{4,0},{6,2},{1,5},{3,7},{5,1},{7,3},{8,12},{10,14},{12... | collective-permute-start | bytes 393224 | tf_op jit(solution)/shard_map/ppermute | solution.py:44
  16.2 2.1 %collective-permute-done.3 = f32[16,2048]{1,0:T(8,128)S(1)} collective-permute-done((f32[16,2048]{1,0:T(8,128)S(1)}, f32[16,2048]{1,0:T(8,128)S(1)}, u32[]{:S(2)}, u32[]{:S(2)}) %collective-permute-start.3) | collective-permute-done | bytes 131104 | tf_op jit(solution)/shard_map/ppermute | solution.py:44
  18.3 3.7 %collective-permute-done.1 = f32[16,2048]{1,0:T(8,128)S(1)} collective-permute-done((f32[16,2048]{1,0:T(8,128)S(1)}, f32[16,2048]{1,0:T(8,128)S(1)}, u32[]{:S(2)}, u32[]{:S(2)}) %collective-permute-start.1) | collective-permute-done | bytes 131104 | tf_op jit(solution)/shard_map/ppermute | solution.py:44
  22.0 1.6 %collective-permute-start.4 = (f32[16,2048]{1,0:T(8,128)S(1)}, f32[16,2048]{1,0:T(8,128)S(1)}, u32[]{:S(2)}, u32[]{:S(2)}) collective-permute-start(f32[16,2048]{1,0:T(8,128)S(1)} %add_add_fusion.2.own), channel_id=1, source_target_pairs={{0,1},{1,0},{2,3},{3,2},{4,5},{5,4},{6,7},{7,6},{8,9},{9,8},{10,11... | collective-permute-start | bytes 393224 | tf_op jit(solution)/shard_map/ppermute | solution.py:44
  23.6 1.0 collective-permute-done.4.sibling
  24.6 1.6 %shard_map.51 = f32[16,1152]{1,0:T(8,128)S(1)} custom-call(f32[16,2048]{1,0:T(8,128)S(1)} %add_add_fusion.2.own, f32[16,2048]{1,0:T(8,128)S(1)} %collective-permute-done.4.sibling, bf16[4096,1024]{1,0:T(8,128)(2,1)S(1)} %copy-done.1), custom_call_target="tpu_custom_call" | custom-call | tf_op jit(solution)/shard_map/pallas_call | solution.py:139
  27.1 3.0 %collective-permute-start.5 = (f32[16,1152]{1,0:T(8,128)S(1)}, f32[16,1152]{1,0:T(8,128)S(1)}, u32[]{:S(2)}, u32[]{:S(2)}) collective-permute-start(f32[16,1152]{1,0:T(8,128)S(1)} %shard_map.51), channel_id=1, source_target_pairs={{0,128},{64,192},{128,0},{192,64},{1,129},{65,193},{129,1},{193,65... | collective-permute-start | bytes 221192 | tf_op jit(solution)/shard_map/ppermute | solution.py:44
  30.6 2.4 %collective-permute-done.5 = f32[16,1152]{1,0:T(8,128)S(1)} collective-permute-done((f32[16,1152]{1,0:T(8,128)S(1)}, f32[16,1152]{1,0:T(8,128)S(1)}, u32[]{:S(2)}, u32[]{:S(2)}) %collective-permute-start.5) | collective-permute-done | bytes 73760 | tf_op jit(solution)/shard_map/ppermute | solution.py:44
  33.0 3.5 %collective-permute-start.10 = (f32[16,1152]{1,0:T(8,128)S(1)}, f32[16,1152]{1,0:T(8,128)S(1)}, u32[]{:S(2)}, u32[]{:S(2)}) collective-permute-start(f32[16,1152]{1,0:T(8,128)S(1)} %add_add_fusion.6), channel_id=1, source_target_pairs={{0,24},{8,16},{16,8},{24,0},{32,56},{40,48},{48,40},{56,32},{1,25}... | collective-permute-start | bytes 221192 | tf_op jit(solution)/shard_map/ppermute | solution.py:44
  36.9 1.4 %collective-permute-done.10 = f32[16,1152]{1,0:T(8,128)S(1)} collective-permute-done((f32[16,1152]{1,0:T(8,128)S(1)}, f32[16,1152]{1,0:T(8,128)S(1)}, u32[]{:S(2)}, u32[]{:S(2)}) %collective-permute-start.10) | collective-permute-done | bytes 73760 | tf_op jit(solution)/shard_map/ppermute | solution.py:44
  38.3 3.0 %collective-permute-done.9 = f32[16,1152]{1,0:T(8,128)S(1)} collective-permute-done((f32[16,1152]{1,0:T(8,128)S(1)}, f32[16,1152]{1,0:T(8,128)S(1)}, u32[]{:S(2)}, u32[]{:S(2)}) %collective-permute-start.9) | collective-permute-done | bytes 73760 | tf_op jit(solution)/shard_map/ppermute | solution.py:44
  41.4 4.0 %collective-permute-start.11 = (f32[16,1152]{1,0:T(8,128)S(1)}, f32[16,1152]{1,0:T(8,128)S(1)}, u32[]{:S(2)}, u32[]{:S(2)}) collective-permute-start(f32[16,1152]{1,0:T(8,128)S(1)} %add_add_fusion.5.mine), channel_id=1, source_target_pairs={{0,48},{8,56},{16,32},{24,40},{32,16},{40,24},{48,0},{56,8},{1,49}... | collective-permute-start | bytes 221192 | tf_op jit(solution)/shard_map/ppermute | solution.py:44
  45.4 1.9 %collective-permute-done.11.theirs = f32[16,1152]{1,0:T(8,128)S(1)} collective-permute-done((f32[16,1152]{1,0:T(8,128)S(1)}, f32[16,1152]{1,0:T(8,128)S(1)}, u32[]{:S(2)}, u32[]{:S(2)}) %collective-permute-start.11) | collective-permute-done | bytes 73760 | tf_op jit(solution)/shard_map/ppermute | solution.py:44
  47.3 2.5 %shard_map.52 = (f32[16,2048]{1,0:T(8,128)S(1)}, f32[16,2048]{1,0:T(8,128)S(1)}) custom-call(f32[16,1152]{1,0:T(8,128)S(1)} %add_add_fusion.5.mine, f32[16,1152]{1,0:T(8,128)S(1)} %collective-permute-done.11.theirs, bf16[4096,1024]{1,0:T(8,128)(2,1)S(1)} %copy-done.1), custom_call_target="tpu_custom_call" | custom-call | tf_op jit(solution)/shard_map/pallas_call | solution.py:139
  49.8 4.0 %collective-permute-start.12 = (f32[16,2048]{1,0:T(8,128)S(1)}, f32[16,2048]{1,0:T(8,128)S(1)}, u32[]{:S(2)}, u32[]{:S(2)}) collective-permute-start(f32[16,2048]{1,0:T(8,128)S(1)} %get-tuple-element.11), channel_id=1, source_target_pairs={{0,1},{1,0},{2,3},{3,2},{4,5},{5,4},{6,7},{7,6},{8,9},{9,8},{10,11... | collective-permute-start | bytes 393224 | tf_op jit(solution)/shard_map/ppermute | solution.py:44
  53.8 1.0 collective-permute-done.12
  54.8 2.8 %collective-permute-start.15 = (f32[16,2048]{1,0:T(8,128)S(1)}, f32[16,2048]{1,0:T(8,128)S(1)}, u32[]{:S(2)}, u32[]{:S(2)}) collective-permute-start(f32[16,2048]{1,0:T(8,128)S(1)} %add.95), channel_id=1, source_target_pairs={{0,6},{2,4},{4,2},{6,0},{1,7},{3,5},{5,3},{7,1},{8,14},{10,12},{12... | collective-permute-start | bytes 393224 | tf_op jit(solution)/shard_map/ppermute | solution.py:44
  57.6 1.3 %collective-permute-start.13 = (f32[16,2048]{1,0:T(8,128)S(1)}, f32[16,2048]{1,0:T(8,128)S(1)}, u32[]{:S(2)}, u32[]{:S(2)}) collective-permute-start(f32[16,2048]{1,0:T(8,128)S(1)} %add.95), channel_id=1, source_target_pairs={{0,4},{2,6},{4,0},{6,2},{1,5},{3,7},{5,1},{7,3},{8,12},{10,14},{12... | collective-permute-start | bytes 393224 | tf_op jit(solution)/shard_map/ppermute | solution.py:44
  58.9 2.1 %collective-permute-done.15 = f32[16,2048]{1,0:T(8,128)S(1)} collective-permute-done((f32[16,2048]{1,0:T(8,128)S(1)}, f32[16,2048]{1,0:T(8,128)S(1)}, u32[]{:S(2)}, u32[]{:S(2)}) %collective-permute-start.15) | collective-permute-done | bytes 131104 | tf_op jit(solution)/shard_map/ppermute | solution.py:44
  61.0 1.0 collective-permute-done.14
  62.0 2.6 %collective-permute-done.13 = f32[16,2048]{1,0:T(8,128)S(1)} collective-permute-done((f32[16,2048]{1,0:T(8,128)S(1)}, f32[16,2048]{1,0:T(8,128)S(1)}, u32[]{:S(2)}, u32[]{:S(2)}) %collective-permute-start.13) | collective-permute-done | bytes 131104 | tf_op jit(solution)/shard_map/ppermute | solution.py:44
  64.7 1.6 %collective-permute-start.16 = (f32[16,2048]{1,0:T(8,128)S(1)}, f32[16,2048]{1,0:T(8,128)S(1)}, u32[]{:S(2)}, u32[]{:S(2)}) collective-permute-start(f32[16,2048]{1,0:T(8,128)S(1)} %add_add_fusion.1.own), channel_id=1, source_target_pairs={{0,1},{1,0},{2,3},{3,2},{4,5},{5,4},{6,7},{7,6},{8,9},{9,8},{10,11... | collective-permute-start | bytes 393224 | tf_op jit(solution)/shard_map/ppermute | solution.py:44
  66.3 1.0 collective-permute-done.16.sibling
  67.3 1.6 %shard_map.53 = f32[16,1152]{1,0:T(8,128)S(1)} custom-call(f32[16,2048]{1,0:T(8,128)S(1)} %add_add_fusion.1.own, f32[16,2048]{1,0:T(8,128)S(1)} %collective-permute-done.16.sibling, bf16[4096,1024]{1,0:T(8,128)(2,1)S(1)} %copy-done.1), custom_call_target="tpu_custom_call" | custom-call | tf_op jit(solution)/shard_map/pallas_call | solution.py:139
  68.8 1.9 %collective-permute-start.19 = (f32[16,1152]{1,0:T(8,128)S(1)}, f32[16,1152]{1,0:T(8,128)S(1)}, u32[]{:S(2)}, u32[]{:S(2)}) collective-permute-start(f32[16,1152]{1,0:T(8,128)S(1)} %shard_map.53), channel_id=1, source_target_pairs={{0,192},{64,128},{128,64},{192,0},{1,193},{65,129},{129,65},{193,1... | collective-permute-start | bytes 221192 | tf_op jit(solution)/shard_map/ppermute | solution.py:44
  70.7 2.0 %collective-permute-start.17 = (f32[16,1152]{1,0:T(8,128)S(1)}, f32[16,1152]{1,0:T(8,128)S(1)}, u32[]{:S(2)}, u32[]{:S(2)}) collective-permute-start(f32[16,1152]{1,0:T(8,128)S(1)} %shard_map.53), channel_id=1, source_target_pairs={{0,128},{64,192},{128,0},{192,64},{1,129},{65,193},{129,1},{193,65... | collective-permute-start | bytes 221192 | tf_op jit(solution)/shard_map/ppermute | solution.py:44
  74.2 1.9 %collective-permute-done.17 = f32[16,1152]{1,0:T(8,128)S(1)} collective-permute-done((f32[16,1152]{1,0:T(8,128)S(1)}, f32[16,1152]{1,0:T(8,128)S(1)}, u32[]{:S(2)}, u32[]{:S(2)}) %collective-permute-start.17) | collective-permute-done | bytes 73760 | tf_op jit(solution)/shard_map/ppermute | solution.py:44
  76.1 2.4 %collective-permute-start.22 = (f32[16,1152]{1,0:T(8,128)S(1)}, f32[16,1152]{1,0:T(8,128)S(1)}, u32[]{:S(2)}, u32[]{:S(2)}) collective-permute-start(f32[16,1152]{1,0:T(8,128)S(1)} %add_add_fusion.4), channel_id=1, source_target_pairs={{0,24},{8,16},{16,8},{24,0},{32,56},{40,48},{48,40},{56,32},{1,25}... | collective-permute-start | bytes 221192 | tf_op jit(solution)/shard_map/ppermute | solution.py:44
  78.5 1.2 collective-permute-start.20
  79.7 1.6 %collective-permute-done.22 = f32[16,1152]{1,0:T(8,128)S(1)} collective-permute-done((f32[16,1152]{1,0:T(8,128)S(1)}, f32[16,1152]{1,0:T(8,128)S(1)}, u32[]{:S(2)}, u32[]{:S(2)}) %collective-permute-start.22) | collective-permute-done | bytes 73760 | tf_op jit(solution)/shard_map/ppermute | solution.py:44
  81.3 1.5 %collective-permute-done.21 = f32[16,1152]{1,0:T(8,128)S(1)} collective-permute-done((f32[16,1152]{1,0:T(8,128)S(1)}, f32[16,1152]{1,0:T(8,128)S(1)}, u32[]{:S(2)}, u32[]{:S(2)}) %collective-permute-start.21) | collective-permute-done | bytes 73760 | tf_op jit(solution)/shard_map/ppermute | solution.py:44
  82.8 2.0 %collective-permute-done.20 = f32[16,1152]{1,0:T(8,128)S(1)} collective-permute-done((f32[16,1152]{1,0:T(8,128)S(1)}, f32[16,1152]{1,0:T(8,128)S(1)}, u32[]{:S(2)}, u32[]{:S(2)}) %collective-permute-start.20) | collective-permute-done | bytes 73760 | tf_op jit(solution)/shard_map/ppermute | solution.py:44
  84.8 2.1 %collective-permute-start.23 = (f32[16,1152]{1,0:T(8,128)S(1)}, f32[16,1152]{1,0:T(8,128)S(1)}, u32[]{:S(2)}, u32[]{:S(2)}) collective-permute-start(f32[16,1152]{1,0:T(8,128)S(1)} %add_add_fusion.3.mine), channel_id=1, source_target_pairs={{0,48},{8,56},{16,32},{24,40},{32,16},{40,24},{48,0},{56,8},{1,49}... | collective-permute-start | bytes 221192 | tf_op jit(solution)/shard_map/ppermute | solution.py:44
  86.9 3.4 %collective-permute-done.23.theirs = f32[16,1152]{1,0:T(8,128)S(1)} collective-permute-done((f32[16,1152]{1,0:T(8,128)S(1)}, f32[16,1152]{1,0:T(8,128)S(1)}, u32[]{:S(2)}, u32[]{:S(2)}) %collective-permute-start.23) | collective-permute-done | bytes 73760 | tf_op jit(solution)/shard_map/ppermute | solution.py:44
  90.3 2.5 %shard_map.54 = (f32[16,2048]{1,0:T(8,128)S(1)}, f32[16,2048]{1,0:T(8,128)S(1)}) custom-call(f32[16,1152]{1,0:T(8,128)S(1)} %add_add_fusion.3.mine, f32[16,1152]{1,0:T(8,128)S(1)} %collective-permute-done.23.theirs, bf16[4096,1024]{1,0:T(8,128)(2,1)S(1)} %copy-done.1), custom_call_target="tpu_custom_call" | custom-call | tf_op jit(solution)/shard_map/pallas_call | solution.py:139
  92.8 3.5 %collective-permute-start.24 = (f32[16,2048]{1,0:T(8,128)S(1)}, f32[16,2048]{1,0:T(8,128)S(1)}, u32[]{:S(2)}, u32[]{:S(2)}) collective-permute-start(f32[16,2048]{1,0:T(8,128)S(1)} %get-tuple-element.13), channel_id=1, source_target_pairs={{0,1},{1,0},{2,3},{3,2},{4,5},{5,4},{6,7},{7,6},{8,9},{9,8},{10,11... | collective-permute-start | bytes 393224 | tf_op jit(solution)/shard_map/ppermute | solution.py:44
  97.3 2.7 %collective-permute-start.27 = (f32[16,2048]{1,0:T(8,128)S(1)}, f32[16,2048]{1,0:T(8,128)S(1)}, u32[]{:S(2)}, u32[]{:S(2)}) collective-permute-start(f32[16,2048]{1,0:T(8,128)S(1)} %add.105), channel_id=1, source_target_pairs={{0,6},{2,4},{4,2},{6,0},{1,7},{3,5},{5,3},{7,1},{8,14},{10,12},{12... | collective-permute-start | bytes 393224 | tf_op jit(solution)/shard_map/ppermute | solution.py:44
  100.0 1.3 %collective-permute-start.25 = (f32[16,2048]{1,0:T(8,128)S(1)}, f32[16,2048]{1,0:T(8,128)S(1)}, u32[]{:S(2)}, u32[]{:S(2)}) collective-permute-start(f32[16,2048]{1,0:T(8,128)S(1)} %add.105), channel_id=1, source_target_pairs={{0,4},{2,6},{4,0},{6,2},{1,5},{3,7},{5,1},{7,3},{8,12},{10,14},{12... | collective-permute-start | bytes 393224 | tf_op jit(solution)/shard_map/ppermute | solution.py:44
  101.3 2.1 %collective-permute-done.27 = f32[16,2048]{1,0:T(8,128)S(1)} collective-permute-done((f32[16,2048]{1,0:T(8,128)S(1)}, f32[16,2048]{1,0:T(8,128)S(1)}, u32[]{:S(2)}, u32[]{:S(2)}) %collective-permute-start.27) | collective-permute-done | bytes 131104 | tf_op jit(solution)/shard_map/ppermute | solution.py:44
  103.4 1.0 collective-permute-done.26
  104.4 2.6 %collective-permute-done.25 = f32[16,2048]{1,0:T(8,128)S(1)} collective-permute-done((f32[16,2048]{1,0:T(8,128)S(1)}, f32[16,2048]{1,0:T(8,128)S(1)}, u32[]{:S(2)}, u32[]{:S(2)}) %collective-permute-start.25) | collective-permute-done | bytes 131104 | tf_op jit(solution)/shard_map/ppermute | solution.py:44
  107.3 1.6 %collective-permute-start.28 = (f32[16,16]{1,0:T(8,128)S(1)}, f32[16,16]{1,0:T(8,128)S(1)}, u32[]{:S(2)}, u32[]{:S(2)}) collective-permute-start(f32[16,16]{1,0:T(8,128)S(1)} %fusion.12), channel_id=1, source_target_pairs={{0,1},{1,0},{2,3},{3,2},{4,5},{5,4},{6,7},{7,6},{8,9},{9,8},{10,11... | collective-permute-start | bytes 3080 | tf_op jit(solution)/shard_map/ppermute | solution.py:44
  109.7 16.7 %all_to_all.5.grams = f32[32,16,128]{2,1,0:T(8,128)S(1)} all-to-all(f32[32,16,128]{2,1,0:T(8,128)S(1)} %broadcast_in_dim.2), channel_id=1, replica_groups=mesh['x'=4,'z'=8,'y'=4,'core'=2] {'x','z'}, dimensions={0} | all-to-all | bytes 524288 | tf_op jit(solution)/shard_map/all_to_all | solution.py:182
  (37 shorter events, 8.4 us)
Async XLA Ops:
  2.4 3.4 %copy-start = (bf16[4096,1024]{1,0:T(8,128)(2,1)S(1)}, bf16[4096,1024]{1,0:T(8,128)(2,1)}, u32[]{:S(2)}) copy-start(bf16[4096,1024]{1,0:T(8,128)(2,1)} %affinity.9) | copy-start | bytes 25165828
  5.7 18.8 %copy-start.1 = (bf16[4096,1024]{1,0:T(8,128)(2,1)S(1)}, bf16[4096,1024]{1,0:T(8,128)(2,1)}, u32[]{:S(2)}) copy-start(bf16[4096,1024]{1,0:T(8,128)(2,1)} %affinity.9) | copy-start | bytes 25165828
  8.0 4.2 %collective-permute-start = (f32[16,2048]{1,0:T(8,128)S(1)}, f32[16,2048]{1,0:T(8,128)S(1)}, u32[]{:S(2)}, u32[]{:S(2)}) collective-permute-start(f32[16,2048]{1,0:T(8,128)S(1)} %get-tuple-element.9), channel_id=1, source_target_pairs={{0,1},{1,0},{2,3},{3,2},{4,5},{5,4},{6,7},{7,6},{8,9},{9,8},{10,11... | collective-permute-start | bytes 393224 | tf_op jit(solution)/shard_map/ppermute | solution.py:44
  12.3 6.0 %collective-permute-start.3 = (f32[16,2048]{1,0:T(8,128)S(1)}, f32[16,2048]{1,0:T(8,128)S(1)}, u32[]{:S(2)}, u32[]{:S(2)}) collective-permute-start(f32[16,2048]{1,0:T(8,128)S(1)} %add.85), channel_id=1, source_target_pairs={{0,6},{2,4},{4,2},{6,0},{1,7},{3,5},{5,3},{7,1},{8,14},{10,12},{12... | collective-permute-start | bytes 393224 | tf_op jit(solution)/shard_map/ppermute | solution.py:44
  13.4 4.9 %collective-permute-start.2 = (f32[16,2048]{1,0:T(8,128)S(1)}, f32[16,2048]{1,0:T(8,128)S(1)}, u32[]{:S(2)}, u32[]{:S(2)}) collective-permute-start(f32[16,2048]{1,0:T(8,128)S(1)} %add.85), channel_id=1, source_target_pairs={{0,2},{2,0},{4,6},{6,4},{1,3},{3,1},{5,7},{7,5},{8,10},{10,8},{12,... | collective-permute-start | bytes 393224 | tf_op jit(solution)/shard_map/ppermute | solution.py:44
  13.4 8.6 %collective-permute-start.1 = (f32[16,2048]{1,0:T(8,128)S(1)}, f32[16,2048]{1,0:T(8,128)S(1)}, u32[]{:S(2)}, u32[]{:S(2)}) collective-permute-start(f32[16,2048]{1,0:T(8,128)S(1)} %add.85), channel_id=1, source_target_pairs={{0,4},{2,6},{4,0},{6,2},{1,5},{3,7},{5,1},{7,3},{8,12},{10,14},{12... | collective-permute-start | bytes 393224 | tf_op jit(solution)/shard_map/ppermute | solution.py:44
  22.0 2.6 %collective-permute-start.4 = (f32[16,2048]{1,0:T(8,128)S(1)}, f32[16,2048]{1,0:T(8,128)S(1)}, u32[]{:S(2)}, u32[]{:S(2)}) collective-permute-start(f32[16,2048]{1,0:T(8,128)S(1)} %add_add_fusion.2.own), channel_id=1, source_target_pairs={{0,1},{1,0},{2,3},{3,2},{4,5},{5,4},{6,7},{7,6},{8,9},{9,8},{10,11... | collective-permute-start | bytes 393224 | tf_op jit(solution)/shard_map/ppermute | solution.py:44
  26.1 4.4 %collective-permute-start.7 = (f32[16,1152]{1,0:T(8,128)S(1)}, f32[16,1152]{1,0:T(8,128)S(1)}, u32[]{:S(2)}, u32[]{:S(2)}) collective-permute-start(f32[16,1152]{1,0:T(8,128)S(1)} %shard_map.51), channel_id=1, source_target_pairs={{0,192},{64,128},{128,64},{192,0},{1,193},{65,129},{129,65},{193,1... | collective-permute-start | bytes 221192 | tf_op jit(solution)/shard_map/ppermute | solution.py:44
  27.1 3.5 %collective-permute-start.6 = (f32[16,1152]{1,0:T(8,128)S(1)}, f32[16,1152]{1,0:T(8,128)S(1)}, u32[]{:S(2)}, u32[]{:S(2)}) collective-permute-start(f32[16,1152]{1,0:T(8,128)S(1)} %shard_map.51), channel_id=1, source_target_pairs={{0,64},{64,0},{128,192},{192,128},{1,65},{65,1},{129,193},{193,129... | collective-permute-start | bytes 221192 | tf_op jit(solution)/shard_map/ppermute | solution.py:44
  27.1 6.0 %collective-permute-start.5 = (f32[16,1152]{1,0:T(8,128)S(1)}, f32[16,1152]{1,0:T(8,128)S(1)}, u32[]{:S(2)}, u32[]{:S(2)}) collective-permute-start(f32[16,1152]{1,0:T(8,128)S(1)} %shard_map.51), channel_id=1, source_target_pairs={{0,128},{64,192},{128,0},{192,64},{1,129},{65,193},{129,1},{193,65... | collective-permute-start | bytes 221192 | tf_op jit(solution)/shard_map/ppermute | solution.py:44
  33.0 5.2 %collective-permute-start.10 = (f32[16,1152]{1,0:T(8,128)S(1)}, f32[16,1152]{1,0:T(8,128)S(1)}, u32[]{:S(2)}, u32[]{:S(2)}) collective-permute-start(f32[16,1152]{1,0:T(8,128)S(1)} %add_add_fusion.6), channel_id=1, source_target_pairs={{0,24},{8,16},{16,8},{24,0},{32,56},{40,48},{48,40},{56,32},{1,25}... | collective-permute-start | bytes 221192 | tf_op jit(solution)/shard_map/ppermute | solution.py:44
  36.5 4.7 %collective-permute-start.9 = (f32[16,1152]{1,0:T(8,128)S(1)}, f32[16,1152]{1,0:T(8,128)S(1)}, u32[]{:S(2)}, u32[]{:S(2)}) collective-permute-start(f32[16,1152]{1,0:T(8,128)S(1)} %add_add_fusion.6), channel_id=1, source_target_pairs={{0,8},{8,0},{16,24},{24,16},{32,40},{40,32},{48,56},{56,48},{1,9},... | collective-permute-start | bytes 221192 | tf_op jit(solution)/shard_map/ppermute | solution.py:44
  36.5 4.8 %collective-permute-start.8 = (f32[16,1152]{1,0:T(8,128)S(1)}, f32[16,1152]{1,0:T(8,128)S(1)}, u32[]{:S(2)}, u32[]{:S(2)}) collective-permute-start(f32[16,1152]{1,0:T(8,128)S(1)} %add_add_fusion.6), channel_id=1, source_target_pairs={{0,16},{8,24},{16,0},{24,8},{32,48},{40,56},{48,32},{56,40},{1,17}... | collective-permute-start | bytes 221192 | tf_op jit(solution)/shard_map/ppermute | solution.py:44
  41.4 6.0 %collective-permute-start.11 = (f32[16,1152]{1,0:T(8,128)S(1)}, f32[16,1152]{1,0:T(8,128)S(1)}, u32[]{:S(2)}, u32[]{:S(2)}) collective-permute-start(f32[16,1152]{1,0:T(8,128)S(1)} %add_add_fusion.5.mine), channel_id=1, source_target_pairs={{0,48},{8,56},{16,32},{24,40},{32,16},{40,24},{48,0},{56,8},{1,49}... | collective-permute-start | bytes 221192 | tf_op jit(solution)/shard_map/ppermute | solution.py:44
  49.8 5.0 %collective-permute-start.12 = (f32[16,2048]{1,0:T(8,128)S(1)}, f32[16,2048]{1,0:T(8,128)S(1)}, u32[]{:S(2)}, u32[]{:S(2)}) collective-permute-start(f32[16,2048]{1,0:T(8,128)S(1)} %get-tuple-element.11), channel_id=1, source_target_pairs={{0,1},{1,0},{2,3},{3,2},{4,5},{5,4},{6,7},{7,6},{8,9},{9,8},{10,11... | collective-permute-start | bytes 393224 | tf_op jit(solution)/shard_map/ppermute | solution.py:44
  54.8 6.2 %collective-permute-start.15 = (f32[16,2048]{1,0:T(8,128)S(1)}, f32[16,2048]{1,0:T(8,128)S(1)}, u32[]{:S(2)}, u32[]{:S(2)}) collective-permute-start(f32[16,2048]{1,0:T(8,128)S(1)} %add.95), channel_id=1, source_target_pairs={{0,6},{2,4},{4,2},{6,0},{1,7},{3,5},{5,3},{7,1},{8,14},{10,12},{12... | collective-permute-start | bytes 393224 | tf_op jit(solution)/shard_map/ppermute | solution.py:44
  57.6 4.4 %collective-permute-start.14 = (f32[16,2048]{1,0:T(8,128)S(1)}, f32[16,2048]{1,0:T(8,128)S(1)}, u32[]{:S(2)}, u32[]{:S(2)}) collective-permute-start(f32[16,2048]{1,0:T(8,128)S(1)} %add.95), channel_id=1, source_target_pairs={{0,2},{2,0},{4,6},{6,4},{1,3},{3,1},{5,7},{7,5},{8,10},{10,8},{12,... | collective-permute-start | bytes 393224 | tf_op jit(solution)/shard_map/ppermute | solution.py:44
  57.6 7.0 %collective-permute-start.13 = (f32[16,2048]{1,0:T(8,128)S(1)}, f32[16,2048]{1,0:T(8,128)S(1)}, u32[]{:S(2)}, u32[]{:S(2)}) collective-permute-start(f32[16,2048]{1,0:T(8,128)S(1)} %add.95), channel_id=1, source_target_pairs={{0,4},{2,6},{4,0},{6,2},{1,5},{3,7},{5,1},{7,3},{8,12},{10,14},{12... | collective-permute-start | bytes 393224 | tf_op jit(solution)/shard_map/ppermute | solution.py:44
  64.7 2.6 %collective-permute-start.16 = (f32[16,2048]{1,0:T(8,128)S(1)}, f32[16,2048]{1,0:T(8,128)S(1)}, u32[]{:S(2)}, u32[]{:S(2)}) collective-permute-start(f32[16,2048]{1,0:T(8,128)S(1)} %add_add_fusion.1.own), channel_id=1, source_target_pairs={{0,1},{1,0},{2,3},{3,2},{4,5},{5,4},{6,7},{7,6},{8,9},{9,8},{10,11... | collective-permute-start | bytes 393224 | tf_op jit(solution)/shard_map/ppermute | solution.py:44
  68.8 4.4 %collective-permute-start.19 = (f32[16,1152]{1,0:T(8,128)S(1)}, f32[16,1152]{1,0:T(8,128)S(1)}, u32[]{:S(2)}, u32[]{:S(2)}) collective-permute-start(f32[16,1152]{1,0:T(8,128)S(1)} %shard_map.53), channel_id=1, source_target_pairs={{0,192},{64,128},{128,64},{192,0},{1,193},{65,129},{129,65},{193,1... | collective-permute-start | bytes 221192 | tf_op jit(solution)/shard_map/ppermute | solution.py:44
  70.7 3.5 %collective-permute-start.18 = (f32[16,1152]{1,0:T(8,128)S(1)}, f32[16,1152]{1,0:T(8,128)S(1)}, u32[]{:S(2)}, u32[]{:S(2)}) collective-permute-start(f32[16,1152]{1,0:T(8,128)S(1)} %shard_map.53), channel_id=1, source_target_pairs={{0,64},{64,0},{128,192},{192,128},{1,65},{65,1},{129,193},{193,129... | collective-permute-start | bytes 221192 | tf_op jit(solution)/shard_map/ppermute | solution.py:44
  70.7 5.3 %collective-permute-start.17 = (f32[16,1152]{1,0:T(8,128)S(1)}, f32[16,1152]{1,0:T(8,128)S(1)}, u32[]{:S(2)}, u32[]{:S(2)}) collective-permute-start(f32[16,1152]{1,0:T(8,128)S(1)} %shard_map.53), channel_id=1, source_target_pairs={{0,128},{64,192},{128,0},{192,64},{1,129},{65,193},{129,1},{193,65... | collective-permute-start | bytes 221192 | tf_op jit(solution)/shard_map/ppermute | solution.py:44
  76.1 5.2 %collective-permute-start.22 = (f32[16,1152]{1,0:T(8,128)S(1)}, f32[16,1152]{1,0:T(8,128)S(1)}, u32[]{:S(2)}, u32[]{:S(2)}) collective-permute-start(f32[16,1152]{1,0:T(8,128)S(1)} %add_add_fusion.4), channel_id=1, source_target_pairs={{0,24},{8,16},{16,8},{24,0},{32,56},{40,48},{48,40},{56,32},{1,25}... | collective-permute-start | bytes 221192 | tf_op jit(solution)/shard_map/ppermute | solution.py:44
  78.5 4.3 %collective-permute-start.21 = (f32[16,1152]{1,0:T(8,128)S(1)}, f32[16,1152]{1,0:T(8,128)S(1)}, u32[]{:S(2)}, u32[]{:S(2)}) collective-permute-start(f32[16,1152]{1,0:T(8,128)S(1)} %add_add_fusion.4), channel_id=1, source_target_pairs={{0,8},{8,0},{16,24},{24,16},{32,40},{40,32},{48,56},{56,48},{1,9},... | collective-permute-start | bytes 221192 | tf_op jit(solution)/shard_map/ppermute | solution.py:44
  78.5 6.3 %collective-permute-start.20 = (f32[16,1152]{1,0:T(8,128)S(1)}, f32[16,1152]{1,0:T(8,128)S(1)}, u32[]{:S(2)}, u32[]{:S(2)}) collective-permute-start(f32[16,1152]{1,0:T(8,128)S(1)} %add_add_fusion.4), channel_id=1, source_target_pairs={{0,16},{8,24},{16,0},{24,8},{32,48},{40,56},{48,32},{56,40},{1,17}... | collective-permute-start | bytes 221192 | tf_op jit(solution)/shard_map/ppermute | solution.py:44
  84.8 5.5 %collective-permute-start.23 = (f32[16,1152]{1,0:T(8,128)S(1)}, f32[16,1152]{1,0:T(8,128)S(1)}, u32[]{:S(2)}, u32[]{:S(2)}) collective-permute-start(f32[16,1152]{1,0:T(8,128)S(1)} %add_add_fusion.3.mine), channel_id=1, source_target_pairs={{0,48},{8,56},{16,32},{24,40},{32,16},{40,24},{48,0},{56,8},{1,49}... | collective-permute-start | bytes 221192 | tf_op jit(solution)/shard_map/ppermute | solution.py:44
  92.8 4.5 %collective-permute-start.24 = (f32[16,2048]{1,0:T(8,128)S(1)}, f32[16,2048]{1,0:T(8,128)S(1)}, u32[]{:S(2)}, u32[]{:S(2)}) collective-permute-start(f32[16,2048]{1,0:T(8,128)S(1)} %get-tuple-element.13), channel_id=1, source_target_pairs={{0,1},{1,0},{2,3},{3,2},{4,5},{5,4},{6,7},{7,6},{8,9},{9,8},{10,11... | collective-permute-start | bytes 393224 | tf_op jit(solution)/shard_map/ppermute | solution.py:44
  97.3 6.0 %collective-permute-start.27 = (f32[16,2048]{1,0:T(8,128)S(1)}, f32[16,2048]{1,0:T(8,128)S(1)}, u32[]{:S(2)}, u32[]{:S(2)}) collective-permute-start(f32[16,2048]{1,0:T(8,128)S(1)} %add.105), channel_id=1, source_target_pairs={{0,6},{2,4},{4,2},{6,0},{1,7},{3,5},{5,3},{7,1},{8,14},{10,12},{12... | collective-permute-start | bytes 393224 | tf_op jit(solution)/shard_map/ppermute | solution.py:44
  100.0 4.4 %collective-permute-start.26 = (f32[16,2048]{1,0:T(8,128)S(1)}, f32[16,2048]{1,0:T(8,128)S(1)}, u32[]{:S(2)}, u32[]{:S(2)}) collective-permute-start(f32[16,2048]{1,0:T(8,128)S(1)} %add.105), channel_id=1, source_target_pairs={{0,2},{2,0},{4,6},{6,4},{1,3},{3,1},{5,7},{7,5},{8,10},{10,8},{12,... | collective-permute-start | bytes 393224 | tf_op jit(solution)/shard_map/ppermute | solution.py:44
  100.0 7.0 %collective-permute-start.25 = (f32[16,2048]{1,0:T(8,128)S(1)}, f32[16,2048]{1,0:T(8,128)S(1)}, u32[]{:S(2)}, u32[]{:S(2)}) collective-permute-start(f32[16,2048]{1,0:T(8,128)S(1)} %add.105), channel_id=1, source_target_pairs={{0,4},{2,6},{4,0},{6,2},{1,5},{3,7},{5,1},{7,3},{8,12},{10,14},{12... | collective-permute-start | bytes 393224 | tf_op jit(solution)/shard_map/ppermute | solution.py:44
  107.3 2.4 %collective-permute-start.28 = (f32[16,16]{1,0:T(8,128)S(1)}, f32[16,16]{1,0:T(8,128)S(1)}, u32[]{:S(2)}, u32[]{:S(2)}) collective-permute-start(f32[16,16]{1,0:T(8,128)S(1)} %fusion.12), channel_id=1, source_target_pairs={{0,1},{1,0},{2,3},{3,2},{4,5},{5,4},{6,7},{7,6},{8,9},{9,8},{10,11... | collective-permute-start | bytes 3080 | tf_op jit(solution)/shard_map/ppermute | solution.py:44

commit v3 on v2

v3 whole, which is shorter than its diff:
```python
import functools
import math

import jax
import jax.numpy as jnp
from jax import lax
from jax.experimental import pallas as pl
from jax.experimental.pallas import tpu as pltpu
from jax.sharding import Mesh, PartitionSpec as P

ITERS = 2
K = 16
PIECE = 512


mix_first = -2048144789
mix_second = -1028477387
golden = -1640531535
salt_value = 1540483477


def shifted(value, amount):
    return lax.shift_right_logical(value, jnp.full(value.shape, amount, jnp.int32))


def scramble(value):
    value = jnp.bitwise_xor(value, shifted(value, 16))
    value = value * jnp.int32(mix_first)
    value = jnp.bitwise_xor(value, shifted(value, 13))
    value = value * jnp.int32(mix_second)
    return jnp.bitwise_xor(value, shifted(value, 16))


def test_matrix(seeds, sku_ids, total_columns):
    first = scramble(jnp.bitwise_xor(seeds, sku_ids * jnp.int32(golden)))
    second = scramble(jnp.bitwise_xor(first, jnp.int32(salt_value)))
    uniform_a = (shifted(first, 9) + 1).astype(jnp.float32) / 8388608.0
    uniform_b = (shifted(second, 9) + 1).astype(jnp.float32) / 8388608.0
    gauss = jnp.sqrt(-2.0 * jnp.log(uniform_a)) * jnp.cos(6.283185307179586 * uniform_b)
    return (gauss / math.sqrt(total_columns)).astype(jnp.bfloat16)


def swap(value, axis, count, offset):
    return lax.ppermute(value, axis, [(i, i ^ offset) for i in range(count)])


def sum_four(value, axis, count, offsets=(1, 2, 3)):
    one, two, three = (swap(value, axis, count, k) for k in offsets)
    return (value + two) + (one + three)


def block_rows(piece, core):
    return pl.ds(pl.multiple_of((2 * piece + core) * PIECE, PIECE), PIECE)


def span(step):
    return slice(step * PIECE, (step + 1) * PIECE)


def project_piece(left, rows, scale):
    part = lax.dot_general(
        left, rows, (((1,), (1,)), ((), ())), preferred_element_type=jnp.float32
    )
    return part if scale is None else part * scale


def split_bf16(value):
    high = value.astype(jnp.bfloat16)
    rest = value - high.astype(jnp.float32)
    low = rest.astype(jnp.bfloat16)
    last = (rest - low.astype(jnp.float32)).astype(jnp.bfloat16)
    return high, low, last


def triple_gram(parts):
    stacked = jnp.concatenate(parts, axis=0)
    return lax.dot_general(
        stacked, stacked, (((1,), (1,)), ((), ())), preferred_element_type=jnp.float32
    )


def fold_gram(gram):
    rows = (gram[2 * K :] + gram[K : 2 * K]) + gram[:K]
    return (rows[:, 2 * K :] + rows[:, K : 2 * K]) + rows[:, :K]


def eliminate(gram, right):
    row = lax.broadcasted_iota(jnp.int32, (K, 128), 0)
    lane = lax.broadcasted_iota(jnp.int32, (K, 128), 1)
    columns = [jnp.broadcast_to(gram[:, k : k + 1], (K, 128)) for k in range(K)]
    lower = jnp.zeros((K, 128), jnp.float32)
    pivots = jnp.ones((K, 128), jnp.float32)
    for k in range(K):
        column = columns[k]
        pivot = jnp.broadcast_to(column[k : k + 1, :], (K, 128))
        factor = column * (1.0 / pivot)
        lower = jnp.where((lane == k) & (row >= k), column / jnp.sqrt(pivot), lower)
        pivots = jnp.where(row == k, pivot, pivots)
        factor = jnp.where(row > k, factor, 0.0)
        for j in range(k + 1, K):
            columns[j] = columns[j] - factor * jnp.broadcast_to(column[j : j + 1, :], (K, 128))
        wide = jnp.tile(factor, (1, right.shape[1] // 128))
        right = right - wide * right[k : k + 1, :]
    root = jnp.sqrt(pivots)
    return lower, right / jnp.tile(root, (1, right.shape[1] // 128))


def first_kernel(seed_values, sku_ids, affinity, omega, held, other, arrived, *, total_columns):
    core = lax.axis_index("core")
    copies = []
    for side in (1 - core, core):
        for step in range(4):
            place = block_rows(step, side)
            copies.append(
                pltpu.make_async_copy(affinity.at[place], held.at[place], arrived.at[len(copies)])
            )
            copies[-1].start()
    row = lax.broadcasted_iota(jnp.int32, (K, 128), 0)
    seeds = jnp.zeros((K, 128), jnp.int32)
    for k in range(K):
        seeds = jnp.where(row == k, seed_values[k], seeds)
    for start in range(0, sku_ids.shape[1], 128):
        ids = jnp.broadcast_to(sku_ids[:, start : start + 128], (K, 128))
        omega[:, start : start + 128] = test_matrix(seeds, ids, total_columns)
    for step in range(4):
        copies[step].wait()
        rows = held[block_rows(step, 1 - core), :]
        other[:, span(step)] = project_piece(omega[...], rows, None)
    for step in range(4, 8):
        copies[step].wait()


def solve_kernel(mine, theirs, held, left, other, *, scale):
    core = lax.axis_index("core")
    wide = held.shape[1]
    total = mine[...] + theirs[...]
    _, back = eliminate(total[:, wide:], total[:, :wide])
    left[...] = back.astype(jnp.bfloat16)
    for step in range(4):
        rows = held[block_rows(step, 1 - core), :]
        other[:, span(step)] = project_piece(left[...], rows, scale)


def own_kernel(left, held, own, *, scale):
    core = lax.axis_index("core")
    for step in range(4):
        rows = held[block_rows(step, core), :]
        own[:, span(step)] = project_piece(left[...], rows, scale)


def back_sums(half, held, side):
    both = jnp.zeros((2 * K, held.shape[1]), jnp.float32)
    gram = jnp.zeros((3 * K, 3 * K), jnp.float32)
    for step in range(4):
        parts = split_bf16(half[:, span(step)])
        both += jnp.dot(
            jnp.concatenate(parts[:2], axis=0),
            held[block_rows(step, side), :],
            preferred_element_type=jnp.float32,
        )
        gram += triple_gram(parts)
    return both[:K] + both[K:], fold_gram(gram)


def back_own_kernel(half, held, packed):
    wide = held.shape[1]
    back, gram = back_sums(half, held, lax.axis_index("core"))
    packed[:, :wide] = back
    packed[:, wide:] = jnp.zeros((K, 128), jnp.float32)
    packed[:, wide : wide + K] = gram


def back_other_kernel(half, held, before, packed):
    wide = held.shape[1]
    back, gram = back_sums(half, held, 1 - lax.axis_index("core"))
    packed[:, :wide] = before[:, :wide] + back
    packed[:, wide:] = jnp.zeros((K, 128), jnp.float32)
    packed[:, wide : wide + K] = before[:, wide : wide + K] + gram


def gram_kernel(half, packed):
    gram = jnp.zeros((3 * K, 3 * K), jnp.float32)
    for step in range(4):
        gram += triple_gram(split_bf16(half[:, span(step)]))
    gram = fold_gram(gram)
    packed[...] = jnp.zeros_like(packed)
    packed[:, :K] = gram[:8]
    packed[:, K : 2 * K] = gram[8:]


def last_kernel(grams, half, basis, factor, *, scale):
    total = None
    for x in range(4):
        one, two, three, four = (grams[4 * x + k] for k in range(4))
        part = (one + three) + (two + four)
        total = part if total is None else total + part
    gram = jnp.concatenate([total[:, :K], total[:, K : 2 * K]], axis=0)
    place = pl.multiple_of(lax.axis_index("y") * PIECE, PIECE)
    lower, ortho = eliminate(gram, half[:, pl.ds(place, PIECE)])
    basis[...] = ortho * scale
    factor[...] = lower.T[:K, :] / scale


def call(kernel, outs, *args, spaces=None, scratch=(), flops=0):
    whole = pl.BlockSpec(memory_space=pltpu.VMEM)
    return pl.pallas_call(
        kernel,
        in_specs=spaces or [whole] * len(args),
        out_specs=[whole] * len(outs),
        out_shape=[jax.ShapeDtypeStruct(*out) for out in outs],
        scratch_shapes=scratch,
        cost_estimate=pl.CostEstimate(
            flops=flops, bytes_accessed=flops // K, transcendentals=0
        ),
        compiler_params=pltpu.CompilerParams(vmem_limit_bytes=32 * 1024 * 1024),
    )(*args)


def body(affinity, seed_values, sku_ids):
    local_rows, local_columns = affinity.shape
    total_columns = local_columns * 8
    total_rows = local_rows * 32
    f32 = jnp.float32
    half_out = ((K, local_rows // 2), f32)
    left_out = ((K, local_columns), jnp.bfloat16)
    packed_out = ((K, local_columns + 128), f32)
    pass_flops = K * local_rows * local_columns
    z = ("cube", "level")

    left, held, other = call(
        functools.partial(first_kernel, total_columns=total_columns),
        [left_out, (affinity.shape, jnp.bfloat16), half_out],
        seed_values,
        sku_ids.reshape(1, -1),
        pltpu.with_memory_space_constraint(affinity, pltpu.HBM),
        spaces=[
            pl.BlockSpec(memory_space=pltpu.SMEM),
            pl.BlockSpec(memory_space=pltpu.VMEM),
            pl.BlockSpec(memory_space=pltpu.HBM),
        ],
        scratch=[pltpu.SemaphoreType.DMA((8,))],
        flops=pass_flops,
    )
    scale = None
    for repeat in range(ITERS + 1):
        arriving = swap(other, "core", 2, 1)
        (own,) = call(
            functools.partial(own_kernel, scale=scale), [half_out], left, held, flops=pass_flops
        )
        half = sum_four(own + arriving, "y", 4)
        if repeat < ITERS:
            sibling = swap(half, "core", 2, 1)
            (packed,) = call(back_own_kernel, [packed_out], half, held, flops=pass_flops)
            (packed,) = call(
                back_other_kernel, [packed_out], sibling, held, packed, flops=pass_flops
            )
            packed = sum_four(packed, "x", 4)
            packed = sum_four(packed, z, 8)
            scale = 1.0 / math.sqrt(total_columns)
            left, other = call(
                functools.partial(solve_kernel, scale=scale),
                [left_out, half_out],
                packed,
                swap(packed, z, 8, 6),
                held,
                flops=pass_flops,
            )
        else:
            (gram,) = call(gram_kernel, [((8, 128), f32)], half)
            gram = sum_four(gram, z + ("core",), 16, (1, 12, 13))
            spread = jnp.broadcast_to(gram[None], (16,) + gram.shape)
            grams = lax.all_to_all(spread, ("x", "level"), 0, 0)
            basis, factor = call(
                functools.partial(last_kernel, scale=math.sqrt(total_rows)),
                [((K, PIECE), f32), ((K, K), f32)],
                grams,
                half,
            )
    return basis, factor


def solution(mesh):
    names = ("x", "cube", "level", "y", "core")
    split = Mesh(mesh.devices.reshape(4, 2, 4, 4, 2), names)
    row, col = names[:3], names[3:]
    return jax.shard_map(
        body,
        mesh=split,
        in_specs=(P(row, col), P(), P(col)),
        out_specs=(P(None, row + col), P()),
        check_vma=False,
    )
```

time: 130 us -> 125 us (0.962)
  blocking collectives: 16.7 us -> 11.8 us
  Pallas kernels: 11.3 us -> 15.4 us
  starting transfers between devices: 48.9 us -> 51.7 us
  local copies, waits for them, and re-layouts: 3.41 us -> 1.34 us
  waiting for transfers between devices: 44.2 us -> 42.4 us
  other arithmetic: 1.96 us -> 0.27 us
    all_to_all x1, blocking collectives: 16.7 us -> 11.8 us  [body(): grams = lax.all_to_all(spread, ('x', 'level'), 0, 0)]
    pallas_call x6 -> x12, Pallas kernels: 11.3 us -> 15.4 us  [call(): pl.pallas_call(kernel, in_specs=spaces or [whole] * len(args), out_specs=...]
    ppermute x29 -> x31, starting transfers between devices: 48.9 us -> 51.7 us  [swap(): return lax.ppermute(value, axis, [(i, i ^ offset) for i in range(count)])]
    unnamed x4, local copies, waits for them, and re-layouts: 3.38 us -> 1.33 us
    ppermute x29 -> x31, waiting for transfers between devices: 44.2 us -> 42.4 us  [swap(): return lax.ppermute(value, axis, [(i, i ^ offset) for i in range(count)])]
  transfers between devices with their start and end apart: 29 -> 31, of which waited for: 27 -> 25; matrix products, arithmetic and copies ran while one was open for 0% -> 0% of each run, Pallas kernels for 0% -> 4%
where the time goes in v3:
time: 125 us; the launch traced here: 124 us
  starting transfers between devices  51.7 us (41%)
  waiting for transfers between devices  42.4 us (34%)
  Pallas kernels  15.4 us (12%)
  blocking collectives  11.8 us (9%)
  local copies, waits for them, and re-layouts  1.34 us (1%)
    ppermute x31, starting transfers between devices, swap(): return lax.ppermute(value, axis, [(i, i ^ offset) for i in range(count)])  51.7 us
    ppermute x31, waiting for transfers between devices, swap(): return lax.ppermute(value, axis, [(i, i ^ offset) for i in range(count)])  42.4 us
    pallas_call x12, Pallas kernels, call(): pl.pallas_call(kernel, in_specs=spaces or [whole] * len(args), out_specs=...  15.4 us
    all_to_all x1, blocking collectives, body(): grams = lax.all_to_all(spread, ('x', 'level'), 0, 0)  11.8 us
  transfers between devices with their start and end apart: 31, of which 25 were waited for; matrix products, arithmetic and copies ran while one was open for 0% of the time, Pallas kernels for 4%

profile of v3, /device:TPU:1, one launch (start us, length us, event | category | flops | bytes accessed | tf_op | source)
XLA Modules:
  0.0 123.6 jit_solution(4447667966048946354)
XLA Ops:
  2.0 4.0 %shard_map.50 = (bf16[16,1024]{1,0:T(8,128)(2,1)S(1)}, bf16[4096,1024]{1,0:T(8,128)(2,1)S(1)}, f32[16,2048]{1,0:T(8,128)S(1)}) custom-call(s32[16]{0:T(128)S(1)} %copy-done.1, s32[1,1024]{1,0:T(1,128)S(1)} %bitcast.1, bf16[4096,1024]{1,0:T(8,128)(2,1)} %affinity.1), custom_call_target="tpu_custom_call" | custom-call | flops 67108864 | bytes 4194304 | tf_op jit(solution)/shard_map/pallas_call | solution.py:206
  6.0 3.3 %collective-permute-start = (f32[16,2048]{1,0:T(8,128)S(1)}, f32[16,2048]{1,0:T(8,128)S(1)}, u32[]{:S(2)}, u32[]{:S(2)}) collective-permute-start(f32[16,2048]{1,0:T(8,128)S(1)} %get-tuple-element.11), channel_id=1, source_target_pairs={{0,1},{1,0},{2,3},{3,2},{4,5},{5,4},{6,7},{7,6},{8,9},{9,8},{10,11... | collective-permute-start | bytes 393224 | tf_op jit(solution)/shard_map/ppermute | solution.py:44
  9.3 1.2 shard_map.51
  10.6 1.1 collective-permute-start.3
  11.7 2.9 %collective-permute-start.1 = (f32[16,2048]{1,0:T(8,128)S(1)}, f32[16,2048]{1,0:T(8,128)S(1)}, u32[]{:S(2)}, u32[]{:S(2)}) collective-permute-start(f32[16,2048]{1,0:T(8,128)S(1)} %add.81), channel_id=1, source_target_pairs={{0,4},{2,6},{4,0},{6,2},{1,5},{3,7},{5,1},{7,3},{8,12},{10,14},{12... | collective-permute-start | bytes 393224 | tf_op jit(solution)/shard_map/ppermute | solution.py:44
  14.5 2.3 %collective-permute-done.3 = f32[16,2048]{1,0:T(8,128)S(1)} collective-permute-done((f32[16,2048]{1,0:T(8,128)S(1)}, f32[16,2048]{1,0:T(8,128)S(1)}, u32[]{:S(2)}, u32[]{:S(2)}) %collective-permute-start.3) | collective-permute-done | bytes 131104 | tf_op jit(solution)/shard_map/ppermute | solution.py:44
  16.8 3.7 %collective-permute-done.1 = f32[16,2048]{1,0:T(8,128)S(1)} collective-permute-done((f32[16,2048]{1,0:T(8,128)S(1)}, f32[16,2048]{1,0:T(8,128)S(1)}, u32[]{:S(2)}, u32[]{:S(2)}) %collective-permute-start.1) | collective-permute-done | bytes 131104 | tf_op jit(solution)/shard_map/ppermute | solution.py:44
  20.5 1.4 %collective-permute-start.4 = (f32[16,2048]{1,0:T(8,128)S(1)}, f32[16,2048]{1,0:T(8,128)S(1)}, u32[]{:S(2)}, u32[]{:S(2)}) collective-permute-start(f32[16,2048]{1,0:T(8,128)S(1)} %add_add_fusion.2.half), channel_id=1, source_target_pairs={{0,1},{1,0},{2,3},{3,2},{4,5},{5,4},{6,7},{7,6},{8,9},{9,8},{10,11... | collective-permute-start | bytes 393224 | tf_op jit(solution)/shard_map/ppermute | solution.py:44
  22.9 0.9 shard_map.53
  24.7 3.0 %collective-permute-start.5 = (f32[16,1152]{1,0:T(8,128)S(1)}, f32[16,1152]{1,0:T(8,128)S(1)}, u32[]{:S(2)}, u32[]{:S(2)}) collective-permute-start(f32[16,1152]{1,0:T(8,128)S(1)} %shard_map.53), channel_id=1, source_target_pairs={{0,128},{64,192},{128,0},{192,64},{1,129},{65,193},{129,1},{193,65... | collective-permute-start | bytes 221192 | tf_op jit(solution)/shard_map/ppermute | solution.py:44
  28.3 2.4 %collective-permute-done.5 = f32[16,1152]{1,0:T(8,128)S(1)} collective-permute-done((f32[16,1152]{1,0:T(8,128)S(1)}, f32[16,1152]{1,0:T(8,128)S(1)}, u32[]{:S(2)}, u32[]{:S(2)}) %collective-permute-start.5) | collective-permute-done | bytes 73760 | tf_op jit(solution)/shard_map/ppermute | solution.py:44
  30.7 3.5 %collective-permute-start.10 = (f32[16,1152]{1,0:T(8,128)S(1)}, f32[16,1152]{1,0:T(8,128)S(1)}, u32[]{:S(2)}, u32[]{:S(2)}) collective-permute-start(f32[16,1152]{1,0:T(8,128)S(1)} %add_add_fusion.6), channel_id=1, source_target_pairs={{0,24},{8,16},{16,8},{24,0},{32,56},{40,48},{48,40},{56,32},{1,25}... | collective-permute-start | bytes 221192 | tf_op jit(solution)/shard_map/ppermute | solution.py:44
  34.6 1.4 %collective-permute-done.10 = f32[16,1152]{1,0:T(8,128)S(1)} collective-permute-done((f32[16,1152]{1,0:T(8,128)S(1)}, f32[16,1152]{1,0:T(8,128)S(1)}, u32[]{:S(2)}, u32[]{:S(2)}) %collective-permute-start.10) | collective-permute-done | bytes 73760 | tf_op jit(solution)/shard_map/ppermute | solution.py:44
  36.0 3.0 %collective-permute-done.9 = f32[16,1152]{1,0:T(8,128)S(1)} collective-permute-done((f32[16,1152]{1,0:T(8,128)S(1)}, f32[16,1152]{1,0:T(8,128)S(1)}, u32[]{:S(2)}, u32[]{:S(2)}) %collective-permute-start.9) | collective-permute-done | bytes 73760 | tf_op jit(solution)/shard_map/ppermute | solution.py:44
  39.0 4.0 %collective-permute-start.11 = (f32[16,1152]{1,0:T(8,128)S(1)}, f32[16,1152]{1,0:T(8,128)S(1)}, u32[]{:S(2)}, u32[]{:S(2)}) collective-permute-start(f32[16,1152]{1,0:T(8,128)S(1)} %add_add_fusion.5.mine), channel_id=1, source_target_pairs={{0,48},{8,56},{16,32},{24,40},{32,16},{40,24},{48,0},{56,8},{1,49}... | collective-permute-start | bytes 221192 | tf_op jit(solution)/shard_map/ppermute | solution.py:44
  43.1 1.9 %collective-permute-done.11.theirs = f32[16,1152]{1,0:T(8,128)S(1)} collective-permute-done((f32[16,1152]{1,0:T(8,128)S(1)}, f32[16,1152]{1,0:T(8,128)S(1)}, u32[]{:S(2)}, u32[]{:S(2)}) %collective-permute-start.11) | collective-permute-done | bytes 73760 | tf_op jit(solution)/shard_map/ppermute | solution.py:44
  45.0 1.4 %shard_map.54 = (bf16[16,1024]{1,0:T(8,128)(2,1)S(1)}, f32[16,2048]{1,0:T(8,128)S(1)}) custom-call(f32[16,1152]{1,0:T(8,128)S(1)} %add_add_fusion.5.mine, f32[16,1152]{1,0:T(8,128)S(1)} %collective-permute-done.11.theirs, bf16[4096,1024]{1,0:T(8,128)(2,1)S(1)} %get-tuple-element.10.held), custom_call_target="tpu_custom_call" | custom-call | flops 67108864 | bytes 4194304 | tf_op jit(solution)/shard_map/pallas_call | solution.py:206
  46.4 4.1 %collective-permute-start.12 = (f32[16,2048]{1,0:T(8,128)S(1)}, f32[16,2048]{1,0:T(8,128)S(1)}, u32[]{:S(2)}, u32[]{:S(2)}) collective-permute-start(f32[16,2048]{1,0:T(8,128)S(1)} %get-tuple-element.13), channel_id=1, source_target_pairs={{0,1},{1,0},{2,3},{3,2},{4,5},{5,4},{6,7},{7,6},{8,9},{9,8},{10,11... | collective-permute-start | bytes 393224 | tf_op jit(solution)/shard_map/ppermute | solution.py:44
  50.5 1.2 shard_map.55
  51.7 2.7 %collective-permute-start.15 = (f32[16,2048]{1,0:T(8,128)S(1)}, f32[16,2048]{1,0:T(8,128)S(1)}, u32[]{:S(2)}, u32[]{:S(2)}) collective-permute-start(f32[16,2048]{1,0:T(8,128)S(1)} %add.91), channel_id=1, source_target_pairs={{0,6},{2,4},{4,2},{6,0},{1,7},{3,5},{5,3},{7,1},{8,14},{10,12},{12... | collective-permute-start | bytes 393224 | tf_op jit(solution)/shard_map/ppermute | solution.py:44
  54.4 1.3 %collective-permute-start.13 = (f32[16,2048]{1,0:T(8,128)S(1)}, f32[16,2048]{1,0:T(8,128)S(1)}, u32[]{:S(2)}, u32[]{:S(2)}) collective-permute-start(f32[16,2048]{1,0:T(8,128)S(1)} %add.91), channel_id=1, source_target_pairs={{0,4},{2,6},{4,0},{6,2},{1,5},{3,7},{5,1},{7,3},{8,12},{10,14},{12... | collective-permute-start | bytes 393224 | tf_op jit(solution)/shard_map/ppermute | solution.py:44
  55.7 2.3 %collective-permute-done.15 = f32[16,2048]{1,0:T(8,128)S(1)} collective-permute-done((f32[16,2048]{1,0:T(8,128)S(1)}, f32[16,2048]{1,0:T(8,128)S(1)}, u32[]{:S(2)}, u32[]{:S(2)}) %collective-permute-start.15) | collective-permute-done | bytes 131104 | tf_op jit(solution)/shard_map/ppermute | solution.py:44
  58.0 1.0 collective-permute-done.14
  59.0 2.6 %collective-permute-done.13 = f32[16,2048]{1,0:T(8,128)S(1)} collective-permute-done((f32[16,2048]{1,0:T(8,128)S(1)}, f32[16,2048]{1,0:T(8,128)S(1)}, u32[]{:S(2)}, u32[]{:S(2)}) %collective-permute-start.13) | collective-permute-done | bytes 131104 | tf_op jit(solution)/shard_map/ppermute | solution.py:44
  61.7 1.4 %collective-permute-start.16 = (f32[16,2048]{1,0:T(8,128)S(1)}, f32[16,2048]{1,0:T(8,128)S(1)}, u32[]{:S(2)}, u32[]{:S(2)}) collective-permute-start(f32[16,2048]{1,0:T(8,128)S(1)} %add_add_fusion.1.half), channel_id=1, source_target_pairs={{0,1},{1,0},{2,3},{3,2},{4,5},{5,4},{6,7},{7,6},{8,9},{9,8},{10,11... | collective-permute-start | bytes 393224 | tf_op jit(solution)/shard_map/ppermute | solution.py:44
  65.0 1.9 %collective-permute-start.19 = (f32[16,1152]{1,0:T(8,128)S(1)}, f32[16,1152]{1,0:T(8,128)S(1)}, u32[]{:S(2)}, u32[]{:S(2)}) collective-permute-start(f32[16,1152]{1,0:T(8,128)S(1)} %shard_map.57), channel_id=1, source_target_pairs={{0,192},{64,128},{128,64},{192,0},{1,193},{65,129},{129,65},{193,1... | collective-permute-start | bytes 221192 | tf_op jit(solution)/shard_map/ppermute | solution.py:44
  66.8 2.0 %collective-permute-start.17 = (f32[16,1152]{1,0:T(8,128)S(1)}, f32[16,1152]{1,0:T(8,128)S(1)}, u32[]{:S(2)}, u32[]{:S(2)}) collective-permute-start(f32[16,1152]{1,0:T(8,128)S(1)} %shard_map.57), channel_id=1, source_target_pairs={{0,128},{64,192},{128,0},{192,64},{1,129},{65,193},{129,1},{193,65... | collective-permute-start | bytes 221192 | tf_op jit(solution)/shard_map/ppermute | solution.py:44
  70.3 1.9 %collective-permute-done.17 = f32[16,1152]{1,0:T(8,128)S(1)} collective-permute-done((f32[16,1152]{1,0:T(8,128)S(1)}, f32[16,1152]{1,0:T(8,128)S(1)}, u32[]{:S(2)}, u32[]{:S(2)}) %collective-permute-start.17) | collective-permute-done | bytes 73760 | tf_op jit(solution)/shard_map/ppermute | solution.py:44
  72.2 2.4 %collective-permute-start.22 = (f32[16,1152]{1,0:T(8,128)S(1)}, f32[16,1152]{1,0:T(8,128)S(1)}, u32[]{:S(2)}, u32[]{:S(2)}) collective-permute-start(f32[16,1152]{1,0:T(8,128)S(1)} %add_add_fusion.4), channel_id=1, source_target_pairs={{0,24},{8,16},{16,8},{24,0},{32,56},{40,48},{48,40},{56,32},{1,25}... | collective-permute-start | bytes 221192 | tf_op jit(solution)/shard_map/ppermute | solution.py:44
  74.6 1.2 collective-permute-start.20
  75.9 1.6 %collective-permute-done.22 = f32[16,1152]{1,0:T(8,128)S(1)} collective-permute-done((f32[16,1152]{1,0:T(8,128)S(1)}, f32[16,1152]{1,0:T(8,128)S(1)}, u32[]{:S(2)}, u32[]{:S(2)}) %collective-permute-start.22) | collective-permute-done | bytes 73760 | tf_op jit(solution)/shard_map/ppermute | solution.py:44
  77.4 1.5 %collective-permute-done.21 = f32[16,1152]{1,0:T(8,128)S(1)} collective-permute-done((f32[16,1152]{1,0:T(8,128)S(1)}, f32[16,1152]{1,0:T(8,128)S(1)}, u32[]{:S(2)}, u32[]{:S(2)}) %collective-permute-start.21) | collective-permute-done | bytes 73760 | tf_op jit(solution)/shard_map/ppermute | solution.py:44
  78.9 2.0 %collective-permute-done.20 = f32[16,1152]{1,0:T(8,128)S(1)} collective-permute-done((f32[16,1152]{1,0:T(8,128)S(1)}, f32[16,1152]{1,0:T(8,128)S(1)}, u32[]{:S(2)}, u32[]{:S(2)}) %collective-permute-start.20) | collective-permute-done | bytes 73760 | tf_op jit(solution)/shard_map/ppermute | solution.py:44
  81.0 2.1 %collective-permute-start.23 = (f32[16,1152]{1,0:T(8,128)S(1)}, f32[16,1152]{1,0:T(8,128)S(1)}, u32[]{:S(2)}, u32[]{:S(2)}) collective-permute-start(f32[16,1152]{1,0:T(8,128)S(1)} %add_add_fusion.3.mine), channel_id=1, source_target_pairs={{0,48},{8,56},{16,32},{24,40},{32,16},{40,24},{48,0},{56,8},{1,49}... | collective-permute-start | bytes 221192 | tf_op jit(solution)/shard_map/ppermute | solution.py:44
  83.0 3.4 %collective-permute-done.23.theirs = f32[16,1152]{1,0:T(8,128)S(1)} collective-permute-done((f32[16,1152]{1,0:T(8,128)S(1)}, f32[16,1152]{1,0:T(8,128)S(1)}, u32[]{:S(2)}, u32[]{:S(2)}) %collective-permute-start.23) | collective-permute-done | bytes 73760 | tf_op jit(solution)/shard_map/ppermute | solution.py:44
  86.5 1.4 %shard_map.58 = (bf16[16,1024]{1,0:T(8,128)(2,1)S(1)}, f32[16,2048]{1,0:T(8,128)S(1)}) custom-call(f32[16,1152]{1,0:T(8,128)S(1)} %add_add_fusion.3.mine, f32[16,1152]{1,0:T(8,128)S(1)} %collective-permute-done.23.theirs, bf16[4096,1024]{1,0:T(8,128)(2,1)S(1)} %get-tuple-element.10.held), custom_call_target="tpu_custom_call" | custom-call | flops 67108864 | bytes 4194304 | tf_op jit(solution)/shard_map/pallas_call | solution.py:206
  87.8 3.5 %collective-permute-start.24 = (f32[16,2048]{1,0:T(8,128)S(1)}, f32[16,2048]{1,0:T(8,128)S(1)}, u32[]{:S(2)}, u32[]{:S(2)}) collective-permute-start(f32[16,2048]{1,0:T(8,128)S(1)} %get-tuple-element.15), channel_id=1, source_target_pairs={{0,1},{1,0},{2,3},{3,2},{4,5},{5,4},{6,7},{7,6},{8,9},{9,8},{10,11... | collective-permute-start | bytes 393224 | tf_op jit(solution)/shard_map/ppermute | solution.py:44
  91.4 1.2 shard_map.59
  92.6 2.7 %collective-permute-start.27 = (f32[16,2048]{1,0:T(8,128)S(1)}, f32[16,2048]{1,0:T(8,128)S(1)}, u32[]{:S(2)}, u32[]{:S(2)}) collective-permute-start(f32[16,2048]{1,0:T(8,128)S(1)} %add.101), channel_id=1, source_target_pairs={{0,6},{2,4},{4,2},{6,0},{1,7},{3,5},{5,3},{7,1},{8,14},{10,12},{12... | collective-permute-start | bytes 393224 | tf_op jit(solution)/shard_map/ppermute | solution.py:44
  95.2 1.3 %collective-permute-start.25 = (f32[16,2048]{1,0:T(8,128)S(1)}, f32[16,2048]{1,0:T(8,128)S(1)}, u32[]{:S(2)}, u32[]{:S(2)}) collective-permute-start(f32[16,2048]{1,0:T(8,128)S(1)} %add.101), channel_id=1, source_target_pairs={{0,4},{2,6},{4,0},{6,2},{1,5},{3,7},{5,1},{7,3},{8,12},{10,14},{12... | collective-permute-start | bytes 393224 | tf_op jit(solution)/shard_map/ppermute | solution.py:44
  96.5 2.3 %collective-permute-done.27 = f32[16,2048]{1,0:T(8,128)S(1)} collective-permute-done((f32[16,2048]{1,0:T(8,128)S(1)}, f32[16,2048]{1,0:T(8,128)S(1)}, u32[]{:S(2)}, u32[]{:S(2)}) %collective-permute-start.27) | collective-permute-done | bytes 131104 | tf_op jit(solution)/shard_map/ppermute | solution.py:44
  98.8 1.0 collective-permute-done.26
  99.9 2.6 %collective-permute-done.25 = f32[16,2048]{1,0:T(8,128)S(1)} collective-permute-done((f32[16,2048]{1,0:T(8,128)S(1)}, f32[16,2048]{1,0:T(8,128)S(1)}, u32[]{:S(2)}, u32[]{:S(2)}) %collective-permute-start.25) | collective-permute-done | bytes 131104 | tf_op jit(solution)/shard_map/ppermute | solution.py:44
  102.9 3.4 %collective-permute-start.30 = (f32[8,128]{1,0:T(8,128)S(1)}, f32[8,128]{1,0:T(8,128)S(1)}, u32[]{:S(2)}, u32[]{:S(2)}) collective-permute-start(f32[8,128]{1,0:T(8,128)S(1)} %shard_map.60), channel_id=1, source_target_pairs={{0,49},{1,48},{8,57},{9,56},{16,33},{17,32},{24,41},{25,40},{32,17... | collective-permute-start | bytes 12296 | tf_op jit(solution)/shard_map/ppermute | solution.py:44
  106.3 1.4 %collective-permute-start.28 = (f32[8,128]{1,0:T(8,128)S(1)}, f32[8,128]{1,0:T(8,128)S(1)}, u32[]{:S(2)}, u32[]{:S(2)}) collective-permute-start(f32[8,128]{1,0:T(8,128)S(1)} %shard_map.60), channel_id=1, source_target_pairs={{0,48},{1,49},{8,56},{9,57},{16,32},{17,33},{24,40},{25,41},{32,16... | collective-permute-start | bytes 12296 | tf_op jit(solution)/shard_map/ppermute | solution.py:44
  108.1 2.8 %collective-permute-done.28 = f32[8,128]{1,0:T(8,128)S(1)} collective-permute-done((f32[8,128]{1,0:T(8,128)S(1)}, f32[8,128]{1,0:T(8,128)S(1)}, u32[]{:S(2)}, u32[]{:S(2)}) %collective-permute-start.28) | collective-permute-done | bytes 4128 | tf_op jit(solution)/shard_map/ppermute | solution.py:44
  110.8 11.8 %all_to_all.5.grams = f32[16,8,128]{2,1,0:T(8,128)S(1)} all-to-all(f32[16,8,128]{2,1,0:T(8,128)S(1)} %broadcast_in_dim.2), channel_id=1, replica_groups=mesh['x'=4,'cube'=2,'level'=4,'y'=4,'core'=2] {'x','level'}, dimensions={0} | all-to-all | bytes 131072 | tf_op jit(solution)/shard_map/all_to_all | solution.py:272
  122.6 1.0 shard_map.61
  (43 shorter events, 8.7 us)
Async XLA Ops:
  0.6 0.7 copy-start
  1.3 0.7 copy-start.1
  6.0 4.5 %collective-permute-start = (f32[16,2048]{1,0:T(8,128)S(1)}, f32[16,2048]{1,0:T(8,128)S(1)}, u32[]{:S(2)}, u32[]{:S(2)}) collective-permute-start(f32[16,2048]{1,0:T(8,128)S(1)} %get-tuple-element.11), channel_id=1, source_target_pairs={{0,1},{1,0},{2,3},{3,2},{4,5},{5,4},{6,7},{7,6},{8,9},{9,8},{10,11... | collective-permute-start | bytes 393224 | tf_op jit(solution)/shard_map/ppermute | solution.py:44
  10.6 6.3 %collective-permute-start.3 = (f32[16,2048]{1,0:T(8,128)S(1)}, f32[16,2048]{1,0:T(8,128)S(1)}, u32[]{:S(2)}, u32[]{:S(2)}) collective-permute-start(f32[16,2048]{1,0:T(8,128)S(1)} %add.81), channel_id=1, source_target_pairs={{0,6},{2,4},{4,2},{6,0},{1,7},{3,5},{5,3},{7,1},{8,14},{10,12},{12... | collective-permute-start | bytes 393224 | tf_op jit(solution)/shard_map/ppermute | solution.py:44
  11.6 5.2 %collective-permute-start.2 = (f32[16,2048]{1,0:T(8,128)S(1)}, f32[16,2048]{1,0:T(8,128)S(1)}, u32[]{:S(2)}, u32[]{:S(2)}) collective-permute-start(f32[16,2048]{1,0:T(8,128)S(1)} %add.81), channel_id=1, source_target_pairs={{0,2},{2,0},{4,6},{6,4},{1,3},{3,1},{5,7},{7,5},{8,10},{10,8},{12,... | collective-permute-start | bytes 393224 | tf_op jit(solution)/shard_map/ppermute | solution.py:44
  11.7 8.8 %collective-permute-start.1 = (f32[16,2048]{1,0:T(8,128)S(1)}, f32[16,2048]{1,0:T(8,128)S(1)}, u32[]{:S(2)}, u32[]{:S(2)}) collective-permute-start(f32[16,2048]{1,0:T(8,128)S(1)} %add.81), channel_id=1, source_target_pairs={{0,4},{2,6},{4,0},{6,2},{1,5},{3,7},{5,1},{7,3},{8,12},{10,14},{12... | collective-permute-start | bytes 393224 | tf_op jit(solution)/shard_map/ppermute | solution.py:44
  20.5 2.3 %collective-permute-start.4 = (f32[16,2048]{1,0:T(8,128)S(1)}, f32[16,2048]{1,0:T(8,128)S(1)}, u32[]{:S(2)}, u32[]{:S(2)}) collective-permute-start(f32[16,2048]{1,0:T(8,128)S(1)} %add_add_fusion.2.half), channel_id=1, source_target_pairs={{0,1},{1,0},{2,3},{3,2},{4,5},{5,4},{6,7},{7,6},{8,9},{9,8},{10,11... | collective-permute-start | bytes 393224 | tf_op jit(solution)/shard_map/ppermute | solution.py:44
  23.8 4.4 %collective-permute-start.7 = (f32[16,1152]{1,0:T(8,128)S(1)}, f32[16,1152]{1,0:T(8,128)S(1)}, u32[]{:S(2)}, u32[]{:S(2)}) collective-permute-start(f32[16,1152]{1,0:T(8,128)S(1)} %shard_map.53), channel_id=1, source_target_pairs={{0,192},{64,128},{128,64},{192,0},{1,193},{65,129},{129,65},{193,1... | collective-permute-start | bytes 221192 | tf_op jit(solution)/shard_map/ppermute | solution.py:44
  24.7 3.5 %collective-permute-start.6 = (f32[16,1152]{1,0:T(8,128)S(1)}, f32[16,1152]{1,0:T(8,128)S(1)}, u32[]{:S(2)}, u32[]{:S(2)}) collective-permute-start(f32[16,1152]{1,0:T(8,128)S(1)} %shard_map.53), channel_id=1, source_target_pairs={{0,64},{64,0},{128,192},{192,128},{1,65},{65,1},{129,193},{193,129... | collective-permute-start | bytes 221192 | tf_op jit(solution)/shard_map/ppermute | solution.py:44
  24.7 6.0 %collective-permute-start.5 = (f32[16,1152]{1,0:T(8,128)S(1)}, f32[16,1152]{1,0:T(8,128)S(1)}, u32[]{:S(2)}, u32[]{:S(2)}) collective-permute-start(f32[16,1152]{1,0:T(8,128)S(1)} %shard_map.53), channel_id=1, source_target_pairs={{0,128},{64,192},{128,0},{192,64},{1,129},{65,193},{129,1},{193,65... | collective-permute-start | bytes 221192 | tf_op jit(solution)/shard_map/ppermute | solution.py:44
  30.7 5.2 %collective-permute-start.10 = (f32[16,1152]{1,0:T(8,128)S(1)}, f32[16,1152]{1,0:T(8,128)S(1)}, u32[]{:S(2)}, u32[]{:S(2)}) collective-permute-start(f32[16,1152]{1,0:T(8,128)S(1)} %add_add_fusion.6), channel_id=1, source_target_pairs={{0,24},{8,16},{16,8},{24,0},{32,56},{40,48},{48,40},{56,32},{1,25}... | collective-permute-start | bytes 221192 | tf_op jit(solution)/shard_map/ppermute | solution.py:44
  34.2 4.7 %collective-permute-start.9 = (f32[16,1152]{1,0:T(8,128)S(1)}, f32[16,1152]{1,0:T(8,128)S(1)}, u32[]{:S(2)}, u32[]{:S(2)}) collective-permute-start(f32[16,1152]{1,0:T(8,128)S(1)} %add_add_fusion.6), channel_id=1, source_target_pairs={{0,8},{8,0},{16,24},{24,16},{32,40},{40,32},{48,56},{56,48},{1,9},... | collective-permute-start | bytes 221192 | tf_op jit(solution)/shard_map/ppermute | solution.py:44
  34.2 4.8 %collective-permute-start.8 = (f32[16,1152]{1,0:T(8,128)S(1)}, f32[16,1152]{1,0:T(8,128)S(1)}, u32[]{:S(2)}, u32[]{:S(2)}) collective-permute-start(f32[16,1152]{1,0:T(8,128)S(1)} %add_add_fusion.6), channel_id=1, source_target_pairs={{0,16},{8,24},{16,0},{24,8},{32,48},{40,56},{48,32},{56,40},{1,17}... | collective-permute-start | bytes 221192 | tf_op jit(solution)/shard_map/ppermute | solution.py:44
  39.0 6.0 %collective-permute-start.11 = (f32[16,1152]{1,0:T(8,128)S(1)}, f32[16,1152]{1,0:T(8,128)S(1)}, u32[]{:S(2)}, u32[]{:S(2)}) collective-permute-start(f32[16,1152]{1,0:T(8,128)S(1)} %add_add_fusion.5.mine), channel_id=1, source_target_pairs={{0,48},{8,56},{16,32},{24,40},{32,16},{40,24},{48,0},{56,8},{1,49}... | collective-permute-start | bytes 221192 | tf_op jit(solution)/shard_map/ppermute | solution.py:44
  46.4 5.3 %collective-permute-start.12 = (f32[16,2048]{1,0:T(8,128)S(1)}, f32[16,2048]{1,0:T(8,128)S(1)}, u32[]{:S(2)}, u32[]{:S(2)}) collective-permute-start(f32[16,2048]{1,0:T(8,128)S(1)} %get-tuple-element.13), channel_id=1, source_target_pairs={{0,1},{1,0},{2,3},{3,2},{4,5},{5,4},{6,7},{7,6},{8,9},{9,8},{10,11... | collective-permute-start | bytes 393224 | tf_op jit(solution)/shard_map/ppermute | solution.py:44
  51.7 6.3 %collective-permute-start.15 = (f32[16,2048]{1,0:T(8,128)S(1)}, f32[16,2048]{1,0:T(8,128)S(1)}, u32[]{:S(2)}, u32[]{:S(2)}) collective-permute-start(f32[16,2048]{1,0:T(8,128)S(1)} %add.91), channel_id=1, source_target_pairs={{0,6},{2,4},{4,2},{6,0},{1,7},{3,5},{5,3},{7,1},{8,14},{10,12},{12... | collective-permute-start | bytes 393224 | tf_op jit(solution)/shard_map/ppermute | solution.py:44
  54.4 4.6 %collective-permute-start.14 = (f32[16,2048]{1,0:T(8,128)S(1)}, f32[16,2048]{1,0:T(8,128)S(1)}, u32[]{:S(2)}, u32[]{:S(2)}) collective-permute-start(f32[16,2048]{1,0:T(8,128)S(1)} %add.91), channel_id=1, source_target_pairs={{0,2},{2,0},{4,6},{6,4},{1,3},{3,1},{5,7},{7,5},{8,10},{10,8},{12,... | collective-permute-start | bytes 393224 | tf_op jit(solution)/shard_map/ppermute | solution.py:44
  54.4 7.3 %collective-permute-start.13 = (f32[16,2048]{1,0:T(8,128)S(1)}, f32[16,2048]{1,0:T(8,128)S(1)}, u32[]{:S(2)}, u32[]{:S(2)}) collective-permute-start(f32[16,2048]{1,0:T(8,128)S(1)} %add.91), channel_id=1, source_target_pairs={{0,4},{2,6},{4,0},{6,2},{1,5},{3,7},{5,1},{7,3},{8,12},{10,14},{12... | collective-permute-start | bytes 393224 | tf_op jit(solution)/shard_map/ppermute | solution.py:44
  61.7 2.3 %collective-permute-start.16 = (f32[16,2048]{1,0:T(8,128)S(1)}, f32[16,2048]{1,0:T(8,128)S(1)}, u32[]{:S(2)}, u32[]{:S(2)}) collective-permute-start(f32[16,2048]{1,0:T(8,128)S(1)} %add_add_fusion.1.half), channel_id=1, source_target_pairs={{0,1},{1,0},{2,3},{3,2},{4,5},{5,4},{6,7},{7,6},{8,9},{9,8},{10,11... | collective-permute-start | bytes 393224 | tf_op jit(solution)/shard_map/ppermute | solution.py:44
  65.0 4.4 %collective-permute-start.19 = (f32[16,1152]{1,0:T(8,128)S(1)}, f32[16,1152]{1,0:T(8,128)S(1)}, u32[]{:S(2)}, u32[]{:S(2)}) collective-permute-start(f32[16,1152]{1,0:T(8,128)S(1)} %shard_map.57), channel_id=1, source_target_pairs={{0,192},{64,128},{128,64},{192,0},{1,193},{65,129},{129,65},{193,1... | collective-permute-start | bytes 221192 | tf_op jit(solution)/shard_map/ppermute | solution.py:44
  66.8 3.5 %collective-permute-start.18 = (f32[16,1152]{1,0:T(8,128)S(1)}, f32[16,1152]{1,0:T(8,128)S(1)}, u32[]{:S(2)}, u32[]{:S(2)}) collective-permute-start(f32[16,1152]{1,0:T(8,128)S(1)} %shard_map.57), channel_id=1, source_target_pairs={{0,64},{64,0},{128,192},{192,128},{1,65},{65,1},{129,193},{193,129... | collective-permute-start | bytes 221192 | tf_op jit(solution)/shard_map/ppermute | solution.py:44
  66.8 5.3 %collective-permute-start.17 = (f32[16,1152]{1,0:T(8,128)S(1)}, f32[16,1152]{1,0:T(8,128)S(1)}, u32[]{:S(2)}, u32[]{:S(2)}) collective-permute-start(f32[16,1152]{1,0:T(8,128)S(1)} %shard_map.57), channel_id=1, source_target_pairs={{0,128},{64,192},{128,0},{192,64},{1,129},{65,193},{129,1},{193,65... | collective-permute-start | bytes 221192 | tf_op jit(solution)/shard_map/ppermute | solution.py:44
  72.2 5.2 %collective-permute-start.22 = (f32[16,1152]{1,0:T(8,128)S(1)}, f32[16,1152]{1,0:T(8,128)S(1)}, u32[]{:S(2)}, u32[]{:S(2)}) collective-permute-start(f32[16,1152]{1,0:T(8,128)S(1)} %add_add_fusion.4), channel_id=1, source_target_pairs={{0,24},{8,16},{16,8},{24,0},{32,56},{40,48},{48,40},{56,32},{1,25}... | collective-permute-start | bytes 221192 | tf_op jit(solution)/shard_map/ppermute | solution.py:44
  74.6 4.3 %collective-permute-start.21 = (f32[16,1152]{1,0:T(8,128)S(1)}, f32[16,1152]{1,0:T(8,128)S(1)}, u32[]{:S(2)}, u32[]{:S(2)}) collective-permute-start(f32[16,1152]{1,0:T(8,128)S(1)} %add_add_fusion.4), channel_id=1, source_target_pairs={{0,8},{8,0},{16,24},{24,16},{32,40},{40,32},{48,56},{56,48},{1,9},... | collective-permute-start | bytes 221192 | tf_op jit(solution)/shard_map/ppermute | solution.py:44
  74.6 6.3 %collective-permute-start.20 = (f32[16,1152]{1,0:T(8,128)S(1)}, f32[16,1152]{1,0:T(8,128)S(1)}, u32[]{:S(2)}, u32[]{:S(2)}) collective-permute-start(f32[16,1152]{1,0:T(8,128)S(1)} %add_add_fusion.4), channel_id=1, source_target_pairs={{0,16},{8,24},{16,0},{24,8},{32,48},{40,56},{48,32},{56,40},{1,17}... | collective-permute-start | bytes 221192 | tf_op jit(solution)/shard_map/ppermute | solution.py:44
  81.0 5.5 %collective-permute-start.23 = (f32[16,1152]{1,0:T(8,128)S(1)}, f32[16,1152]{1,0:T(8,128)S(1)}, u32[]{:S(2)}, u32[]{:S(2)}) collective-permute-start(f32[16,1152]{1,0:T(8,128)S(1)} %add_add_fusion.3.mine), channel_id=1, source_target_pairs={{0,48},{8,56},{16,32},{24,40},{32,16},{40,24},{48,0},{56,8},{1,49}... | collective-permute-start | bytes 221192 | tf_op jit(solution)/shard_map/ppermute | solution.py:44
  87.8 4.7 %collective-permute-start.24 = (f32[16,2048]{1,0:T(8,128)S(1)}, f32[16,2048]{1,0:T(8,128)S(1)}, u32[]{:S(2)}, u32[]{:S(2)}) collective-permute-start(f32[16,2048]{1,0:T(8,128)S(1)} %get-tuple-element.15), channel_id=1, source_target_pairs={{0,1},{1,0},{2,3},{3,2},{4,5},{5,4},{6,7},{7,6},{8,9},{9,8},{10,11... | collective-permute-start | bytes 393224 | tf_op jit(solution)/shard_map/ppermute | solution.py:44
  92.6 6.3 %collective-permute-start.27 = (f32[16,2048]{1,0:T(8,128)S(1)}, f32[16,2048]{1,0:T(8,128)S(1)}, u32[]{:S(2)}, u32[]{:S(2)}) collective-permute-start(f32[16,2048]{1,0:T(8,128)S(1)} %add.101), channel_id=1, source_target_pairs={{0,6},{2,4},{4,2},{6,0},{1,7},{3,5},{5,3},{7,1},{8,14},{10,12},{12... | collective-permute-start | bytes 393224 | tf_op jit(solution)/shard_map/ppermute | solution.py:44
  95.2 4.6 %collective-permute-start.26 = (f32[16,2048]{1,0:T(8,128)S(1)}, f32[16,2048]{1,0:T(8,128)S(1)}, u32[]{:S(2)}, u32[]{:S(2)}) collective-permute-start(f32[16,2048]{1,0:T(8,128)S(1)} %add.101), channel_id=1, source_target_pairs={{0,2},{2,0},{4,6},{6,4},{1,3},{3,1},{5,7},{7,5},{8,10},{10,8},{12,... | collective-permute-start | bytes 393224 | tf_op jit(solution)/shard_map/ppermute | solution.py:44
  95.2 7.3 %collective-permute-start.25 = (f32[16,2048]{1,0:T(8,128)S(1)}, f32[16,2048]{1,0:T(8,128)S(1)}, u32[]{:S(2)}, u32[]{:S(2)}) collective-permute-start(f32[16,2048]{1,0:T(8,128)S(1)} %add.101), channel_id=1, source_target_pairs={{0,4},{2,6},{4,0},{6,2},{1,5},{3,7},{5,1},{7,3},{8,12},{10,14},{12... | collective-permute-start | bytes 393224 | tf_op jit(solution)/shard_map/ppermute | solution.py:44
  102.9 5.2 %collective-permute-start.30 = (f32[8,128]{1,0:T(8,128)S(1)}, f32[8,128]{1,0:T(8,128)S(1)}, u32[]{:S(2)}, u32[]{:S(2)}) collective-permute-start(f32[8,128]{1,0:T(8,128)S(1)} %shard_map.60), channel_id=1, source_target_pairs={{0,49},{1,48},{8,57},{9,56},{16,33},{17,32},{24,41},{25,40},{32,17... | collective-permute-start | bytes 12296 | tf_op jit(solution)/shard_map/ppermute | solution.py:44
  106.3 1.8 %collective-permute-start.29 = (f32[8,128]{1,0:T(8,128)S(1)}, f32[8,128]{1,0:T(8,128)S(1)}, u32[]{:S(2)}, u32[]{:S(2)}) collective-permute-start(f32[8,128]{1,0:T(8,128)S(1)} %shard_map.60), channel_id=1, source_target_pairs={{0,1},{1,0},{8,9},{9,8},{16,17},{17,16},{24,25},{25,24},{32,33},{3... | collective-permute-start | bytes 12296 | tf_op jit(solution)/shard_map/ppermute | solution.py:44
  106.3 4.6 %collective-permute-start.28 = (f32[8,128]{1,0:T(8,128)S(1)}, f32[8,128]{1,0:T(8,128)S(1)}, u32[]{:S(2)}, u32[]{:S(2)}) collective-permute-start(f32[8,128]{1,0:T(8,128)S(1)} %shard_map.60), channel_id=1, source_target_pairs={{0,48},{1,49},{8,56},{9,57},{16,32},{17,33},{24,40},{25,41},{32,16... | collective-permute-start | bytes 12296 | tf_op jit(solution)/shard_map/ppermute | solution.py:44

commit v4 on v3

--- a/solution.py
+++ b/solution.py
@@ -47,10 +47,6 @@
 def sum_four(value, axis, count, offsets=(1, 2, 3)):
     one, two, three = (swap(value, axis, count, k) for k in offsets)
     return (value + two) + (one + three)
-
-
-def block_rows(piece, core):
-    return pl.ds(pl.multiple_of((2 * piece + core) * PIECE, PIECE), PIECE)
 
 
 def span(step):
@@ -105,57 +101,73 @@
     return lower, right / jnp.tile(root, (1, right.shape[1] // 128))
 
 
-def first_kernel(seed_values, sku_ids, affinity, omega, held, other, arrived, *, total_columns):
-    core = lax.axis_index("core")
+def load_half(affinity, held, arrived, side):
     copies = []
-    for side in (1 - core, core):
-        for step in range(4):
-            place = block_rows(step, side)
-            copies.append(
-                pltpu.make_async_copy(affinity.at[place], held.at[place], arrived.at[len(copies)])
-            )
-            copies[-1].start()
+    for step in range(4):
+        place = pl.multiple_of((2 * step + side) * PIECE, PIECE)
+        copies.append(
+            pltpu.make_async_copy(
+                affinity.at[pl.ds(place, PIECE)], held.at[span(step)], arrived.at[step]
+            )
+        )
+        copies[-1].start()
+    return copies
+
+
+def project_half(left, held, target, scale, copies=None):
+    for step in range(4):
+        if copies is not None:
+            copies[step].wait()
+        target[:, span(step)] = project_piece(left[...], held[span(step), :], scale)
+
+
+def first_kernel(
+    seed_values, sku_ids, affinity, left, held, other, seeds_here, ids_here, arrived, *, columns
+):
+    small = [
+        pltpu.make_async_copy(seed_values, seeds_here, arrived.at[4]),
+        pltpu.make_async_copy(sku_ids, ids_here, arrived.at[5]),
+    ]
+    for copy in small:
+        copy.start()
+    copies = load_half(affinity, held, arrived, 1 - lax.axis_index("core"))
+    for copy in small:
+        copy.wait()
     row = lax.broadcasted_iota(jnp.int32, (K, 128), 0)
     seeds = jnp.zeros((K, 128), jnp.int32)
     for k in range(K):
-        seeds = jnp.where(row == k, seed_values[k], seeds)
-    for start in range(0, sku_ids.shape[1], 128):
-        ids = jnp.broadcast_to(sku_ids[:, start : start + 128], (K, 128))
-        omega[:, start : start + 128] = test_matrix(seeds, ids, total_columns)
-    for step in range(4):
-        copies[step].wait()
-        rows = held[block_rows(step, 1 - core), :]
-        other[:, span(step)] = project_piece(omega[...], rows, None)
-    for step in range(4, 8):
-        copies[step].wait()
+        seeds = jnp.where(row == k, seeds_here[k], seeds)
+    for start in range(0, ids_here.shape[1], 128):
+        ids = jnp.broadcast_to(ids_here[:, start : start + 128], (K, 128))
+        left[:, start : start + 128] = test_matrix(seeds, ids, columns)
+    project_half(left, held, other, None, copies)
+
+
+def first_own_kernel(left, affinity, held, own, arrived):
+    copies = load_half(affinity, held, arrived, lax.axis_index("core"))
+    project_half(left, held, own, None, copies)
 
 
 def solve_kernel(mine, theirs, held, left, other, *, scale):
-    core = lax.axis_index("core")
     wide = held.shape[1]
     total = mine[...] + theirs[...]
     _, back = eliminate(total[:, wide:], total[:, :wide])
     left[...] = back.astype(jnp.bfloat16)
-    for step in range(4):
-        rows = held[block_rows(step, 1 - core), :]
-        other[:, span(step)] = project_piece(left[...], rows, scale)
+    project_half(left, held, other, scale)
 
 
 def own_kernel(left, held, own, *, scale):
-    core = lax.axis_index("core")
-    for step in range(4):
-        rows = held[block_rows(step, core), :]
-        own[:, span(step)] = project_piece(left[...], rows, scale)
-
-
-def back_sums(half, held, side):
+    project_half(left, held, own, scale)
+
+
+def back_sums(half, held):
     both = jnp.zeros((2 * K, held.shape[1]), jnp.float32)
     gram = jnp.zeros((3 * K, 3 * K), jnp.float32)
     for step in range(4):
         parts = split_bf16(half[:, span(step)])
         both += jnp.dot(
             jnp.concatenate(parts[:2], axis=0),
-            held[block_rows(step, side), :],
+            held[span(step), :],
             preferred_element_type=jnp.float32,
         )
         gram += triple_gram(parts)
@@ -164,7 +176,7 @@
 
 def back_own_kernel(half, held, packed):
     wide = held.shape[1]
-    back, gram = back_sums(half, held, lax.axis_index("core"))
+    back, gram = back_sums(half, held)
     packed[:, :wide] = back
     packed[:, wide:] = jnp.zeros((K, 128), jnp.float32)
     packed[:, wide : wide + K] = gram
@@ -172,7 +184,7 @@
 
 def back_other_kernel(half, held, before, packed):
     wide = held.shape[1]
-    back, gram = back_sums(half, held, 1 - lax.axis_index("core"))
+    back, gram = back_sums(half, held)
     packed[:, :wide] = before[:, :wide] + back
     packed[:, wide:] = jnp.zeros((K, 128), jnp.float32)
     packed[:, wide : wide + K] = before[:, wide : wide + K] + gram
@@ -227,42 +239,64 @@
     pass_flops = K * local_rows * local_columns
     z = ("cube", "level")
 
-    left, held, other = call(
-        functools.partial(first_kernel, total_columns=total_columns),
-        [left_out, (affinity.shape, jnp.bfloat16), half_out],
+    held_out = ((local_rows // 2, local_columns), jnp.bfloat16)
+    far = pl.BlockSpec(memory_space=pltpu.HBM)
+    near = pl.BlockSpec(memory_space=pltpu.VMEM)
+    affinity, seed_values, sku_ids = (
+        pltpu.with_memory_space_constraint(value, pltpu.HBM)
+        for value in (affinity, seed_values, sku_ids.reshape(1, -1))
+    )
+
+    left, held_other, other = call(
+        functools.partial(first_kernel, columns=total_columns),
+        [left_out, held_out, half_out],
         seed_values,
-        sku_ids.reshape(1, -1),
-        pltpu.with_memory_space_constraint(affinity, pltpu.HBM),
-        spaces=[
-            pl.BlockSpec(memory_space=pltpu.SMEM),
-            pl.BlockSpec(memory_space=pltpu.VMEM),
-            pl.BlockSpec(memory_space=pltpu.HBM),
+        sku_ids,
+        affinity,
+        spaces=[far, far, far],
+        scratch=[
+            pltpu.SMEM(seed_values.shape, jnp.int32),
+            pltpu.VMEM(sku_ids.shape, jnp.int32),
+            pltpu.SemaphoreType.DMA((6,)),
         ],
-        scratch=[pltpu.SemaphoreType.DMA((8,))],
         flops=pass_flops,
     )
-    scale = None
+    scale = 1.0 / math.sqrt(total_columns)
     for repeat in range(ITERS + 1):
         arriving = swap(other, "core", 2, 1)
-        (own,) = call(
-            functools.partial(own_kernel, scale=scale), [half_out], left, held, flops=pass_flops
-        )
+        if repeat == 0:
+            held_own, own = call(
+                first_own_kernel,
+                [held_out, half_out],
+                left,
+                affinity,
+                spaces=[near, far],
+                scratch=[pltpu.SemaphoreType.DMA((4,))],
+                flops=pass_flops,
+            )
+        else:
+            (own,) = call(
+                functools.partial(own_kernel, scale=scale),
+                [half_out],
+                left,
+                held_own,
+                flops=pass_flops,
+            )
         half = sum_four(own + arriving, "y", 4)
         if repeat < ITERS:
             sibling = swap(half, "core", 2, 1)
-            (packed,) = call(back_own_kernel, [packed_out], half, held, flops=pass_flops)
+            (packed,) = call(back_own_kernel, [packed_out], half, held_own, flops=pass_flops)
             (packed,) = call(
-                back_other_kernel, [packed_out], sibling, held, packed, flops=pass_flops
+                back_other_kernel, [packed_out], sibling, held_other, packed, flops=pass_flops
             )
             packed = sum_four(packed, "x", 4)
             packed = sum_four(packed, z, 8)
-            scale = 1.0 / math.sqrt(total_columns)
             left, other = call(
                 functools.partial(solve_kernel, scale=scale),
                 [left_out, half_out],
                 packed,
                 swap(packed, z, 8, 6),
-                held,
+                held_other,
                 flops=pass_flops,
             )
         else:

time: 125 us -> 124 us (level)
  local copies, waits for them, and re-layouts: 1.34 us -> 0.01 us
    unnamed x4 -> x0, local copies, waits for them, and re-layouts: 1.33 us -> none
  transfers between devices with their start and end apart: 31 -> 31, of which waited for: 25 -> 25; matrix products, arithmetic and copies ran while one was open for 0% -> 0% of each run, Pallas kernels for 4% -> 6%
where the time goes in v4:
time: 124 us; the launch traced here: 123 us
  starting transfers between devices  51.5 us (42%)
  waiting for transfers between devices  42.6 us (34%)
  Pallas kernels  15.8 us (13%)
  blocking collectives  11.8 us (10%)
    ppermute x31, starting transfers between devices, swap(): return lax.ppermute(value, axis, [(i, i ^ offset) for i in range(count)])  51.5 us
    ppermute x31, waiting for transfers between devices, swap(): return lax.ppermute(value, axis, [(i, i ^ offset) for i in range(count)])  42.6 us
    pallas_call x12, Pallas kernels, call(): pl.pallas_call(kernel, in_specs=spaces or [whole] * len(args), out_specs=...  15.8 us
    all_to_all x1, blocking collectives, body(): grams = lax.all_to_all(spread, ('x', 'level'), 0, 0)  11.8 us
  transfers between devices with their start and end apart: 31, of which 25 were waited for; matrix products, arithmetic and copies ran while one was open for 0% of the time, Pallas kernels for 6%

profile of v4, /device:TPU:1, one launch (start us, length us, event | category | flops | bytes accessed | tf_op | source)
XLA Modules:
  0.0 122.7 jit_solution(9121431009590906895)
XLA Ops:
  0.6 2.9 %shard_map.50 = (bf16[16,1024]{1,0:T(8,128)(2,1)S(1)}, bf16[2048,1024]{1,0:T(8,128)(2,1)S(1)}, f32[16,2048]{1,0:T(8,128)S(1)}) custom-call(s32[16]{0:T(128)} %seed_values.1, s32[1,1024]{1,0:T(1,128)} %bitcast.1, bf16[4096,1024]{1,0:T(8,128)(2,1)} %affinity.3), custom_call_target="tpu_custom_call" | custom-call | flops 67108864 | bytes 4194304 | tf_op jit(solution)/shard_map/pallas_call | solution.py:218
  3.5 3.3 %collective-permute-start = (f32[16,2048]{1,0:T(8,128)S(1)}, f32[16,2048]{1,0:T(8,128)S(1)}, u32[]{:S(2)}, u32[]{:S(2)}) collective-permute-start(f32[16,2048]{1,0:T(8,128)S(1)} %get-tuple-element.13), channel_id=1, source_target_pairs={{0,1},{1,0},{2,3},{3,2},{4,5},{5,4},{6,7},{7,6},{8,9},{9,8},{10,11... | collective-permute-start | bytes 393224 | tf_op jit(solution)/shard_map/ppermute | solution.py:44
  6.8 2.8 %shard_map.51 = (bf16[2048,1024]{1,0:T(8,128)(2,1)S(1)}, f32[16,2048]{1,0:T(8,128)S(1)}) custom-call(bf16[16,1024]{1,0:T(8,128)(2,1)S(1)} %get-tuple-element.11.left, bf16[4096,1024]{1,0:T(8,128)(2,1)} %affinity.3), custom_call_target="tpu_custom_call" | custom-call | flops 67108864 | bytes 4194304 | tf_op jit(solution)/shard_map/pallas_call | solution.py:218
  9.7 1.1 collective-permute-start.3
  10.8 2.9 %collective-permute-start.1 = (f32[16,2048]{1,0:T(8,128)S(1)}, f32[16,2048]{1,0:T(8,128)S(1)}, u32[]{:S(2)}, u32[]{:S(2)}) collective-permute-start(f32[16,2048]{1,0:T(8,128)S(1)} %add.81), channel_id=1, source_target_pairs={{0,4},{2,6},{4,0},{6,2},{1,5},{3,7},{5,1},{7,3},{8,12},{10,14},{12... | collective-permute-start | bytes 393224 | tf_op jit(solution)/shard_map/ppermute | solution.py:44
  13.6 2.5 %collective-permute-done.3 = f32[16,2048]{1,0:T(8,128)S(1)} collective-permute-done((f32[16,2048]{1,0:T(8,128)S(1)}, f32[16,2048]{1,0:T(8,128)S(1)}, u32[]{:S(2)}, u32[]{:S(2)}) %collective-permute-start.3) | collective-permute-done | bytes 131104 | tf_op jit(solution)/shard_map/ppermute | solution.py:44
  16.1 3.7 %collective-permute-done.1 = f32[16,2048]{1,0:T(8,128)S(1)} collective-permute-done((f32[16,2048]{1,0:T(8,128)S(1)}, f32[16,2048]{1,0:T(8,128)S(1)}, u32[]{:S(2)}, u32[]{:S(2)}) %collective-permute-start.1) | collective-permute-done | bytes 131104 | tf_op jit(solution)/shard_map/ppermute | solution.py:44
  19.8 1.2 collective-permute-start.4
  22.0 0.9 shard_map.53
  23.8 3.0 %collective-permute-start.5 = (f32[16,1152]{1,0:T(8,128)S(1)}, f32[16,1152]{1,0:T(8,128)S(1)}, u32[]{:S(2)}, u32[]{:S(2)}) collective-permute-start(f32[16,1152]{1,0:T(8,128)S(1)} %shard_map.53), channel_id=1, source_target_pairs={{0,128},{64,192},{128,0},{192,64},{1,129},{65,193},{129,1},{193,65... | collective-permute-start | bytes 221192 | tf_op jit(solution)/shard_map/ppermute | solution.py:44
  27.4 2.4 %collective-permute-done.5 = f32[16,1152]{1,0:T(8,128)S(1)} collective-permute-done((f32[16,1152]{1,0:T(8,128)S(1)}, f32[16,1152]{1,0:T(8,128)S(1)}, u32[]{:S(2)}, u32[]{:S(2)}) %collective-permute-start.5) | collective-permute-done | bytes 73760 | tf_op jit(solution)/shard_map/ppermute | solution.py:44
  29.8 3.5 %collective-permute-start.10 = (f32[16,1152]{1,0:T(8,128)S(1)}, f32[16,1152]{1,0:T(8,128)S(1)}, u32[]{:S(2)}, u32[]{:S(2)}) collective-permute-start(f32[16,1152]{1,0:T(8,128)S(1)} %add_add_fusion.6), channel_id=1, source_target_pairs={{0,24},{8,16},{16,8},{24,0},{32,56},{40,48},{48,40},{56,32},{1,25}... | collective-permute-start | bytes 221192 | tf_op jit(solution)/shard_map/ppermute | solution.py:44
  33.7 1.4 %collective-permute-done.10 = f32[16,1152]{1,0:T(8,128)S(1)} collective-permute-done((f32[16,1152]{1,0:T(8,128)S(1)}, f32[16,1152]{1,0:T(8,128)S(1)}, u32[]{:S(2)}, u32[]{:S(2)}) %collective-permute-start.10) | collective-permute-done | bytes 73760 | tf_op jit(solution)/shard_map/ppermute | solution.py:44
  35.1 3.0 %collective-permute-done.9 = f32[16,1152]{1,0:T(8,128)S(1)} collective-permute-done((f32[16,1152]{1,0:T(8,128)S(1)}, f32[16,1152]{1,0:T(8,128)S(1)}, u32[]{:S(2)}, u32[]{:S(2)}) %collective-permute-start.9) | collective-permute-done | bytes 73760 | tf_op jit(solution)/shard_map/ppermute | solution.py:44
  38.1 4.0 %collective-permute-start.11 = (f32[16,1152]{1,0:T(8,128)S(1)}, f32[16,1152]{1,0:T(8,128)S(1)}, u32[]{:S(2)}, u32[]{:S(2)}) collective-permute-start(f32[16,1152]{1,0:T(8,128)S(1)} %add_add_fusion.5.mine), channel_id=1, source_target_pairs={{0,48},{8,56},{16,32},{24,40},{32,16},{40,24},{48,0},{56,8},{1,49}... | collective-permute-start | bytes 221192 | tf_op jit(solution)/shard_map/ppermute | solution.py:44
  42.2 1.9 %collective-permute-done.11.theirs = f32[16,1152]{1,0:T(8,128)S(1)} collective-permute-done((f32[16,1152]{1,0:T(8,128)S(1)}, f32[16,1152]{1,0:T(8,128)S(1)}, u32[]{:S(2)}, u32[]{:S(2)}) %collective-permute-start.11) | collective-permute-done | bytes 73760 | tf_op jit(solution)/shard_map/ppermute | solution.py:44
  44.1 1.4 %shard_map.54 = (bf16[16,1024]{1,0:T(8,128)(2,1)S(1)}, f32[16,2048]{1,0:T(8,128)S(1)}) custom-call(f32[16,1152]{1,0:T(8,128)S(1)} %add_add_fusion.5.mine, f32[16,1152]{1,0:T(8,128)S(1)} %collective-permute-done.11.theirs, bf16[2048,1024]{1,0:T(8,128)(2,1)S(1)} %get-tuple-element.14.held), custom_call_target="tpu_custom_call" | custom-call | flops 67108864 | bytes 4194304 | tf_op jit(solution)/shard_map/pallas_call | solution.py:218
  45.5 4.1 %collective-permute-start.12 = (f32[16,2048]{1,0:T(8,128)S(1)}, f32[16,2048]{1,0:T(8,128)S(1)}, u32[]{:S(2)}, u32[]{:S(2)}) collective-permute-start(f32[16,2048]{1,0:T(8,128)S(1)} %get-tuple-element.17), channel_id=1, source_target_pairs={{0,1},{1,0},{2,3},{3,2},{4,5},{5,4},{6,7},{7,6},{8,9},{9,8},{10,11... | collective-permute-start | bytes 393224 | tf_op jit(solution)/shard_map/ppermute | solution.py:44
  49.6 1.2 shard_map.55
  50.8 2.7 %collective-permute-start.15 = (f32[16,2048]{1,0:T(8,128)S(1)}, f32[16,2048]{1,0:T(8,128)S(1)}, u32[]{:S(2)}, u32[]{:S(2)}) collective-permute-start(f32[16,2048]{1,0:T(8,128)S(1)} %add.91), channel_id=1, source_target_pairs={{0,6},{2,4},{4,2},{6,0},{1,7},{3,5},{5,3},{7,1},{8,14},{10,12},{12... | collective-permute-start | bytes 393224 | tf_op jit(solution)/shard_map/ppermute | solution.py:44
  53.5 1.3 %collective-permute-start.13 = (f32[16,2048]{1,0:T(8,128)S(1)}, f32[16,2048]{1,0:T(8,128)S(1)}, u32[]{:S(2)}, u32[]{:S(2)}) collective-permute-start(f32[16,2048]{1,0:T(8,128)S(1)} %add.91), channel_id=1, source_target_pairs={{0,4},{2,6},{4,0},{6,2},{1,5},{3,7},{5,1},{7,3},{8,12},{10,14},{12... | collective-permute-start | bytes 393224 | tf_op jit(solution)/shard_map/ppermute | solution.py:44
  54.8 2.3 %collective-permute-done.15 = f32[16,2048]{1,0:T(8,128)S(1)} collective-permute-done((f32[16,2048]{1,0:T(8,128)S(1)}, f32[16,2048]{1,0:T(8,128)S(1)}, u32[]{:S(2)}, u32[]{:S(2)}) %collective-permute-start.15) | collective-permute-done | bytes 131104 | tf_op jit(solution)/shard_map/ppermute | solution.py:44
  57.1 1.0 collective-permute-done.14
  58.1 2.6 %collective-permute-done.13 = f32[16,2048]{1,0:T(8,128)S(1)} collective-permute-done((f32[16,2048]{1,0:T(8,128)S(1)}, f32[16,2048]{1,0:T(8,128)S(1)}, u32[]{:S(2)}, u32[]{:S(2)}) %collective-permute-start.13) | collective-permute-done | bytes 131104 | tf_op jit(solution)/shard_map/ppermute | solution.py:44
  60.8 1.4 %collective-permute-start.16 = (f32[16,2048]{1,0:T(8,128)S(1)}, f32[16,2048]{1,0:T(8,128)S(1)}, u32[]{:S(2)}, u32[]{:S(2)}) collective-permute-start(f32[16,2048]{1,0:T(8,128)S(1)} %add_add_fusion.1.half), channel_id=1, source_target_pairs={{0,1},{1,0},{2,3},{3,2},{4,5},{5,4},{6,7},{7,6},{8,9},{9,8},{10,11... | collective-permute-start | bytes 393224 | tf_op jit(solution)/shard_map/ppermute | solution.py:44
  64.1 1.9 %collective-permute-start.19 = (f32[16,1152]{1,0:T(8,128)S(1)}, f32[16,1152]{1,0:T(8,128)S(1)}, u32[]{:S(2)}, u32[]{:S(2)}) collective-permute-start(f32[16,1152]{1,0:T(8,128)S(1)} %shard_map.57), channel_id=1, source_target_pairs={{0,192},{64,128},{128,64},{192,0},{1,193},{65,129},{129,65},{193,1... | collective-permute-start | bytes 221192 | tf_op jit(solution)/shard_map/ppermute | solution.py:44
  65.9 2.0 %collective-permute-start.17 = (f32[16,1152]{1,0:T(8,128)S(1)}, f32[16,1152]{1,0:T(8,128)S(1)}, u32[]{:S(2)}, u32[]{:S(2)}) collective-permute-start(f32[16,1152]{1,0:T(8,128)S(1)} %shard_map.57), channel_id=1, source_target_pairs={{0,128},{64,192},{128,0},{192,64},{1,129},{65,193},{129,1},{193,65... | collective-permute-start | bytes 221192 | tf_op jit(solution)/shard_map/ppermute | solution.py:44
  69.4 1.8 %collective-permute-done.17 = f32[16,1152]{1,0:T(8,128)S(1)} collective-permute-done((f32[16,1152]{1,0:T(8,128)S(1)}, f32[16,1152]{1,0:T(8,128)S(1)}, u32[]{:S(2)}, u32[]{:S(2)}) %collective-permute-start.17) | collective-permute-done | bytes 73760 | tf_op jit(solution)/shard_map/ppermute | solution.py:44
  71.3 2.4 %collective-permute-start.22 = (f32[16,1152]{1,0:T(8,128)S(1)}, f32[16,1152]{1,0:T(8,128)S(1)}, u32[]{:S(2)}, u32[]{:S(2)}) collective-permute-start(f32[16,1152]{1,0:T(8,128)S(1)} %add_add_fusion.4), channel_id=1, source_target_pairs={{0,24},{8,16},{16,8},{24,0},{32,56},{40,48},{48,40},{56,32},{1,25}... | collective-permute-start | bytes 221192 | tf_op jit(solution)/shard_map/ppermute | solution.py:44
  73.7 1.2 collective-permute-start.20
  74.9 1.6 %collective-permute-done.22 = f32[16,1152]{1,0:T(8,128)S(1)} collective-permute-done((f32[16,1152]{1,0:T(8,128)S(1)}, f32[16,1152]{1,0:T(8,128)S(1)}, u32[]{:S(2)}, u32[]{:S(2)}) %collective-permute-start.22) | collective-permute-done | bytes 73760 | tf_op jit(solution)/shard_map/ppermute | solution.py:44
  76.5 1.2 collective-permute-done.21
  77.7 2.3 %collective-permute-done.20 = f32[16,1152]{1,0:T(8,128)S(1)} collective-permute-done((f32[16,1152]{1,0:T(8,128)S(1)}, f32[16,1152]{1,0:T(8,128)S(1)}, u32[]{:S(2)}, u32[]{:S(2)}) %collective-permute-start.20) | collective-permute-done | bytes 73760 | tf_op jit(solution)/shard_map/ppermute | solution.py:44
  80.1 2.1 %collective-permute-start.23 = (f32[16,1152]{1,0:T(8,128)S(1)}, f32[16,1152]{1,0:T(8,128)S(1)}, u32[]{:S(2)}, u32[]{:S(2)}) collective-permute-start(f32[16,1152]{1,0:T(8,128)S(1)} %add_add_fusion.3.mine), channel_id=1, source_target_pairs={{0,48},{8,56},{16,32},{24,40},{32,16},{40,24},{48,0},{56,8},{1,49}... | collective-permute-start | bytes 221192 | tf_op jit(solution)/shard_map/ppermute | solution.py:44
  82.1 3.4 %collective-permute-done.23.theirs = f32[16,1152]{1,0:T(8,128)S(1)} collective-permute-done((f32[16,1152]{1,0:T(8,128)S(1)}, f32[16,1152]{1,0:T(8,128)S(1)}, u32[]{:S(2)}, u32[]{:S(2)}) %collective-permute-start.23) | collective-permute-done | bytes 73760 | tf_op jit(solution)/shard_map/ppermute | solution.py:44
  85.6 1.4 %shard_map.58 = (bf16[16,1024]{1,0:T(8,128)(2,1)S(1)}, f32[16,2048]{1,0:T(8,128)S(1)}) custom-call(f32[16,1152]{1,0:T(8,128)S(1)} %add_add_fusion.3.mine, f32[16,1152]{1,0:T(8,128)S(1)} %collective-permute-done.23.theirs, bf16[2048,1024]{1,0:T(8,128)(2,1)S(1)} %get-tuple-element.14.held), custom_call_target="tpu_custom_call" | custom-call | flops 67108864 | bytes 4194304 | tf_op jit(solution)/shard_map/pallas_call | solution.py:218
  86.9 3.5 %collective-permute-start.24 = (f32[16,2048]{1,0:T(8,128)S(1)}, f32[16,2048]{1,0:T(8,128)S(1)}, u32[]{:S(2)}, u32[]{:S(2)}) collective-permute-start(f32[16,2048]{1,0:T(8,128)S(1)} %get-tuple-element.19), channel_id=1, source_target_pairs={{0,1},{1,0},{2,3},{3,2},{4,5},{5,4},{6,7},{7,6},{8,9},{9,8},{10,11... | collective-permute-start | bytes 393224 | tf_op jit(solution)/shard_map/ppermute | solution.py:44
  90.4 1.2 shard_map.59
  91.7 2.7 %collective-permute-start.27 = (f32[16,2048]{1,0:T(8,128)S(1)}, f32[16,2048]{1,0:T(8,128)S(1)}, u32[]{:S(2)}, u32[]{:S(2)}) collective-permute-start(f32[16,2048]{1,0:T(8,128)S(1)} %add.101), channel_id=1, source_target_pairs={{0,6},{2,4},{4,2},{6,0},{1,7},{3,5},{5,3},{7,1},{8,14},{10,12},{12... | collective-permute-start | bytes 393224 | tf_op jit(solution)/shard_map/ppermute | solution.py:44
  94.3 1.3 %collective-permute-start.25 = (f32[16,2048]{1,0:T(8,128)S(1)}, f32[16,2048]{1,0:T(8,128)S(1)}, u32[]{:S(2)}, u32[]{:S(2)}) collective-permute-start(f32[16,2048]{1,0:T(8,128)S(1)} %add.101), channel_id=1, source_target_pairs={{0,4},{2,6},{4,0},{6,2},{1,5},{3,7},{5,1},{7,3},{8,12},{10,14},{12... | collective-permute-start | bytes 393224 | tf_op jit(solution)/shard_map/ppermute | solution.py:44
  95.6 2.3 %collective-permute-done.27 = f32[16,2048]{1,0:T(8,128)S(1)} collective-permute-done((f32[16,2048]{1,0:T(8,128)S(1)}, f32[16,2048]{1,0:T(8,128)S(1)}, u32[]{:S(2)}, u32[]{:S(2)}) %collective-permute-start.27) | collective-permute-done | bytes 131104 | tf_op jit(solution)/shard_map/ppermute | solution.py:44
  97.9 1.0 collective-permute-done.26
  99.0 2.6 %collective-permute-done.25 = f32[16,2048]{1,0:T(8,128)S(1)} collective-permute-done((f32[16,2048]{1,0:T(8,128)S(1)}, f32[16,2048]{1,0:T(8,128)S(1)}, u32[]{:S(2)}, u32[]{:S(2)}) %collective-permute-start.25) | collective-permute-done | bytes 131104 | tf_op jit(solution)/shard_map/ppermute | solution.py:44
  102.0 3.4 %collective-permute-start.30 = (f32[8,128]{1,0:T(8,128)S(1)}, f32[8,128]{1,0:T(8,128)S(1)}, u32[]{:S(2)}, u32[]{:S(2)}) collective-permute-start(f32[8,128]{1,0:T(8,128)S(1)} %shard_map.60), channel_id=1, source_target_pairs={{0,49},{1,48},{8,57},{9,56},{16,33},{17,32},{24,41},{25,40},{32,17... | collective-permute-start | bytes 12296 | tf_op jit(solution)/shard_map/ppermute | solution.py:44
  105.4 1.4 %collective-permute-start.28 = (f32[8,128]{1,0:T(8,128)S(1)}, f32[8,128]{1,0:T(8,128)S(1)}, u32[]{:S(2)}, u32[]{:S(2)}) collective-permute-start(f32[8,128]{1,0:T(8,128)S(1)} %shard_map.60), channel_id=1, source_target_pairs={{0,48},{1,49},{8,56},{9,57},{16,32},{17,33},{24,40},{25,41},{32,16... | collective-permute-start | bytes 12296 | tf_op jit(solution)/shard_map/ppermute | solution.py:44
  107.1 2.8 %collective-permute-done.28 = f32[8,128]{1,0:T(8,128)S(1)} collective-permute-done((f32[8,128]{1,0:T(8,128)S(1)}, f32[8,128]{1,0:T(8,128)S(1)}, u32[]{:S(2)}, u32[]{:S(2)}) %collective-permute-start.28) | collective-permute-done | bytes 4128 | tf_op jit(solution)/shard_map/ppermute | solution.py:44
  109.9 11.8 %all_to_all.5.grams = f32[16,8,128]{2,1,0:T(8,128)S(1)} all-to-all(f32[16,8,128]{2,1,0:T(8,128)S(1)} %broadcast_in_dim.2), channel_id=1, replica_groups=mesh['x'=4,'cube'=2,'level'=4,'y'=4,'core'=2] {'x','level'}, dimensions={0} | all-to-all | bytes 131072 | tf_op jit(solution)/shard_map/all_to_all | solution.py:306
  121.7 1.0 shard_map.61
  (39 shorter events, 7.4 us)
Async XLA Ops:
  3.5 6.2 %collective-permute-start = (f32[16,2048]{1,0:T(8,128)S(1)}, f32[16,2048]{1,0:T(8,128)S(1)}, u32[]{:S(2)}, u32[]{:S(2)}) collective-permute-start(f32[16,2048]{1,0:T(8,128)S(1)} %get-tuple-element.13), channel_id=1, source_target_pairs={{0,1},{1,0},{2,3},{3,2},{4,5},{5,4},{6,7},{7,6},{8,9},{9,8},{10,11... | collective-permute-start | bytes 393224 | tf_op jit(solution)/shard_map/ppermute | solution.py:44
  9.7 6.4 %collective-permute-start.3 = (f32[16,2048]{1,0:T(8,128)S(1)}, f32[16,2048]{1,0:T(8,128)S(1)}, u32[]{:S(2)}, u32[]{:S(2)}) collective-permute-start(f32[16,2048]{1,0:T(8,128)S(1)} %add.81), channel_id=1, source_target_pairs={{0,6},{2,4},{4,2},{6,0},{1,7},{3,5},{5,3},{7,1},{8,14},{10,12},{12... | collective-permute-start | bytes 393224 | tf_op jit(solution)/shard_map/ppermute | solution.py:44
  10.8 5.3 %collective-permute-start.2 = (f32[16,2048]{1,0:T(8,128)S(1)}, f32[16,2048]{1,0:T(8,128)S(1)}, u32[]{:S(2)}, u32[]{:S(2)}) collective-permute-start(f32[16,2048]{1,0:T(8,128)S(1)} %add.81), channel_id=1, source_target_pairs={{0,2},{2,0},{4,6},{6,4},{1,3},{3,1},{5,7},{7,5},{8,10},{10,8},{12,... | collective-permute-start | bytes 393224 | tf_op jit(solution)/shard_map/ppermute | solution.py:44
  10.8 9.0 %collective-permute-start.1 = (f32[16,2048]{1,0:T(8,128)S(1)}, f32[16,2048]{1,0:T(8,128)S(1)}, u32[]{:S(2)}, u32[]{:S(2)}) collective-permute-start(f32[16,2048]{1,0:T(8,128)S(1)} %add.81), channel_id=1, source_target_pairs={{0,4},{2,6},{4,0},{6,2},{1,5},{3,7},{5,1},{7,3},{8,12},{10,14},{12... | collective-permute-start | bytes 393224 | tf_op jit(solution)/shard_map/ppermute | solution.py:44
  19.8 2.2 %collective-permute-start.4 = (f32[16,2048]{1,0:T(8,128)S(1)}, f32[16,2048]{1,0:T(8,128)S(1)}, u32[]{:S(2)}, u32[]{:S(2)}) collective-permute-start(f32[16,2048]{1,0:T(8,128)S(1)} %add_add_fusion.2.half), channel_id=1, source_target_pairs={{0,1},{1,0},{2,3},{3,2},{4,5},{5,4},{6,7},{7,6},{8,9},{9,8},{10,11... | collective-permute-start | bytes 393224 | tf_op jit(solution)/shard_map/ppermute | solution.py:44
  22.9 4.4 %collective-permute-start.7 = (f32[16,1152]{1,0:T(8,128)S(1)}, f32[16,1152]{1,0:T(8,128)S(1)}, u32[]{:S(2)}, u32[]{:S(2)}) collective-permute-start(f32[16,1152]{1,0:T(8,128)S(1)} %shard_map.53), channel_id=1, source_target_pairs={{0,192},{64,128},{128,64},{192,0},{1,193},{65,129},{129,65},{193,1... | collective-permute-start | bytes 221192 | tf_op jit(solution)/shard_map/ppermute | solution.py:44
  23.8 3.5 %collective-permute-start.6 = (f32[16,1152]{1,0:T(8,128)S(1)}, f32[16,1152]{1,0:T(8,128)S(1)}, u32[]{:S(2)}, u32[]{:S(2)}) collective-permute-start(f32[16,1152]{1,0:T(8,128)S(1)} %shard_map.53), channel_id=1, source_target_pairs={{0,64},{64,0},{128,192},{192,128},{1,65},{65,1},{129,193},{193,129... | collective-permute-start | bytes 221192 | tf_op jit(solution)/shard_map/ppermute | solution.py:44
  23.8 6.0 %collective-permute-start.5 = (f32[16,1152]{1,0:T(8,128)S(1)}, f32[16,1152]{1,0:T(8,128)S(1)}, u32[]{:S(2)}, u32[]{:S(2)}) collective-permute-start(f32[16,1152]{1,0:T(8,128)S(1)} %shard_map.53), channel_id=1, source_target_pairs={{0,128},{64,192},{128,0},{192,64},{1,129},{65,193},{129,1},{193,65... | collective-permute-start | bytes 221192 | tf_op jit(solution)/shard_map/ppermute | solution.py:44
  29.8 5.2 %collective-permute-start.10 = (f32[16,1152]{1,0:T(8,128)S(1)}, f32[16,1152]{1,0:T(8,128)S(1)}, u32[]{:S(2)}, u32[]{:S(2)}) collective-permute-start(f32[16,1152]{1,0:T(8,128)S(1)} %add_add_fusion.6), channel_id=1, source_target_pairs={{0,24},{8,16},{16,8},{24,0},{32,56},{40,48},{48,40},{56,32},{1,25}... | collective-permute-start | bytes 221192 | tf_op jit(solution)/shard_map/ppermute | solution.py:44
  33.3 4.7 %collective-permute-start.9 = (f32[16,1152]{1,0:T(8,128)S(1)}, f32[16,1152]{1,0:T(8,128)S(1)}, u32[]{:S(2)}, u32[]{:S(2)}) collective-permute-start(f32[16,1152]{1,0:T(8,128)S(1)} %add_add_fusion.6), channel_id=1, source_target_pairs={{0,8},{8,0},{16,24},{24,16},{32,40},{40,32},{48,56},{56,48},{1,9},... | collective-permute-start | bytes 221192 | tf_op jit(solution)/shard_map/ppermute | solution.py:44
  33.3 4.8 %collective-permute-start.8 = (f32[16,1152]{1,0:T(8,128)S(1)}, f32[16,1152]{1,0:T(8,128)S(1)}, u32[]{:S(2)}, u32[]{:S(2)}) collective-permute-start(f32[16,1152]{1,0:T(8,128)S(1)} %add_add_fusion.6), channel_id=1, source_target_pairs={{0,16},{8,24},{16,0},{24,8},{32,48},{40,56},{48,32},{56,40},{1,17}... | collective-permute-start | bytes 221192 | tf_op jit(solution)/shard_map/ppermute | solution.py:44
  38.1 6.0 %collective-permute-start.11 = (f32[16,1152]{1,0:T(8,128)S(1)}, f32[16,1152]{1,0:T(8,128)S(1)}, u32[]{:S(2)}, u32[]{:S(2)}) collective-permute-start(f32[16,1152]{1,0:T(8,128)S(1)} %add_add_fusion.5.mine), channel_id=1, source_target_pairs={{0,48},{8,56},{16,32},{24,40},{32,16},{40,24},{48,0},{56,8},{1,49}... | collective-permute-start | bytes 221192 | tf_op jit(solution)/shard_map/ppermute | solution.py:44
  45.5 5.3 %collective-permute-start.12 = (f32[16,2048]{1,0:T(8,128)S(1)}, f32[16,2048]{1,0:T(8,128)S(1)}, u32[]{:S(2)}, u32[]{:S(2)}) collective-permute-start(f32[16,2048]{1,0:T(8,128)S(1)} %get-tuple-element.17), channel_id=1, source_target_pairs={{0,1},{1,0},{2,3},{3,2},{4,5},{5,4},{6,7},{7,6},{8,9},{9,8},{10,11... | collective-permute-start | bytes 393224 | tf_op jit(solution)/shard_map/ppermute | solution.py:44
  50.8 6.2 %collective-permute-start.15 = (f32[16,2048]{1,0:T(8,128)S(1)}, f32[16,2048]{1,0:T(8,128)S(1)}, u32[]{:S(2)}, u32[]{:S(2)}) collective-permute-start(f32[16,2048]{1,0:T(8,128)S(1)} %add.91), channel_id=1, source_target_pairs={{0,6},{2,4},{4,2},{6,0},{1,7},{3,5},{5,3},{7,1},{8,14},{10,12},{12... | collective-permute-start | bytes 393224 | tf_op jit(solution)/shard_map/ppermute | solution.py:44
  53.5 4.6 %collective-permute-start.14 = (f32[16,2048]{1,0:T(8,128)S(1)}, f32[16,2048]{1,0:T(8,128)S(1)}, u32[]{:S(2)}, u32[]{:S(2)}) collective-permute-start(f32[16,2048]{1,0:T(8,128)S(1)} %add.91), channel_id=1, source_target_pairs={{0,2},{2,0},{4,6},{6,4},{1,3},{3,1},{5,7},{7,5},{8,10},{10,8},{12,... | collective-permute-start | bytes 393224 | tf_op jit(solution)/shard_map/ppermute | solution.py:44
  53.5 7.3 %collective-permute-start.13 = (f32[16,2048]{1,0:T(8,128)S(1)}, f32[16,2048]{1,0:T(8,128)S(1)}, u32[]{:S(2)}, u32[]{:S(2)}) collective-permute-start(f32[16,2048]{1,0:T(8,128)S(1)} %add.91), channel_id=1, source_target_pairs={{0,4},{2,6},{4,0},{6,2},{1,5},{3,7},{5,1},{7,3},{8,12},{10,14},{12... | collective-permute-start | bytes 393224 | tf_op jit(solution)/shard_map/ppermute | solution.py:44
  60.8 2.4 %collective-permute-start.16 = (f32[16,2048]{1,0:T(8,128)S(1)}, f32[16,2048]{1,0:T(8,128)S(1)}, u32[]{:S(2)}, u32[]{:S(2)}) collective-permute-start(f32[16,2048]{1,0:T(8,128)S(1)} %add_add_fusion.1.half), channel_id=1, source_target_pairs={{0,1},{1,0},{2,3},{3,2},{4,5},{5,4},{6,7},{7,6},{8,9},{9,8},{10,11... | collective-permute-start | bytes 393224 | tf_op jit(solution)/shard_map/ppermute | solution.py:44
  64.1 4.4 %collective-permute-start.19 = (f32[16,1152]{1,0:T(8,128)S(1)}, f32[16,1152]{1,0:T(8,128)S(1)}, u32[]{:S(2)}, u32[]{:S(2)}) collective-permute-start(f32[16,1152]{1,0:T(8,128)S(1)} %shard_map.57), channel_id=1, source_target_pairs={{0,192},{64,128},{128,64},{192,0},{1,193},{65,129},{129,65},{193,1... | collective-permute-start | bytes 221192 | tf_op jit(solution)/shard_map/ppermute | solution.py:44
  65.9 3.5 %collective-permute-start.18 = (f32[16,1152]{1,0:T(8,128)S(1)}, f32[16,1152]{1,0:T(8,128)S(1)}, u32[]{:S(2)}, u32[]{:S(2)}) collective-permute-start(f32[16,1152]{1,0:T(8,128)S(1)} %shard_map.57), channel_id=1, source_target_pairs={{0,64},{64,0},{128,192},{192,128},{1,65},{65,1},{129,193},{193,129... | collective-permute-start | bytes 221192 | tf_op jit(solution)/shard_map/ppermute | solution.py:44
  65.9 5.3 %collective-permute-start.17 = (f32[16,1152]{1,0:T(8,128)S(1)}, f32[16,1152]{1,0:T(8,128)S(1)}, u32[]{:S(2)}, u32[]{:S(2)}) collective-permute-start(f32[16,1152]{1,0:T(8,128)S(1)} %shard_map.57), channel_id=1, source_target_pairs={{0,128},{64,192},{128,0},{192,64},{1,129},{65,193},{129,1},{193,65... | collective-permute-start | bytes 221192 | tf_op jit(solution)/shard_map/ppermute | solution.py:44
  71.3 5.2 %collective-permute-start.22 = (f32[16,1152]{1,0:T(8,128)S(1)}, f32[16,1152]{1,0:T(8,128)S(1)}, u32[]{:S(2)}, u32[]{:S(2)}) collective-permute-start(f32[16,1152]{1,0:T(8,128)S(1)} %add_add_fusion.4), channel_id=1, source_target_pairs={{0,24},{8,16},{16,8},{24,0},{32,56},{40,48},{48,40},{56,32},{1,25}... | collective-permute-start | bytes 221192 | tf_op jit(solution)/shard_map/ppermute | solution.py:44
  73.7 4.0 %collective-permute-start.21 = (f32[16,1152]{1,0:T(8,128)S(1)}, f32[16,1152]{1,0:T(8,128)S(1)}, u32[]{:S(2)}, u32[]{:S(2)}) collective-permute-start(f32[16,1152]{1,0:T(8,128)S(1)} %add_add_fusion.4), channel_id=1, source_target_pairs={{0,8},{8,0},{16,24},{24,16},{32,40},{40,32},{48,56},{56,48},{1,9},... | collective-permute-start | bytes 221192 | tf_op jit(solution)/shard_map/ppermute | solution.py:44
  73.7 6.3 %collective-permute-start.20 = (f32[16,1152]{1,0:T(8,128)S(1)}, f32[16,1152]{1,0:T(8,128)S(1)}, u32[]{:S(2)}, u32[]{:S(2)}) collective-permute-start(f32[16,1152]{1,0:T(8,128)S(1)} %add_add_fusion.4), channel_id=1, source_target_pairs={{0,16},{8,24},{16,0},{24,8},{32,48},{40,56},{48,32},{56,40},{1,17}... | collective-permute-start | bytes 221192 | tf_op jit(solution)/shard_map/ppermute | solution.py:44
  80.1 5.5 %collective-permute-start.23 = (f32[16,1152]{1,0:T(8,128)S(1)}, f32[16,1152]{1,0:T(8,128)S(1)}, u32[]{:S(2)}, u32[]{:S(2)}) collective-permute-start(f32[16,1152]{1,0:T(8,128)S(1)} %add_add_fusion.3.mine), channel_id=1, source_target_pairs={{0,48},{8,56},{16,32},{24,40},{32,16},{40,24},{48,0},{56,8},{1,49}... | collective-permute-start | bytes 221192 | tf_op jit(solution)/shard_map/ppermute | solution.py:44
  86.9 4.7 %collective-permute-start.24 = (f32[16,2048]{1,0:T(8,128)S(1)}, f32[16,2048]{1,0:T(8,128)S(1)}, u32[]{:S(2)}, u32[]{:S(2)}) collective-permute-start(f32[16,2048]{1,0:T(8,128)S(1)} %get-tuple-element.19), channel_id=1, source_target_pairs={{0,1},{1,0},{2,3},{3,2},{4,5},{5,4},{6,7},{7,6},{8,9},{9,8},{10,11... | collective-permute-start | bytes 393224 | tf_op jit(solution)/shard_map/ppermute | solution.py:44
  91.7 6.2 %collective-permute-start.27 = (f32[16,2048]{1,0:T(8,128)S(1)}, f32[16,2048]{1,0:T(8,128)S(1)}, u32[]{:S(2)}, u32[]{:S(2)}) collective-permute-start(f32[16,2048]{1,0:T(8,128)S(1)} %add.101), channel_id=1, source_target_pairs={{0,6},{2,4},{4,2},{6,0},{1,7},{3,5},{5,3},{7,1},{8,14},{10,12},{12... | collective-permute-start | bytes 393224 | tf_op jit(solution)/shard_map/ppermute | solution.py:44
  94.3 4.6 %collective-permute-start.26 = (f32[16,2048]{1,0:T(8,128)S(1)}, f32[16,2048]{1,0:T(8,128)S(1)}, u32[]{:S(2)}, u32[]{:S(2)}) collective-permute-start(f32[16,2048]{1,0:T(8,128)S(1)} %add.101), channel_id=1, source_target_pairs={{0,2},{2,0},{4,6},{6,4},{1,3},{3,1},{5,7},{7,5},{8,10},{10,8},{12,... | collective-permute-start | bytes 393224 | tf_op jit(solution)/shard_map/ppermute | solution.py:44
  94.3 7.3 %collective-permute-start.25 = (f32[16,2048]{1,0:T(8,128)S(1)}, f32[16,2048]{1,0:T(8,128)S(1)}, u32[]{:S(2)}, u32[]{:S(2)}) collective-permute-start(f32[16,2048]{1,0:T(8,128)S(1)} %add.101), channel_id=1, source_target_pairs={{0,4},{2,6},{4,0},{6,2},{1,5},{3,7},{5,1},{7,3},{8,12},{10,14},{12... | collective-permute-start | bytes 393224 | tf_op jit(solution)/shard_map/ppermute | solution.py:44
  102.0 5.2 %collective-permute-start.30 = (f32[8,128]{1,0:T(8,128)S(1)}, f32[8,128]{1,0:T(8,128)S(1)}, u32[]{:S(2)}, u32[]{:S(2)}) collective-permute-start(f32[8,128]{1,0:T(8,128)S(1)} %shard_map.60), channel_id=1, source_target_pairs={{0,49},{1,48},{8,57},{9,56},{16,33},{17,32},{24,41},{25,40},{32,17... | collective-permute-start | bytes 12296 | tf_op jit(solution)/shard_map/ppermute | solution.py:44
  105.4 1.8 %collective-permute-start.29 = (f32[8,128]{1,0:T(8,128)S(1)}, f32[8,128]{1,0:T(8,128)S(1)}, u32[]{:S(2)}, u32[]{:S(2)}) collective-permute-start(f32[8,128]{1,0:T(8,128)S(1)} %shard_map.60), channel_id=1, source_target_pairs={{0,1},{1,0},{8,9},{9,8},{16,17},{17,16},{24,25},{25,24},{32,33},{3... | collective-permute-start | bytes 12296 | tf_op jit(solution)/shard_map/ppermute | solution.py:44
  105.4 4.6 %collective-permute-start.28 = (f32[8,128]{1,0:T(8,128)S(1)}, f32[8,128]{1,0:T(8,128)S(1)}, u32[]{:S(2)}, u32[]{:S(2)}) collective-permute-start(f32[8,128]{1,0:T(8,128)S(1)} %shard_map.60), channel_id=1, source_target_pairs={{0,48},{1,49},{8,56},{9,57},{16,32},{17,33},{24,40},{25,41},{32,16... | collective-permute-start | bytes 12296 | tf_op jit(solution)/shard_map/ppermute | solution.py:44

commit v5 on v4

--- a/solution.py
+++ b/solution.py
@@ -46,6 +46,15 @@
 
 def sum_four(value, axis, count, offsets=(1, 2, 3)):
     one, two, three = (swap(value, axis, count, k) for k in offsets)
+    return (value + two) + (one + three)
+
+
+def sum_crossed(value, axes, first, second):
+    def swap_by_core(k):
+        pairs = [(i, i ^ ((first * k) if i % 2 == 0 else (second * k))) for i in range(64)]
+        return lax.ppermute(value, axes, pairs)
+
+    one, two, three = (swap_by_core(k) for k in (1, 2, 3))
     return (value + two) + (one + three)
 
 
@@ -101,36 +110,55 @@
     return lower, right / jnp.tile(root, (1, right.shape[1] // 128))
 
 
-def load_half(affinity, held, arrived, side):
+def load_pieces(affinity, held, arrived, side, steps):
     copies = []
-    for step in range(4):
+    for slot, step in enumerate(steps):
         place = pl.multiple_of((2 * step + side) * PIECE, PIECE)
         copies.append(
             pltpu.make_async_copy(
-                affinity.at[pl.ds(place, PIECE)], held.at[span(step)], arrived.at[step]
+                affinity.at[pl.ds(place, PIECE)], held.at[span(slot)], arrived.at[slot]
             )
         )
         copies[-1].start()
     return copies
 
 
-def project_half(left, held, target, scale, copies=None):
-    for step in range(4):
+def pieces(*helds):
+    return [(held, slot) for held in helds for slot in range(held.shape[0] // PIECE)]
+
+
+def project_half(left, helds, target, scale, copies=None):
+    for step, (held, slot) in enumerate(pieces(*helds)):
         if copies is not None:
             copies[step].wait()
-        target[:, span(step)] = project_piece(left[...], held[span(step), :], scale)
+        target[:, span(step)] = project_piece(left[...], held[span(slot), :], scale)
 
 
 def first_kernel(
-    seed_values, sku_ids, affinity, left, held, other, seeds_here, ids_here, arrived, *, columns
+    seed_values,
+    sku_ids,
+    affinity,
+    left,
+    held_other,
+    held_own,
+    other,
+    seeds_here,
+    ids_here,
+    small_arrived,
+    other_arrived,
+    own_arrived,
+    *,
+    columns,
 ):
+    core = lax.axis_index("core")
     small = [
-        pltpu.make_async_copy(seed_values, seeds_here, arrived.at[4]),
-        pltpu.make_async_copy(sku_ids, ids_here, arrived.at[5]),
+        pltpu.make_async_copy(seed_values, seeds_here, small_arrived.at[0]),
+        pltpu.make_async_copy(sku_ids, ids_here, small_arrived.at[1]),
     ]
     for copy in small:
         copy.start()
-    copies = load_half(affinity, held, arrived, 1 - lax.axis_index("core"))
+    copies = load_pieces(affinity, held_other, other_arrived, 1 - core, range(4))
+    ahead = load_pieces(affinity, held_own, own_arrived, core, range(3))
     for copy in small:
         copy.wait()
     row = lax.broadcasted_iota(jnp.int32, (K, 128), 0)
@@ -140,12 +168,16 @@
     for start in range(0, ids_here.shape[1], 128):
         ids = jnp.broadcast_to(ids_here[:, start : start + 128], (K, 128))
         left[:, start : start + 128] = test_matrix(seeds, ids, columns)
-    project_half(left, held, other, None, copies)
-
-
-def first_own_kernel(left, affinity, held, own, arrived):
-    copies = load_half(affinity, held, arrived, lax.axis_index("core"))
-    project_half(left, held, own, None, copies)
+    project_half(left, [held_other], other, None, copies)
+    for copy in ahead:
+        copy.wait()
+
+
+def first_own_kernel(left, held_own, affinity, held_last, own, arrived):
+    copies = load_pieces(affinity, held_last, arrived, lax.axis_index("core"), [3])
+    project_half(left, [held_own], own, None)
+    copies[0].wait()
+    own[:, span(3)] = project_piece(left[...], held_last[...], None)
 
 
 def solve_kernel(mine, theirs, held, left, other, *, scale):
@@ -153,30 +185,30 @@
     total = mine[...] + theirs[...]
     _, back = eliminate(total[:, wide:], total[:, :wide])
     left[...] = back.astype(jnp.bfloat16)
-    project_half(left, held, other, scale)
-
-
-def own_kernel(left, held, own, *, scale):
-    project_half(left, held, own, scale)
-
-
-def back_sums(half, held):
-    both = jnp.zeros((2 * K, held.shape[1]), jnp.float32)
+    project_half(left, [held], other, scale)
+
+
+def own_kernel(left, held_own, held_last, own, *, scale):
+    project_half(left, [held_own, held_last], own, scale)
+
+
+def back_sums(half, *helds):
+    both = jnp.zeros((2 * K, helds[0].shape[1]), jnp.float32)
     gram = jnp.zeros((3 * K, 3 * K), jnp.float32)
-    for step in range(4):
+    for step, (held, slot) in enumerate(pieces(*helds)):
         parts = split_bf16(half[:, span(step)])
         both += jnp.dot(
             jnp.concatenate(parts[:2], axis=0),
-            held[span(step), :],
+            held[span(slot), :],
             preferred_element_type=jnp.float32,
         )
         gram += triple_gram(parts)
     return both[:K] + both[K:], fold_gram(gram)
 
 
-def back_own_kernel(half, held, packed):
-    wide = held.shape[1]
-    back, gram = back_sums(half, held)
+def back_own_kernel(half, held_own, held_last, packed):
+    wide = held_own.shape[1]
+    back, gram = back_sums(half, held_own, held_last)
     packed[:, :wide] = back
     packed[:, wide:] = jnp.zeros((K, 128), jnp.float32)
     packed[:, wide : wide + K] = gram
@@ -238,8 +270,11 @@
     packed_out = ((K, local_columns + 128), f32)
     pass_flops = K * local_rows * local_columns
     z = ("cube", "level")
-
-    held_out = ((local_rows // 2, local_columns), jnp.bfloat16)
+    chips = ("x", "cube", "level", "core")
+
+    held_out, ahead_out, last_out = (
+        ((count * PIECE, local_columns), jnp.bfloat16) for count in (4, 3, 1)
+    )
     far = pl.BlockSpec(memory_space=pltpu.HBM)
     near = pl.BlockSpec(memory_space=pltpu.VMEM)
     affinity, seed_values, sku_ids = (
@@ -247,9 +282,9 @@
         for value in (affinity, seed_values, sku_ids.reshape(1, -1))
     )
 
-    left, held_other, other = call(
+    left, held_other, held_own, other = call(
         functools.partial(first_kernel, columns=total_columns),
-        [left_out, held_out, half_out],
+        [left_out, held_out, ahead_out, half_out],
         seed_values,
         sku_ids,
         affinity,
@@ -257,7 +292,9 @@
         scratch=[
             pltpu.SMEM(seed_values.shape, jnp.int32),
             pltpu.VMEM(sku_ids.shape, jnp.int32),
-            pltpu.SemaphoreType.DMA((6,)),
+            pltpu.SemaphoreType.DMA((2,)),
+            pltpu.SemaphoreType.DMA((4,)),
+            pltpu.SemaphoreType.DMA((3,)),
         ],
         flops=pass_flops,
     )
@@ -265,13 +302,14 @@
     for repeat in range(ITERS + 1):
         arriving = swap(other, "core", 2, 1)
         if repeat == 0:
-            held_own, own = call(
+            held_last, own = call(
                 first_own_kernel,
-                [held_out, half_out],
+                [last_out, half_out],
                 left,
+                held_own,
                 affinity,
-                spaces=[near, far],
-                scratch=[pltpu.SemaphoreType.DMA((4,))],
+                spaces=[near, near, far],
+                scratch=[pltpu.SemaphoreType.DMA((1,))],
                 flops=pass_flops,
             )
         else:
@@ -280,17 +318,20 @@
                 [half_out],
                 left,
                 held_own,
+                held_last,
                 flops=pass_flops,
             )
         half = sum_four(own + arriving, "y", 4)
         if repeat < ITERS:
             sibling = swap(half, "core", 2, 1)
-            (packed,) = call(back_own_kernel, [packed_out], half, held_own, flops=pass_flops)
+            (packed,) = call(
+                back_own_kernel, [packed_out], half, held_own, held_last, flops=pass_flops
+            )
             (packed,) = call(
                 back_other_kernel, [packed_out], sibling, held_other, packed, flops=pass_flops
             )
-            packed = sum_four(packed, "x", 4)
-            packed = sum_four(packed, z, 8)
+            packed = sum_crossed(packed, chips, 16, 2)
+            packed = sum_crossed(packed, chips, 2, 16)
             left, other = call(
                 functools.partial(solve_kernel, scale=scale),
                 [left_out, half_out],

time: 124 us -> 125 us (level)
  waiting for transfers between devices: 42.6 us -> 39.7 us
  starting transfers between devices: 51.5 us -> 53.8 us
    ppermute x31 -> x19, waiting for transfers between devices: 42.6 us -> 27.4 us  [swap(): return lax.ppermute(value, axis, [(i, i ^ offset) for i in range(count)])]
    ppermute x0 -> x12, starting transfers between devices: none -> 15 us  [swap_by_core(): return lax.ppermute(value, axes, pairs)]
    ppermute x31 -> x19, starting transfers between devices: 51.5 us -> 38.7 us  [swap(): return lax.ppermute(value, axis, [(i, i ^ offset) for i in range(count)])]
    ppermute x0 -> x12, waiting for transfers between devices: none -> 12.3 us  [swap_by_core(): return lax.ppermute(value, axes, pairs)]
  transfers between devices with their start and end apart: 31 -> 31, of which waited for: 25 -> 25; matrix products, arithmetic and copies ran while one was open for 0% -> 0% of each run, Pallas kernels for 6% -> 5%
where the time goes in v5:
time: 125 us; the launch traced here: 123 us
  starting transfers between devices  53.8 us (43%)
  waiting for transfers between devices  39.7 us (32%)
  Pallas kernels  16.8 us (13%)
  blocking collectives  12.2 us (10%)
    ppermute x19, starting transfers between devices, swap(): return lax.ppermute(value, axis, [(i, i ^ offset) for i in range(count)])  38.7 us
    ppermute x19, waiting for transfers between devices, swap(): return lax.ppermute(value, axis, [(i, i ^ offset) for i in range(count)])  27.4 us
    pallas_call x12, Pallas kernels, call(): pl.pallas_call(kernel, in_specs=spaces or [whole] * len(args), out_specs=...  16.8 us
    ppermute x12, starting transfers between devices, swap_by_core(): return lax.ppermute(value, axes, pairs)  15 us
    ppermute x12, waiting for transfers between devices, swap_by_core(): return lax.ppermute(value, axes, pairs)  12.3 us
    all_to_all x1, blocking collectives, body(): grams = lax.all_to_all(spread, ('x', 'level'), 0, 0)  12.2 us
  transfers between devices with their start and end apart: 31, of which 25 were waited for; matrix products, arithmetic and copies ran while one was open for 0% of the time, Pallas kernels for 5%

profile of v5, /device:TPU:1, one launch (start us, length us, event | category | flops | bytes accessed | tf_op | source)
XLA Modules:
  0.0 123.5 jit_solution(253792344947648989)
XLA Ops:
  0.6 4.2 %shard_map.50 = (bf16[16,1024]{1,0:T(8,128)(2,1)S(1)}, bf16[2048,1024]{1,0:T(8,128)(2,1)S(1)}, bf16[1536,1024]{1,0:T(8,128)(2,1)S(1)}, f32[16,2048]{1,0:T(8,128)S(1)}) custom-call(s32[16]{0:T(128)} %seed_values.1, s32[1,1024]{1,0:T(1,128)} %bitcast.1, bf16[4096,1024]{1,0:T(8,128)(2,1)} %affinity.3), custom_call_target="tpu_custom_call" | custom-call | flops 67108864 | bytes 4194304 | tf_op jit(solution)/shard_map/pallas_call | solution.py:250
  4.9 3.3 %collective-permute-start = (f32[16,2048]{1,0:T(8,128)S(1)}, f32[16,2048]{1,0:T(8,128)S(1)}, u32[]{:S(2)}, u32[]{:S(2)}) collective-permute-start(f32[16,2048]{1,0:T(8,128)S(1)} %get-tuple-element.15), channel_id=1, source_target_pairs={{0,1},{1,0},{2,3},{3,2},{4,5},{5,4},{6,7},{7,6},{8,9},{9,8},{10,11... | collective-permute-start | bytes 393224 | tf_op jit(solution)/shard_map/ppermute | solution.py:44
  8.2 2.4 %shard_map.51 = (bf16[512,1024]{1,0:T(8,128)(2,1)S(1)}, f32[16,2048]{1,0:T(8,128)S(1)}) custom-call(bf16[16,1024]{1,0:T(8,128)(2,1)S(1)} %get-tuple-element.12.left, bf16[1536,1024]{1,0:T(8,128)(2,1)S(1)} %get-tuple-element.13.held_own, bf16[4096,1024]{1,0:T(8,128)(2,1)} %affinity.3), custom_call_target="tpu_custom_call" | custom-call | flops 67108864 | bytes 4194304 | tf_op jit(solution)/shard_map/pallas_call | solution.py:250
  10.6 1.1 collective-permute-start.3
  11.7 2.9 %collective-permute-start.1 = (f32[16,2048]{1,0:T(8,128)S(1)}, f32[16,2048]{1,0:T(8,128)S(1)}, u32[]{:S(2)}, u32[]{:S(2)}) collective-permute-start(f32[16,2048]{1,0:T(8,128)S(1)} %add.81), channel_id=1, source_target_pairs={{0,4},{2,6},{4,0},{6,2},{1,5},{3,7},{5,1},{7,3},{8,12},{10,14},{12... | collective-permute-start | bytes 393224 | tf_op jit(solution)/shard_map/ppermute | solution.py:44
  14.6 2.5 %collective-permute-done.3 = f32[16,2048]{1,0:T(8,128)S(1)} collective-permute-done((f32[16,2048]{1,0:T(8,128)S(1)}, f32[16,2048]{1,0:T(8,128)S(1)}, u32[]{:S(2)}, u32[]{:S(2)}) %collective-permute-start.3) | collective-permute-done | bytes 131104 | tf_op jit(solution)/shard_map/ppermute | solution.py:44
  17.1 3.7 %collective-permute-done.1 = f32[16,2048]{1,0:T(8,128)S(1)} collective-permute-done((f32[16,2048]{1,0:T(8,128)S(1)}, f32[16,2048]{1,0:T(8,128)S(1)}, u32[]{:S(2)}, u32[]{:S(2)}) %collective-permute-start.1) | collective-permute-done | bytes 131104 | tf_op jit(solution)/shard_map/ppermute | solution.py:44
  20.8 1.2 collective-permute-start.4
  23.9 2.8 %collective-permute-start.7 = (f32[16,1152]{1,0:T(8,128)S(1)}, f32[16,1152]{1,0:T(8,128)S(1)}, u32[]{:S(2)}, u32[]{:S(2)}) collective-permute-start(f32[16,1152]{1,0:T(8,128)S(1)} %shard_map.53), channel_id=1, source_target_pairs={{0,192},{1,25},{8,200},{9,17},{16,208},{17,9},{24,216},{25,1},{32,... | collective-permute-start | bytes 221192 | tf_op jit(solution)/shard_map/ppermute | solution.py:55
  27.5 1.5 %collective-permute-done.7 = f32[16,1152]{1,0:T(8,128)S(1)} collective-permute-done((f32[16,1152]{1,0:T(8,128)S(1)}, f32[16,1152]{1,0:T(8,128)S(1)}, u32[]{:S(2)}, u32[]{:S(2)}) %collective-permute-start.7) | collective-permute-done | bytes 73760 | tf_op jit(solution)/shard_map/ppermute | solution.py:55
  28.9 1.0 collective-permute-done.6
  29.9 1.2 collective-permute-done.5
  31.1 2.3 %collective-permute-start.10 = (f32[16,1152]{1,0:T(8,128)S(1)}, f32[16,1152]{1,0:T(8,128)S(1)}, u32[]{:S(2)}, u32[]{:S(2)}) collective-permute-start(f32[16,1152]{1,0:T(8,128)S(1)} %add_add_fusion.6), channel_id=1, source_target_pairs={{0,24},{1,193},{8,16},{9,201},{16,8},{17,209},{24,0},{25,217},{32,... | collective-permute-start | bytes 221192 | tf_op jit(solution)/shard_map/ppermute | solution.py:55
  33.6 1.4 %collective-permute-start.8 = (f32[16,1152]{1,0:T(8,128)S(1)}, f32[16,1152]{1,0:T(8,128)S(1)}, u32[]{:S(2)}, u32[]{:S(2)}) collective-permute-start(f32[16,1152]{1,0:T(8,128)S(1)} %add_add_fusion.6), channel_id=1, source_target_pairs={{0,16},{1,129},{8,24},{9,137},{16,0},{17,145},{24,8},{25,153},{32,... | collective-permute-start | bytes 221192 | tf_op jit(solution)/shard_map/ppermute | solution.py:55
  35.6 1.0 collective-permute-done.9
  36.6 1.7 %collective-permute-done.8 = f32[16,1152]{1,0:T(8,128)S(1)} collective-permute-done((f32[16,1152]{1,0:T(8,128)S(1)}, f32[16,1152]{1,0:T(8,128)S(1)}, u32[]{:S(2)}, u32[]{:S(2)}) %collective-permute-start.8) | collective-permute-done | bytes 73760 | tf_op jit(solution)/shard_map/ppermute | solution.py:55
  38.3 4.1 %collective-permute-start.11 = (f32[16,1152]{1,0:T(8,128)S(1)}, f32[16,1152]{1,0:T(8,128)S(1)}, u32[]{:S(2)}, u32[]{:S(2)}) collective-permute-start(f32[16,1152]{1,0:T(8,128)S(1)} %add_add_fusion.5.mine), channel_id=1, source_target_pairs={{0,48},{8,56},{16,32},{24,40},{32,16},{40,24},{48,0},{56,8},{1,49}... | collective-permute-start | bytes 221192 | tf_op jit(solution)/shard_map/ppermute | solution.py:44
  42.5 2.3 %collective-permute-done.11.theirs = f32[16,1152]{1,0:T(8,128)S(1)} collective-permute-done((f32[16,1152]{1,0:T(8,128)S(1)}, f32[16,1152]{1,0:T(8,128)S(1)}, u32[]{:S(2)}, u32[]{:S(2)}) %collective-permute-start.11) | collective-permute-done | bytes 73760 | tf_op jit(solution)/shard_map/ppermute | solution.py:44
  44.8 1.4 %shard_map.54 = (bf16[16,1024]{1,0:T(8,128)(2,1)S(1)}, f32[16,2048]{1,0:T(8,128)S(1)}) custom-call(f32[16,1152]{1,0:T(8,128)S(1)} %add_add_fusion.5.mine, f32[16,1152]{1,0:T(8,128)S(1)} %collective-permute-done.11.theirs, bf16[2048,1024]{1,0:T(8,128)(2,1)S(1)} %get-tuple-element.16.held), custom_call_target="tpu_custom_call" | custom-call | flops 67108864 | bytes 4194304 | tf_op jit(solution)/shard_map/pallas_call | solution.py:250
  46.1 4.3 %collective-permute-start.12 = (f32[16,2048]{1,0:T(8,128)S(1)}, f32[16,2048]{1,0:T(8,128)S(1)}, u32[]{:S(2)}, u32[]{:S(2)}) collective-permute-start(f32[16,2048]{1,0:T(8,128)S(1)} %get-tuple-element.19), channel_id=1, source_target_pairs={{0,1},{1,0},{2,3},{3,2},{4,5},{5,4},{6,7},{7,6},{8,9},{9,8},{10,11... | collective-permute-start | bytes 393224 | tf_op jit(solution)/shard_map/ppermute | solution.py:44
  50.5 1.2 shard_map.55
  51.7 2.7 %collective-permute-start.15 = (f32[16,2048]{1,0:T(8,128)S(1)}, f32[16,2048]{1,0:T(8,128)S(1)}, u32[]{:S(2)}, u32[]{:S(2)}) collective-permute-start(f32[16,2048]{1,0:T(8,128)S(1)} %add.91), channel_id=1, source_target_pairs={{0,6},{2,4},{4,2},{6,0},{1,7},{3,5},{5,3},{7,1},{8,14},{10,12},{12... | collective-permute-start | bytes 393224 | tf_op jit(solution)/shard_map/ppermute | solution.py:44
  54.4 1.3 %collective-permute-start.13 = (f32[16,2048]{1,0:T(8,128)S(1)}, f32[16,2048]{1,0:T(8,128)S(1)}, u32[]{:S(2)}, u32[]{:S(2)}) collective-permute-start(f32[16,2048]{1,0:T(8,128)S(1)} %add.91), channel_id=1, source_target_pairs={{0,4},{2,6},{4,0},{6,2},{1,5},{3,7},{5,1},{7,3},{8,12},{10,14},{12... | collective-permute-start | bytes 393224 | tf_op jit(solution)/shard_map/ppermute | solution.py:44
  55.6 2.3 %collective-permute-done.15 = f32[16,2048]{1,0:T(8,128)S(1)} collective-permute-done((f32[16,2048]{1,0:T(8,128)S(1)}, f32[16,2048]{1,0:T(8,128)S(1)}, u32[]{:S(2)}, u32[]{:S(2)}) %collective-permute-start.15) | collective-permute-done | bytes 131104 | tf_op jit(solution)/shard_map/ppermute | solution.py:44
  57.9 1.0 collective-permute-done.14
  59.0 2.6 %collective-permute-done.13 = f32[16,2048]{1,0:T(8,128)S(1)} collective-permute-done((f32[16,2048]{1,0:T(8,128)S(1)}, f32[16,2048]{1,0:T(8,128)S(1)}, u32[]{:S(2)}, u32[]{:S(2)}) %collective-permute-start.13) | collective-permute-done | bytes 131104 | tf_op jit(solution)/shard_map/ppermute | solution.py:44
  61.6 1.4 %collective-permute-start.16 = (f32[16,2048]{1,0:T(8,128)S(1)}, f32[16,2048]{1,0:T(8,128)S(1)}, u32[]{:S(2)}, u32[]{:S(2)}) collective-permute-start(f32[16,2048]{1,0:T(8,128)S(1)} %add_add_fusion.1.half), channel_id=1, source_target_pairs={{0,1},{1,0},{2,3},{3,2},{4,5},{5,4},{6,7},{7,6},{8,9},{9,8},{10,11... | collective-permute-start | bytes 393224 | tf_op jit(solution)/shard_map/ppermute | solution.py:44
  64.9 1.7 %collective-permute-start.19 = (f32[16,1152]{1,0:T(8,128)S(1)}, f32[16,1152]{1,0:T(8,128)S(1)}, u32[]{:S(2)}, u32[]{:S(2)}) collective-permute-start(f32[16,1152]{1,0:T(8,128)S(1)} %shard_map.57), channel_id=1, source_target_pairs={{0,192},{1,25},{8,200},{9,17},{16,208},{17,9},{24,216},{25,1},{32,... | collective-permute-start | bytes 221192 | tf_op jit(solution)/shard_map/ppermute | solution.py:55
  66.7 1.8 %collective-permute-start.17 = (f32[16,1152]{1,0:T(8,128)S(1)}, f32[16,1152]{1,0:T(8,128)S(1)}, u32[]{:S(2)}, u32[]{:S(2)}) collective-permute-start(f32[16,1152]{1,0:T(8,128)S(1)} %shard_map.57), channel_id=1, source_target_pairs={{0,128},{1,17},{8,136},{9,25},{16,144},{17,1},{24,152},{25,9},{32,... | collective-permute-start | bytes 221192 | tf_op jit(solution)/shard_map/ppermute | solution.py:55
  68.5 1.6 %collective-permute-done.19 = f32[16,1152]{1,0:T(8,128)S(1)} collective-permute-done((f32[16,1152]{1,0:T(8,128)S(1)}, f32[16,1152]{1,0:T(8,128)S(1)}, u32[]{:S(2)}, u32[]{:S(2)}) %collective-permute-start.19) | collective-permute-done | bytes 73760 | tf_op jit(solution)/shard_map/ppermute | solution.py:55
  70.1 1.3 %collective-permute-done.18 = f32[16,1152]{1,0:T(8,128)S(1)} collective-permute-done((f32[16,1152]{1,0:T(8,128)S(1)}, f32[16,1152]{1,0:T(8,128)S(1)}, u32[]{:S(2)}, u32[]{:S(2)}) %collective-permute-start.18) | collective-permute-done | bytes 73760 | tf_op jit(solution)/shard_map/ppermute | solution.py:55
  71.4 1.5 %collective-permute-start.22 = (f32[16,1152]{1,0:T(8,128)S(1)}, f32[16,1152]{1,0:T(8,128)S(1)}, u32[]{:S(2)}, u32[]{:S(2)}) collective-permute-start(f32[16,1152]{1,0:T(8,128)S(1)} %add_add_fusion.4), channel_id=1, source_target_pairs={{0,24},{1,193},{8,16},{9,201},{16,8},{17,209},{24,0},{25,217},{32,... | collective-permute-start | bytes 221192 | tf_op jit(solution)/shard_map/ppermute | solution.py:55
  73.1 2.2 %collective-permute-start.20 = (f32[16,1152]{1,0:T(8,128)S(1)}, f32[16,1152]{1,0:T(8,128)S(1)}, u32[]{:S(2)}, u32[]{:S(2)}) collective-permute-start(f32[16,1152]{1,0:T(8,128)S(1)} %add_add_fusion.4), channel_id=1, source_target_pairs={{0,16},{1,129},{8,24},{9,137},{16,0},{17,145},{24,8},{25,153},{32,... | collective-permute-start | bytes 221192 | tf_op jit(solution)/shard_map/ppermute | solution.py:55
  76.2 1.7 %collective-permute-done.20 = f32[16,1152]{1,0:T(8,128)S(1)} collective-permute-done((f32[16,1152]{1,0:T(8,128)S(1)}, f32[16,1152]{1,0:T(8,128)S(1)}, u32[]{:S(2)}, u32[]{:S(2)}) %collective-permute-start.20) | collective-permute-done | bytes 73760 | tf_op jit(solution)/shard_map/ppermute | solution.py:55
  77.9 3.7 %collective-permute-start.23 = (f32[16,1152]{1,0:T(8,128)S(1)}, f32[16,1152]{1,0:T(8,128)S(1)}, u32[]{:S(2)}, u32[]{:S(2)}) collective-permute-start(f32[16,1152]{1,0:T(8,128)S(1)} %add_add_fusion.3.mine), channel_id=1, source_target_pairs={{0,48},{8,56},{16,32},{24,40},{32,16},{40,24},{48,0},{56,8},{1,49}... | collective-permute-start | bytes 221192 | tf_op jit(solution)/shard_map/ppermute | solution.py:44
  81.6 2.5 %collective-permute-done.23.theirs = f32[16,1152]{1,0:T(8,128)S(1)} collective-permute-done((f32[16,1152]{1,0:T(8,128)S(1)}, f32[16,1152]{1,0:T(8,128)S(1)}, u32[]{:S(2)}, u32[]{:S(2)}) %collective-permute-start.23) | collective-permute-done | bytes 73760 | tf_op jit(solution)/shard_map/ppermute | solution.py:44
  84.1 1.4 %shard_map.58 = (bf16[16,1024]{1,0:T(8,128)(2,1)S(1)}, f32[16,2048]{1,0:T(8,128)S(1)}) custom-call(f32[16,1152]{1,0:T(8,128)S(1)} %add_add_fusion.3.mine, f32[16,1152]{1,0:T(8,128)S(1)} %collective-permute-done.23.theirs, bf16[2048,1024]{1,0:T(8,128)(2,1)S(1)} %get-tuple-element.16.held), custom_call_target="tpu_custom_call" | custom-call | flops 67108864 | bytes 4194304 | tf_op jit(solution)/shard_map/pallas_call | solution.py:250
  85.5 3.7 %collective-permute-start.24 = (f32[16,2048]{1,0:T(8,128)S(1)}, f32[16,2048]{1,0:T(8,128)S(1)}, u32[]{:S(2)}, u32[]{:S(2)}) collective-permute-start(f32[16,2048]{1,0:T(8,128)S(1)} %get-tuple-element.21), channel_id=1, source_target_pairs={{0,1},{1,0},{2,3},{3,2},{4,5},{5,4},{6,7},{7,6},{8,9},{9,8},{10,11... | collective-permute-start | bytes 393224 | tf_op jit(solution)/shard_map/ppermute | solution.py:44
  89.2 1.2 shard_map.59
  90.4 2.7 %collective-permute-start.27 = (f32[16,2048]{1,0:T(8,128)S(1)}, f32[16,2048]{1,0:T(8,128)S(1)}, u32[]{:S(2)}, u32[]{:S(2)}) collective-permute-start(f32[16,2048]{1,0:T(8,128)S(1)} %add.101), channel_id=1, source_target_pairs={{0,6},{2,4},{4,2},{6,0},{1,7},{3,5},{5,3},{7,1},{8,14},{10,12},{12... | collective-permute-start | bytes 393224 | tf_op jit(solution)/shard_map/ppermute | solution.py:44
  93.1 1.3 %collective-permute-start.25 = (f32[16,2048]{1,0:T(8,128)S(1)}, f32[16,2048]{1,0:T(8,128)S(1)}, u32[]{:S(2)}, u32[]{:S(2)}) collective-permute-start(f32[16,2048]{1,0:T(8,128)S(1)} %add.101), channel_id=1, source_target_pairs={{0,4},{2,6},{4,0},{6,2},{1,5},{3,7},{5,1},{7,3},{8,12},{10,14},{12... | collective-permute-start | bytes 393224 | tf_op jit(solution)/shard_map/ppermute | solution.py:44
  94.4 2.3 %collective-permute-done.27 = f32[16,2048]{1,0:T(8,128)S(1)} collective-permute-done((f32[16,2048]{1,0:T(8,128)S(1)}, f32[16,2048]{1,0:T(8,128)S(1)}, u32[]{:S(2)}, u32[]{:S(2)}) %collective-permute-start.27) | collective-permute-done | bytes 131104 | tf_op jit(solution)/shard_map/ppermute | solution.py:44
  96.7 1.0 collective-permute-done.26
  97.7 2.6 %collective-permute-done.25 = f32[16,2048]{1,0:T(8,128)S(1)} collective-permute-done((f32[16,2048]{1,0:T(8,128)S(1)}, f32[16,2048]{1,0:T(8,128)S(1)}, u32[]{:S(2)}, u32[]{:S(2)}) %collective-permute-start.25) | collective-permute-done | bytes 131104 | tf_op jit(solution)/shard_map/ppermute | solution.py:44
  100.7 5.0 %collective-permute-start.30 = (f32[8,128]{1,0:T(8,128)S(1)}, f32[8,128]{1,0:T(8,128)S(1)}, u32[]{:S(2)}, u32[]{:S(2)}) collective-permute-start(f32[8,128]{1,0:T(8,128)S(1)} %shard_map.60), channel_id=1, source_target_pairs={{0,49},{1,48},{8,57},{9,56},{16,33},{17,32},{24,41},{25,40},{32,17... | collective-permute-start | bytes 12296 | tf_op jit(solution)/shard_map/ppermute | solution.py:44
  105.9 1.1 collective-permute-done.30
  107.0 3.3 %collective-permute-done.28 = f32[8,128]{1,0:T(8,128)S(1)} collective-permute-done((f32[8,128]{1,0:T(8,128)S(1)}, f32[8,128]{1,0:T(8,128)S(1)}, u32[]{:S(2)}, u32[]{:S(2)}) %collective-permute-start.28) | collective-permute-done | bytes 4128 | tf_op jit(solution)/shard_map/ppermute | solution.py:44
  110.3 12.2 %all_to_all.5.grams = f32[16,8,128]{2,1,0:T(8,128)S(1)} all-to-all(f32[16,8,128]{2,1,0:T(8,128)S(1)} %broadcast_in_dim.2), channel_id=1, replica_groups=mesh['x'=4,'cube'=2,'level'=4,'y'=4,'core'=2] {'x','level'}, dimensions={0} | all-to-all | bytes 131072 | tf_op jit(solution)/shard_map/all_to_all | solution.py:347
  (39 shorter events, 8.3 us)
Async XLA Ops:
  4.9 5.7 %collective-permute-start = (f32[16,2048]{1,0:T(8,128)S(1)}, f32[16,2048]{1,0:T(8,128)S(1)}, u32[]{:S(2)}, u32[]{:S(2)}) collective-permute-start(f32[16,2048]{1,0:T(8,128)S(1)} %get-tuple-element.15), channel_id=1, source_target_pairs={{0,1},{1,0},{2,3},{3,2},{4,5},{5,4},{6,7},{7,6},{8,9},{9,8},{10,11... | collective-permute-start | bytes 393224 | tf_op jit(solution)/shard_map/ppermute | solution.py:44
  10.6 6.4 %collective-permute-start.3 = (f32[16,2048]{1,0:T(8,128)S(1)}, f32[16,2048]{1,0:T(8,128)S(1)}, u32[]{:S(2)}, u32[]{:S(2)}) collective-permute-start(f32[16,2048]{1,0:T(8,128)S(1)} %add.81), channel_id=1, source_target_pairs={{0,6},{2,4},{4,2},{6,0},{1,7},{3,5},{5,3},{7,1},{8,14},{10,12},{12... | collective-permute-start | bytes 393224 | tf_op jit(solution)/shard_map/ppermute | solution.py:44
  11.7 5.3 %collective-permute-start.2 = (f32[16,2048]{1,0:T(8,128)S(1)}, f32[16,2048]{1,0:T(8,128)S(1)}, u32[]{:S(2)}, u32[]{:S(2)}) collective-permute-start(f32[16,2048]{1,0:T(8,128)S(1)} %add.81), channel_id=1, source_target_pairs={{0,2},{2,0},{4,6},{6,4},{1,3},{3,1},{5,7},{7,5},{8,10},{10,8},{12,... | collective-permute-start | bytes 393224 | tf_op jit(solution)/shard_map/ppermute | solution.py:44
  11.7 9.0 %collective-permute-start.1 = (f32[16,2048]{1,0:T(8,128)S(1)}, f32[16,2048]{1,0:T(8,128)S(1)}, u32[]{:S(2)}, u32[]{:S(2)}) collective-permute-start(f32[16,2048]{1,0:T(8,128)S(1)} %add.81), channel_id=1, source_target_pairs={{0,4},{2,6},{4,0},{6,2},{1,5},{3,7},{5,1},{7,3},{8,12},{10,14},{12... | collective-permute-start | bytes 393224 | tf_op jit(solution)/shard_map/ppermute | solution.py:44
  20.8 2.2 %collective-permute-start.4 = (f32[16,2048]{1,0:T(8,128)S(1)}, f32[16,2048]{1,0:T(8,128)S(1)}, u32[]{:S(2)}, u32[]{:S(2)}) collective-permute-start(f32[16,2048]{1,0:T(8,128)S(1)} %add_add_fusion.2.half), channel_id=1, source_target_pairs={{0,1},{1,0},{2,3},{3,2},{4,5},{5,4},{6,7},{7,6},{8,9},{9,8},{10,11... | collective-permute-start | bytes 393224 | tf_op jit(solution)/shard_map/ppermute | solution.py:44
  23.9 5.0 %collective-permute-start.7 = (f32[16,1152]{1,0:T(8,128)S(1)}, f32[16,1152]{1,0:T(8,128)S(1)}, u32[]{:S(2)}, u32[]{:S(2)}) collective-permute-start(f32[16,1152]{1,0:T(8,128)S(1)} %shard_map.53), channel_id=1, source_target_pairs={{0,192},{1,25},{8,200},{9,17},{16,208},{17,9},{24,216},{25,1},{32,... | collective-permute-start | bytes 221192 | tf_op jit(solution)/shard_map/ppermute | solution.py:55
  26.7 3.2 %collective-permute-start.6 = (f32[16,1152]{1,0:T(8,128)S(1)}, f32[16,1152]{1,0:T(8,128)S(1)}, u32[]{:S(2)}, u32[]{:S(2)}) collective-permute-start(f32[16,1152]{1,0:T(8,128)S(1)} %shard_map.53), channel_id=1, source_target_pairs={{0,64},{1,9},{8,72},{9,1},{16,80},{17,25},{24,88},{25,17},{32,96},... | collective-permute-start | bytes 221192 | tf_op jit(solution)/shard_map/ppermute | solution.py:55
  26.7 4.4 %collective-permute-start.5 = (f32[16,1152]{1,0:T(8,128)S(1)}, f32[16,1152]{1,0:T(8,128)S(1)}, u32[]{:S(2)}, u32[]{:S(2)}) collective-permute-start(f32[16,1152]{1,0:T(8,128)S(1)} %shard_map.53), channel_id=1, source_target_pairs={{0,128},{1,17},{8,136},{9,25},{16,144},{17,1},{24,152},{25,9},{32,... | collective-permute-start | bytes 221192 | tf_op jit(solution)/shard_map/ppermute | solution.py:55
  31.1 4.5 %collective-permute-start.10 = (f32[16,1152]{1,0:T(8,128)S(1)}, f32[16,1152]{1,0:T(8,128)S(1)}, u32[]{:S(2)}, u32[]{:S(2)}) collective-permute-start(f32[16,1152]{1,0:T(8,128)S(1)} %add_add_fusion.6), channel_id=1, source_target_pairs={{0,24},{1,193},{8,16},{9,201},{16,8},{17,209},{24,0},{25,217},{32,... | collective-permute-start | bytes 221192 | tf_op jit(solution)/shard_map/ppermute | solution.py:55
  33.4 3.2 %collective-permute-start.9 = (f32[16,1152]{1,0:T(8,128)S(1)}, f32[16,1152]{1,0:T(8,128)S(1)}, u32[]{:S(2)}, u32[]{:S(2)}) collective-permute-start(f32[16,1152]{1,0:T(8,128)S(1)} %add_add_fusion.6), channel_id=1, source_target_pairs={{0,8},{1,65},{8,0},{9,73},{16,24},{17,81},{24,16},{25,89},{32,40},... | collective-permute-start | bytes 221192 | tf_op jit(solution)/shard_map/ppermute | solution.py:55
  33.6 4.7 %collective-permute-start.8 = (f32[16,1152]{1,0:T(8,128)S(1)}, f32[16,1152]{1,0:T(8,128)S(1)}, u32[]{:S(2)}, u32[]{:S(2)}) collective-permute-start(f32[16,1152]{1,0:T(8,128)S(1)} %add_add_fusion.6), channel_id=1, source_target_pairs={{0,16},{1,129},{8,24},{9,137},{16,0},{17,145},{24,8},{25,153},{32,... | collective-permute-start | bytes 221192 | tf_op jit(solution)/shard_map/ppermute | solution.py:55
  38.3 6.4 %collective-permute-start.11 = (f32[16,1152]{1,0:T(8,128)S(1)}, f32[16,1152]{1,0:T(8,128)S(1)}, u32[]{:S(2)}, u32[]{:S(2)}) collective-permute-start(f32[16,1152]{1,0:T(8,128)S(1)} %add_add_fusion.5.mine), channel_id=1, source_target_pairs={{0,48},{8,56},{16,32},{24,40},{32,16},{40,24},{48,0},{56,8},{1,49}... | collective-permute-start | bytes 221192 | tf_op jit(solution)/shard_map/ppermute | solution.py:44
  46.1 5.5 %collective-permute-start.12 = (f32[16,2048]{1,0:T(8,128)S(1)}, f32[16,2048]{1,0:T(8,128)S(1)}, u32[]{:S(2)}, u32[]{:S(2)}) collective-permute-start(f32[16,2048]{1,0:T(8,128)S(1)} %get-tuple-element.19), channel_id=1, source_target_pairs={{0,1},{1,0},{2,3},{3,2},{4,5},{5,4},{6,7},{7,6},{8,9},{9,8},{10,11... | collective-permute-start | bytes 393224 | tf_op jit(solution)/shard_map/ppermute | solution.py:44
  51.7 6.2 %collective-permute-start.15 = (f32[16,2048]{1,0:T(8,128)S(1)}, f32[16,2048]{1,0:T(8,128)S(1)}, u32[]{:S(2)}, u32[]{:S(2)}) collective-permute-start(f32[16,2048]{1,0:T(8,128)S(1)} %add.91), channel_id=1, source_target_pairs={{0,6},{2,4},{4,2},{6,0},{1,7},{3,5},{5,3},{7,1},{8,14},{10,12},{12... | collective-permute-start | bytes 393224 | tf_op jit(solution)/shard_map/ppermute | solution.py:44
  54.4 4.6 %collective-permute-start.14 = (f32[16,2048]{1,0:T(8,128)S(1)}, f32[16,2048]{1,0:T(8,128)S(1)}, u32[]{:S(2)}, u32[]{:S(2)}) collective-permute-start(f32[16,2048]{1,0:T(8,128)S(1)} %add.91), channel_id=1, source_target_pairs={{0,2},{2,0},{4,6},{6,4},{1,3},{3,1},{5,7},{7,5},{8,10},{10,8},{12,... | collective-permute-start | bytes 393224 | tf_op jit(solution)/shard_map/ppermute | solution.py:44
  54.4 7.3 %collective-permute-start.13 = (f32[16,2048]{1,0:T(8,128)S(1)}, f32[16,2048]{1,0:T(8,128)S(1)}, u32[]{:S(2)}, u32[]{:S(2)}) collective-permute-start(f32[16,2048]{1,0:T(8,128)S(1)} %add.91), channel_id=1, source_target_pairs={{0,4},{2,6},{4,0},{6,2},{1,5},{3,7},{5,1},{7,3},{8,12},{10,14},{12... | collective-permute-start | bytes 393224 | tf_op jit(solution)/shard_map/ppermute | solution.py:44
  61.6 2.4 %collective-permute-start.16 = (f32[16,2048]{1,0:T(8,128)S(1)}, f32[16,2048]{1,0:T(8,128)S(1)}, u32[]{:S(2)}, u32[]{:S(2)}) collective-permute-start(f32[16,2048]{1,0:T(8,128)S(1)} %add_add_fusion.1.half), channel_id=1, source_target_pairs={{0,1},{1,0},{2,3},{3,2},{4,5},{5,4},{6,7},{7,6},{8,9},{9,8},{10,11... | collective-permute-start | bytes 393224 | tf_op jit(solution)/shard_map/ppermute | solution.py:44
  64.9 5.2 %collective-permute-start.19 = (f32[16,1152]{1,0:T(8,128)S(1)}, f32[16,1152]{1,0:T(8,128)S(1)}, u32[]{:S(2)}, u32[]{:S(2)}) collective-permute-start(f32[16,1152]{1,0:T(8,128)S(1)} %shard_map.57), channel_id=1, source_target_pairs={{0,192},{1,25},{8,200},{9,17},{16,208},{17,9},{24,216},{25,1},{32,... | collective-permute-start | bytes 221192 | tf_op jit(solution)/shard_map/ppermute | solution.py:55
  66.6 4.8 %collective-permute-start.18 = (f32[16,1152]{1,0:T(8,128)S(1)}, f32[16,1152]{1,0:T(8,128)S(1)}, u32[]{:S(2)}, u32[]{:S(2)}) collective-permute-start(f32[16,1152]{1,0:T(8,128)S(1)} %shard_map.57), channel_id=1, source_target_pairs={{0,64},{1,9},{8,72},{9,1},{16,80},{17,25},{24,88},{25,17},{32,96},... | collective-permute-start | bytes 221192 | tf_op jit(solution)/shard_map/ppermute | solution.py:55
  66.7 4.6 %collective-permute-start.17 = (f32[16,1152]{1,0:T(8,128)S(1)}, f32[16,1152]{1,0:T(8,128)S(1)}, u32[]{:S(2)}, u32[]{:S(2)}) collective-permute-start(f32[16,1152]{1,0:T(8,128)S(1)} %shard_map.57), channel_id=1, source_target_pairs={{0,128},{1,17},{8,136},{9,25},{16,144},{17,1},{24,152},{25,9},{32,... | collective-permute-start | bytes 221192 | tf_op jit(solution)/shard_map/ppermute | solution.py:55
  71.4 4.5 %collective-permute-start.22 = (f32[16,1152]{1,0:T(8,128)S(1)}, f32[16,1152]{1,0:T(8,128)S(1)}, u32[]{:S(2)}, u32[]{:S(2)}) collective-permute-start(f32[16,1152]{1,0:T(8,128)S(1)} %add_add_fusion.4), channel_id=1, source_target_pairs={{0,24},{1,193},{8,16},{9,201},{16,8},{17,209},{24,0},{25,217},{32,... | collective-permute-start | bytes 221192 | tf_op jit(solution)/shard_map/ppermute | solution.py:55
  73.0 3.2 %collective-permute-start.21 = (f32[16,1152]{1,0:T(8,128)S(1)}, f32[16,1152]{1,0:T(8,128)S(1)}, u32[]{:S(2)}, u32[]{:S(2)}) collective-permute-start(f32[16,1152]{1,0:T(8,128)S(1)} %add_add_fusion.4), channel_id=1, source_target_pairs={{0,8},{1,65},{8,0},{9,73},{16,24},{17,81},{24,16},{25,89},{32,40},... | collective-permute-start | bytes 221192 | tf_op jit(solution)/shard_map/ppermute | solution.py:55
  73.1 4.8 %collective-permute-start.20 = (f32[16,1152]{1,0:T(8,128)S(1)}, f32[16,1152]{1,0:T(8,128)S(1)}, u32[]{:S(2)}, u32[]{:S(2)}) collective-permute-start(f32[16,1152]{1,0:T(8,128)S(1)} %add_add_fusion.4), channel_id=1, source_target_pairs={{0,16},{1,129},{8,24},{9,137},{16,0},{17,145},{24,8},{25,153},{32,... | collective-permute-start | bytes 221192 | tf_op jit(solution)/shard_map/ppermute | solution.py:55
  77.9 6.2 %collective-permute-start.23 = (f32[16,1152]{1,0:T(8,128)S(1)}, f32[16,1152]{1,0:T(8,128)S(1)}, u32[]{:S(2)}, u32[]{:S(2)}) collective-permute-start(f32[16,1152]{1,0:T(8,128)S(1)} %add_add_fusion.3.mine), channel_id=1, source_target_pairs={{0,48},{8,56},{16,32},{24,40},{32,16},{40,24},{48,0},{56,8},{1,49}... | collective-permute-start | bytes 221192 | tf_op jit(solution)/shard_map/ppermute | solution.py:44
  85.5 4.9 %collective-permute-start.24 = (f32[16,2048]{1,0:T(8,128)S(1)}, f32[16,2048]{1,0:T(8,128)S(1)}, u32[]{:S(2)}, u32[]{:S(2)}) collective-permute-start(f32[16,2048]{1,0:T(8,128)S(1)} %get-tuple-element.21), channel_id=1, source_target_pairs={{0,1},{1,0},{2,3},{3,2},{4,5},{5,4},{6,7},{7,6},{8,9},{9,8},{10,11... | collective-permute-start | bytes 393224 | tf_op jit(solution)/shard_map/ppermute | solution.py:44
  90.4 6.2 %collective-permute-start.27 = (f32[16,2048]{1,0:T(8,128)S(1)}, f32[16,2048]{1,0:T(8,128)S(1)}, u32[]{:S(2)}, u32[]{:S(2)}) collective-permute-start(f32[16,2048]{1,0:T(8,128)S(1)} %add.101), channel_id=1, source_target_pairs={{0,6},{2,4},{4,2},{6,0},{1,7},{3,5},{5,3},{7,1},{8,14},{10,12},{12... | collective-permute-start | bytes 393224 | tf_op jit(solution)/shard_map/ppermute | solution.py:44
  93.1 4.6 %collective-permute-start.26 = (f32[16,2048]{1,0:T(8,128)S(1)}, f32[16,2048]{1,0:T(8,128)S(1)}, u32[]{:S(2)}, u32[]{:S(2)}) collective-permute-start(f32[16,2048]{1,0:T(8,128)S(1)} %add.101), channel_id=1, source_target_pairs={{0,2},{2,0},{4,6},{6,4},{1,3},{3,1},{5,7},{7,5},{8,10},{10,8},{12,... | collective-permute-start | bytes 393224 | tf_op jit(solution)/shard_map/ppermute | solution.py:44
  93.1 7.3 %collective-permute-start.25 = (f32[16,2048]{1,0:T(8,128)S(1)}, f32[16,2048]{1,0:T(8,128)S(1)}, u32[]{:S(2)}, u32[]{:S(2)}) collective-permute-start(f32[16,2048]{1,0:T(8,128)S(1)} %add.101), channel_id=1, source_target_pairs={{0,4},{2,6},{4,0},{6,2},{1,5},{3,7},{5,1},{7,3},{8,12},{10,14},{12... | collective-permute-start | bytes 393224 | tf_op jit(solution)/shard_map/ppermute | solution.py:44
  100.7 6.3 %collective-permute-start.30 = (f32[8,128]{1,0:T(8,128)S(1)}, f32[8,128]{1,0:T(8,128)S(1)}, u32[]{:S(2)}, u32[]{:S(2)}) collective-permute-start(f32[8,128]{1,0:T(8,128)S(1)} %shard_map.60), channel_id=1, source_target_pairs={{0,49},{1,48},{8,57},{9,56},{16,33},{17,32},{24,41},{25,40},{32,17... | collective-permute-start | bytes 12296 | tf_op jit(solution)/shard_map/ppermute | solution.py:44
  105.7 1.3 %collective-permute-start.29 = (f32[8,128]{1,0:T(8,128)S(1)}, f32[8,128]{1,0:T(8,128)S(1)}, u32[]{:S(2)}, u32[]{:S(2)}) collective-permute-start(f32[8,128]{1,0:T(8,128)S(1)} %shard_map.60), channel_id=1, source_target_pairs={{0,1},{1,0},{8,9},{9,8},{16,17},{17,16},{24,25},{25,24},{32,33},{3... | collective-permute-start | bytes 12296 | tf_op jit(solution)/shard_map/ppermute | solution.py:44
  105.7 4.6 %collective-permute-start.28 = (f32[8,128]{1,0:T(8,128)S(1)}, f32[8,128]{1,0:T(8,128)S(1)}, u32[]{:S(2)}, u32[]{:S(2)}) collective-permute-start(f32[8,128]{1,0:T(8,128)S(1)} %shard_map.60), channel_id=1, source_target_pairs={{0,48},{1,49},{8,56},{9,57},{16,32},{17,33},{24,40},{25,41},{32,16... | collective-permute-start | bytes 12296 | tf_op jit(solution)/shard_map/ppermute | solution.py:44

commit v6 on v4

--- a/solution.py
+++ b/solution.py
@@ -44,7 +44,7 @@
     return lax.ppermute(value, axis, [(i, i ^ offset) for i in range(count)])
 
 
-def sum_four(value, axis, count, offsets=(1, 2, 3)):
+def sum_four(value, axis, count, offsets=(2, 1, 3)):
     one, two, three = (swap(value, axis, count, k) for k in offsets)
     return (value + two) + (one + three)
 
@@ -290,12 +290,12 @@
                 back_other_kernel, [packed_out], sibling, held_other, packed, flops=pass_flops
             )
             packed = sum_four(packed, "x", 4)
-            packed = sum_four(packed, z, 8)
+            packed = sum_four(packed, z, 8, (1, 6, 7))
             left, other = call(
                 functools.partial(solve_kernel, scale=scale),
                 [left_out, half_out],
                 packed,
-                swap(packed, z, 8, 6),
+                swap(packed, z, 8, 2),
                 held_other,
                 flops=pass_flops,
             )

time: 124 us -> 123 us (level)
  no operation moved by 1% of the time
where the time goes in v6:
time: 123 us; the launch traced here: 122 us
  starting transfers between devices  50.9 us (41%)
  waiting for transfers between devices  42.7 us (35%)
  Pallas kernels  15.8 us (13%)
  blocking collectives  11.1 us (9%)
    ppermute x31, starting transfers between devices, swap(): return lax.ppermute(value, axis, [(i, i ^ offset) for i in range(count)])  50.9 us
    ppermute x31, waiting for transfers between devices, swap(): return lax.ppermute(value, axis, [(i, i ^ offset) for i in range(count)])  42.7 us
    pallas_call x12, Pallas kernels, call(): pl.pallas_call(kernel, in_specs=spaces or [whole] * len(args), out_specs=...  15.8 us
    all_to_all x1, blocking collectives, body(): grams = lax.all_to_all(spread, ('x', 'level'), 0, 0)  11.1 us
  transfers between devices with their start and end apart: 31, of which 25 were waited for; matrix products, arithmetic and copies ran while one was open for 0% of the time, Pallas kernels for 6%

profile of v6, /device:TPU:1, one launch (start us, length us, event | category | flops | bytes accessed | tf_op | source)
XLA Modules:
  0.0 121.5 jit_solution(1273652677725187176)
XLA Ops:
  0.6 2.9 %shard_map.50 = (bf16[16,1024]{1,0:T(8,128)(2,1)S(1)}, bf16[2048,1024]{1,0:T(8,128)(2,1)S(1)}, f32[16,2048]{1,0:T(8,128)S(1)}) custom-call(s32[16]{0:T(128)} %seed_values.1, s32[1,1024]{1,0:T(1,128)} %bitcast.1, bf16[4096,1024]{1,0:T(8,128)(2,1)} %affinity.3), custom_call_target="tpu_custom_call" | custom-call | flops 67108864 | bytes 4194304 | tf_op jit(solution)/shard_map/pallas_call | solution.py:218
  3.5 3.3 %collective-permute-start = (f32[16,2048]{1,0:T(8,128)S(1)}, f32[16,2048]{1,0:T(8,128)S(1)}, u32[]{:S(2)}, u32[]{:S(2)}) collective-permute-start(f32[16,2048]{1,0:T(8,128)S(1)} %get-tuple-element.13), channel_id=1, source_target_pairs={{0,1},{1,0},{2,3},{3,2},{4,5},{5,4},{6,7},{7,6},{8,9},{9,8},{10,11... | collective-permute-start | bytes 393224 | tf_op jit(solution)/shard_map/ppermute | solution.py:44
  6.8 2.8 %shard_map.51 = (bf16[2048,1024]{1,0:T(8,128)(2,1)S(1)}, f32[16,2048]{1,0:T(8,128)S(1)}) custom-call(bf16[16,1024]{1,0:T(8,128)(2,1)S(1)} %get-tuple-element.11.left, bf16[4096,1024]{1,0:T(8,128)(2,1)} %affinity.3), custom_call_target="tpu_custom_call" | custom-call | flops 67108864 | bytes 4194304 | tf_op jit(solution)/shard_map/pallas_call | solution.py:218
  9.7 1.1 collective-permute-start.3
  11.1 1.9 %collective-permute-start.1 = (f32[16,2048]{1,0:T(8,128)S(1)}, f32[16,2048]{1,0:T(8,128)S(1)}, u32[]{:S(2)}, u32[]{:S(2)}) collective-permute-start(f32[16,2048]{1,0:T(8,128)S(1)} %add.81), channel_id=1, source_target_pairs={{0,2},{2,0},{4,6},{6,4},{1,3},{3,1},{5,7},{7,5},{8,10},{10,8},{12,... | collective-permute-start | bytes 393224 | tf_op jit(solution)/shard_map/ppermute | solution.py:44
  13.0 5.9 %collective-permute-done.3 = f32[16,2048]{1,0:T(8,128)S(1)} collective-permute-done((f32[16,2048]{1,0:T(8,128)S(1)}, f32[16,2048]{1,0:T(8,128)S(1)}, u32[]{:S(2)}, u32[]{:S(2)}) %collective-permute-start.3) | collective-permute-done | bytes 131104 | tf_op jit(solution)/shard_map/ppermute | solution.py:44
  19.2 1.2 %collective-permute-start.4 = (f32[16,2048]{1,0:T(8,128)S(1)}, f32[16,2048]{1,0:T(8,128)S(1)}, u32[]{:S(2)}, u32[]{:S(2)}) collective-permute-start(f32[16,2048]{1,0:T(8,128)S(1)} %add_add_fusion.2.half), channel_id=1, source_target_pairs={{0,1},{1,0},{2,3},{3,2},{4,5},{5,4},{6,7},{7,6},{8,9},{9,8},{10,11... | collective-permute-start | bytes 393224 | tf_op jit(solution)/shard_map/ppermute | solution.py:44
  20.4 0.9 shard_map.52.before
  21.4 0.9 shard_map.53
  22.4 1.1 collective-permute-start.7
  24.0 1.7 %collective-permute-start.5 = (f32[16,1152]{1,0:T(8,128)S(1)}, f32[16,1152]{1,0:T(8,128)S(1)}, u32[]{:S(2)}, u32[]{:S(2)}) collective-permute-start(f32[16,1152]{1,0:T(8,128)S(1)} %shard_map.53), channel_id=1, source_target_pairs={{0,64},{64,0},{128,192},{192,128},{1,65},{65,1},{129,193},{193,129... | collective-permute-start | bytes 221192 | tf_op jit(solution)/shard_map/ppermute | solution.py:44
  25.6 1.2 collective-permute-done.7
  26.8 1.5 %collective-permute-done.6 = f32[16,1152]{1,0:T(8,128)S(1)} collective-permute-done((f32[16,1152]{1,0:T(8,128)S(1)}, f32[16,1152]{1,0:T(8,128)S(1)}, u32[]{:S(2)}, u32[]{:S(2)}) %collective-permute-start.6) | collective-permute-done | bytes 73760 | tf_op jit(solution)/shard_map/ppermute | solution.py:44
  29.0 4.9 %collective-permute-start.10 = (f32[16,1152]{1,0:T(8,128)S(1)}, f32[16,1152]{1,0:T(8,128)S(1)}, u32[]{:S(2)}, u32[]{:S(2)}) collective-permute-start(f32[16,1152]{1,0:T(8,128)S(1)} %add_add_fusion.6), channel_id=1, source_target_pairs={{0,56},{8,48},{16,40},{24,32},{32,24},{40,16},{48,8},{56,0},{1,57}... | collective-permute-start | bytes 221192 | tf_op jit(solution)/shard_map/ppermute | solution.py:44
  33.9 1.6 %collective-permute-start.9 = (f32[16,1152]{1,0:T(8,128)S(1)}, f32[16,1152]{1,0:T(8,128)S(1)}, u32[]{:S(2)}, u32[]{:S(2)}) collective-permute-start(f32[16,1152]{1,0:T(8,128)S(1)} %add_add_fusion.6), channel_id=1, source_target_pairs={{0,8},{8,0},{16,24},{24,16},{32,40},{40,32},{48,56},{56,48},{1,9},... | collective-permute-start | bytes 221192 | tf_op jit(solution)/shard_map/ppermute | solution.py:44
  35.5 0.9 collective-permute-done.10
  36.4 1.9 %collective-permute-done.9 = f32[16,1152]{1,0:T(8,128)S(1)} collective-permute-done((f32[16,1152]{1,0:T(8,128)S(1)}, f32[16,1152]{1,0:T(8,128)S(1)}, u32[]{:S(2)}, u32[]{:S(2)}) %collective-permute-start.9) | collective-permute-done | bytes 73760 | tf_op jit(solution)/shard_map/ppermute | solution.py:44
  38.3 2.5 %collective-permute-done.8 = f32[16,1152]{1,0:T(8,128)S(1)} collective-permute-done((f32[16,1152]{1,0:T(8,128)S(1)}, f32[16,1152]{1,0:T(8,128)S(1)}, u32[]{:S(2)}, u32[]{:S(2)}) %collective-permute-start.8) | collective-permute-done | bytes 73760 | tf_op jit(solution)/shard_map/ppermute | solution.py:44
  41.5 4.2 %collective-permute-done.11.theirs = f32[16,1152]{1,0:T(8,128)S(1)} collective-permute-done((f32[16,1152]{1,0:T(8,128)S(1)}, f32[16,1152]{1,0:T(8,128)S(1)}, u32[]{:S(2)}, u32[]{:S(2)}) %collective-permute-start.11) | collective-permute-done | bytes 73760 | tf_op jit(solution)/shard_map/ppermute | solution.py:44
  45.7 1.4 %shard_map.54 = (bf16[16,1024]{1,0:T(8,128)(2,1)S(1)}, f32[16,2048]{1,0:T(8,128)S(1)}) custom-call(f32[16,1152]{1,0:T(8,128)S(1)} %add_add_fusion.5.mine, f32[16,1152]{1,0:T(8,128)S(1)} %collective-permute-done.11.theirs, bf16[2048,1024]{1,0:T(8,128)(2,1)S(1)} %get-tuple-element.14.held), custom_call_target="tpu_custom_call" | custom-call | flops 67108864 | bytes 4194304 | tf_op jit(solution)/shard_map/pallas_call | solution.py:218
  47.0 5.0 %collective-permute-start.12 = (f32[16,2048]{1,0:T(8,128)S(1)}, f32[16,2048]{1,0:T(8,128)S(1)}, u32[]{:S(2)}, u32[]{:S(2)}) collective-permute-start(f32[16,2048]{1,0:T(8,128)S(1)} %get-tuple-element.17), channel_id=1, source_target_pairs={{0,1},{1,0},{2,3},{3,2},{4,5},{5,4},{6,7},{7,6},{8,9},{9,8},{10,11... | collective-permute-start | bytes 393224 | tf_op jit(solution)/shard_map/ppermute | solution.py:44
  52.0 1.2 shard_map.55
  53.3 2.4 %collective-permute-start.15 = (f32[16,2048]{1,0:T(8,128)S(1)}, f32[16,2048]{1,0:T(8,128)S(1)}, u32[]{:S(2)}, u32[]{:S(2)}) collective-permute-start(f32[16,2048]{1,0:T(8,128)S(1)} %add.91), channel_id=1, source_target_pairs={{0,6},{2,4},{4,2},{6,0},{1,7},{3,5},{5,3},{7,1},{8,14},{10,12},{12... | collective-permute-start | bytes 393224 | tf_op jit(solution)/shard_map/ppermute | solution.py:44
  56.6 4.5 %collective-permute-done.15 = f32[16,2048]{1,0:T(8,128)S(1)} collective-permute-done((f32[16,2048]{1,0:T(8,128)S(1)}, f32[16,2048]{1,0:T(8,128)S(1)}, u32[]{:S(2)}, u32[]{:S(2)}) %collective-permute-start.15) | collective-permute-done | bytes 131104 | tf_op jit(solution)/shard_map/ppermute | solution.py:44
  62.6 1.5 %collective-permute-start.16 = (f32[16,2048]{1,0:T(8,128)S(1)}, f32[16,2048]{1,0:T(8,128)S(1)}, u32[]{:S(2)}, u32[]{:S(2)}) collective-permute-start(f32[16,2048]{1,0:T(8,128)S(1)} %add_add_fusion.1.half), channel_id=1, source_target_pairs={{0,1},{1,0},{2,3},{3,2},{4,5},{5,4},{6,7},{7,6},{8,9},{9,8},{10,11... | collective-permute-start | bytes 393224 | tf_op jit(solution)/shard_map/ppermute | solution.py:44
  64.2 0.9 shard_map.56.before
  65.1 0.9 shard_map.57
  66.1 1.1 collective-permute-start.19
  68.0 1.4 %collective-permute-start.17 = (f32[16,1152]{1,0:T(8,128)S(1)}, f32[16,1152]{1,0:T(8,128)S(1)}, u32[]{:S(2)}, u32[]{:S(2)}) collective-permute-start(f32[16,1152]{1,0:T(8,128)S(1)} %shard_map.57), channel_id=1, source_target_pairs={{0,64},{64,0},{128,192},{192,128},{1,65},{65,1},{129,193},{193,129... | collective-permute-start | bytes 221192 | tf_op jit(solution)/shard_map/ppermute | solution.py:44
  69.4 1.2 collective-permute-done.19
  70.5 1.5 %collective-permute-done.18 = f32[16,1152]{1,0:T(8,128)S(1)} collective-permute-done((f32[16,1152]{1,0:T(8,128)S(1)}, f32[16,1152]{1,0:T(8,128)S(1)}, u32[]{:S(2)}, u32[]{:S(2)}) %collective-permute-start.18) | collective-permute-done | bytes 73760 | tf_op jit(solution)/shard_map/ppermute | solution.py:44
  72.8 2.0 %collective-permute-start.21 = (f32[16,1152]{1,0:T(8,128)S(1)}, f32[16,1152]{1,0:T(8,128)S(1)}, u32[]{:S(2)}, u32[]{:S(2)}) collective-permute-start(f32[16,1152]{1,0:T(8,128)S(1)} %add_add_fusion.4), channel_id=1, source_target_pairs={{0,8},{8,0},{16,24},{24,16},{32,40},{40,32},{48,56},{56,48},{1,9},... | collective-permute-start | bytes 221192 | tf_op jit(solution)/shard_map/ppermute | solution.py:44
  74.8 1.9 %collective-permute-start.20 = (f32[16,1152]{1,0:T(8,128)S(1)}, f32[16,1152]{1,0:T(8,128)S(1)}, u32[]{:S(2)}, u32[]{:S(2)}) collective-permute-start(f32[16,1152]{1,0:T(8,128)S(1)} %add_add_fusion.4), channel_id=1, source_target_pairs={{0,48},{8,56},{16,32},{24,40},{32,16},{40,24},{48,0},{56,8},{1,49}... | collective-permute-start | bytes 221192 | tf_op jit(solution)/shard_map/ppermute | solution.py:44
  76.6 1.3 %collective-permute-done.22 = f32[16,1152]{1,0:T(8,128)S(1)} collective-permute-done((f32[16,1152]{1,0:T(8,128)S(1)}, f32[16,1152]{1,0:T(8,128)S(1)}, u32[]{:S(2)}, u32[]{:S(2)}) %collective-permute-start.22) | collective-permute-done | bytes 73760 | tf_op jit(solution)/shard_map/ppermute | solution.py:44
  78.0 2.5 %collective-permute-done.20 = f32[16,1152]{1,0:T(8,128)S(1)} collective-permute-done((f32[16,1152]{1,0:T(8,128)S(1)}, f32[16,1152]{1,0:T(8,128)S(1)}, u32[]{:S(2)}, u32[]{:S(2)}) %collective-permute-start.20) | collective-permute-done | bytes 73760 | tf_op jit(solution)/shard_map/ppermute | solution.py:44
  80.5 2.2 %collective-permute-start.23 = (f32[16,1152]{1,0:T(8,128)S(1)}, f32[16,1152]{1,0:T(8,128)S(1)}, u32[]{:S(2)}, u32[]{:S(2)}) collective-permute-start(f32[16,1152]{1,0:T(8,128)S(1)} %add_add_fusion.3.mine), channel_id=1, source_target_pairs={{0,16},{8,24},{16,0},{24,8},{32,48},{40,56},{48,32},{56,40},{1,17}... | collective-permute-start | bytes 221192 | tf_op jit(solution)/shard_map/ppermute | solution.py:44
  82.8 2.0 %collective-permute-done.23.theirs = f32[16,1152]{1,0:T(8,128)S(1)} collective-permute-done((f32[16,1152]{1,0:T(8,128)S(1)}, f32[16,1152]{1,0:T(8,128)S(1)}, u32[]{:S(2)}, u32[]{:S(2)}) %collective-permute-start.23) | collective-permute-done | bytes 73760 | tf_op jit(solution)/shard_map/ppermute | solution.py:44
  84.7 1.4 %shard_map.58 = (bf16[16,1024]{1,0:T(8,128)(2,1)S(1)}, f32[16,2048]{1,0:T(8,128)S(1)}) custom-call(f32[16,1152]{1,0:T(8,128)S(1)} %add_add_fusion.3.mine, f32[16,1152]{1,0:T(8,128)S(1)} %collective-permute-done.23.theirs, bf16[2048,1024]{1,0:T(8,128)(2,1)S(1)} %get-tuple-element.14.held), custom_call_target="tpu_custom_call" | custom-call | flops 67108864 | bytes 4194304 | tf_op jit(solution)/shard_map/pallas_call | solution.py:218
  86.1 5.1 %collective-permute-start.24 = (f32[16,2048]{1,0:T(8,128)S(1)}, f32[16,2048]{1,0:T(8,128)S(1)}, u32[]{:S(2)}, u32[]{:S(2)}) collective-permute-start(f32[16,2048]{1,0:T(8,128)S(1)} %get-tuple-element.19), channel_id=1, source_target_pairs={{0,1},{1,0},{2,3},{3,2},{4,5},{5,4},{6,7},{7,6},{8,9},{9,8},{10,11... | collective-permute-start | bytes 393224 | tf_op jit(solution)/shard_map/ppermute | solution.py:44
  91.2 1.2 shard_map.59
  92.4 2.3 %collective-permute-start.27 = (f32[16,2048]{1,0:T(8,128)S(1)}, f32[16,2048]{1,0:T(8,128)S(1)}, u32[]{:S(2)}, u32[]{:S(2)}) collective-permute-start(f32[16,2048]{1,0:T(8,128)S(1)} %add.101), channel_id=1, source_target_pairs={{0,6},{2,4},{4,2},{6,0},{1,7},{3,5},{5,3},{7,1},{8,14},{10,12},{12... | collective-permute-start | bytes 393224 | tf_op jit(solution)/shard_map/ppermute | solution.py:44
  95.8 4.4 %collective-permute-done.27 = f32[16,2048]{1,0:T(8,128)S(1)} collective-permute-done((f32[16,2048]{1,0:T(8,128)S(1)}, f32[16,2048]{1,0:T(8,128)S(1)}, u32[]{:S(2)}, u32[]{:S(2)}) %collective-permute-start.27) | collective-permute-done | bytes 131104 | tf_op jit(solution)/shard_map/ppermute | solution.py:44
  100.9 0.9 collective-permute-done.25
  102.2 2.7 %collective-permute-start.30 = (f32[8,128]{1,0:T(8,128)S(1)}, f32[8,128]{1,0:T(8,128)S(1)}, u32[]{:S(2)}, u32[]{:S(2)}) collective-permute-start(f32[8,128]{1,0:T(8,128)S(1)} %shard_map.60), channel_id=1, source_target_pairs={{0,49},{1,48},{8,57},{9,56},{16,33},{17,32},{24,41},{25,40},{32,17... | collective-permute-start | bytes 12296 | tf_op jit(solution)/shard_map/ppermute | solution.py:44
  104.9 2.1 %collective-permute-start.28 = (f32[8,128]{1,0:T(8,128)S(1)}, f32[8,128]{1,0:T(8,128)S(1)}, u32[]{:S(2)}, u32[]{:S(2)}) collective-permute-start(f32[8,128]{1,0:T(8,128)S(1)} %shard_map.60), channel_id=1, source_target_pairs={{0,48},{1,49},{8,56},{9,57},{16,32},{17,33},{24,40},{25,41},{32,16... | collective-permute-start | bytes 12296 | tf_op jit(solution)/shard_map/ppermute | solution.py:44
  107.3 2.1 %collective-permute-done.28 = f32[8,128]{1,0:T(8,128)S(1)} collective-permute-done((f32[8,128]{1,0:T(8,128)S(1)}, f32[8,128]{1,0:T(8,128)S(1)}, u32[]{:S(2)}, u32[]{:S(2)}) %collective-permute-start.28) | collective-permute-done | bytes 4128 | tf_op jit(solution)/shard_map/ppermute | solution.py:44
  109.4 11.1 %all_to_all.5.grams = f32[16,8,128]{2,1,0:T(8,128)S(1)} all-to-all(f32[16,8,128]{2,1,0:T(8,128)S(1)} %broadcast_in_dim.2), channel_id=1, replica_groups=mesh['x'=4,'cube'=2,'level'=4,'y'=4,'core'=2] {'x','level'}, dimensions={0} | all-to-all | bytes 131072 | tf_op jit(solution)/shard_map/all_to_all | solution.py:306
  120.6 1.0 shard_map.61
  (39 shorter events, 9.3 us)
Async XLA Ops:
  3.5 6.2 %collective-permute-start = (f32[16,2048]{1,0:T(8,128)S(1)}, f32[16,2048]{1,0:T(8,128)S(1)}, u32[]{:S(2)}, u32[]{:S(2)}) collective-permute-start(f32[16,2048]{1,0:T(8,128)S(1)} %get-tuple-element.13), channel_id=1, source_target_pairs={{0,1},{1,0},{2,3},{3,2},{4,5},{5,4},{6,7},{7,6},{8,9},{9,8},{10,11... | collective-permute-start | bytes 393224 | tf_op jit(solution)/shard_map/ppermute | solution.py:44
  9.7 9.2 %collective-permute-start.3 = (f32[16,2048]{1,0:T(8,128)S(1)}, f32[16,2048]{1,0:T(8,128)S(1)}, u32[]{:S(2)}, u32[]{:S(2)}) collective-permute-start(f32[16,2048]{1,0:T(8,128)S(1)} %add.81), channel_id=1, source_target_pairs={{0,6},{2,4},{4,2},{6,0},{1,7},{3,5},{5,3},{7,1},{8,14},{10,12},{12... | collective-permute-start | bytes 393224 | tf_op jit(solution)/shard_map/ppermute | solution.py:44
  10.8 8.1 %collective-permute-start.2 = (f32[16,2048]{1,0:T(8,128)S(1)}, f32[16,2048]{1,0:T(8,128)S(1)}, u32[]{:S(2)}, u32[]{:S(2)}) collective-permute-start(f32[16,2048]{1,0:T(8,128)S(1)} %add.81), channel_id=1, source_target_pairs={{0,4},{2,6},{4,0},{6,2},{1,5},{3,7},{5,1},{7,3},{8,12},{10,14},{12... | collective-permute-start | bytes 393224 | tf_op jit(solution)/shard_map/ppermute | solution.py:44
  11.1 8.1 %collective-permute-start.1 = (f32[16,2048]{1,0:T(8,128)S(1)}, f32[16,2048]{1,0:T(8,128)S(1)}, u32[]{:S(2)}, u32[]{:S(2)}) collective-permute-start(f32[16,2048]{1,0:T(8,128)S(1)} %add.81), channel_id=1, source_target_pairs={{0,2},{2,0},{4,6},{6,4},{1,3},{3,1},{5,7},{7,5},{8,10},{10,8},{12,... | collective-permute-start | bytes 393224 | tf_op jit(solution)/shard_map/ppermute | solution.py:44
  19.2 2.2 %collective-permute-start.4 = (f32[16,2048]{1,0:T(8,128)S(1)}, f32[16,2048]{1,0:T(8,128)S(1)}, u32[]{:S(2)}, u32[]{:S(2)}) collective-permute-start(f32[16,2048]{1,0:T(8,128)S(1)} %add_add_fusion.2.half), channel_id=1, source_target_pairs={{0,1},{1,0},{2,3},{3,2},{4,5},{5,4},{6,7},{7,6},{8,9},{9,8},{10,11... | collective-permute-start | bytes 393224 | tf_op jit(solution)/shard_map/ppermute | solution.py:44
  22.4 4.4 %collective-permute-start.7 = (f32[16,1152]{1,0:T(8,128)S(1)}, f32[16,1152]{1,0:T(8,128)S(1)}, u32[]{:S(2)}, u32[]{:S(2)}) collective-permute-start(f32[16,1152]{1,0:T(8,128)S(1)} %shard_map.53), channel_id=1, source_target_pairs={{0,192},{64,128},{128,64},{192,0},{1,193},{65,129},{129,65},{193,1... | collective-permute-start | bytes 221192 | tf_op jit(solution)/shard_map/ppermute | solution.py:44
  23.5 4.8 %collective-permute-start.6 = (f32[16,1152]{1,0:T(8,128)S(1)}, f32[16,1152]{1,0:T(8,128)S(1)}, u32[]{:S(2)}, u32[]{:S(2)}) collective-permute-start(f32[16,1152]{1,0:T(8,128)S(1)} %shard_map.53), channel_id=1, source_target_pairs={{0,128},{64,192},{128,0},{192,64},{1,129},{65,193},{129,1},{193,65... | collective-permute-start | bytes 221192 | tf_op jit(solution)/shard_map/ppermute | solution.py:44
  24.0 5.0 %collective-permute-start.5 = (f32[16,1152]{1,0:T(8,128)S(1)}, f32[16,1152]{1,0:T(8,128)S(1)}, u32[]{:S(2)}, u32[]{:S(2)}) collective-permute-start(f32[16,1152]{1,0:T(8,128)S(1)} %shard_map.53), channel_id=1, source_target_pairs={{0,64},{64,0},{128,192},{192,128},{1,65},{65,1},{129,193},{193,129... | collective-permute-start | bytes 221192 | tf_op jit(solution)/shard_map/ppermute | solution.py:44
  29.0 7.5 %collective-permute-start.10 = (f32[16,1152]{1,0:T(8,128)S(1)}, f32[16,1152]{1,0:T(8,128)S(1)}, u32[]{:S(2)}, u32[]{:S(2)}) collective-permute-start(f32[16,1152]{1,0:T(8,128)S(1)} %add_add_fusion.6), channel_id=1, source_target_pairs={{0,56},{8,48},{16,40},{24,32},{32,24},{40,16},{48,8},{56,0},{1,57}... | collective-permute-start | bytes 221192 | tf_op jit(solution)/shard_map/ppermute | solution.py:44
  33.9 4.5 %collective-permute-start.9 = (f32[16,1152]{1,0:T(8,128)S(1)}, f32[16,1152]{1,0:T(8,128)S(1)}, u32[]{:S(2)}, u32[]{:S(2)}) collective-permute-start(f32[16,1152]{1,0:T(8,128)S(1)} %add_add_fusion.6), channel_id=1, source_target_pairs={{0,8},{8,0},{16,24},{24,16},{32,40},{40,32},{48,56},{56,48},{1,9},... | collective-permute-start | bytes 221192 | tf_op jit(solution)/shard_map/ppermute | solution.py:44
  35.5 5.3 %collective-permute-start.8 = (f32[16,1152]{1,0:T(8,128)S(1)}, f32[16,1152]{1,0:T(8,128)S(1)}, u32[]{:S(2)}, u32[]{:S(2)}) collective-permute-start(f32[16,1152]{1,0:T(8,128)S(1)} %add_add_fusion.6), channel_id=1, source_target_pairs={{0,48},{8,56},{16,32},{24,40},{32,16},{40,24},{48,0},{56,8},{1,49}... | collective-permute-start | bytes 221192 | tf_op jit(solution)/shard_map/ppermute | solution.py:44
  40.8 4.8 %collective-permute-start.11 = (f32[16,1152]{1,0:T(8,128)S(1)}, f32[16,1152]{1,0:T(8,128)S(1)}, u32[]{:S(2)}, u32[]{:S(2)}) collective-permute-start(f32[16,1152]{1,0:T(8,128)S(1)} %add_add_fusion.5.mine), channel_id=1, source_target_pairs={{0,16},{8,24},{16,0},{24,8},{32,48},{40,56},{48,32},{56,40},{1,17}... | collective-permute-start | bytes 221192 | tf_op jit(solution)/shard_map/ppermute | solution.py:44
  47.0 6.2 %collective-permute-start.12 = (f32[16,2048]{1,0:T(8,128)S(1)}, f32[16,2048]{1,0:T(8,128)S(1)}, u32[]{:S(2)}, u32[]{:S(2)}) collective-permute-start(f32[16,2048]{1,0:T(8,128)S(1)} %get-tuple-element.17), channel_id=1, source_target_pairs={{0,1},{1,0},{2,3},{3,2},{4,5},{5,4},{6,7},{7,6},{8,9},{9,8},{10,11... | collective-permute-start | bytes 393224 | tf_op jit(solution)/shard_map/ppermute | solution.py:44
  53.3 7.9 %collective-permute-start.15 = (f32[16,2048]{1,0:T(8,128)S(1)}, f32[16,2048]{1,0:T(8,128)S(1)}, u32[]{:S(2)}, u32[]{:S(2)}) collective-permute-start(f32[16,2048]{1,0:T(8,128)S(1)} %add.91), channel_id=1, source_target_pairs={{0,6},{2,4},{4,2},{6,0},{1,7},{3,5},{5,3},{7,1},{8,14},{10,12},{12... | collective-permute-start | bytes 393224 | tf_op jit(solution)/shard_map/ppermute | solution.py:44
  55.7 6.2 %collective-permute-start.14 = (f32[16,2048]{1,0:T(8,128)S(1)}, f32[16,2048]{1,0:T(8,128)S(1)}, u32[]{:S(2)}, u32[]{:S(2)}) collective-permute-start(f32[16,2048]{1,0:T(8,128)S(1)} %add.91), channel_id=1, source_target_pairs={{0,4},{2,6},{4,0},{6,2},{1,5},{3,7},{5,1},{7,3},{8,12},{10,14},{12... | collective-permute-start | bytes 393224 | tf_op jit(solution)/shard_map/ppermute | solution.py:44
  56.1 6.5 %collective-permute-start.13 = (f32[16,2048]{1,0:T(8,128)S(1)}, f32[16,2048]{1,0:T(8,128)S(1)}, u32[]{:S(2)}, u32[]{:S(2)}) collective-permute-start(f32[16,2048]{1,0:T(8,128)S(1)} %add.91), channel_id=1, source_target_pairs={{0,2},{2,0},{4,6},{6,4},{1,3},{3,1},{5,7},{7,5},{8,10},{10,8},{12,... | collective-permute-start | bytes 393224 | tf_op jit(solution)/shard_map/ppermute | solution.py:44
  62.6 2.5 %collective-permute-start.16 = (f32[16,2048]{1,0:T(8,128)S(1)}, f32[16,2048]{1,0:T(8,128)S(1)}, u32[]{:S(2)}, u32[]{:S(2)}) collective-permute-start(f32[16,2048]{1,0:T(8,128)S(1)} %add_add_fusion.1.half), channel_id=1, source_target_pairs={{0,1},{1,0},{2,3},{3,2},{4,5},{5,4},{6,7},{7,6},{8,9},{9,8},{10,11... | collective-permute-start | bytes 393224 | tf_op jit(solution)/shard_map/ppermute | solution.py:44
  66.1 4.4 %collective-permute-start.19 = (f32[16,1152]{1,0:T(8,128)S(1)}, f32[16,1152]{1,0:T(8,128)S(1)}, u32[]{:S(2)}, u32[]{:S(2)}) collective-permute-start(f32[16,1152]{1,0:T(8,128)S(1)} %shard_map.57), channel_id=1, source_target_pairs={{0,192},{64,128},{128,64},{192,0},{1,193},{65,129},{129,65},{193,1... | collective-permute-start | bytes 221192 | tf_op jit(solution)/shard_map/ppermute | solution.py:44
  67.2 4.8 %collective-permute-start.18 = (f32[16,1152]{1,0:T(8,128)S(1)}, f32[16,1152]{1,0:T(8,128)S(1)}, u32[]{:S(2)}, u32[]{:S(2)}) collective-permute-start(f32[16,1152]{1,0:T(8,128)S(1)} %shard_map.57), channel_id=1, source_target_pairs={{0,128},{64,192},{128,0},{192,64},{1,129},{65,193},{129,1},{193,65... | collective-permute-start | bytes 221192 | tf_op jit(solution)/shard_map/ppermute | solution.py:44
  68.0 4.7 %collective-permute-start.17 = (f32[16,1152]{1,0:T(8,128)S(1)}, f32[16,1152]{1,0:T(8,128)S(1)}, u32[]{:S(2)}, u32[]{:S(2)}) collective-permute-start(f32[16,1152]{1,0:T(8,128)S(1)} %shard_map.57), channel_id=1, source_target_pairs={{0,64},{64,0},{128,192},{192,128},{1,65},{65,1},{129,193},{193,129... | collective-permute-start | bytes 221192 | tf_op jit(solution)/shard_map/ppermute | solution.py:44
  72.7 5.3 %collective-permute-start.22 = (f32[16,1152]{1,0:T(8,128)S(1)}, f32[16,1152]{1,0:T(8,128)S(1)}, u32[]{:S(2)}, u32[]{:S(2)}) collective-permute-start(f32[16,1152]{1,0:T(8,128)S(1)} %add_add_fusion.4), channel_id=1, source_target_pairs={{0,56},{8,48},{16,40},{24,32},{32,24},{40,16},{48,8},{56,0},{1,57}... | collective-permute-start | bytes 221192 | tf_op jit(solution)/shard_map/ppermute | solution.py:44
  72.8 5.2 %collective-permute-start.21 = (f32[16,1152]{1,0:T(8,128)S(1)}, f32[16,1152]{1,0:T(8,128)S(1)}, u32[]{:S(2)}, u32[]{:S(2)}) collective-permute-start(f32[16,1152]{1,0:T(8,128)S(1)} %add_add_fusion.4), channel_id=1, source_target_pairs={{0,8},{8,0},{16,24},{24,16},{32,40},{40,32},{48,56},{56,48},{1,9},... | collective-permute-start | bytes 221192 | tf_op jit(solution)/shard_map/ppermute | solution.py:44
  74.8 5.7 %collective-permute-start.20 = (f32[16,1152]{1,0:T(8,128)S(1)}, f32[16,1152]{1,0:T(8,128)S(1)}, u32[]{:S(2)}, u32[]{:S(2)}) collective-permute-start(f32[16,1152]{1,0:T(8,128)S(1)} %add_add_fusion.4), channel_id=1, source_target_pairs={{0,48},{8,56},{16,32},{24,40},{32,16},{40,24},{48,0},{56,8},{1,49}... | collective-permute-start | bytes 221192 | tf_op jit(solution)/shard_map/ppermute | solution.py:44
  80.5 4.2 %collective-permute-start.23 = (f32[16,1152]{1,0:T(8,128)S(1)}, f32[16,1152]{1,0:T(8,128)S(1)}, u32[]{:S(2)}, u32[]{:S(2)}) collective-permute-start(f32[16,1152]{1,0:T(8,128)S(1)} %add_add_fusion.3.mine), channel_id=1, source_target_pairs={{0,16},{8,24},{16,0},{24,8},{32,48},{40,56},{48,32},{56,40},{1,17}... | collective-permute-start | bytes 221192 | tf_op jit(solution)/shard_map/ppermute | solution.py:44
  86.1 6.3 %collective-permute-start.24 = (f32[16,2048]{1,0:T(8,128)S(1)}, f32[16,2048]{1,0:T(8,128)S(1)}, u32[]{:S(2)}, u32[]{:S(2)}) collective-permute-start(f32[16,2048]{1,0:T(8,128)S(1)} %get-tuple-element.19), channel_id=1, source_target_pairs={{0,1},{1,0},{2,3},{3,2},{4,5},{5,4},{6,7},{7,6},{8,9},{9,8},{10,11... | collective-permute-start | bytes 393224 | tf_op jit(solution)/shard_map/ppermute | solution.py:44
  92.4 7.7 %collective-permute-start.27 = (f32[16,2048]{1,0:T(8,128)S(1)}, f32[16,2048]{1,0:T(8,128)S(1)}, u32[]{:S(2)}, u32[]{:S(2)}) collective-permute-start(f32[16,2048]{1,0:T(8,128)S(1)} %add.101), channel_id=1, source_target_pairs={{0,6},{2,4},{4,2},{6,0},{1,7},{3,5},{5,3},{7,1},{8,14},{10,12},{12... | collective-permute-start | bytes 393224 | tf_op jit(solution)/shard_map/ppermute | solution.py:44
  94.7 6.2 %collective-permute-start.26 = (f32[16,2048]{1,0:T(8,128)S(1)}, f32[16,2048]{1,0:T(8,128)S(1)}, u32[]{:S(2)}, u32[]{:S(2)}) collective-permute-start(f32[16,2048]{1,0:T(8,128)S(1)} %add.101), channel_id=1, source_target_pairs={{0,4},{2,6},{4,0},{6,2},{1,5},{3,7},{5,1},{7,3},{8,12},{10,14},{12... | collective-permute-start | bytes 393224 | tf_op jit(solution)/shard_map/ppermute | solution.py:44
  95.1 6.7 %collective-permute-start.25 = (f32[16,2048]{1,0:T(8,128)S(1)}, f32[16,2048]{1,0:T(8,128)S(1)}, u32[]{:S(2)}, u32[]{:S(2)}) collective-permute-start(f32[16,2048]{1,0:T(8,128)S(1)} %add.101), channel_id=1, source_target_pairs={{0,2},{2,0},{4,6},{6,4},{1,3},{3,1},{5,7},{7,5},{8,10},{10,8},{12,... | collective-permute-start | bytes 393224 | tf_op jit(solution)/shard_map/ppermute | solution.py:44
  102.2 5.2 %collective-permute-start.30 = (f32[8,128]{1,0:T(8,128)S(1)}, f32[8,128]{1,0:T(8,128)S(1)}, u32[]{:S(2)}, u32[]{:S(2)}) collective-permute-start(f32[8,128]{1,0:T(8,128)S(1)} %shard_map.60), channel_id=1, source_target_pairs={{0,49},{1,48},{8,57},{9,56},{16,33},{17,32},{24,41},{25,40},{32,17... | collective-permute-start | bytes 12296 | tf_op jit(solution)/shard_map/ppermute | solution.py:44
  104.9 2.5 %collective-permute-start.29 = (f32[8,128]{1,0:T(8,128)S(1)}, f32[8,128]{1,0:T(8,128)S(1)}, u32[]{:S(2)}, u32[]{:S(2)}) collective-permute-start(f32[8,128]{1,0:T(8,128)S(1)} %shard_map.60), channel_id=1, source_target_pairs={{0,1},{1,0},{8,9},{9,8},{16,17},{17,16},{24,25},{25,24},{32,33},{3... | collective-permute-start | bytes 12296 | tf_op jit(solution)/shard_map/ppermute | solution.py:44
  104.9 4.6 %collective-permute-start.28 = (f32[8,128]{1,0:T(8,128)S(1)}, f32[8,128]{1,0:T(8,128)S(1)}, u32[]{:S(2)}, u32[]{:S(2)}) collective-permute-start(f32[8,128]{1,0:T(8,128)S(1)} %shard_map.60), channel_id=1, source_target_pairs={{0,48},{1,49},{8,56},{9,57},{16,32},{17,33},{24,40},{25,41},{32,16... | collective-permute-start | bytes 12296 | tf_op jit(solution)/shard_map/ppermute | solution.py:44

commit v7 on v4

--- a/solution.py
+++ b/solution.py
@@ -44,7 +44,7 @@
     return lax.ppermute(value, axis, [(i, i ^ offset) for i in range(count)])
 
 
-def sum_four(value, axis, count, offsets=(1, 2, 3)):
+def sum_four(value, axis, count, offsets=(2, 1, 3)):
     one, two, three = (swap(value, axis, count, k) for k in offsets)
     return (value + two) + (one + three)
 
@@ -301,7 +301,7 @@
             )
         else:
             (gram,) = call(gram_kernel, [((8, 128), f32)], half)
-            gram = sum_four(gram, z + ("core",), 16, (1, 12, 13))
+            gram = sum_four(gram, z + ("core",), 16, (12, 1, 13))
             spread = jnp.broadcast_to(gram[None], (16,) + gram.shape)
             grams = lax.all_to_all(spread, ("x", "level"), 0, 0)
             basis, factor = call(

time: 124 us -> 121 us (0.976); the launches traced: 123 us -> 121 us
  starting transfers between devices: 51.5 us -> 47.1 us
  waiting for transfers between devices: 42.6 us -> 45.4 us
    ppermute x31, starting transfers between devices: 51.5 us -> 47.1 us  [swap(): return lax.ppermute(value, axis, [(i, i ^ offset) for i in range(count)])]
    ppermute x31, waiting for transfers between devices: 42.6 us -> 45.4 us  [swap(): return lax.ppermute(value, axis, [(i, i ^ offset) for i in range(count)])]
  transfers between devices with their start and end apart: 31 -> 31, of which waited for: 25 -> 24; matrix products, arithmetic and copies ran while one was open for 0% -> 0% of each run, Pallas kernels for 6% -> 6%
where the time goes in v7:
time: 121 us
  starting transfers between devices  47.1 us (39%)
  waiting for transfers between devices  45.4 us (38%)
  Pallas kernels  15.8 us (13%)
  blocking collectives  11.9 us (10%)
    ppermute x31, starting transfers between devices, swap(): return lax.ppermute(value, axis, [(i, i ^ offset) for i in range(count)])  47.1 us
    ppermute x31, waiting for transfers between devices, swap(): return lax.ppermute(value, axis, [(i, i ^ offset) for i in range(count)])  45.4 us
    pallas_call x12, Pallas kernels, call(): pl.pallas_call(kernel, in_specs=spaces or [whole] * len(args), out_specs=...  15.8 us
    all_to_all x1, blocking collectives, body(): grams = lax.all_to_all(spread, ('x', 'level'), 0, 0)  11.9 us
  transfers between devices with their start and end apart: 31, of which 24 were waited for; matrix products, arithmetic and copies ran while one was open for 0% of the time, Pallas kernels for 6%

profile of v7, /device:TPU:1, one launch (start us, length us, event | category | flops | bytes accessed | tf_op | source)
XLA Modules:
  0.0 121.2 jit_solution(13516628719482603419)
XLA Ops:
  0.6 2.9 %shard_map.50 = (bf16[16,1024]{1,0:T(8,128)(2,1)S(1)}, bf16[2048,1024]{1,0:T(8,128)(2,1)S(1)}, f32[16,2048]{1,0:T(8,128)S(1)}) custom-call(s32[16]{0:T(128)} %seed_values.1, s32[1,1024]{1,0:T(1,128)} %bitcast.1, bf16[4096,1024]{1,0:T(8,128)(2,1)} %affinity.3), custom_call_target="tpu_custom_call" | custom-call | flops 67108864 | bytes 4194304 | tf_op jit(solution)/shard_map/pallas_call | solution.py:218
  3.5 3.3 %collective-permute-start = (f32[16,2048]{1,0:T(8,128)S(1)}, f32[16,2048]{1,0:T(8,128)S(1)}, u32[]{:S(2)}, u32[]{:S(2)}) collective-permute-start(f32[16,2048]{1,0:T(8,128)S(1)} %get-tuple-element.13), channel_id=1, source_target_pairs={{0,1},{1,0},{2,3},{3,2},{4,5},{5,4},{6,7},{7,6},{8,9},{9,8},{10,11... | collective-permute-start | bytes 393224 | tf_op jit(solution)/shard_map/ppermute | solution.py:44
  6.8 2.8 %shard_map.51 = (bf16[2048,1024]{1,0:T(8,128)(2,1)S(1)}, f32[16,2048]{1,0:T(8,128)S(1)}) custom-call(bf16[16,1024]{1,0:T(8,128)(2,1)S(1)} %get-tuple-element.11.left, bf16[4096,1024]{1,0:T(8,128)(2,1)} %affinity.3), custom_call_target="tpu_custom_call" | custom-call | flops 67108864 | bytes 4194304 | tf_op jit(solution)/shard_map/pallas_call | solution.py:218
  9.7 1.1 collective-permute-start.3
  11.1 1.9 %collective-permute-start.1 = (f32[16,2048]{1,0:T(8,128)S(1)}, f32[16,2048]{1,0:T(8,128)S(1)}, u32[]{:S(2)}, u32[]{:S(2)}) collective-permute-start(f32[16,2048]{1,0:T(8,128)S(1)} %add.81), channel_id=1, source_target_pairs={{0,2},{2,0},{4,6},{6,4},{1,3},{3,1},{5,7},{7,5},{8,10},{10,8},{12,... | collective-permute-start | bytes 393224 | tf_op jit(solution)/shard_map/ppermute | solution.py:44
  13.0 5.9 %collective-permute-done.3 = f32[16,2048]{1,0:T(8,128)S(1)} collective-permute-done((f32[16,2048]{1,0:T(8,128)S(1)}, f32[16,2048]{1,0:T(8,128)S(1)}, u32[]{:S(2)}, u32[]{:S(2)}) %collective-permute-start.3) | collective-permute-done | bytes 131104 | tf_op jit(solution)/shard_map/ppermute | solution.py:44
  19.2 1.2 %collective-permute-start.4 = (f32[16,2048]{1,0:T(8,128)S(1)}, f32[16,2048]{1,0:T(8,128)S(1)}, u32[]{:S(2)}, u32[]{:S(2)}) collective-permute-start(f32[16,2048]{1,0:T(8,128)S(1)} %add_add_fusion.2.half), channel_id=1, source_target_pairs={{0,1},{1,0},{2,3},{3,2},{4,5},{5,4},{6,7},{7,6},{8,9},{9,8},{10,11... | collective-permute-start | bytes 393224 | tf_op jit(solution)/shard_map/ppermute | solution.py:44
  20.4 0.9 shard_map.52.before
  21.4 0.9 shard_map.53
  22.4 1.1 collective-permute-start.7
  24.0 1.7 %collective-permute-start.5 = (f32[16,1152]{1,0:T(8,128)S(1)}, f32[16,1152]{1,0:T(8,128)S(1)}, u32[]{:S(2)}, u32[]{:S(2)}) collective-permute-start(f32[16,1152]{1,0:T(8,128)S(1)} %shard_map.53), channel_id=1, source_target_pairs={{0,64},{64,0},{128,192},{192,128},{1,65},{65,1},{129,193},{193,129... | collective-permute-start | bytes 221192 | tf_op jit(solution)/shard_map/ppermute | solution.py:44
  25.6 1.2 collective-permute-done.7
  26.8 1.5 %collective-permute-done.6 = f32[16,1152]{1,0:T(8,128)S(1)} collective-permute-done((f32[16,1152]{1,0:T(8,128)S(1)}, f32[16,1152]{1,0:T(8,128)S(1)}, u32[]{:S(2)}, u32[]{:S(2)}) %collective-permute-start.6) | collective-permute-done | bytes 73760 | tf_op jit(solution)/shard_map/ppermute | solution.py:44
  29.0 3.7 %collective-permute-start.10 = (f32[16,1152]{1,0:T(8,128)S(1)}, f32[16,1152]{1,0:T(8,128)S(1)}, u32[]{:S(2)}, u32[]{:S(2)}) collective-permute-start(f32[16,1152]{1,0:T(8,128)S(1)} %add_add_fusion.6), channel_id=1, source_target_pairs={{0,24},{8,16},{16,8},{24,0},{32,56},{40,48},{48,40},{56,32},{1,25}... | collective-permute-start | bytes 221192 | tf_op jit(solution)/shard_map/ppermute | solution.py:44
  33.0 1.4 %collective-permute-done.10 = f32[16,1152]{1,0:T(8,128)S(1)} collective-permute-done((f32[16,1152]{1,0:T(8,128)S(1)}, f32[16,1152]{1,0:T(8,128)S(1)}, u32[]{:S(2)}, u32[]{:S(2)}) %collective-permute-start.10) | collective-permute-done | bytes 73760 | tf_op jit(solution)/shard_map/ppermute | solution.py:44
  34.4 3.6 %collective-permute-done.9 = f32[16,1152]{1,0:T(8,128)S(1)} collective-permute-done((f32[16,1152]{1,0:T(8,128)S(1)}, f32[16,1152]{1,0:T(8,128)S(1)}, u32[]{:S(2)}, u32[]{:S(2)}) %collective-permute-start.9) | collective-permute-done | bytes 73760 | tf_op jit(solution)/shard_map/ppermute | solution.py:44
  38.0 2.8 %collective-permute-start.11 = (f32[16,1152]{1,0:T(8,128)S(1)}, f32[16,1152]{1,0:T(8,128)S(1)}, u32[]{:S(2)}, u32[]{:S(2)}) collective-permute-start(f32[16,1152]{1,0:T(8,128)S(1)} %add_add_fusion.5.mine), channel_id=1, source_target_pairs={{0,48},{8,56},{16,32},{24,40},{32,16},{40,24},{48,0},{56,8},{1,49}... | collective-permute-start | bytes 221192 | tf_op jit(solution)/shard_map/ppermute | solution.py:44
  40.8 3.4 %collective-permute-done.11.theirs = f32[16,1152]{1,0:T(8,128)S(1)} collective-permute-done((f32[16,1152]{1,0:T(8,128)S(1)}, f32[16,1152]{1,0:T(8,128)S(1)}, u32[]{:S(2)}, u32[]{:S(2)}) %collective-permute-start.11) | collective-permute-done | bytes 73760 | tf_op jit(solution)/shard_map/ppermute | solution.py:44
  44.2 1.4 %shard_map.54 = (bf16[16,1024]{1,0:T(8,128)(2,1)S(1)}, f32[16,2048]{1,0:T(8,128)S(1)}) custom-call(f32[16,1152]{1,0:T(8,128)S(1)} %add_add_fusion.5.mine, f32[16,1152]{1,0:T(8,128)S(1)} %collective-permute-done.11.theirs, bf16[2048,1024]{1,0:T(8,128)(2,1)S(1)} %get-tuple-element.14.held), custom_call_target="tpu_custom_call" | custom-call | flops 67108864 | bytes 4194304 | tf_op jit(solution)/shard_map/pallas_call | solution.py:218
  45.5 3.1 %collective-permute-start.12 = (f32[16,2048]{1,0:T(8,128)S(1)}, f32[16,2048]{1,0:T(8,128)S(1)}, u32[]{:S(2)}, u32[]{:S(2)}) collective-permute-start(f32[16,2048]{1,0:T(8,128)S(1)} %get-tuple-element.17), channel_id=1, source_target_pairs={{0,1},{1,0},{2,3},{3,2},{4,5},{5,4},{6,7},{7,6},{8,9},{9,8},{10,11... | collective-permute-start | bytes 393224 | tf_op jit(solution)/shard_map/ppermute | solution.py:44
  48.6 1.2 shard_map.55
  49.9 2.4 %collective-permute-start.15 = (f32[16,2048]{1,0:T(8,128)S(1)}, f32[16,2048]{1,0:T(8,128)S(1)}, u32[]{:S(2)}, u32[]{:S(2)}) collective-permute-start(f32[16,2048]{1,0:T(8,128)S(1)} %add.91), channel_id=1, source_target_pairs={{0,6},{2,4},{4,2},{6,0},{1,7},{3,5},{5,3},{7,1},{8,14},{10,12},{12... | collective-permute-start | bytes 393224 | tf_op jit(solution)/shard_map/ppermute | solution.py:44
  53.2 4.5 %collective-permute-done.15 = f32[16,2048]{1,0:T(8,128)S(1)} collective-permute-done((f32[16,2048]{1,0:T(8,128)S(1)}, f32[16,2048]{1,0:T(8,128)S(1)}, u32[]{:S(2)}, u32[]{:S(2)}) %collective-permute-start.15) | collective-permute-done | bytes 131104 | tf_op jit(solution)/shard_map/ppermute | solution.py:44
  59.3 1.5 %collective-permute-start.16 = (f32[16,2048]{1,0:T(8,128)S(1)}, f32[16,2048]{1,0:T(8,128)S(1)}, u32[]{:S(2)}, u32[]{:S(2)}) collective-permute-start(f32[16,2048]{1,0:T(8,128)S(1)} %add_add_fusion.1.half), channel_id=1, source_target_pairs={{0,1},{1,0},{2,3},{3,2},{4,5},{5,4},{6,7},{7,6},{8,9},{9,8},{10,11... | collective-permute-start | bytes 393224 | tf_op jit(solution)/shard_map/ppermute | solution.py:44
  60.8 0.9 shard_map.56.before
  61.8 0.9 shard_map.57
  62.7 1.3 %collective-permute-start.19 = (f32[16,1152]{1,0:T(8,128)S(1)}, f32[16,1152]{1,0:T(8,128)S(1)}, u32[]{:S(2)}, u32[]{:S(2)}) collective-permute-start(f32[16,1152]{1,0:T(8,128)S(1)} %shard_map.57), channel_id=1, source_target_pairs={{0,192},{64,128},{128,64},{192,0},{1,193},{65,129},{129,65},{193,1... | collective-permute-start | bytes 221192 | tf_op jit(solution)/shard_map/ppermute | solution.py:44
  64.6 1.4 %collective-permute-start.17 = (f32[16,1152]{1,0:T(8,128)S(1)}, f32[16,1152]{1,0:T(8,128)S(1)}, u32[]{:S(2)}, u32[]{:S(2)}) collective-permute-start(f32[16,1152]{1,0:T(8,128)S(1)} %shard_map.57), channel_id=1, source_target_pairs={{0,64},{64,0},{128,192},{192,128},{1,65},{65,1},{129,193},{193,129... | collective-permute-start | bytes 221192 | tf_op jit(solution)/shard_map/ppermute | solution.py:44
  66.0 1.2 collective-permute-done.19
  67.1 1.6 %collective-permute-done.18 = f32[16,1152]{1,0:T(8,128)S(1)} collective-permute-done((f32[16,1152]{1,0:T(8,128)S(1)}, f32[16,1152]{1,0:T(8,128)S(1)}, u32[]{:S(2)}, u32[]{:S(2)}) %collective-permute-start.18) | collective-permute-done | bytes 73760 | tf_op jit(solution)/shard_map/ppermute | solution.py:44
  69.0 2.2 %collective-permute-start.22 = (f32[16,1152]{1,0:T(8,128)S(1)}, f32[16,1152]{1,0:T(8,128)S(1)}, u32[]{:S(2)}, u32[]{:S(2)}) collective-permute-start(f32[16,1152]{1,0:T(8,128)S(1)} %add_add_fusion.4), channel_id=1, source_target_pairs={{0,24},{8,16},{16,8},{24,0},{32,56},{40,48},{48,40},{56,32},{1,25}... | collective-permute-start | bytes 221192 | tf_op jit(solution)/shard_map/ppermute | solution.py:44
  71.2 1.0 collective-permute-start.21
  72.6 1.6 %collective-permute-done.22 = f32[16,1152]{1,0:T(8,128)S(1)} collective-permute-done((f32[16,1152]{1,0:T(8,128)S(1)}, f32[16,1152]{1,0:T(8,128)S(1)}, u32[]{:S(2)}, u32[]{:S(2)}) %collective-permute-start.22) | collective-permute-done | bytes 73760 | tf_op jit(solution)/shard_map/ppermute | solution.py:44
  74.2 3.3 %collective-permute-done.21 = f32[16,1152]{1,0:T(8,128)S(1)} collective-permute-done((f32[16,1152]{1,0:T(8,128)S(1)}, f32[16,1152]{1,0:T(8,128)S(1)}, u32[]{:S(2)}, u32[]{:S(2)}) %collective-permute-start.21) | collective-permute-done | bytes 73760 | tf_op jit(solution)/shard_map/ppermute | solution.py:44
  77.6 2.5 %collective-permute-start.23 = (f32[16,1152]{1,0:T(8,128)S(1)}, f32[16,1152]{1,0:T(8,128)S(1)}, u32[]{:S(2)}, u32[]{:S(2)}) collective-permute-start(f32[16,1152]{1,0:T(8,128)S(1)} %add_add_fusion.3.mine), channel_id=1, source_target_pairs={{0,48},{8,56},{16,32},{24,40},{32,16},{40,24},{48,0},{56,8},{1,49}... | collective-permute-start | bytes 221192 | tf_op jit(solution)/shard_map/ppermute | solution.py:44
  80.0 3.4 %collective-permute-done.23.theirs = f32[16,1152]{1,0:T(8,128)S(1)} collective-permute-done((f32[16,1152]{1,0:T(8,128)S(1)}, f32[16,1152]{1,0:T(8,128)S(1)}, u32[]{:S(2)}, u32[]{:S(2)}) %collective-permute-start.23) | collective-permute-done | bytes 73760 | tf_op jit(solution)/shard_map/ppermute | solution.py:44
  83.4 1.4 %shard_map.58 = (bf16[16,1024]{1,0:T(8,128)(2,1)S(1)}, f32[16,2048]{1,0:T(8,128)S(1)}) custom-call(f32[16,1152]{1,0:T(8,128)S(1)} %add_add_fusion.3.mine, f32[16,1152]{1,0:T(8,128)S(1)} %collective-permute-done.23.theirs, bf16[2048,1024]{1,0:T(8,128)(2,1)S(1)} %get-tuple-element.14.held), custom_call_target="tpu_custom_call" | custom-call | flops 67108864 | bytes 4194304 | tf_op jit(solution)/shard_map/pallas_call | solution.py:218
  84.8 3.4 %collective-permute-start.24 = (f32[16,2048]{1,0:T(8,128)S(1)}, f32[16,2048]{1,0:T(8,128)S(1)}, u32[]{:S(2)}, u32[]{:S(2)}) collective-permute-start(f32[16,2048]{1,0:T(8,128)S(1)} %get-tuple-element.19), channel_id=1, source_target_pairs={{0,1},{1,0},{2,3},{3,2},{4,5},{5,4},{6,7},{7,6},{8,9},{9,8},{10,11... | collective-permute-start | bytes 393224 | tf_op jit(solution)/shard_map/ppermute | solution.py:44
  88.2 1.2 shard_map.59
  89.4 2.3 %collective-permute-start.27 = (f32[16,2048]{1,0:T(8,128)S(1)}, f32[16,2048]{1,0:T(8,128)S(1)}, u32[]{:S(2)}, u32[]{:S(2)}) collective-permute-start(f32[16,2048]{1,0:T(8,128)S(1)} %add.101), channel_id=1, source_target_pairs={{0,6},{2,4},{4,2},{6,0},{1,7},{3,5},{5,3},{7,1},{8,14},{10,12},{12... | collective-permute-start | bytes 393224 | tf_op jit(solution)/shard_map/ppermute | solution.py:44
  92.8 4.4 %collective-permute-done.27 = f32[16,2048]{1,0:T(8,128)S(1)} collective-permute-done((f32[16,2048]{1,0:T(8,128)S(1)}, f32[16,2048]{1,0:T(8,128)S(1)}, u32[]{:S(2)}, u32[]{:S(2)}) %collective-permute-start.27) | collective-permute-done | bytes 131104 | tf_op jit(solution)/shard_map/ppermute | solution.py:44
  97.1 0.8 collective-permute-done.26
  97.9 0.9 collective-permute-done.25
  99.2 4.6 %collective-permute-start.30 = (f32[8,128]{1,0:T(8,128)S(1)}, f32[8,128]{1,0:T(8,128)S(1)}, u32[]{:S(2)}, u32[]{:S(2)}) collective-permute-start(f32[8,128]{1,0:T(8,128)S(1)} %shard_map.60), channel_id=1, source_target_pairs={{0,49},{1,48},{8,57},{9,56},{16,33},{17,32},{24,41},{25,40},{32,17... | collective-permute-start | bytes 12296 | tf_op jit(solution)/shard_map/ppermute | solution.py:44
  104.2 1.0 collective-permute-done.30
  105.2 3.1 %collective-permute-done.29 = f32[8,128]{1,0:T(8,128)S(1)} collective-permute-done((f32[8,128]{1,0:T(8,128)S(1)}, f32[8,128]{1,0:T(8,128)S(1)}, u32[]{:S(2)}, u32[]{:S(2)}) %collective-permute-start.29) | collective-permute-done | bytes 4128 | tf_op jit(solution)/shard_map/ppermute | solution.py:44
  108.3 11.9 %all_to_all.5.grams = f32[16,8,128]{2,1,0:T(8,128)S(1)} all-to-all(f32[16,8,128]{2,1,0:T(8,128)S(1)} %broadcast_in_dim.2), channel_id=1, replica_groups=mesh['x'=4,'cube'=2,'level'=4,'y'=4,'core'=2] {'x','level'}, dimensions={0} | all-to-all | bytes 131072 | tf_op jit(solution)/shard_map/all_to_all | solution.py:306
  120.3 1.0 shard_map.61
  (39 shorter events, 8.1 us)
Async XLA Ops:
  3.5 6.2 %collective-permute-start = (f32[16,2048]{1,0:T(8,128)S(1)}, f32[16,2048]{1,0:T(8,128)S(1)}, u32[]{:S(2)}, u32[]{:S(2)}) collective-permute-start(f32[16,2048]{1,0:T(8,128)S(1)} %get-tuple-element.13), channel_id=1, source_target_pairs={{0,1},{1,0},{2,3},{3,2},{4,5},{5,4},{6,7},{7,6},{8,9},{9,8},{10,11... | collective-permute-start | bytes 393224 | tf_op jit(solution)/shard_map/ppermute | solution.py:44
  9.7 9.2 %collective-permute-start.3 = (f32[16,2048]{1,0:T(8,128)S(1)}, f32[16,2048]{1,0:T(8,128)S(1)}, u32[]{:S(2)}, u32[]{:S(2)}) collective-permute-start(f32[16,2048]{1,0:T(8,128)S(1)} %add.81), channel_id=1, source_target_pairs={{0,6},{2,4},{4,2},{6,0},{1,7},{3,5},{5,3},{7,1},{8,14},{10,12},{12... | collective-permute-start | bytes 393224 | tf_op jit(solution)/shard_map/ppermute | solution.py:44
  10.8 8.1 %collective-permute-start.2 = (f32[16,2048]{1,0:T(8,128)S(1)}, f32[16,2048]{1,0:T(8,128)S(1)}, u32[]{:S(2)}, u32[]{:S(2)}) collective-permute-start(f32[16,2048]{1,0:T(8,128)S(1)} %add.81), channel_id=1, source_target_pairs={{0,4},{2,6},{4,0},{6,2},{1,5},{3,7},{5,1},{7,3},{8,12},{10,14},{12... | collective-permute-start | bytes 393224 | tf_op jit(solution)/shard_map/ppermute | solution.py:44
  11.1 8.1 %collective-permute-start.1 = (f32[16,2048]{1,0:T(8,128)S(1)}, f32[16,2048]{1,0:T(8,128)S(1)}, u32[]{:S(2)}, u32[]{:S(2)}) collective-permute-start(f32[16,2048]{1,0:T(8,128)S(1)} %add.81), channel_id=1, source_target_pairs={{0,2},{2,0},{4,6},{6,4},{1,3},{3,1},{5,7},{7,5},{8,10},{10,8},{12,... | collective-permute-start | bytes 393224 | tf_op jit(solution)/shard_map/ppermute | solution.py:44
  19.2 2.2 %collective-permute-start.4 = (f32[16,2048]{1,0:T(8,128)S(1)}, f32[16,2048]{1,0:T(8,128)S(1)}, u32[]{:S(2)}, u32[]{:S(2)}) collective-permute-start(f32[16,2048]{1,0:T(8,128)S(1)} %add_add_fusion.2.half), channel_id=1, source_target_pairs={{0,1},{1,0},{2,3},{3,2},{4,5},{5,4},{6,7},{7,6},{8,9},{9,8},{10,11... | collective-permute-start | bytes 393224 | tf_op jit(solution)/shard_map/ppermute | solution.py:44
  22.4 4.4 %collective-permute-start.7 = (f32[16,1152]{1,0:T(8,128)S(1)}, f32[16,1152]{1,0:T(8,128)S(1)}, u32[]{:S(2)}, u32[]{:S(2)}) collective-permute-start(f32[16,1152]{1,0:T(8,128)S(1)} %shard_map.53), channel_id=1, source_target_pairs={{0,192},{64,128},{128,64},{192,0},{1,193},{65,129},{129,65},{193,1... | collective-permute-start | bytes 221192 | tf_op jit(solution)/shard_map/ppermute | solution.py:44
  23.5 4.8 %collective-permute-start.6 = (f32[16,1152]{1,0:T(8,128)S(1)}, f32[16,1152]{1,0:T(8,128)S(1)}, u32[]{:S(2)}, u32[]{:S(2)}) collective-permute-start(f32[16,1152]{1,0:T(8,128)S(1)} %shard_map.53), channel_id=1, source_target_pairs={{0,128},{64,192},{128,0},{192,64},{1,129},{65,193},{129,1},{193,65... | collective-permute-start | bytes 221192 | tf_op jit(solution)/shard_map/ppermute | solution.py:44
  24.0 5.0 %collective-permute-start.5 = (f32[16,1152]{1,0:T(8,128)S(1)}, f32[16,1152]{1,0:T(8,128)S(1)}, u32[]{:S(2)}, u32[]{:S(2)}) collective-permute-start(f32[16,1152]{1,0:T(8,128)S(1)} %shard_map.53), channel_id=1, source_target_pairs={{0,64},{64,0},{128,192},{192,128},{1,65},{65,1},{129,193},{193,129... | collective-permute-start | bytes 221192 | tf_op jit(solution)/shard_map/ppermute | solution.py:44
  29.0 5.4 %collective-permute-start.10 = (f32[16,1152]{1,0:T(8,128)S(1)}, f32[16,1152]{1,0:T(8,128)S(1)}, u32[]{:S(2)}, u32[]{:S(2)}) collective-permute-start(f32[16,1152]{1,0:T(8,128)S(1)} %add_add_fusion.6), channel_id=1, source_target_pairs={{0,24},{8,16},{16,8},{24,0},{32,56},{40,48},{48,40},{56,32},{1,25}... | collective-permute-start | bytes 221192 | tf_op jit(solution)/shard_map/ppermute | solution.py:44
  32.7 5.4 %collective-permute-start.9 = (f32[16,1152]{1,0:T(8,128)S(1)}, f32[16,1152]{1,0:T(8,128)S(1)}, u32[]{:S(2)}, u32[]{:S(2)}) collective-permute-start(f32[16,1152]{1,0:T(8,128)S(1)} %add_add_fusion.6), channel_id=1, source_target_pairs={{0,16},{8,24},{16,0},{24,8},{32,48},{40,56},{48,32},{56,40},{1,17}... | collective-permute-start | bytes 221192 | tf_op jit(solution)/shard_map/ppermute | solution.py:44
  32.7 5.4 %collective-permute-start.8 = (f32[16,1152]{1,0:T(8,128)S(1)}, f32[16,1152]{1,0:T(8,128)S(1)}, u32[]{:S(2)}, u32[]{:S(2)}) collective-permute-start(f32[16,1152]{1,0:T(8,128)S(1)} %add_add_fusion.6), channel_id=1, source_target_pairs={{0,8},{8,0},{16,24},{24,16},{32,40},{40,32},{48,56},{56,48},{1,9},... | collective-permute-start | bytes 221192 | tf_op jit(solution)/shard_map/ppermute | solution.py:44
  38.0 6.1 %collective-permute-start.11 = (f32[16,1152]{1,0:T(8,128)S(1)}, f32[16,1152]{1,0:T(8,128)S(1)}, u32[]{:S(2)}, u32[]{:S(2)}) collective-permute-start(f32[16,1152]{1,0:T(8,128)S(1)} %add_add_fusion.5.mine), channel_id=1, source_target_pairs={{0,48},{8,56},{16,32},{24,40},{32,16},{40,24},{48,0},{56,8},{1,49}... | collective-permute-start | bytes 221192 | tf_op jit(solution)/shard_map/ppermute | solution.py:44
  45.5 4.3 %collective-permute-start.12 = (f32[16,2048]{1,0:T(8,128)S(1)}, f32[16,2048]{1,0:T(8,128)S(1)}, u32[]{:S(2)}, u32[]{:S(2)}) collective-permute-start(f32[16,2048]{1,0:T(8,128)S(1)} %get-tuple-element.17), channel_id=1, source_target_pairs={{0,1},{1,0},{2,3},{3,2},{4,5},{5,4},{6,7},{7,6},{8,9},{9,8},{10,11... | collective-permute-start | bytes 393224 | tf_op jit(solution)/shard_map/ppermute | solution.py:44
  49.9 7.9 %collective-permute-start.15 = (f32[16,2048]{1,0:T(8,128)S(1)}, f32[16,2048]{1,0:T(8,128)S(1)}, u32[]{:S(2)}, u32[]{:S(2)}) collective-permute-start(f32[16,2048]{1,0:T(8,128)S(1)} %add.91), channel_id=1, source_target_pairs={{0,6},{2,4},{4,2},{6,0},{1,7},{3,5},{5,3},{7,1},{8,14},{10,12},{12... | collective-permute-start | bytes 393224 | tf_op jit(solution)/shard_map/ppermute | solution.py:44
  52.3 6.2 %collective-permute-start.14 = (f32[16,2048]{1,0:T(8,128)S(1)}, f32[16,2048]{1,0:T(8,128)S(1)}, u32[]{:S(2)}, u32[]{:S(2)}) collective-permute-start(f32[16,2048]{1,0:T(8,128)S(1)} %add.91), channel_id=1, source_target_pairs={{0,4},{2,6},{4,0},{6,2},{1,5},{3,7},{5,1},{7,3},{8,12},{10,14},{12... | collective-permute-start | bytes 393224 | tf_op jit(solution)/shard_map/ppermute | solution.py:44
  52.7 6.5 %collective-permute-start.13 = (f32[16,2048]{1,0:T(8,128)S(1)}, f32[16,2048]{1,0:T(8,128)S(1)}, u32[]{:S(2)}, u32[]{:S(2)}) collective-permute-start(f32[16,2048]{1,0:T(8,128)S(1)} %add.91), channel_id=1, source_target_pairs={{0,2},{2,0},{4,6},{6,4},{1,3},{3,1},{5,7},{7,5},{8,10},{10,8},{12,... | collective-permute-start | bytes 393224 | tf_op jit(solution)/shard_map/ppermute | solution.py:44
  59.3 2.5 %collective-permute-start.16 = (f32[16,2048]{1,0:T(8,128)S(1)}, f32[16,2048]{1,0:T(8,128)S(1)}, u32[]{:S(2)}, u32[]{:S(2)}) collective-permute-start(f32[16,2048]{1,0:T(8,128)S(1)} %add_add_fusion.1.half), channel_id=1, source_target_pairs={{0,1},{1,0},{2,3},{3,2},{4,5},{5,4},{6,7},{7,6},{8,9},{9,8},{10,11... | collective-permute-start | bytes 393224 | tf_op jit(solution)/shard_map/ppermute | solution.py:44
  62.7 4.4 %collective-permute-start.19 = (f32[16,1152]{1,0:T(8,128)S(1)}, f32[16,1152]{1,0:T(8,128)S(1)}, u32[]{:S(2)}, u32[]{:S(2)}) collective-permute-start(f32[16,1152]{1,0:T(8,128)S(1)} %shard_map.57), channel_id=1, source_target_pairs={{0,192},{64,128},{128,64},{192,0},{1,193},{65,129},{129,65},{193,1... | collective-permute-start | bytes 221192 | tf_op jit(solution)/shard_map/ppermute | solution.py:44
  64.0 4.7 %collective-permute-start.18 = (f32[16,1152]{1,0:T(8,128)S(1)}, f32[16,1152]{1,0:T(8,128)S(1)}, u32[]{:S(2)}, u32[]{:S(2)}) collective-permute-start(f32[16,1152]{1,0:T(8,128)S(1)} %shard_map.57), channel_id=1, source_target_pairs={{0,128},{64,192},{128,0},{192,64},{1,129},{65,193},{129,1},{193,65... | collective-permute-start | bytes 221192 | tf_op jit(solution)/shard_map/ppermute | solution.py:44
  64.6 4.4 %collective-permute-start.17 = (f32[16,1152]{1,0:T(8,128)S(1)}, f32[16,1152]{1,0:T(8,128)S(1)}, u32[]{:S(2)}, u32[]{:S(2)}) collective-permute-start(f32[16,1152]{1,0:T(8,128)S(1)} %shard_map.57), channel_id=1, source_target_pairs={{0,64},{64,0},{128,192},{192,128},{1,65},{65,1},{129,193},{193,129... | collective-permute-start | bytes 221192 | tf_op jit(solution)/shard_map/ppermute | solution.py:44
  69.0 5.2 %collective-permute-start.22 = (f32[16,1152]{1,0:T(8,128)S(1)}, f32[16,1152]{1,0:T(8,128)S(1)}, u32[]{:S(2)}, u32[]{:S(2)}) collective-permute-start(f32[16,1152]{1,0:T(8,128)S(1)} %add_add_fusion.4), channel_id=1, source_target_pairs={{0,24},{8,16},{16,8},{24,0},{32,56},{40,48},{48,40},{56,32},{1,25}... | collective-permute-start | bytes 221192 | tf_op jit(solution)/shard_map/ppermute | solution.py:44
  71.2 6.3 %collective-permute-start.21 = (f32[16,1152]{1,0:T(8,128)S(1)}, f32[16,1152]{1,0:T(8,128)S(1)}, u32[]{:S(2)}, u32[]{:S(2)}) collective-permute-start(f32[16,1152]{1,0:T(8,128)S(1)} %add_add_fusion.4), channel_id=1, source_target_pairs={{0,16},{8,24},{16,0},{24,8},{32,48},{40,56},{48,32},{56,40},{1,17}... | collective-permute-start | bytes 221192 | tf_op jit(solution)/shard_map/ppermute | solution.py:44
  72.2 5.4 %collective-permute-start.20 = (f32[16,1152]{1,0:T(8,128)S(1)}, f32[16,1152]{1,0:T(8,128)S(1)}, u32[]{:S(2)}, u32[]{:S(2)}) collective-permute-start(f32[16,1152]{1,0:T(8,128)S(1)} %add_add_fusion.4), channel_id=1, source_target_pairs={{0,8},{8,0},{16,24},{24,16},{32,40},{40,32},{48,56},{56,48},{1,9},... | collective-permute-start | bytes 221192 | tf_op jit(solution)/shard_map/ppermute | solution.py:44
  77.6 5.8 %collective-permute-start.23 = (f32[16,1152]{1,0:T(8,128)S(1)}, f32[16,1152]{1,0:T(8,128)S(1)}, u32[]{:S(2)}, u32[]{:S(2)}) collective-permute-start(f32[16,1152]{1,0:T(8,128)S(1)} %add_add_fusion.3.mine), channel_id=1, source_target_pairs={{0,48},{8,56},{16,32},{24,40},{32,16},{40,24},{48,0},{56,8},{1,49}... | collective-permute-start | bytes 221192 | tf_op jit(solution)/shard_map/ppermute | solution.py:44
  84.8 4.6 %collective-permute-start.24 = (f32[16,2048]{1,0:T(8,128)S(1)}, f32[16,2048]{1,0:T(8,128)S(1)}, u32[]{:S(2)}, u32[]{:S(2)}) collective-permute-start(f32[16,2048]{1,0:T(8,128)S(1)} %get-tuple-element.19), channel_id=1, source_target_pairs={{0,1},{1,0},{2,3},{3,2},{4,5},{5,4},{6,7},{7,6},{8,9},{9,8},{10,11... | collective-permute-start | bytes 393224 | tf_op jit(solution)/shard_map/ppermute | solution.py:44
  89.4 7.7 %collective-permute-start.27 = (f32[16,2048]{1,0:T(8,128)S(1)}, f32[16,2048]{1,0:T(8,128)S(1)}, u32[]{:S(2)}, u32[]{:S(2)}) collective-permute-start(f32[16,2048]{1,0:T(8,128)S(1)} %add.101), channel_id=1, source_target_pairs={{0,6},{2,4},{4,2},{6,0},{1,7},{3,5},{5,3},{7,1},{8,14},{10,12},{12... | collective-permute-start | bytes 393224 | tf_op jit(solution)/shard_map/ppermute | solution.py:44
  91.7 6.2 %collective-permute-start.26 = (f32[16,2048]{1,0:T(8,128)S(1)}, f32[16,2048]{1,0:T(8,128)S(1)}, u32[]{:S(2)}, u32[]{:S(2)}) collective-permute-start(f32[16,2048]{1,0:T(8,128)S(1)} %add.101), channel_id=1, source_target_pairs={{0,4},{2,6},{4,0},{6,2},{1,5},{3,7},{5,1},{7,3},{8,12},{10,14},{12... | collective-permute-start | bytes 393224 | tf_op jit(solution)/shard_map/ppermute | solution.py:44
  92.1 6.7 %collective-permute-start.25 = (f32[16,2048]{1,0:T(8,128)S(1)}, f32[16,2048]{1,0:T(8,128)S(1)}, u32[]{:S(2)}, u32[]{:S(2)}) collective-permute-start(f32[16,2048]{1,0:T(8,128)S(1)} %add.101), channel_id=1, source_target_pairs={{0,2},{2,0},{4,6},{6,4},{1,3},{3,1},{5,7},{7,5},{8,10},{10,8},{12,... | collective-permute-start | bytes 393224 | tf_op jit(solution)/shard_map/ppermute | solution.py:44
  99.2 6.0 %collective-permute-start.30 = (f32[8,128]{1,0:T(8,128)S(1)}, f32[8,128]{1,0:T(8,128)S(1)}, u32[]{:S(2)}, u32[]{:S(2)}) collective-permute-start(f32[8,128]{1,0:T(8,128)S(1)} %shard_map.60), channel_id=1, source_target_pairs={{0,49},{1,48},{8,57},{9,56},{16,33},{17,32},{24,41},{25,40},{32,17... | collective-permute-start | bytes 12296 | tf_op jit(solution)/shard_map/ppermute | solution.py:44
  103.7 4.6 %collective-permute-start.29 = (f32[8,128]{1,0:T(8,128)S(1)}, f32[8,128]{1,0:T(8,128)S(1)}, u32[]{:S(2)}, u32[]{:S(2)}) collective-permute-start(f32[8,128]{1,0:T(8,128)S(1)} %shard_map.60), channel_id=1, source_target_pairs={{0,48},{1,49},{8,56},{9,57},{16,32},{17,33},{24,40},{25,41},{32,16... | collective-permute-start | bytes 12296 | tf_op jit(solution)/shard_map/ppermute | solution.py:44
  103.9 4.4 %collective-permute-start.28 = (f32[8,128]{1,0:T(8,128)S(1)}, f32[8,128]{1,0:T(8,128)S(1)}, u32[]{:S(2)}, u32[]{:S(2)}) collective-permute-start(f32[8,128]{1,0:T(8,128)S(1)} %shard_map.60), channel_id=1, source_target_pairs={{0,1},{1,0},{8,9},{9,8},{16,17},{17,16},{24,25},{25,24},{32,33},{3... | collective-permute-start | bytes 12296 | tf_op jit(solution)/shard_map/ppermute | solution.py:44

commit v8 on v7

--- a/solution.py
+++ b/solution.py
@@ -122,15 +122,30 @@
 
 
 def first_kernel(
-    seed_values, sku_ids, affinity, left, held, other, seeds_here, ids_here, arrived, *, columns
+    seed_values,
+    sku_ids,
+    affinity,
+    left,
+    held_other,
+    held_own,
+    other,
+    seeds_here,
+    ids_here,
+    small_arrived,
+    other_arrived,
+    own_arrived,
+    *,
+    columns,
 ):
+    core = lax.axis_index("core")
     small = [
-        pltpu.make_async_copy(seed_values, seeds_here, arrived.at[4]),
-        pltpu.make_async_copy(sku_ids, ids_here, arrived.at[5]),
+        pltpu.make_async_copy(seed_values, seeds_here, small_arrived.at[0]),
+        pltpu.make_async_copy(sku_ids, ids_here, small_arrived.at[1]),
     ]
     for copy in small:
         copy.start()
-    copies = load_half(affinity, held, arrived, 1 - lax.axis_index("core"))
+    copies = load_half(affinity, held_other, other_arrived, 1 - core)
+    later = load_half(affinity, held_own, own_arrived, core)
     for copy in small:
         copy.wait()
     row = lax.broadcasted_iota(jnp.int32, (K, 128), 0)
@@ -140,18 +155,16 @@
     for start in range(0, ids_here.shape[1], 128):
         ids = jnp.broadcast_to(ids_here[:, start : start + 128], (K, 128))
         left[:, start : start + 128] = test_matrix(seeds, ids, columns)
-    project_half(left, held, other, None, copies)
-
-
-def first_own_kernel(left, affinity, held, own, arrived):
-    copies = load_half(affinity, held, arrived, lax.axis_index("core"))
-    project_half(left, held, own, None, copies)
+    project_half(left, held_other, other, None, copies)
+    for copy in later:
+        copy.wait()
 
 
 def solve_kernel(mine, theirs, held, left, other, *, scale):
-    wide = held.shape[1]
     total = mine[...] + theirs[...]
-    _, back = eliminate(total[:, wide:], total[:, :wide])
+    tiles = held.shape[1] // 128
+    back = jnp.concatenate([total[tile * K : (tile + 1) * K] for tile in range(tiles)], axis=1)
+    _, back = eliminate(unpack_gram(total[tiles * K :]), back)
     left[...] = back.astype(jnp.bfloat16)
     project_half(left, held, other, scale)
 
@@ -174,30 +187,33 @@
     return both[:K] + both[K:], fold_gram(gram)
 
 
+def pack_gram(gram):
+    blank = jnp.zeros((8, 128 - 2 * K), jnp.float32)
+    return jnp.concatenate([gram[:8], gram[8:], blank], axis=1)
+
+
+def unpack_gram(packed):
+    return jnp.concatenate([packed[:, :K], packed[:, K : 2 * K]], axis=0)
+
+
 def back_own_kernel(half, held, packed):
-    wide = held.shape[1]
     back, gram = back_sums(half, held)
-    packed[:, :wide] = back
-    packed[:, wide:] = jnp.zeros((K, 128), jnp.float32)
-    packed[:, wide : wide + K] = gram
+    tiles = held.shape[1] // 128
+    for tile in range(tiles):
+        packed[tile * K : (tile + 1) * K, :] = back[:, tile * 128 : (tile + 1) * 128]
+    packed[tiles * K :, :] = pack_gram(gram)
 
 
 def back_other_kernel(half, held, before, packed):
-    wide = held.shape[1]
-    back, gram = back_sums(half, held)
-    packed[:, :wide] = before[:, :wide] + back
-    packed[:, wide:] = jnp.zeros((K, 128), jnp.float32)
-    packed[:, wide : wide + K] = before[:, wide : wide + K] + gram
+    back_own_kernel(half, held, packed)
+    packed[...] = before[...] + packed[...]
 
 
 def gram_kernel(half, packed):
     gram = jnp.zeros((3 * K, 3 * K), jnp.float32)
     for step in range(4):
         gram += triple_gram(split_bf16(half[:, span(step)]))
-    gram = fold_gram(gram)
-    packed[...] = jnp.zeros_like(packed)
-    packed[:, :K] = gram[:8]
-    packed[:, K : 2 * K] = gram[8:]
+    packed[...] = pack_gram(fold_gram(gram))
 
 
 def last_kernel(grams, half, basis, factor, *, scale):
@@ -206,7 +222,7 @@
         one, two, three, four = (grams[4 * x + k] for k in range(4))
         part = (one + three) + (two + four)
         total = part if total is None else total + part
-    gram = jnp.concatenate([total[:, :K], total[:, K : 2 * K]], axis=0)
+    gram = unpack_gram(total)
     place = pl.multiple_of(lax.axis_index("y") * PIECE, PIECE)
     lower, ortho = eliminate(gram, half[:, pl.ds(place, PIECE)])
     basis[...] = ortho * scale
@@ -235,21 +251,20 @@
     f32 = jnp.float32
     half_out = ((K, local_rows // 2), f32)
     left_out = ((K, local_columns), jnp.bfloat16)
-    packed_out = ((K, local_columns + 128), f32)
+    packed_out = ((local_columns // 128 * K + 8, 128), f32)
     pass_flops = K * local_rows * local_columns
     z = ("cube", "level")
 
     held_out = ((local_rows // 2, local_columns), jnp.bfloat16)
     far = pl.BlockSpec(memory_space=pltpu.HBM)
-    near = pl.BlockSpec(memory_space=pltpu.VMEM)
     affinity, seed_values, sku_ids = (
         pltpu.with_memory_space_constraint(value, pltpu.HBM)
         for value in (affinity, seed_values, sku_ids.reshape(1, -1))
     )
 
-    left, held_other, other = call(
+    left, held_other, held_own, other = call(
         functools.partial(first_kernel, columns=total_columns),
-        [left_out, held_out, half_out],
+        [left_out, held_out, held_out, half_out],
         seed_values,
         sku_ids,
         affinity,
@@ -257,31 +272,23 @@
         scratch=[
             pltpu.SMEM(seed_values.shape, jnp.int32),
             pltpu.VMEM(sku_ids.shape, jnp.int32),
-            pltpu.SemaphoreType.DMA((6,)),
+            pltpu.SemaphoreType.DMA((2,)),
+            pltpu.SemaphoreType.DMA((4,)),
+            pltpu.SemaphoreType.DMA((4,)),
         ],
         flops=pass_flops,
     )
     scale = 1.0 / math.sqrt(total_columns)
     for repeat in range(ITERS + 1):
         arriving = swap(other, "core", 2, 1)
-        if repeat == 0:
-            held_own, own = call(
-                first_own_kernel,
-                [held_out, half_out],
-                left,
-                affinity,
-                spaces=[near, far],
-                scratch=[pltpu.SemaphoreType.DMA((4,))],
-                flops=pass_flops,
-            )
-        else:
-            (own,) = call(
-                functools.partial(own_kernel, scale=scale),
-                [half_out],
-                left,
-                held_own,
-                flops=pass_flops,
-            )
+        own_scale = None if repeat == 0 else scale
+        (own,) = call(
+            functools.partial(own_kernel, scale=own_scale),
+            [half_out],
+            left,
+            held_own,
+            flops=pass_flops,
+        )
         half = sum_four(own + arriving, "y", 4)
         if repeat < ITERS:
             sibling = swap(half, "core", 2, 1)

time: 121 us -> 120 us (level)
  starting transfers between devices: 47.1 us -> 49.8 us
  waiting for transfers between devices: 45.4 us -> 42.8 us
    ppermute x31, starting transfers between devices: 47.1 us -> 49.8 us  [swap(): return lax.ppermute(value, axis, [(i, i ^ offset) for i in range(count)])]
    ppermute x31, waiting for transfers between devices: 45.4 us -> 42.8 us  [swap(): return lax.ppermute(value, axis, [(i, i ^ offset) for i in range(count)])]
  transfers between devices with their start and end apart: 31 -> 31, of which waited for: 24 -> 24; matrix products, arithmetic and copies ran while one was open for 0% -> 0% of each run, Pallas kernels for 6% -> 5%
where the time goes in v8:
time: 120 us
  starting transfers between devices  49.8 us (42%)
  waiting for transfers between devices  42.8 us (36%)
  Pallas kernels  15.9 us (13%)
  blocking collectives  10.9 us (9%)
    ppermute x31, starting transfers between devices, swap(): return lax.ppermute(value, axis, [(i, i ^ offset) for i in range(count)])  49.8 us
    ppermute x31, waiting for transfers between devices, swap(): return lax.ppermute(value, axis, [(i, i ^ offset) for i in range(count)])  42.8 us
    pallas_call x12, Pallas kernels, call(): pl.pallas_call(kernel, in_specs=spaces or [whole] * len(args), out_specs=...  15.9 us
    all_to_all x1, blocking collectives, body(): grams = lax.all_to_all(spread, ('x', 'level'), 0, 0)  10.9 us
  transfers between devices with their start and end apart: 31, of which 24 were waited for; matrix products, arithmetic and copies ran while one was open for 0% of the time, Pallas kernels for 5%

profile of v8, /device:TPU:1, one launch (start us, length us, event | category | flops | bytes accessed | tf_op | source)
XLA Modules:
  0.0 120.4 jit_solution(3596337975487071872)
XLA Ops:
  0.6 4.6 %shard_map.50 = (bf16[16,1024]{1,0:T(8,128)(2,1)S(1)}, bf16[2048,1024]{1,0:T(8,128)(2,1)S(1)}, bf16[2048,1024]{1,0:T(8,128)(2,1)S(1)}, f32[16,2048]{1,0:T(8,128)S(1)}) custom-call(s32[16]{0:T(128)} %seed_values.1, s32[1,1024]{1,0:T(1,128)} %bitcast.1, bf16[4096,1024]{1,0:T(8,128)(2,1)} %affinity.1), custom_call_target="tpu_custom_call" | custom-call | flops 67108864 | bytes 4194304 | tf_op jit(solution)/shard_map/pallas_call | solution.py:234
  5.2 3.3 %collective-permute-start = (f32[16,2048]{1,0:T(8,128)S(1)}, f32[16,2048]{1,0:T(8,128)S(1)}, u32[]{:S(2)}, u32[]{:S(2)}) collective-permute-start(f32[16,2048]{1,0:T(8,128)S(1)} %get-tuple-element.12), channel_id=1, source_target_pairs={{0,1},{1,0},{2,3},{3,2},{4,5},{5,4},{6,7},{7,6},{8,9},{9,8},{10,11... | collective-permute-start | bytes 393224 | tf_op jit(solution)/shard_map/ppermute | solution.py:44
  8.5 1.2 shard_map.51
  9.7 1.1 collective-permute-start.3
  11.2 1.9 %collective-permute-start.1 = (f32[16,2048]{1,0:T(8,128)S(1)}, f32[16,2048]{1,0:T(8,128)S(1)}, u32[]{:S(2)}, u32[]{:S(2)}) collective-permute-start(f32[16,2048]{1,0:T(8,128)S(1)} %add.81), channel_id=1, source_target_pairs={{0,2},{2,0},{4,6},{6,4},{1,3},{3,1},{5,7},{7,5},{8,10},{10,8},{12,... | collective-permute-start | bytes 393224 | tf_op jit(solution)/shard_map/ppermute | solution.py:44
  13.1 5.7 %collective-permute-done.3 = f32[16,2048]{1,0:T(8,128)S(1)} collective-permute-done((f32[16,2048]{1,0:T(8,128)S(1)}, f32[16,2048]{1,0:T(8,128)S(1)}, u32[]{:S(2)}, u32[]{:S(2)}) %collective-permute-start.3) | collective-permute-done | bytes 131104 | tf_op jit(solution)/shard_map/ppermute | solution.py:44
  19.1 1.4 %collective-permute-start.4 = (f32[16,2048]{1,0:T(8,128)S(1)}, f32[16,2048]{1,0:T(8,128)S(1)}, u32[]{:S(2)}, u32[]{:S(2)}) collective-permute-start(f32[16,2048]{1,0:T(8,128)S(1)} %add_add_fusion.2.half), channel_id=1, source_target_pairs={{0,1},{1,0},{2,3},{3,2},{4,5},{5,4},{6,7},{7,6},{8,9},{9,8},{10,11... | collective-permute-start | bytes 393224 | tf_op jit(solution)/shard_map/ppermute | solution.py:44
  20.5 0.9 shard_map.52.before
  21.5 0.9 shard_map.53
  22.4 1.2 %collective-permute-start.7 = (f32[136,128]{1,0:T(8,128)S(1)}, f32[136,128]{1,0:T(8,128)S(1)}, u32[]{:S(2)}, u32[]{:S(2)}) collective-permute-start(f32[136,128]{1,0:T(8,128)S(1)} %shard_map.53), channel_id=1, source_target_pairs={{0,192},{64,128},{128,64},{192,0},{1,193},{65,129},{129,65},{193,1... | collective-permute-start | bytes 208904 | tf_op jit(solution)/shard_map/ppermute | solution.py:44
  24.2 1.5 %collective-permute-start.5 = (f32[136,128]{1,0:T(8,128)S(1)}, f32[136,128]{1,0:T(8,128)S(1)}, u32[]{:S(2)}, u32[]{:S(2)}) collective-permute-start(f32[136,128]{1,0:T(8,128)S(1)} %shard_map.53), channel_id=1, source_target_pairs={{0,64},{64,0},{128,192},{192,128},{1,65},{65,1},{129,193},{193,129... | collective-permute-start | bytes 208904 | tf_op jit(solution)/shard_map/ppermute | solution.py:44
  25.7 1.1 collective-permute-done.7
  26.8 1.6 %collective-permute-done.6 = f32[136,128]{1,0:T(8,128)S(1)} collective-permute-done((f32[136,128]{1,0:T(8,128)S(1)}, f32[136,128]{1,0:T(8,128)S(1)}, u32[]{:S(2)}, u32[]{:S(2)}) %collective-permute-start.6) | collective-permute-done | bytes 69664 | tf_op jit(solution)/shard_map/ppermute | solution.py:44
  28.6 4.2 %collective-permute-start.10 = (f32[136,128]{1,0:T(8,128)S(1)}, f32[136,128]{1,0:T(8,128)S(1)}, u32[]{:S(2)}, u32[]{:S(2)}) collective-permute-start(f32[136,128]{1,0:T(8,128)S(1)} %add_add_fusion.6), channel_id=1, source_target_pairs={{0,24},{8,16},{16,8},{24,0},{32,56},{40,48},{48,40},{56,32},{1,25}... | collective-permute-start | bytes 208904 | tf_op jit(solution)/shard_map/ppermute | solution.py:44
  33.2 1.3 %collective-permute-done.10 = f32[136,128]{1,0:T(8,128)S(1)} collective-permute-done((f32[136,128]{1,0:T(8,128)S(1)}, f32[136,128]{1,0:T(8,128)S(1)}, u32[]{:S(2)}, u32[]{:S(2)}) %collective-permute-start.10) | collective-permute-done | bytes 69664 | tf_op jit(solution)/shard_map/ppermute | solution.py:44
  34.5 3.3 %collective-permute-done.9 = f32[136,128]{1,0:T(8,128)S(1)} collective-permute-done((f32[136,128]{1,0:T(8,128)S(1)}, f32[136,128]{1,0:T(8,128)S(1)}, u32[]{:S(2)}, u32[]{:S(2)}) %collective-permute-start.9) | collective-permute-done | bytes 69664 | tf_op jit(solution)/shard_map/ppermute | solution.py:44
  37.8 3.1 %collective-permute-start.11 = (f32[136,128]{1,0:T(8,128)S(1)}, f32[136,128]{1,0:T(8,128)S(1)}, u32[]{:S(2)}, u32[]{:S(2)}) collective-permute-start(f32[136,128]{1,0:T(8,128)S(1)} %add_add_fusion.5.mine), channel_id=1, source_target_pairs={{0,48},{8,56},{16,32},{24,40},{32,16},{40,24},{48,0},{56,8},{1,49}... | collective-permute-start | bytes 208904 | tf_op jit(solution)/shard_map/ppermute | solution.py:44
  40.9 3.0 %collective-permute-done.11.theirs = f32[136,128]{1,0:T(8,128)S(1)} collective-permute-done((f32[136,128]{1,0:T(8,128)S(1)}, f32[136,128]{1,0:T(8,128)S(1)}, u32[]{:S(2)}, u32[]{:S(2)}) %collective-permute-start.11) | collective-permute-done | bytes 69664 | tf_op jit(solution)/shard_map/ppermute | solution.py:44
  43.9 1.4 %shard_map.54 = (bf16[16,1024]{1,0:T(8,128)(2,1)S(1)}, f32[16,2048]{1,0:T(8,128)S(1)}) custom-call(f32[136,128]{1,0:T(8,128)S(1)} %add_add_fusion.5.mine, f32[136,128]{1,0:T(8,128)S(1)} %collective-permute-done.11.theirs, bf16[2048,1024]{1,0:T(8,128)(2,1)S(1)} %get-tuple-element.13.held), custom_call_target="tpu_custom_call" | custom-call | flops 67108864 | bytes 4194304 | tf_op jit(solution)/shard_map/pallas_call | solution.py:234
  45.3 3.4 %collective-permute-start.12 = (f32[16,2048]{1,0:T(8,128)S(1)}, f32[16,2048]{1,0:T(8,128)S(1)}, u32[]{:S(2)}, u32[]{:S(2)}) collective-permute-start(f32[16,2048]{1,0:T(8,128)S(1)} %get-tuple-element.15), channel_id=1, source_target_pairs={{0,1},{1,0},{2,3},{3,2},{4,5},{5,4},{6,7},{7,6},{8,9},{9,8},{10,11... | collective-permute-start | bytes 393224 | tf_op jit(solution)/shard_map/ppermute | solution.py:44
  48.7 1.2 shard_map.55
  49.9 2.3 %collective-permute-start.15 = (f32[16,2048]{1,0:T(8,128)S(1)}, f32[16,2048]{1,0:T(8,128)S(1)}, u32[]{:S(2)}, u32[]{:S(2)}) collective-permute-start(f32[16,2048]{1,0:T(8,128)S(1)} %add.91), channel_id=1, source_target_pairs={{0,6},{2,4},{4,2},{6,0},{1,7},{3,5},{5,3},{7,1},{8,14},{10,12},{12... | collective-permute-start | bytes 393224 | tf_op jit(solution)/shard_map/ppermute | solution.py:44
  53.3 4.4 %collective-permute-done.15 = f32[16,2048]{1,0:T(8,128)S(1)} collective-permute-done((f32[16,2048]{1,0:T(8,128)S(1)}, f32[16,2048]{1,0:T(8,128)S(1)}, u32[]{:S(2)}, u32[]{:S(2)}) %collective-permute-start.15) | collective-permute-done | bytes 131104 | tf_op jit(solution)/shard_map/ppermute | solution.py:44
  58.4 0.9 collective-permute-done.13
  59.3 1.4 %collective-permute-start.16 = (f32[16,2048]{1,0:T(8,128)S(1)}, f32[16,2048]{1,0:T(8,128)S(1)}, u32[]{:S(2)}, u32[]{:S(2)}) collective-permute-start(f32[16,2048]{1,0:T(8,128)S(1)} %add_add_fusion.1.half), channel_id=1, source_target_pairs={{0,1},{1,0},{2,3},{3,2},{4,5},{5,4},{6,7},{7,6},{8,9},{9,8},{10,11... | collective-permute-start | bytes 393224 | tf_op jit(solution)/shard_map/ppermute | solution.py:44
  60.7 0.9 shard_map.56.before
  61.7 0.9 shard_map.57
  62.6 1.2 collective-permute-start.19
  64.5 1.3 %collective-permute-start.17 = (f32[136,128]{1,0:T(8,128)S(1)}, f32[136,128]{1,0:T(8,128)S(1)}, u32[]{:S(2)}, u32[]{:S(2)}) collective-permute-start(f32[136,128]{1,0:T(8,128)S(1)} %shard_map.57), channel_id=1, source_target_pairs={{0,64},{64,0},{128,192},{192,128},{1,65},{65,1},{129,193},{193,129... | collective-permute-start | bytes 208904 | tf_op jit(solution)/shard_map/ppermute | solution.py:44
  65.9 1.1 collective-permute-done.19
  67.0 1.5 %collective-permute-done.18 = f32[136,128]{1,0:T(8,128)S(1)} collective-permute-done((f32[136,128]{1,0:T(8,128)S(1)}, f32[136,128]{1,0:T(8,128)S(1)}, u32[]{:S(2)}, u32[]{:S(2)}) %collective-permute-start.18) | collective-permute-done | bytes 69664 | tf_op jit(solution)/shard_map/ppermute | solution.py:44
  68.9 1.9 %collective-permute-start.22 = (f32[136,128]{1,0:T(8,128)S(1)}, f32[136,128]{1,0:T(8,128)S(1)}, u32[]{:S(2)}, u32[]{:S(2)}) collective-permute-start(f32[136,128]{1,0:T(8,128)S(1)} %add_add_fusion.4), channel_id=1, source_target_pairs={{0,24},{8,16},{16,8},{24,0},{32,56},{40,48},{48,40},{56,32},{1,25}... | collective-permute-start | bytes 208904 | tf_op jit(solution)/shard_map/ppermute | solution.py:44
  70.7 1.0 collective-permute-start.21
  72.5 1.5 %collective-permute-done.22 = f32[136,128]{1,0:T(8,128)S(1)} collective-permute-done((f32[136,128]{1,0:T(8,128)S(1)}, f32[136,128]{1,0:T(8,128)S(1)}, u32[]{:S(2)}, u32[]{:S(2)}) %collective-permute-start.22) | collective-permute-done | bytes 69664 | tf_op jit(solution)/shard_map/ppermute | solution.py:44
  74.0 2.5 %collective-permute-done.21 = f32[136,128]{1,0:T(8,128)S(1)} collective-permute-done((f32[136,128]{1,0:T(8,128)S(1)}, f32[136,128]{1,0:T(8,128)S(1)}, u32[]{:S(2)}, u32[]{:S(2)}) %collective-permute-start.21) | collective-permute-done | bytes 69664 | tf_op jit(solution)/shard_map/ppermute | solution.py:44
  76.6 2.9 %collective-permute-start.23 = (f32[136,128]{1,0:T(8,128)S(1)}, f32[136,128]{1,0:T(8,128)S(1)}, u32[]{:S(2)}, u32[]{:S(2)}) collective-permute-start(f32[136,128]{1,0:T(8,128)S(1)} %add_add_fusion.3.mine), channel_id=1, source_target_pairs={{0,48},{8,56},{16,32},{24,40},{32,16},{40,24},{48,0},{56,8},{1,49}... | collective-permute-start | bytes 208904 | tf_op jit(solution)/shard_map/ppermute | solution.py:44
  79.5 3.1 %collective-permute-done.23.theirs = f32[136,128]{1,0:T(8,128)S(1)} collective-permute-done((f32[136,128]{1,0:T(8,128)S(1)}, f32[136,128]{1,0:T(8,128)S(1)}, u32[]{:S(2)}, u32[]{:S(2)}) %collective-permute-start.23) | collective-permute-done | bytes 69664 | tf_op jit(solution)/shard_map/ppermute | solution.py:44
  82.6 1.4 %shard_map.58 = (bf16[16,1024]{1,0:T(8,128)(2,1)S(1)}, f32[16,2048]{1,0:T(8,128)S(1)}) custom-call(f32[136,128]{1,0:T(8,128)S(1)} %add_add_fusion.3.mine, f32[136,128]{1,0:T(8,128)S(1)} %collective-permute-done.23.theirs, bf16[2048,1024]{1,0:T(8,128)(2,1)S(1)} %get-tuple-element.13.held), custom_call_target="tpu_custom_call" | custom-call | flops 67108864 | bytes 4194304 | tf_op jit(solution)/shard_map/pallas_call | solution.py:234
  84.0 3.4 %collective-permute-start.24 = (f32[16,2048]{1,0:T(8,128)S(1)}, f32[16,2048]{1,0:T(8,128)S(1)}, u32[]{:S(2)}, u32[]{:S(2)}) collective-permute-start(f32[16,2048]{1,0:T(8,128)S(1)} %get-tuple-element.17), channel_id=1, source_target_pairs={{0,1},{1,0},{2,3},{3,2},{4,5},{5,4},{6,7},{7,6},{8,9},{9,8},{10,11... | collective-permute-start | bytes 393224 | tf_op jit(solution)/shard_map/ppermute | solution.py:44
  87.4 1.2 shard_map.59
  88.6 2.3 %collective-permute-start.27 = (f32[16,2048]{1,0:T(8,128)S(1)}, f32[16,2048]{1,0:T(8,128)S(1)}, u32[]{:S(2)}, u32[]{:S(2)}) collective-permute-start(f32[16,2048]{1,0:T(8,128)S(1)} %add.101), channel_id=1, source_target_pairs={{0,6},{2,4},{4,2},{6,0},{1,7},{3,5},{5,3},{7,1},{8,14},{10,12},{12... | collective-permute-start | bytes 393224 | tf_op jit(solution)/shard_map/ppermute | solution.py:44
  92.0 4.4 %collective-permute-done.27 = f32[16,2048]{1,0:T(8,128)S(1)} collective-permute-done((f32[16,2048]{1,0:T(8,128)S(1)}, f32[16,2048]{1,0:T(8,128)S(1)}, u32[]{:S(2)}, u32[]{:S(2)}) %collective-permute-start.27) | collective-permute-done | bytes 131104 | tf_op jit(solution)/shard_map/ppermute | solution.py:44
  97.1 0.9 collective-permute-done.25
  98.3 5.6 %collective-permute-start.30 = (f32[8,128]{1,0:T(8,128)S(1)}, f32[8,128]{1,0:T(8,128)S(1)}, u32[]{:S(2)}, u32[]{:S(2)}) collective-permute-start(f32[8,128]{1,0:T(8,128)S(1)} %shard_map.60), channel_id=1, source_target_pairs={{0,49},{1,48},{8,57},{9,56},{16,33},{17,32},{24,41},{25,40},{32,17... | collective-permute-start | bytes 12296 | tf_op jit(solution)/shard_map/ppermute | solution.py:44
  104.4 0.8 collective-permute-done.30
  105.2 3.3 %collective-permute-done.29 = f32[8,128]{1,0:T(8,128)S(1)} collective-permute-done((f32[8,128]{1,0:T(8,128)S(1)}, f32[8,128]{1,0:T(8,128)S(1)}, u32[]{:S(2)}, u32[]{:S(2)}) %collective-permute-start.29) | collective-permute-done | bytes 4128 | tf_op jit(solution)/shard_map/ppermute | solution.py:44
  108.5 10.9 %all_to_all.5.grams = f32[16,8,128]{2,1,0:T(8,128)S(1)} all-to-all(f32[16,8,128]{2,1,0:T(8,128)S(1)} %broadcast_in_dim.2), channel_id=1, replica_groups=mesh['x'=4,'cube'=2,'level'=4,'y'=4,'core'=2] {'x','level'}, dimensions={0} | all-to-all | bytes 131072 | tf_op jit(solution)/shard_map/all_to_all | solution.py:313
  119.4 1.0 shard_map.61
  (39 shorter events, 8.3 us)
Async XLA Ops:
  5.2 4.5 %collective-permute-start = (f32[16,2048]{1,0:T(8,128)S(1)}, f32[16,2048]{1,0:T(8,128)S(1)}, u32[]{:S(2)}, u32[]{:S(2)}) collective-permute-start(f32[16,2048]{1,0:T(8,128)S(1)} %get-tuple-element.12), channel_id=1, source_target_pairs={{0,1},{1,0},{2,3},{3,2},{4,5},{5,4},{6,7},{7,6},{8,9},{9,8},{10,11... | collective-permute-start | bytes 393224 | tf_op jit(solution)/shard_map/ppermute | solution.py:44
  9.7 9.1 %collective-permute-start.3 = (f32[16,2048]{1,0:T(8,128)S(1)}, f32[16,2048]{1,0:T(8,128)S(1)}, u32[]{:S(2)}, u32[]{:S(2)}) collective-permute-start(f32[16,2048]{1,0:T(8,128)S(1)} %add.81), channel_id=1, source_target_pairs={{0,6},{2,4},{4,2},{6,0},{1,7},{3,5},{5,3},{7,1},{8,14},{10,12},{12... | collective-permute-start | bytes 393224 | tf_op jit(solution)/shard_map/ppermute | solution.py:44
  10.8 8.0 %collective-permute-start.2 = (f32[16,2048]{1,0:T(8,128)S(1)}, f32[16,2048]{1,0:T(8,128)S(1)}, u32[]{:S(2)}, u32[]{:S(2)}) collective-permute-start(f32[16,2048]{1,0:T(8,128)S(1)} %add.81), channel_id=1, source_target_pairs={{0,4},{2,6},{4,0},{6,2},{1,5},{3,7},{5,1},{7,3},{8,12},{10,14},{12... | collective-permute-start | bytes 393224 | tf_op jit(solution)/shard_map/ppermute | solution.py:44
  11.2 7.9 %collective-permute-start.1 = (f32[16,2048]{1,0:T(8,128)S(1)}, f32[16,2048]{1,0:T(8,128)S(1)}, u32[]{:S(2)}, u32[]{:S(2)}) collective-permute-start(f32[16,2048]{1,0:T(8,128)S(1)} %add.81), channel_id=1, source_target_pairs={{0,2},{2,0},{4,6},{6,4},{1,3},{3,1},{5,7},{7,5},{8,10},{10,8},{12,... | collective-permute-start | bytes 393224 | tf_op jit(solution)/shard_map/ppermute | solution.py:44
  19.1 2.4 %collective-permute-start.4 = (f32[16,2048]{1,0:T(8,128)S(1)}, f32[16,2048]{1,0:T(8,128)S(1)}, u32[]{:S(2)}, u32[]{:S(2)}) collective-permute-start(f32[16,2048]{1,0:T(8,128)S(1)} %add_add_fusion.2.half), channel_id=1, source_target_pairs={{0,1},{1,0},{2,3},{3,2},{4,5},{5,4},{6,7},{7,6},{8,9},{9,8},{10,11... | collective-permute-start | bytes 393224 | tf_op jit(solution)/shard_map/ppermute | solution.py:44
  22.4 4.4 %collective-permute-start.7 = (f32[136,128]{1,0:T(8,128)S(1)}, f32[136,128]{1,0:T(8,128)S(1)}, u32[]{:S(2)}, u32[]{:S(2)}) collective-permute-start(f32[136,128]{1,0:T(8,128)S(1)} %shard_map.53), channel_id=1, source_target_pairs={{0,192},{64,128},{128,64},{192,0},{1,193},{65,129},{129,65},{193,1... | collective-permute-start | bytes 208904 | tf_op jit(solution)/shard_map/ppermute | solution.py:44
  23.7 4.7 %collective-permute-start.6 = (f32[136,128]{1,0:T(8,128)S(1)}, f32[136,128]{1,0:T(8,128)S(1)}, u32[]{:S(2)}, u32[]{:S(2)}) collective-permute-start(f32[136,128]{1,0:T(8,128)S(1)} %shard_map.53), channel_id=1, source_target_pairs={{0,128},{64,192},{128,0},{192,64},{1,129},{65,193},{129,1},{193,65... | collective-permute-start | bytes 208904 | tf_op jit(solution)/shard_map/ppermute | solution.py:44
  24.2 4.3 %collective-permute-start.5 = (f32[136,128]{1,0:T(8,128)S(1)}, f32[136,128]{1,0:T(8,128)S(1)}, u32[]{:S(2)}, u32[]{:S(2)}) collective-permute-start(f32[136,128]{1,0:T(8,128)S(1)} %shard_map.53), channel_id=1, source_target_pairs={{0,64},{64,0},{128,192},{192,128},{1,65},{65,1},{129,193},{193,129... | collective-permute-start | bytes 208904 | tf_op jit(solution)/shard_map/ppermute | solution.py:44
  28.6 5.9 %collective-permute-start.10 = (f32[136,128]{1,0:T(8,128)S(1)}, f32[136,128]{1,0:T(8,128)S(1)}, u32[]{:S(2)}, u32[]{:S(2)}) collective-permute-start(f32[136,128]{1,0:T(8,128)S(1)} %add_add_fusion.6), channel_id=1, source_target_pairs={{0,24},{8,16},{16,8},{24,0},{32,56},{40,48},{48,40},{56,32},{1,25}... | collective-permute-start | bytes 208904 | tf_op jit(solution)/shard_map/ppermute | solution.py:44
  32.8 5.0 %collective-permute-start.9 = (f32[136,128]{1,0:T(8,128)S(1)}, f32[136,128]{1,0:T(8,128)S(1)}, u32[]{:S(2)}, u32[]{:S(2)}) collective-permute-start(f32[136,128]{1,0:T(8,128)S(1)} %add_add_fusion.6), channel_id=1, source_target_pairs={{0,16},{8,24},{16,0},{24,8},{32,48},{40,56},{48,32},{56,40},{1,17}... | collective-permute-start | bytes 208904 | tf_op jit(solution)/shard_map/ppermute | solution.py:44
  32.8 5.0 %collective-permute-start.8 = (f32[136,128]{1,0:T(8,128)S(1)}, f32[136,128]{1,0:T(8,128)S(1)}, u32[]{:S(2)}, u32[]{:S(2)}) collective-permute-start(f32[136,128]{1,0:T(8,128)S(1)} %add_add_fusion.6), channel_id=1, source_target_pairs={{0,8},{8,0},{16,24},{24,16},{32,40},{40,32},{48,56},{56,48},{1,9},... | collective-permute-start | bytes 208904 | tf_op jit(solution)/shard_map/ppermute | solution.py:44
  37.8 6.1 %collective-permute-start.11 = (f32[136,128]{1,0:T(8,128)S(1)}, f32[136,128]{1,0:T(8,128)S(1)}, u32[]{:S(2)}, u32[]{:S(2)}) collective-permute-start(f32[136,128]{1,0:T(8,128)S(1)} %add_add_fusion.5.mine), channel_id=1, source_target_pairs={{0,48},{8,56},{16,32},{24,40},{32,16},{40,24},{48,0},{56,8},{1,49}... | collective-permute-start | bytes 208904 | tf_op jit(solution)/shard_map/ppermute | solution.py:44
  45.3 4.6 %collective-permute-start.12 = (f32[16,2048]{1,0:T(8,128)S(1)}, f32[16,2048]{1,0:T(8,128)S(1)}, u32[]{:S(2)}, u32[]{:S(2)}) collective-permute-start(f32[16,2048]{1,0:T(8,128)S(1)} %get-tuple-element.15), channel_id=1, source_target_pairs={{0,1},{1,0},{2,3},{3,2},{4,5},{5,4},{6,7},{7,6},{8,9},{9,8},{10,11... | collective-permute-start | bytes 393224 | tf_op jit(solution)/shard_map/ppermute | solution.py:44
  49.9 7.7 %collective-permute-start.15 = (f32[16,2048]{1,0:T(8,128)S(1)}, f32[16,2048]{1,0:T(8,128)S(1)}, u32[]{:S(2)}, u32[]{:S(2)}) collective-permute-start(f32[16,2048]{1,0:T(8,128)S(1)} %add.91), channel_id=1, source_target_pairs={{0,6},{2,4},{4,2},{6,0},{1,7},{3,5},{5,3},{7,1},{8,14},{10,12},{12... | collective-permute-start | bytes 393224 | tf_op jit(solution)/shard_map/ppermute | solution.py:44
  52.2 6.2 %collective-permute-start.14 = (f32[16,2048]{1,0:T(8,128)S(1)}, f32[16,2048]{1,0:T(8,128)S(1)}, u32[]{:S(2)}, u32[]{:S(2)}) collective-permute-start(f32[16,2048]{1,0:T(8,128)S(1)} %add.91), channel_id=1, source_target_pairs={{0,4},{2,6},{4,0},{6,2},{1,5},{3,7},{5,1},{7,3},{8,12},{10,14},{12... | collective-permute-start | bytes 393224 | tf_op jit(solution)/shard_map/ppermute | solution.py:44
  52.6 6.7 %collective-permute-start.13 = (f32[16,2048]{1,0:T(8,128)S(1)}, f32[16,2048]{1,0:T(8,128)S(1)}, u32[]{:S(2)}, u32[]{:S(2)}) collective-permute-start(f32[16,2048]{1,0:T(8,128)S(1)} %add.91), channel_id=1, source_target_pairs={{0,2},{2,0},{4,6},{6,4},{1,3},{3,1},{5,7},{7,5},{8,10},{10,8},{12,... | collective-permute-start | bytes 393224 | tf_op jit(solution)/shard_map/ppermute | solution.py:44
  59.3 2.4 %collective-permute-start.16 = (f32[16,2048]{1,0:T(8,128)S(1)}, f32[16,2048]{1,0:T(8,128)S(1)}, u32[]{:S(2)}, u32[]{:S(2)}) collective-permute-start(f32[16,2048]{1,0:T(8,128)S(1)} %add_add_fusion.1.half), channel_id=1, source_target_pairs={{0,1},{1,0},{2,3},{3,2},{4,5},{5,4},{6,7},{7,6},{8,9},{9,8},{10,11... | collective-permute-start | bytes 393224 | tf_op jit(solution)/shard_map/ppermute | solution.py:44
  62.6 4.4 %collective-permute-start.19 = (f32[136,128]{1,0:T(8,128)S(1)}, f32[136,128]{1,0:T(8,128)S(1)}, u32[]{:S(2)}, u32[]{:S(2)}) collective-permute-start(f32[136,128]{1,0:T(8,128)S(1)} %shard_map.57), channel_id=1, source_target_pairs={{0,192},{64,128},{128,64},{192,0},{1,193},{65,129},{129,65},{193,1... | collective-permute-start | bytes 208904 | tf_op jit(solution)/shard_map/ppermute | solution.py:44
  63.8 4.8 %collective-permute-start.18 = (f32[136,128]{1,0:T(8,128)S(1)}, f32[136,128]{1,0:T(8,128)S(1)}, u32[]{:S(2)}, u32[]{:S(2)}) collective-permute-start(f32[136,128]{1,0:T(8,128)S(1)} %shard_map.57), channel_id=1, source_target_pairs={{0,128},{64,192},{128,0},{192,64},{1,129},{65,193},{129,1},{193,65... | collective-permute-start | bytes 208904 | tf_op jit(solution)/shard_map/ppermute | solution.py:44
  64.5 4.3 %collective-permute-start.17 = (f32[136,128]{1,0:T(8,128)S(1)}, f32[136,128]{1,0:T(8,128)S(1)}, u32[]{:S(2)}, u32[]{:S(2)}) collective-permute-start(f32[136,128]{1,0:T(8,128)S(1)} %shard_map.57), channel_id=1, source_target_pairs={{0,64},{64,0},{128,192},{192,128},{1,65},{65,1},{129,193},{193,129... | collective-permute-start | bytes 208904 | tf_op jit(solution)/shard_map/ppermute | solution.py:44
  68.9 5.2 %collective-permute-start.22 = (f32[136,128]{1,0:T(8,128)S(1)}, f32[136,128]{1,0:T(8,128)S(1)}, u32[]{:S(2)}, u32[]{:S(2)}) collective-permute-start(f32[136,128]{1,0:T(8,128)S(1)} %add_add_fusion.4), channel_id=1, source_target_pairs={{0,24},{8,16},{16,8},{24,0},{32,56},{40,48},{48,40},{56,32},{1,25}... | collective-permute-start | bytes 208904 | tf_op jit(solution)/shard_map/ppermute | solution.py:44
  70.7 5.8 %collective-permute-start.21 = (f32[136,128]{1,0:T(8,128)S(1)}, f32[136,128]{1,0:T(8,128)S(1)}, u32[]{:S(2)}, u32[]{:S(2)}) collective-permute-start(f32[136,128]{1,0:T(8,128)S(1)} %add_add_fusion.4), channel_id=1, source_target_pairs={{0,16},{8,24},{16,0},{24,8},{32,48},{40,56},{48,32},{56,40},{1,17}... | collective-permute-start | bytes 208904 | tf_op jit(solution)/shard_map/ppermute | solution.py:44
  71.7 4.9 %collective-permute-start.20 = (f32[136,128]{1,0:T(8,128)S(1)}, f32[136,128]{1,0:T(8,128)S(1)}, u32[]{:S(2)}, u32[]{:S(2)}) collective-permute-start(f32[136,128]{1,0:T(8,128)S(1)} %add_add_fusion.4), channel_id=1, source_target_pairs={{0,8},{8,0},{16,24},{24,16},{32,40},{40,32},{48,56},{56,48},{1,9},... | collective-permute-start | bytes 208904 | tf_op jit(solution)/shard_map/ppermute | solution.py:44
  76.6 6.0 %collective-permute-start.23 = (f32[136,128]{1,0:T(8,128)S(1)}, f32[136,128]{1,0:T(8,128)S(1)}, u32[]{:S(2)}, u32[]{:S(2)}) collective-permute-start(f32[136,128]{1,0:T(8,128)S(1)} %add_add_fusion.3.mine), channel_id=1, source_target_pairs={{0,48},{8,56},{16,32},{24,40},{32,16},{40,24},{48,0},{56,8},{1,49}... | collective-permute-start | bytes 208904 | tf_op jit(solution)/shard_map/ppermute | solution.py:44
  84.0 4.6 %collective-permute-start.24 = (f32[16,2048]{1,0:T(8,128)S(1)}, f32[16,2048]{1,0:T(8,128)S(1)}, u32[]{:S(2)}, u32[]{:S(2)}) collective-permute-start(f32[16,2048]{1,0:T(8,128)S(1)} %get-tuple-element.17), channel_id=1, source_target_pairs={{0,1},{1,0},{2,3},{3,2},{4,5},{5,4},{6,7},{7,6},{8,9},{9,8},{10,11... | collective-permute-start | bytes 393224 | tf_op jit(solution)/shard_map/ppermute | solution.py:44
  88.6 7.7 %collective-permute-start.27 = (f32[16,2048]{1,0:T(8,128)S(1)}, f32[16,2048]{1,0:T(8,128)S(1)}, u32[]{:S(2)}, u32[]{:S(2)}) collective-permute-start(f32[16,2048]{1,0:T(8,128)S(1)} %add.101), channel_id=1, source_target_pairs={{0,6},{2,4},{4,2},{6,0},{1,7},{3,5},{5,3},{7,1},{8,14},{10,12},{12... | collective-permute-start | bytes 393224 | tf_op jit(solution)/shard_map/ppermute | solution.py:44
  90.9 6.2 %collective-permute-start.26 = (f32[16,2048]{1,0:T(8,128)S(1)}, f32[16,2048]{1,0:T(8,128)S(1)}, u32[]{:S(2)}, u32[]{:S(2)}) collective-permute-start(f32[16,2048]{1,0:T(8,128)S(1)} %add.101), channel_id=1, source_target_pairs={{0,4},{2,6},{4,0},{6,2},{1,5},{3,7},{5,1},{7,3},{8,12},{10,14},{12... | collective-permute-start | bytes 393224 | tf_op jit(solution)/shard_map/ppermute | solution.py:44
  91.3 6.7 %collective-permute-start.25 = (f32[16,2048]{1,0:T(8,128)S(1)}, f32[16,2048]{1,0:T(8,128)S(1)}, u32[]{:S(2)}, u32[]{:S(2)}) collective-permute-start(f32[16,2048]{1,0:T(8,128)S(1)} %add.101), channel_id=1, source_target_pairs={{0,2},{2,0},{4,6},{6,4},{1,3},{3,1},{5,7},{7,5},{8,10},{10,8},{12,... | collective-permute-start | bytes 393224 | tf_op jit(solution)/shard_map/ppermute | solution.py:44
  98.3 6.9 %collective-permute-start.30 = (f32[8,128]{1,0:T(8,128)S(1)}, f32[8,128]{1,0:T(8,128)S(1)}, u32[]{:S(2)}, u32[]{:S(2)}) collective-permute-start(f32[8,128]{1,0:T(8,128)S(1)} %shard_map.60), channel_id=1, source_target_pairs={{0,49},{1,48},{8,57},{9,56},{16,33},{17,32},{24,41},{25,40},{32,17... | collective-permute-start | bytes 12296 | tf_op jit(solution)/shard_map/ppermute | solution.py:44
  103.9 4.6 %collective-permute-start.29 = (f32[8,128]{1,0:T(8,128)S(1)}, f32[8,128]{1,0:T(8,128)S(1)}, u32[]{:S(2)}, u32[]{:S(2)}) collective-permute-start(f32[8,128]{1,0:T(8,128)S(1)} %shard_map.60), channel_id=1, source_target_pairs={{0,48},{1,49},{8,56},{9,57},{16,32},{17,33},{24,40},{25,41},{32,16... | collective-permute-start | bytes 12296 | tf_op jit(solution)/shard_map/ppermute | solution.py:44
  103.9 4.6 %collective-permute-start.28 = (f32[8,128]{1,0:T(8,128)S(1)}, f32[8,128]{1,0:T(8,128)S(1)}, u32[]{:S(2)}, u32[]{:S(2)}) collective-permute-start(f32[8,128]{1,0:T(8,128)S(1)} %shard_map.60), channel_id=1, source_target_pairs={{0,1},{1,0},{8,9},{9,8},{16,17},{17,16},{24,25},{25,24},{32,33},{3... | collective-permute-start | bytes 12296 | tf_op jit(solution)/shard_map/ppermute | solution.py:44

commit v9 on v8

--- a/solution.py
+++ b/solution.py
@@ -142,9 +142,9 @@
         pltpu.make_async_copy(seed_values, seeds_here, small_arrived.at[0]),
         pltpu.make_async_copy(sku_ids, ids_here, small_arrived.at[1]),
     ]
+    copies = load_half(affinity, held_other, other_arrived, 1 - core)
     for copy in small:
         copy.start()
-    copies = load_half(affinity, held_other, other_arrived, 1 - core)
     later = load_half(affinity, held_own, own_arrived, core)
     for copy in small:
         copy.wait()
@@ -296,7 +296,7 @@
             (packed,) = call(
                 back_other_kernel, [packed_out], sibling, held_other, packed, flops=pass_flops
             )
-            packed = sum_four(packed, "x", 4)
+            packed = sum_four(packed, "x", 4, (3, 1, 2))
             packed = sum_four(packed, z, 8)
             left, other = call(
                 functools.partial(solve_kernel, scale=scale),

time: 120 us -> 121 us (level)
  starting transfers between devices: 49.8 us -> 48.3 us
    ppermute x31, starting transfers between devices: 49.8 us -> 48.3 us  [swap(): return lax.ppermute(value, axis, [(i, i ^ offset) for i in range(count)])]
  transfers between devices with their start and end apart: 31 -> 31, of which waited for: 24 -> 22; matrix products, arithmetic and copies ran while one was open for 0% -> 0% of each run, Pallas kernels for 5% -> 4%
where the time goes in v9:
time: 121 us
  starting transfers between devices  48.3 us (40%)
  waiting for transfers between devices  43.7 us (36%)
  Pallas kernels  16.2 us (13%)
  blocking collectives  11.4 us (9%)
    ppermute x31, starting transfers between devices, swap(): return lax.ppermute(value, axis, [(i, i ^ offset) for i in range(count)])  48.3 us
    ppermute x31, waiting for transfers between devices, swap(): return lax.ppermute(value, axis, [(i, i ^ offset) for i in range(count)])  43.7 us
    pallas_call x12, Pallas kernels, call(): pl.pallas_call(kernel, in_specs=spaces or [whole] * len(args), out_specs=...  16.2 us
    all_to_all x1, blocking collectives, body(): grams = lax.all_to_all(spread, ('x', 'level'), 0, 0)  11.4 us
  transfers between devices with their start and end apart: 31, of which 22 were waited for; matrix products, arithmetic and copies ran while one was open for 0% of the time, Pallas kernels for 4%

profile of v9, /device:TPU:1, one launch (start us, length us, event | category | flops | bytes accessed | tf_op | source)
XLA Modules:
  0.0 120.6 jit_solution(16714795094533361822)
XLA Ops:
  0.6 4.8 %shard_map.50 = (bf16[16,1024]{1,0:T(8,128)(2,1)S(1)}, bf16[2048,1024]{1,0:T(8,128)(2,1)S(1)}, bf16[2048,1024]{1,0:T(8,128)(2,1)S(1)}, f32[16,2048]{1,0:T(8,128)S(1)}) custom-call(s32[16]{0:T(128)} %seed_values.1, s32[1,1024]{1,0:T(1,128)} %bitcast.1, bf16[4096,1024]{1,0:T(8,128)(2,1)} %affinity.1), custom_call_target="tpu_custom_call" | custom-call | flops 67108864 | bytes 4194304 | tf_op jit(solution)/shard_map/pallas_call | solution.py:234
  5.5 3.3 %collective-permute-start = (f32[16,2048]{1,0:T(8,128)S(1)}, f32[16,2048]{1,0:T(8,128)S(1)}, u32[]{:S(2)}, u32[]{:S(2)}) collective-permute-start(f32[16,2048]{1,0:T(8,128)S(1)} %get-tuple-element.12), channel_id=1, source_target_pairs={{0,1},{1,0},{2,3},{3,2},{4,5},{5,4},{6,7},{7,6},{8,9},{9,8},{10,11... | collective-permute-start | bytes 393224 | tf_op jit(solution)/shard_map/ppermute | solution.py:44
  8.8 1.2 shard_map.51
  10.0 1.1 collective-permute-start.3
  11.5 1.9 %collective-permute-start.1 = (f32[16,2048]{1,0:T(8,128)S(1)}, f32[16,2048]{1,0:T(8,128)S(1)}, u32[]{:S(2)}, u32[]{:S(2)}) collective-permute-start(f32[16,2048]{1,0:T(8,128)S(1)} %add.81), channel_id=1, source_target_pairs={{0,2},{2,0},{4,6},{6,4},{1,3},{3,1},{5,7},{7,5},{8,10},{10,8},{12,... | collective-permute-start | bytes 393224 | tf_op jit(solution)/shard_map/ppermute | solution.py:44
  13.4 5.7 %collective-permute-done.3 = f32[16,2048]{1,0:T(8,128)S(1)} collective-permute-done((f32[16,2048]{1,0:T(8,128)S(1)}, f32[16,2048]{1,0:T(8,128)S(1)}, u32[]{:S(2)}, u32[]{:S(2)}) %collective-permute-start.3) | collective-permute-done | bytes 131104 | tf_op jit(solution)/shard_map/ppermute | solution.py:44
  19.4 1.4 %collective-permute-start.4 = (f32[16,2048]{1,0:T(8,128)S(1)}, f32[16,2048]{1,0:T(8,128)S(1)}, u32[]{:S(2)}, u32[]{:S(2)}) collective-permute-start(f32[16,2048]{1,0:T(8,128)S(1)} %add_add_fusion.2.half), channel_id=1, source_target_pairs={{0,1},{1,0},{2,3},{3,2},{4,5},{5,4},{6,7},{7,6},{8,9},{9,8},{10,11... | collective-permute-start | bytes 393224 | tf_op jit(solution)/shard_map/ppermute | solution.py:44
  20.8 0.9 shard_map.52.before
  21.8 0.9 shard_map.53
  22.7 1.5 %collective-permute-start.7 = (f32[136,128]{1,0:T(8,128)S(1)}, f32[136,128]{1,0:T(8,128)S(1)}, u32[]{:S(2)}, u32[]{:S(2)}) collective-permute-start(f32[136,128]{1,0:T(8,128)S(1)} %shard_map.53), channel_id=1, source_target_pairs={{0,128},{64,192},{128,0},{192,64},{1,129},{65,193},{129,1},{193,65... | collective-permute-start | bytes 208904 | tf_op jit(solution)/shard_map/ppermute | solution.py:44
  24.2 0.9 collective-permute-start.6
  25.4 2.0 %collective-permute-done.7 = f32[136,128]{1,0:T(8,128)S(1)} collective-permute-done((f32[136,128]{1,0:T(8,128)S(1)}, f32[136,128]{1,0:T(8,128)S(1)}, u32[]{:S(2)}, u32[]{:S(2)}) %collective-permute-start.7) | collective-permute-done | bytes 69664 | tf_op jit(solution)/shard_map/ppermute | solution.py:44
  27.4 1.9 %collective-permute-done.6 = f32[136,128]{1,0:T(8,128)S(1)} collective-permute-done((f32[136,128]{1,0:T(8,128)S(1)}, f32[136,128]{1,0:T(8,128)S(1)}, u32[]{:S(2)}, u32[]{:S(2)}) %collective-permute-start.6) | collective-permute-done | bytes 69664 | tf_op jit(solution)/shard_map/ppermute | solution.py:44
  29.3 3.8 %collective-permute-start.10 = (f32[136,128]{1,0:T(8,128)S(1)}, f32[136,128]{1,0:T(8,128)S(1)}, u32[]{:S(2)}, u32[]{:S(2)}) collective-permute-start(f32[136,128]{1,0:T(8,128)S(1)} %add_add_fusion.6), channel_id=1, source_target_pairs={{0,24},{8,16},{16,8},{24,0},{32,56},{40,48},{48,40},{56,32},{1,25}... | collective-permute-start | bytes 208904 | tf_op jit(solution)/shard_map/ppermute | solution.py:44
  33.5 1.3 %collective-permute-done.10 = f32[136,128]{1,0:T(8,128)S(1)} collective-permute-done((f32[136,128]{1,0:T(8,128)S(1)}, f32[136,128]{1,0:T(8,128)S(1)}, u32[]{:S(2)}, u32[]{:S(2)}) %collective-permute-start.10) | collective-permute-done | bytes 69664 | tf_op jit(solution)/shard_map/ppermute | solution.py:44
  34.8 3.2 %collective-permute-done.9 = f32[136,128]{1,0:T(8,128)S(1)} collective-permute-done((f32[136,128]{1,0:T(8,128)S(1)}, f32[136,128]{1,0:T(8,128)S(1)}, u32[]{:S(2)}, u32[]{:S(2)}) %collective-permute-start.9) | collective-permute-done | bytes 69664 | tf_op jit(solution)/shard_map/ppermute | solution.py:44
  38.0 3.6 %collective-permute-start.11 = (f32[136,128]{1,0:T(8,128)S(1)}, f32[136,128]{1,0:T(8,128)S(1)}, u32[]{:S(2)}, u32[]{:S(2)}) collective-permute-start(f32[136,128]{1,0:T(8,128)S(1)} %add_add_fusion.5.mine), channel_id=1, source_target_pairs={{0,48},{8,56},{16,32},{24,40},{32,16},{40,24},{48,0},{56,8},{1,49}... | collective-permute-start | bytes 208904 | tf_op jit(solution)/shard_map/ppermute | solution.py:44
  41.5 2.6 %collective-permute-done.11.theirs = f32[136,128]{1,0:T(8,128)S(1)} collective-permute-done((f32[136,128]{1,0:T(8,128)S(1)}, f32[136,128]{1,0:T(8,128)S(1)}, u32[]{:S(2)}, u32[]{:S(2)}) %collective-permute-start.11) | collective-permute-done | bytes 69664 | tf_op jit(solution)/shard_map/ppermute | solution.py:44
  44.1 1.4 %shard_map.54 = (bf16[16,1024]{1,0:T(8,128)(2,1)S(1)}, f32[16,2048]{1,0:T(8,128)S(1)}) custom-call(f32[136,128]{1,0:T(8,128)S(1)} %add_add_fusion.5.mine, f32[136,128]{1,0:T(8,128)S(1)} %collective-permute-done.11.theirs, bf16[2048,1024]{1,0:T(8,128)(2,1)S(1)} %get-tuple-element.13.held), custom_call_target="tpu_custom_call" | custom-call | flops 67108864 | bytes 4194304 | tf_op jit(solution)/shard_map/pallas_call | solution.py:234
  45.5 3.0 %collective-permute-start.12 = (f32[16,2048]{1,0:T(8,128)S(1)}, f32[16,2048]{1,0:T(8,128)S(1)}, u32[]{:S(2)}, u32[]{:S(2)}) collective-permute-start(f32[16,2048]{1,0:T(8,128)S(1)} %get-tuple-element.15), channel_id=1, source_target_pairs={{0,1},{1,0},{2,3},{3,2},{4,5},{5,4},{6,7},{7,6},{8,9},{9,8},{10,11... | collective-permute-start | bytes 393224 | tf_op jit(solution)/shard_map/ppermute | solution.py:44
  48.6 1.2 shard_map.55
  49.8 2.3 %collective-permute-start.15 = (f32[16,2048]{1,0:T(8,128)S(1)}, f32[16,2048]{1,0:T(8,128)S(1)}, u32[]{:S(2)}, u32[]{:S(2)}) collective-permute-start(f32[16,2048]{1,0:T(8,128)S(1)} %add.91), channel_id=1, source_target_pairs={{0,6},{2,4},{4,2},{6,0},{1,7},{3,5},{5,3},{7,1},{8,14},{10,12},{12... | collective-permute-start | bytes 393224 | tf_op jit(solution)/shard_map/ppermute | solution.py:44
  53.1 4.4 %collective-permute-done.15 = f32[16,2048]{1,0:T(8,128)S(1)} collective-permute-done((f32[16,2048]{1,0:T(8,128)S(1)}, f32[16,2048]{1,0:T(8,128)S(1)}, u32[]{:S(2)}, u32[]{:S(2)}) %collective-permute-start.15) | collective-permute-done | bytes 131104 | tf_op jit(solution)/shard_map/ppermute | solution.py:44
  58.3 0.9 collective-permute-done.13
  59.2 1.4 %collective-permute-start.16 = (f32[16,2048]{1,0:T(8,128)S(1)}, f32[16,2048]{1,0:T(8,128)S(1)}, u32[]{:S(2)}, u32[]{:S(2)}) collective-permute-start(f32[16,2048]{1,0:T(8,128)S(1)} %add_add_fusion.1.half), channel_id=1, source_target_pairs={{0,1},{1,0},{2,3},{3,2},{4,5},{5,4},{6,7},{7,6},{8,9},{9,8},{10,11... | collective-permute-start | bytes 393224 | tf_op jit(solution)/shard_map/ppermute | solution.py:44
  60.6 0.9 shard_map.56.before
  61.5 0.9 shard_map.57
  62.5 1.3 %collective-permute-start.19 = (f32[136,128]{1,0:T(8,128)S(1)}, f32[136,128]{1,0:T(8,128)S(1)}, u32[]{:S(2)}, u32[]{:S(2)}) collective-permute-start(f32[136,128]{1,0:T(8,128)S(1)} %shard_map.57), channel_id=1, source_target_pairs={{0,128},{64,192},{128,0},{192,64},{1,129},{65,193},{129,1},{193,65... | collective-permute-start | bytes 208904 | tf_op jit(solution)/shard_map/ppermute | solution.py:44
  63.8 1.7 %collective-permute-start.18 = (f32[136,128]{1,0:T(8,128)S(1)}, f32[136,128]{1,0:T(8,128)S(1)}, u32[]{:S(2)}, u32[]{:S(2)}) collective-permute-start(f32[136,128]{1,0:T(8,128)S(1)} %shard_map.57), channel_id=1, source_target_pairs={{0,192},{64,128},{128,64},{192,0},{1,193},{65,129},{129,65},{193,1... | collective-permute-start | bytes 208904 | tf_op jit(solution)/shard_map/ppermute | solution.py:44
  65.5 1.7 %collective-permute-done.19 = f32[136,128]{1,0:T(8,128)S(1)} collective-permute-done((f32[136,128]{1,0:T(8,128)S(1)}, f32[136,128]{1,0:T(8,128)S(1)}, u32[]{:S(2)}, u32[]{:S(2)}) %collective-permute-start.19) | collective-permute-done | bytes 69664 | tf_op jit(solution)/shard_map/ppermute | solution.py:44
  67.2 2.0 %collective-permute-done.18 = f32[136,128]{1,0:T(8,128)S(1)} collective-permute-done((f32[136,128]{1,0:T(8,128)S(1)}, f32[136,128]{1,0:T(8,128)S(1)}, u32[]{:S(2)}, u32[]{:S(2)}) %collective-permute-start.18) | collective-permute-done | bytes 69664 | tf_op jit(solution)/shard_map/ppermute | solution.py:44
  69.2 2.0 %collective-permute-start.22 = (f32[136,128]{1,0:T(8,128)S(1)}, f32[136,128]{1,0:T(8,128)S(1)}, u32[]{:S(2)}, u32[]{:S(2)}) collective-permute-start(f32[136,128]{1,0:T(8,128)S(1)} %add_add_fusion.4), channel_id=1, source_target_pairs={{0,24},{8,16},{16,8},{24,0},{32,56},{40,48},{48,40},{56,32},{1,25}... | collective-permute-start | bytes 208904 | tf_op jit(solution)/shard_map/ppermute | solution.py:44
  71.3 1.1 collective-permute-start.21
  72.9 1.5 %collective-permute-done.22 = f32[136,128]{1,0:T(8,128)S(1)} collective-permute-done((f32[136,128]{1,0:T(8,128)S(1)}, f32[136,128]{1,0:T(8,128)S(1)}, u32[]{:S(2)}, u32[]{:S(2)}) %collective-permute-start.22) | collective-permute-done | bytes 69664 | tf_op jit(solution)/shard_map/ppermute | solution.py:44
  74.4 2.9 %collective-permute-done.21 = f32[136,128]{1,0:T(8,128)S(1)} collective-permute-done((f32[136,128]{1,0:T(8,128)S(1)}, f32[136,128]{1,0:T(8,128)S(1)}, u32[]{:S(2)}, u32[]{:S(2)}) %collective-permute-start.21) | collective-permute-done | bytes 69664 | tf_op jit(solution)/shard_map/ppermute | solution.py:44
  77.3 3.6 %collective-permute-start.23 = (f32[136,128]{1,0:T(8,128)S(1)}, f32[136,128]{1,0:T(8,128)S(1)}, u32[]{:S(2)}, u32[]{:S(2)}) collective-permute-start(f32[136,128]{1,0:T(8,128)S(1)} %add_add_fusion.3.mine), channel_id=1, source_target_pairs={{0,48},{8,56},{16,32},{24,40},{32,16},{40,24},{48,0},{56,8},{1,49}... | collective-permute-start | bytes 208904 | tf_op jit(solution)/shard_map/ppermute | solution.py:44
  81.0 2.2 %collective-permute-done.23.theirs = f32[136,128]{1,0:T(8,128)S(1)} collective-permute-done((f32[136,128]{1,0:T(8,128)S(1)}, f32[136,128]{1,0:T(8,128)S(1)}, u32[]{:S(2)}, u32[]{:S(2)}) %collective-permute-start.23) | collective-permute-done | bytes 69664 | tf_op jit(solution)/shard_map/ppermute | solution.py:44
  83.2 1.4 %shard_map.58 = (bf16[16,1024]{1,0:T(8,128)(2,1)S(1)}, f32[16,2048]{1,0:T(8,128)S(1)}) custom-call(f32[136,128]{1,0:T(8,128)S(1)} %add_add_fusion.3.mine, f32[136,128]{1,0:T(8,128)S(1)} %collective-permute-done.23.theirs, bf16[2048,1024]{1,0:T(8,128)(2,1)S(1)} %get-tuple-element.13.held), custom_call_target="tpu_custom_call" | custom-call | flops 67108864 | bytes 4194304 | tf_op jit(solution)/shard_map/pallas_call | solution.py:234
  84.6 3.4 %collective-permute-start.24 = (f32[16,2048]{1,0:T(8,128)S(1)}, f32[16,2048]{1,0:T(8,128)S(1)}, u32[]{:S(2)}, u32[]{:S(2)}) collective-permute-start(f32[16,2048]{1,0:T(8,128)S(1)} %get-tuple-element.17), channel_id=1, source_target_pairs={{0,1},{1,0},{2,3},{3,2},{4,5},{5,4},{6,7},{7,6},{8,9},{9,8},{10,11... | collective-permute-start | bytes 393224 | tf_op jit(solution)/shard_map/ppermute | solution.py:44
  88.0 1.2 shard_map.59
  89.3 2.3 %collective-permute-start.27 = (f32[16,2048]{1,0:T(8,128)S(1)}, f32[16,2048]{1,0:T(8,128)S(1)}, u32[]{:S(2)}, u32[]{:S(2)}) collective-permute-start(f32[16,2048]{1,0:T(8,128)S(1)} %add.101), channel_id=1, source_target_pairs={{0,6},{2,4},{4,2},{6,0},{1,7},{3,5},{5,3},{7,1},{8,14},{10,12},{12... | collective-permute-start | bytes 393224 | tf_op jit(solution)/shard_map/ppermute | solution.py:44
  92.6 4.4 %collective-permute-done.27 = f32[16,2048]{1,0:T(8,128)S(1)} collective-permute-done((f32[16,2048]{1,0:T(8,128)S(1)}, f32[16,2048]{1,0:T(8,128)S(1)}, u32[]{:S(2)}, u32[]{:S(2)}) %collective-permute-start.27) | collective-permute-done | bytes 131104 | tf_op jit(solution)/shard_map/ppermute | solution.py:44
  97.8 0.9 collective-permute-done.25
  99.0 4.6 %collective-permute-start.30 = (f32[8,128]{1,0:T(8,128)S(1)}, f32[8,128]{1,0:T(8,128)S(1)}, u32[]{:S(2)}, u32[]{:S(2)}) collective-permute-start(f32[8,128]{1,0:T(8,128)S(1)} %shard_map.60), channel_id=1, source_target_pairs={{0,49},{1,48},{8,57},{9,56},{16,33},{17,32},{24,41},{25,40},{32,17... | collective-permute-start | bytes 12296 | tf_op jit(solution)/shard_map/ppermute | solution.py:44
  104.1 1.0 collective-permute-done.30
  105.1 3.1 %collective-permute-done.29 = f32[8,128]{1,0:T(8,128)S(1)} collective-permute-done((f32[8,128]{1,0:T(8,128)S(1)}, f32[8,128]{1,0:T(8,128)S(1)}, u32[]{:S(2)}, u32[]{:S(2)}) %collective-permute-start.29) | collective-permute-done | bytes 4128 | tf_op jit(solution)/shard_map/ppermute | solution.py:44
  108.2 11.4 %all_to_all.5.grams = f32[16,8,128]{2,1,0:T(8,128)S(1)} all-to-all(f32[16,8,128]{2,1,0:T(8,128)S(1)} %broadcast_in_dim.2), channel_id=1, replica_groups=mesh['x'=4,'cube'=2,'level'=4,'y'=4,'core'=2] {'x','level'}, dimensions={0} | all-to-all | bytes 131072 | tf_op jit(solution)/shard_map/all_to_all | solution.py:313
  119.6 1.0 shard_map.61
  (39 shorter events, 6.6 us)
Async XLA Ops:
  5.5 4.5 %collective-permute-start = (f32[16,2048]{1,0:T(8,128)S(1)}, f32[16,2048]{1,0:T(8,128)S(1)}, u32[]{:S(2)}, u32[]{:S(2)}) collective-permute-start(f32[16,2048]{1,0:T(8,128)S(1)} %get-tuple-element.12), channel_id=1, source_target_pairs={{0,1},{1,0},{2,3},{3,2},{4,5},{5,4},{6,7},{7,6},{8,9},{9,8},{10,11... | collective-permute-start | bytes 393224 | tf_op jit(solution)/shard_map/ppermute | solution.py:44
  10.0 9.1 %collective-permute-start.3 = (f32[16,2048]{1,0:T(8,128)S(1)}, f32[16,2048]{1,0:T(8,128)S(1)}, u32[]{:S(2)}, u32[]{:S(2)}) collective-permute-start(f32[16,2048]{1,0:T(8,128)S(1)} %add.81), channel_id=1, source_target_pairs={{0,6},{2,4},{4,2},{6,0},{1,7},{3,5},{5,3},{7,1},{8,14},{10,12},{12... | collective-permute-start | bytes 393224 | tf_op jit(solution)/shard_map/ppermute | solution.py:44
  11.1 8.0 %collective-permute-start.2 = (f32[16,2048]{1,0:T(8,128)S(1)}, f32[16,2048]{1,0:T(8,128)S(1)}, u32[]{:S(2)}, u32[]{:S(2)}) collective-permute-start(f32[16,2048]{1,0:T(8,128)S(1)} %add.81), channel_id=1, source_target_pairs={{0,4},{2,6},{4,0},{6,2},{1,5},{3,7},{5,1},{7,3},{8,12},{10,14},{12... | collective-permute-start | bytes 393224 | tf_op jit(solution)/shard_map/ppermute | solution.py:44
  11.5 7.9 %collective-permute-start.1 = (f32[16,2048]{1,0:T(8,128)S(1)}, f32[16,2048]{1,0:T(8,128)S(1)}, u32[]{:S(2)}, u32[]{:S(2)}) collective-permute-start(f32[16,2048]{1,0:T(8,128)S(1)} %add.81), channel_id=1, source_target_pairs={{0,2},{2,0},{4,6},{6,4},{1,3},{3,1},{5,7},{7,5},{8,10},{10,8},{12,... | collective-permute-start | bytes 393224 | tf_op jit(solution)/shard_map/ppermute | solution.py:44
  19.4 2.4 %collective-permute-start.4 = (f32[16,2048]{1,0:T(8,128)S(1)}, f32[16,2048]{1,0:T(8,128)S(1)}, u32[]{:S(2)}, u32[]{:S(2)}) collective-permute-start(f32[16,2048]{1,0:T(8,128)S(1)} %add_add_fusion.2.half), channel_id=1, source_target_pairs={{0,1},{1,0},{2,3},{3,2},{4,5},{5,4},{6,7},{7,6},{8,9},{9,8},{10,11... | collective-permute-start | bytes 393224 | tf_op jit(solution)/shard_map/ppermute | solution.py:44
  22.7 4.7 %collective-permute-start.7 = (f32[136,128]{1,0:T(8,128)S(1)}, f32[136,128]{1,0:T(8,128)S(1)}, u32[]{:S(2)}, u32[]{:S(2)}) collective-permute-start(f32[136,128]{1,0:T(8,128)S(1)} %shard_map.53), channel_id=1, source_target_pairs={{0,128},{64,192},{128,0},{192,64},{1,129},{65,193},{129,1},{193,65... | collective-permute-start | bytes 208904 | tf_op jit(solution)/shard_map/ppermute | solution.py:44
  24.2 5.0 %collective-permute-start.6 = (f32[136,128]{1,0:T(8,128)S(1)}, f32[136,128]{1,0:T(8,128)S(1)}, u32[]{:S(2)}, u32[]{:S(2)}) collective-permute-start(f32[136,128]{1,0:T(8,128)S(1)} %shard_map.53), channel_id=1, source_target_pairs={{0,192},{64,128},{128,64},{192,0},{1,193},{65,129},{129,65},{193,1... | collective-permute-start | bytes 208904 | tf_op jit(solution)/shard_map/ppermute | solution.py:44
  25.1 4.2 %collective-permute-start.5 = (f32[136,128]{1,0:T(8,128)S(1)}, f32[136,128]{1,0:T(8,128)S(1)}, u32[]{:S(2)}, u32[]{:S(2)}) collective-permute-start(f32[136,128]{1,0:T(8,128)S(1)} %shard_map.53), channel_id=1, source_target_pairs={{0,64},{64,0},{128,192},{192,128},{1,65},{65,1},{129,193},{193,129... | collective-permute-start | bytes 208904 | tf_op jit(solution)/shard_map/ppermute | solution.py:44
  29.3 5.5 %collective-permute-start.10 = (f32[136,128]{1,0:T(8,128)S(1)}, f32[136,128]{1,0:T(8,128)S(1)}, u32[]{:S(2)}, u32[]{:S(2)}) collective-permute-start(f32[136,128]{1,0:T(8,128)S(1)} %add_add_fusion.6), channel_id=1, source_target_pairs={{0,24},{8,16},{16,8},{24,0},{32,56},{40,48},{48,40},{56,32},{1,25}... | collective-permute-start | bytes 208904 | tf_op jit(solution)/shard_map/ppermute | solution.py:44
  33.1 4.9 %collective-permute-start.9 = (f32[136,128]{1,0:T(8,128)S(1)}, f32[136,128]{1,0:T(8,128)S(1)}, u32[]{:S(2)}, u32[]{:S(2)}) collective-permute-start(f32[136,128]{1,0:T(8,128)S(1)} %add_add_fusion.6), channel_id=1, source_target_pairs={{0,16},{8,24},{16,0},{24,8},{32,48},{40,56},{48,32},{56,40},{1,17}... | collective-permute-start | bytes 208904 | tf_op jit(solution)/shard_map/ppermute | solution.py:44
  33.1 4.9 %collective-permute-start.8 = (f32[136,128]{1,0:T(8,128)S(1)}, f32[136,128]{1,0:T(8,128)S(1)}, u32[]{:S(2)}, u32[]{:S(2)}) collective-permute-start(f32[136,128]{1,0:T(8,128)S(1)} %add_add_fusion.6), channel_id=1, source_target_pairs={{0,8},{8,0},{16,24},{24,16},{32,40},{40,32},{48,56},{56,48},{1,9},... | collective-permute-start | bytes 208904 | tf_op jit(solution)/shard_map/ppermute | solution.py:44
  38.0 6.2 %collective-permute-start.11 = (f32[136,128]{1,0:T(8,128)S(1)}, f32[136,128]{1,0:T(8,128)S(1)}, u32[]{:S(2)}, u32[]{:S(2)}) collective-permute-start(f32[136,128]{1,0:T(8,128)S(1)} %add_add_fusion.5.mine), channel_id=1, source_target_pairs={{0,48},{8,56},{16,32},{24,40},{32,16},{40,24},{48,0},{56,8},{1,49}... | collective-permute-start | bytes 208904 | tf_op jit(solution)/shard_map/ppermute | solution.py:44
  45.5 4.2 %collective-permute-start.12 = (f32[16,2048]{1,0:T(8,128)S(1)}, f32[16,2048]{1,0:T(8,128)S(1)}, u32[]{:S(2)}, u32[]{:S(2)}) collective-permute-start(f32[16,2048]{1,0:T(8,128)S(1)} %get-tuple-element.15), channel_id=1, source_target_pairs={{0,1},{1,0},{2,3},{3,2},{4,5},{5,4},{6,7},{7,6},{8,9},{9,8},{10,11... | collective-permute-start | bytes 393224 | tf_op jit(solution)/shard_map/ppermute | solution.py:44
  49.8 7.7 %collective-permute-start.15 = (f32[16,2048]{1,0:T(8,128)S(1)}, f32[16,2048]{1,0:T(8,128)S(1)}, u32[]{:S(2)}, u32[]{:S(2)}) collective-permute-start(f32[16,2048]{1,0:T(8,128)S(1)} %add.91), channel_id=1, source_target_pairs={{0,6},{2,4},{4,2},{6,0},{1,7},{3,5},{5,3},{7,1},{8,14},{10,12},{12... | collective-permute-start | bytes 393224 | tf_op jit(solution)/shard_map/ppermute | solution.py:44
  52.1 6.2 %collective-permute-start.14 = (f32[16,2048]{1,0:T(8,128)S(1)}, f32[16,2048]{1,0:T(8,128)S(1)}, u32[]{:S(2)}, u32[]{:S(2)}) collective-permute-start(f32[16,2048]{1,0:T(8,128)S(1)} %add.91), channel_id=1, source_target_pairs={{0,4},{2,6},{4,0},{6,2},{1,5},{3,7},{5,1},{7,3},{8,12},{10,14},{12... | collective-permute-start | bytes 393224 | tf_op jit(solution)/shard_map/ppermute | solution.py:44
  52.5 6.7 %collective-permute-start.13 = (f32[16,2048]{1,0:T(8,128)S(1)}, f32[16,2048]{1,0:T(8,128)S(1)}, u32[]{:S(2)}, u32[]{:S(2)}) collective-permute-start(f32[16,2048]{1,0:T(8,128)S(1)} %add.91), channel_id=1, source_target_pairs={{0,2},{2,0},{4,6},{6,4},{1,3},{3,1},{5,7},{7,5},{8,10},{10,8},{12,... | collective-permute-start | bytes 393224 | tf_op jit(solution)/shard_map/ppermute | solution.py:44
  59.2 2.4 %collective-permute-start.16 = (f32[16,2048]{1,0:T(8,128)S(1)}, f32[16,2048]{1,0:T(8,128)S(1)}, u32[]{:S(2)}, u32[]{:S(2)}) collective-permute-start(f32[16,2048]{1,0:T(8,128)S(1)} %add_add_fusion.1.half), channel_id=1, source_target_pairs={{0,1},{1,0},{2,3},{3,2},{4,5},{5,4},{6,7},{7,6},{8,9},{9,8},{10,11... | collective-permute-start | bytes 393224 | tf_op jit(solution)/shard_map/ppermute | solution.py:44
  62.5 4.7 %collective-permute-start.19 = (f32[136,128]{1,0:T(8,128)S(1)}, f32[136,128]{1,0:T(8,128)S(1)}, u32[]{:S(2)}, u32[]{:S(2)}) collective-permute-start(f32[136,128]{1,0:T(8,128)S(1)} %shard_map.57), channel_id=1, source_target_pairs={{0,128},{64,192},{128,0},{192,64},{1,129},{65,193},{129,1},{193,65... | collective-permute-start | bytes 208904 | tf_op jit(solution)/shard_map/ppermute | solution.py:44
  63.8 5.4 %collective-permute-start.18 = (f32[136,128]{1,0:T(8,128)S(1)}, f32[136,128]{1,0:T(8,128)S(1)}, u32[]{:S(2)}, u32[]{:S(2)}) collective-permute-start(f32[136,128]{1,0:T(8,128)S(1)} %shard_map.57), channel_id=1, source_target_pairs={{0,192},{64,128},{128,64},{192,0},{1,193},{65,129},{129,65},{193,1... | collective-permute-start | bytes 208904 | tf_op jit(solution)/shard_map/ppermute | solution.py:44
  65.5 3.8 %collective-permute-start.17 = (f32[136,128]{1,0:T(8,128)S(1)}, f32[136,128]{1,0:T(8,128)S(1)}, u32[]{:S(2)}, u32[]{:S(2)}) collective-permute-start(f32[136,128]{1,0:T(8,128)S(1)} %shard_map.57), channel_id=1, source_target_pairs={{0,64},{64,0},{128,192},{192,128},{1,65},{65,1},{129,193},{193,129... | collective-permute-start | bytes 208904 | tf_op jit(solution)/shard_map/ppermute | solution.py:44
  69.2 5.2 %collective-permute-start.22 = (f32[136,128]{1,0:T(8,128)S(1)}, f32[136,128]{1,0:T(8,128)S(1)}, u32[]{:S(2)}, u32[]{:S(2)}) collective-permute-start(f32[136,128]{1,0:T(8,128)S(1)} %add_add_fusion.4), channel_id=1, source_target_pairs={{0,24},{8,16},{16,8},{24,0},{32,56},{40,48},{48,40},{56,32},{1,25}... | collective-permute-start | bytes 208904 | tf_op jit(solution)/shard_map/ppermute | solution.py:44
  71.3 6.0 %collective-permute-start.21 = (f32[136,128]{1,0:T(8,128)S(1)}, f32[136,128]{1,0:T(8,128)S(1)}, u32[]{:S(2)}, u32[]{:S(2)}) collective-permute-start(f32[136,128]{1,0:T(8,128)S(1)} %add_add_fusion.4), channel_id=1, source_target_pairs={{0,16},{8,24},{16,0},{24,8},{32,48},{40,56},{48,32},{56,40},{1,17}... | collective-permute-start | bytes 208904 | tf_op jit(solution)/shard_map/ppermute | solution.py:44
  72.4 4.9 %collective-permute-start.20 = (f32[136,128]{1,0:T(8,128)S(1)}, f32[136,128]{1,0:T(8,128)S(1)}, u32[]{:S(2)}, u32[]{:S(2)}) collective-permute-start(f32[136,128]{1,0:T(8,128)S(1)} %add_add_fusion.4), channel_id=1, source_target_pairs={{0,8},{8,0},{16,24},{24,16},{32,40},{40,32},{48,56},{56,48},{1,9},... | collective-permute-start | bytes 208904 | tf_op jit(solution)/shard_map/ppermute | solution.py:44
  77.3 5.9 %collective-permute-start.23 = (f32[136,128]{1,0:T(8,128)S(1)}, f32[136,128]{1,0:T(8,128)S(1)}, u32[]{:S(2)}, u32[]{:S(2)}) collective-permute-start(f32[136,128]{1,0:T(8,128)S(1)} %add_add_fusion.3.mine), channel_id=1, source_target_pairs={{0,48},{8,56},{16,32},{24,40},{32,16},{40,24},{48,0},{56,8},{1,49}... | collective-permute-start | bytes 208904 | tf_op jit(solution)/shard_map/ppermute | solution.py:44
  84.6 4.6 %collective-permute-start.24 = (f32[16,2048]{1,0:T(8,128)S(1)}, f32[16,2048]{1,0:T(8,128)S(1)}, u32[]{:S(2)}, u32[]{:S(2)}) collective-permute-start(f32[16,2048]{1,0:T(8,128)S(1)} %get-tuple-element.17), channel_id=1, source_target_pairs={{0,1},{1,0},{2,3},{3,2},{4,5},{5,4},{6,7},{7,6},{8,9},{9,8},{10,11... | collective-permute-start | bytes 393224 | tf_op jit(solution)/shard_map/ppermute | solution.py:44
  89.3 7.7 %collective-permute-start.27 = (f32[16,2048]{1,0:T(8,128)S(1)}, f32[16,2048]{1,0:T(8,128)S(1)}, u32[]{:S(2)}, u32[]{:S(2)}) collective-permute-start(f32[16,2048]{1,0:T(8,128)S(1)} %add.101), channel_id=1, source_target_pairs={{0,6},{2,4},{4,2},{6,0},{1,7},{3,5},{5,3},{7,1},{8,14},{10,12},{12... | collective-permute-start | bytes 393224 | tf_op jit(solution)/shard_map/ppermute | solution.py:44
  91.6 6.2 %collective-permute-start.26 = (f32[16,2048]{1,0:T(8,128)S(1)}, f32[16,2048]{1,0:T(8,128)S(1)}, u32[]{:S(2)}, u32[]{:S(2)}) collective-permute-start(f32[16,2048]{1,0:T(8,128)S(1)} %add.101), channel_id=1, source_target_pairs={{0,4},{2,6},{4,0},{6,2},{1,5},{3,7},{5,1},{7,3},{8,12},{10,14},{12... | collective-permute-start | bytes 393224 | tf_op jit(solution)/shard_map/ppermute | solution.py:44
  92.0 6.7 %collective-permute-start.25 = (f32[16,2048]{1,0:T(8,128)S(1)}, f32[16,2048]{1,0:T(8,128)S(1)}, u32[]{:S(2)}, u32[]{:S(2)}) collective-permute-start(f32[16,2048]{1,0:T(8,128)S(1)} %add.101), channel_id=1, source_target_pairs={{0,2},{2,0},{4,6},{6,4},{1,3},{3,1},{5,7},{7,5},{8,10},{10,8},{12,... | collective-permute-start | bytes 393224 | tf_op jit(solution)/shard_map/ppermute | solution.py:44
  99.0 6.1 %collective-permute-start.30 = (f32[8,128]{1,0:T(8,128)S(1)}, f32[8,128]{1,0:T(8,128)S(1)}, u32[]{:S(2)}, u32[]{:S(2)}) collective-permute-start(f32[8,128]{1,0:T(8,128)S(1)} %shard_map.60), channel_id=1, source_target_pairs={{0,49},{1,48},{8,57},{9,56},{16,33},{17,32},{24,41},{25,40},{32,17... | collective-permute-start | bytes 12296 | tf_op jit(solution)/shard_map/ppermute | solution.py:44
  103.6 4.6 %collective-permute-start.29 = (f32[8,128]{1,0:T(8,128)S(1)}, f32[8,128]{1,0:T(8,128)S(1)}, u32[]{:S(2)}, u32[]{:S(2)}) collective-permute-start(f32[8,128]{1,0:T(8,128)S(1)} %shard_map.60), channel_id=1, source_target_pairs={{0,48},{1,49},{8,56},{9,57},{16,32},{17,33},{24,40},{25,41},{32,16... | collective-permute-start | bytes 12296 | tf_op jit(solution)/shard_map/ppermute | solution.py:44
  103.8 4.4 %collective-permute-start.28 = (f32[8,128]{1,0:T(8,128)S(1)}, f32[8,128]{1,0:T(8,128)S(1)}, u32[]{:S(2)}, u32[]{:S(2)}) collective-permute-start(f32[8,128]{1,0:T(8,128)S(1)} %shard_map.60), channel_id=1, source_target_pairs={{0,1},{1,0},{8,9},{9,8},{16,17},{17,16},{24,25},{25,24},{32,33},{3... | collective-permute-start | bytes 12296 | tf_op jit(solution)/shard_map/ppermute | solution.py:44

commit v10 on v8

--- a/solution.py
+++ b/solution.py
@@ -145,7 +145,6 @@
     for copy in small:
         copy.start()
     copies = load_half(affinity, held_other, other_arrived, 1 - core)
-    later = load_half(affinity, held_own, own_arrived, core)
     for copy in small:
         copy.wait()
     row = lax.broadcasted_iota(jnp.int32, (K, 128), 0)
@@ -155,6 +154,7 @@
     for start in range(0, ids_here.shape[1], 128):
         ids = jnp.broadcast_to(ids_here[:, start : start + 128], (K, 128))
         left[:, start : start + 128] = test_matrix(seeds, ids, columns)
+    later = load_half(affinity, held_own, own_arrived, core)
     project_half(left, held_other, other, None, copies)
     for copy in later:
         copy.wait()

time: 120 us -> 120 us (level)
  no operation moved by 1% of the time
where the time goes in v10:
time: 120 us
  starting transfers between devices  49.1 us (41%)
  waiting for transfers between devices  42.8 us (36%)
  Pallas kernels  15.1 us (13%)
  blocking collectives  11.6 us (10%)
    ppermute x31, starting transfers between devices, swap(): return lax.ppermute(value, axis, [(i, i ^ offset) for i in range(count)])  49.1 us
    ppermute x31, waiting for transfers between devices, swap(): return lax.ppermute(value, axis, [(i, i ^ offset) for i in range(count)])  42.8 us
    pallas_call x12, Pallas kernels, call(): pl.pallas_call(kernel, in_specs=spaces or [whole] * len(args), out_specs=...  15.1 us
    all_to_all x1, blocking collectives, body(): grams = lax.all_to_all(spread, ('x', 'level'), 0, 0)  11.6 us
  transfers between devices with their start and end apart: 31, of which 24 were waited for; matrix products, arithmetic and copies ran while one was open for 0% of the time, Pallas kernels for 5%

profile of v10, /device:TPU:1, one launch (start us, length us, event | category | flops | bytes accessed | tf_op | source)
XLA Modules:
  0.0 119.6 jit_solution(12582862739947966924)
XLA Ops:
  0.6 3.7 %shard_map.50 = (bf16[16,1024]{1,0:T(8,128)(2,1)S(1)}, bf16[2048,1024]{1,0:T(8,128)(2,1)S(1)}, bf16[2048,1024]{1,0:T(8,128)(2,1)S(1)}, f32[16,2048]{1,0:T(8,128)S(1)}) custom-call(s32[16]{0:T(128)} %seed_values.1, s32[1,1024]{1,0:T(1,128)} %bitcast.1, bf16[4096,1024]{1,0:T(8,128)(2,1)} %affinity.1), custom_call_target="tpu_custom_call" | custom-call | flops 67108864 | bytes 4194304 | tf_op jit(solution)/shard_map/pallas_call | solution.py:234
  4.3 3.3 %collective-permute-start = (f32[16,2048]{1,0:T(8,128)S(1)}, f32[16,2048]{1,0:T(8,128)S(1)}, u32[]{:S(2)}, u32[]{:S(2)}) collective-permute-start(f32[16,2048]{1,0:T(8,128)S(1)} %get-tuple-element.12), channel_id=1, source_target_pairs={{0,1},{1,0},{2,3},{3,2},{4,5},{5,4},{6,7},{7,6},{8,9},{9,8},{10,11... | collective-permute-start | bytes 393224 | tf_op jit(solution)/shard_map/ppermute | solution.py:44
  7.6 1.2 shard_map.51
  8.9 1.1 collective-permute-start.3
  10.3 1.9 %collective-permute-start.1 = (f32[16,2048]{1,0:T(8,128)S(1)}, f32[16,2048]{1,0:T(8,128)S(1)}, u32[]{:S(2)}, u32[]{:S(2)}) collective-permute-start(f32[16,2048]{1,0:T(8,128)S(1)} %add.81), channel_id=1, source_target_pairs={{0,2},{2,0},{4,6},{6,4},{1,3},{3,1},{5,7},{7,5},{8,10},{10,8},{12,... | collective-permute-start | bytes 393224 | tf_op jit(solution)/shard_map/ppermute | solution.py:44
  12.2 5.7 %collective-permute-done.3 = f32[16,2048]{1,0:T(8,128)S(1)} collective-permute-done((f32[16,2048]{1,0:T(8,128)S(1)}, f32[16,2048]{1,0:T(8,128)S(1)}, u32[]{:S(2)}, u32[]{:S(2)}) %collective-permute-start.3) | collective-permute-done | bytes 131104 | tf_op jit(solution)/shard_map/ppermute | solution.py:44
  18.3 1.4 %collective-permute-start.4 = (f32[16,2048]{1,0:T(8,128)S(1)}, f32[16,2048]{1,0:T(8,128)S(1)}, u32[]{:S(2)}, u32[]{:S(2)}) collective-permute-start(f32[16,2048]{1,0:T(8,128)S(1)} %add_add_fusion.2.half), channel_id=1, source_target_pairs={{0,1},{1,0},{2,3},{3,2},{4,5},{5,4},{6,7},{7,6},{8,9},{9,8},{10,11... | collective-permute-start | bytes 393224 | tf_op jit(solution)/shard_map/ppermute | solution.py:44
  19.6 0.9 shard_map.52.before
  20.6 0.9 shard_map.53
  21.6 1.2 %collective-permute-start.7 = (f32[136,128]{1,0:T(8,128)S(1)}, f32[136,128]{1,0:T(8,128)S(1)}, u32[]{:S(2)}, u32[]{:S(2)}) collective-permute-start(f32[136,128]{1,0:T(8,128)S(1)} %shard_map.53), channel_id=1, source_target_pairs={{0,192},{64,128},{128,64},{192,0},{1,193},{65,129},{129,65},{193,1... | collective-permute-start | bytes 208904 | tf_op jit(solution)/shard_map/ppermute | solution.py:44
  23.3 1.5 %collective-permute-start.5 = (f32[136,128]{1,0:T(8,128)S(1)}, f32[136,128]{1,0:T(8,128)S(1)}, u32[]{:S(2)}, u32[]{:S(2)}) collective-permute-start(f32[136,128]{1,0:T(8,128)S(1)} %shard_map.53), channel_id=1, source_target_pairs={{0,64},{64,0},{128,192},{192,128},{1,65},{65,1},{129,193},{193,129... | collective-permute-start | bytes 208904 | tf_op jit(solution)/shard_map/ppermute | solution.py:44
  24.8 1.1 collective-permute-done.7
  26.0 1.6 %collective-permute-done.6 = f32[136,128]{1,0:T(8,128)S(1)} collective-permute-done((f32[136,128]{1,0:T(8,128)S(1)}, f32[136,128]{1,0:T(8,128)S(1)}, u32[]{:S(2)}, u32[]{:S(2)}) %collective-permute-start.6) | collective-permute-done | bytes 69664 | tf_op jit(solution)/shard_map/ppermute | solution.py:44
  27.7 4.2 %collective-permute-start.10 = (f32[136,128]{1,0:T(8,128)S(1)}, f32[136,128]{1,0:T(8,128)S(1)}, u32[]{:S(2)}, u32[]{:S(2)}) collective-permute-start(f32[136,128]{1,0:T(8,128)S(1)} %add_add_fusion.6), channel_id=1, source_target_pairs={{0,24},{8,16},{16,8},{24,0},{32,56},{40,48},{48,40},{56,32},{1,25}... | collective-permute-start | bytes 208904 | tf_op jit(solution)/shard_map/ppermute | solution.py:44
  32.3 1.3 %collective-permute-done.10 = f32[136,128]{1,0:T(8,128)S(1)} collective-permute-done((f32[136,128]{1,0:T(8,128)S(1)}, f32[136,128]{1,0:T(8,128)S(1)}, u32[]{:S(2)}, u32[]{:S(2)}) %collective-permute-start.10) | collective-permute-done | bytes 69664 | tf_op jit(solution)/shard_map/ppermute | solution.py:44
  33.6 3.3 %collective-permute-done.9 = f32[136,128]{1,0:T(8,128)S(1)} collective-permute-done((f32[136,128]{1,0:T(8,128)S(1)}, f32[136,128]{1,0:T(8,128)S(1)}, u32[]{:S(2)}, u32[]{:S(2)}) %collective-permute-start.9) | collective-permute-done | bytes 69664 | tf_op jit(solution)/shard_map/ppermute | solution.py:44
  36.9 3.1 %collective-permute-start.11 = (f32[136,128]{1,0:T(8,128)S(1)}, f32[136,128]{1,0:T(8,128)S(1)}, u32[]{:S(2)}, u32[]{:S(2)}) collective-permute-start(f32[136,128]{1,0:T(8,128)S(1)} %add_add_fusion.5.mine), channel_id=1, source_target_pairs={{0,48},{8,56},{16,32},{24,40},{32,16},{40,24},{48,0},{56,8},{1,49}... | collective-permute-start | bytes 208904 | tf_op jit(solution)/shard_map/ppermute | solution.py:44
  40.1 3.0 %collective-permute-done.11.theirs = f32[136,128]{1,0:T(8,128)S(1)} collective-permute-done((f32[136,128]{1,0:T(8,128)S(1)}, f32[136,128]{1,0:T(8,128)S(1)}, u32[]{:S(2)}, u32[]{:S(2)}) %collective-permute-start.11) | collective-permute-done | bytes 69664 | tf_op jit(solution)/shard_map/ppermute | solution.py:44
  43.0 1.4 %shard_map.54 = (bf16[16,1024]{1,0:T(8,128)(2,1)S(1)}, f32[16,2048]{1,0:T(8,128)S(1)}) custom-call(f32[136,128]{1,0:T(8,128)S(1)} %add_add_fusion.5.mine, f32[136,128]{1,0:T(8,128)S(1)} %collective-permute-done.11.theirs, bf16[2048,1024]{1,0:T(8,128)(2,1)S(1)} %get-tuple-element.13.held), custom_call_target="tpu_custom_call" | custom-call | flops 67108864 | bytes 4194304 | tf_op jit(solution)/shard_map/pallas_call | solution.py:234
  44.4 3.4 %collective-permute-start.12 = (f32[16,2048]{1,0:T(8,128)S(1)}, f32[16,2048]{1,0:T(8,128)S(1)}, u32[]{:S(2)}, u32[]{:S(2)}) collective-permute-start(f32[16,2048]{1,0:T(8,128)S(1)} %get-tuple-element.15), channel_id=1, source_target_pairs={{0,1},{1,0},{2,3},{3,2},{4,5},{5,4},{6,7},{7,6},{8,9},{9,8},{10,11... | collective-permute-start | bytes 393224 | tf_op jit(solution)/shard_map/ppermute | solution.py:44
  47.8 1.2 shard_map.55
  49.0 2.3 %collective-permute-start.15 = (f32[16,2048]{1,0:T(8,128)S(1)}, f32[16,2048]{1,0:T(8,128)S(1)}, u32[]{:S(2)}, u32[]{:S(2)}) collective-permute-start(f32[16,2048]{1,0:T(8,128)S(1)} %add.91), channel_id=1, source_target_pairs={{0,6},{2,4},{4,2},{6,0},{1,7},{3,5},{5,3},{7,1},{8,14},{10,12},{12... | collective-permute-start | bytes 393224 | tf_op jit(solution)/shard_map/ppermute | solution.py:44
  52.4 4.4 %collective-permute-done.15 = f32[16,2048]{1,0:T(8,128)S(1)} collective-permute-done((f32[16,2048]{1,0:T(8,128)S(1)}, f32[16,2048]{1,0:T(8,128)S(1)}, u32[]{:S(2)}, u32[]{:S(2)}) %collective-permute-start.15) | collective-permute-done | bytes 131104 | tf_op jit(solution)/shard_map/ppermute | solution.py:44
  57.5 0.9 collective-permute-done.13
  58.4 1.4 %collective-permute-start.16 = (f32[16,2048]{1,0:T(8,128)S(1)}, f32[16,2048]{1,0:T(8,128)S(1)}, u32[]{:S(2)}, u32[]{:S(2)}) collective-permute-start(f32[16,2048]{1,0:T(8,128)S(1)} %add_add_fusion.1.half), channel_id=1, source_target_pairs={{0,1},{1,0},{2,3},{3,2},{4,5},{5,4},{6,7},{7,6},{8,9},{9,8},{10,11... | collective-permute-start | bytes 393224 | tf_op jit(solution)/shard_map/ppermute | solution.py:44
  59.8 0.9 shard_map.56.before
  60.8 0.9 shard_map.57
  61.7 1.2 collective-permute-start.19
  63.7 1.4 %collective-permute-start.17 = (f32[136,128]{1,0:T(8,128)S(1)}, f32[136,128]{1,0:T(8,128)S(1)}, u32[]{:S(2)}, u32[]{:S(2)}) collective-permute-start(f32[136,128]{1,0:T(8,128)S(1)} %shard_map.57), channel_id=1, source_target_pairs={{0,64},{64,0},{128,192},{192,128},{1,65},{65,1},{129,193},{193,129... | collective-permute-start | bytes 208904 | tf_op jit(solution)/shard_map/ppermute | solution.py:44
  65.0 1.1 collective-permute-done.19
  66.1 1.5 %collective-permute-done.18 = f32[136,128]{1,0:T(8,128)S(1)} collective-permute-done((f32[136,128]{1,0:T(8,128)S(1)}, f32[136,128]{1,0:T(8,128)S(1)}, u32[]{:S(2)}, u32[]{:S(2)}) %collective-permute-start.18) | collective-permute-done | bytes 69664 | tf_op jit(solution)/shard_map/ppermute | solution.py:44
  68.0 1.9 %collective-permute-start.22 = (f32[136,128]{1,0:T(8,128)S(1)}, f32[136,128]{1,0:T(8,128)S(1)}, u32[]{:S(2)}, u32[]{:S(2)}) collective-permute-start(f32[136,128]{1,0:T(8,128)S(1)} %add_add_fusion.4), channel_id=1, source_target_pairs={{0,24},{8,16},{16,8},{24,0},{32,56},{40,48},{48,40},{56,32},{1,25}... | collective-permute-start | bytes 208904 | tf_op jit(solution)/shard_map/ppermute | solution.py:44
  69.9 1.0 collective-permute-start.21
  71.7 1.5 %collective-permute-done.22 = f32[136,128]{1,0:T(8,128)S(1)} collective-permute-done((f32[136,128]{1,0:T(8,128)S(1)}, f32[136,128]{1,0:T(8,128)S(1)}, u32[]{:S(2)}, u32[]{:S(2)}) %collective-permute-start.22) | collective-permute-done | bytes 69664 | tf_op jit(solution)/shard_map/ppermute | solution.py:44
  73.2 2.6 %collective-permute-done.21 = f32[136,128]{1,0:T(8,128)S(1)} collective-permute-done((f32[136,128]{1,0:T(8,128)S(1)}, f32[136,128]{1,0:T(8,128)S(1)}, u32[]{:S(2)}, u32[]{:S(2)}) %collective-permute-start.21) | collective-permute-done | bytes 69664 | tf_op jit(solution)/shard_map/ppermute | solution.py:44
  75.8 2.9 %collective-permute-start.23 = (f32[136,128]{1,0:T(8,128)S(1)}, f32[136,128]{1,0:T(8,128)S(1)}, u32[]{:S(2)}, u32[]{:S(2)}) collective-permute-start(f32[136,128]{1,0:T(8,128)S(1)} %add_add_fusion.3.mine), channel_id=1, source_target_pairs={{0,48},{8,56},{16,32},{24,40},{32,16},{40,24},{48,0},{56,8},{1,49}... | collective-permute-start | bytes 208904 | tf_op jit(solution)/shard_map/ppermute | solution.py:44
  78.7 3.1 %collective-permute-done.23.theirs = f32[136,128]{1,0:T(8,128)S(1)} collective-permute-done((f32[136,128]{1,0:T(8,128)S(1)}, f32[136,128]{1,0:T(8,128)S(1)}, u32[]{:S(2)}, u32[]{:S(2)}) %collective-permute-start.23) | collective-permute-done | bytes 69664 | tf_op jit(solution)/shard_map/ppermute | solution.py:44
  81.7 1.4 %shard_map.58 = (bf16[16,1024]{1,0:T(8,128)(2,1)S(1)}, f32[16,2048]{1,0:T(8,128)S(1)}) custom-call(f32[136,128]{1,0:T(8,128)S(1)} %add_add_fusion.3.mine, f32[136,128]{1,0:T(8,128)S(1)} %collective-permute-done.23.theirs, bf16[2048,1024]{1,0:T(8,128)(2,1)S(1)} %get-tuple-element.13.held), custom_call_target="tpu_custom_call" | custom-call | flops 67108864 | bytes 4194304 | tf_op jit(solution)/shard_map/pallas_call | solution.py:234
  83.1 3.4 %collective-permute-start.24 = (f32[16,2048]{1,0:T(8,128)S(1)}, f32[16,2048]{1,0:T(8,128)S(1)}, u32[]{:S(2)}, u32[]{:S(2)}) collective-permute-start(f32[16,2048]{1,0:T(8,128)S(1)} %get-tuple-element.17), channel_id=1, source_target_pairs={{0,1},{1,0},{2,3},{3,2},{4,5},{5,4},{6,7},{7,6},{8,9},{9,8},{10,11... | collective-permute-start | bytes 393224 | tf_op jit(solution)/shard_map/ppermute | solution.py:44
  86.5 1.2 shard_map.59
  87.7 2.3 %collective-permute-start.27 = (f32[16,2048]{1,0:T(8,128)S(1)}, f32[16,2048]{1,0:T(8,128)S(1)}, u32[]{:S(2)}, u32[]{:S(2)}) collective-permute-start(f32[16,2048]{1,0:T(8,128)S(1)} %add.101), channel_id=1, source_target_pairs={{0,6},{2,4},{4,2},{6,0},{1,7},{3,5},{5,3},{7,1},{8,14},{10,12},{12... | collective-permute-start | bytes 393224 | tf_op jit(solution)/shard_map/ppermute | solution.py:44
  91.1 4.4 %collective-permute-done.27 = f32[16,2048]{1,0:T(8,128)S(1)} collective-permute-done((f32[16,2048]{1,0:T(8,128)S(1)}, f32[16,2048]{1,0:T(8,128)S(1)}, u32[]{:S(2)}, u32[]{:S(2)}) %collective-permute-start.27) | collective-permute-done | bytes 131104 | tf_op jit(solution)/shard_map/ppermute | solution.py:44
  96.2 0.9 collective-permute-done.25
  97.5 4.9 %collective-permute-start.30 = (f32[8,128]{1,0:T(8,128)S(1)}, f32[8,128]{1,0:T(8,128)S(1)}, u32[]{:S(2)}, u32[]{:S(2)}) collective-permute-start(f32[8,128]{1,0:T(8,128)S(1)} %shard_map.60), channel_id=1, source_target_pairs={{0,49},{1,48},{8,57},{9,56},{16,33},{17,32},{24,41},{25,40},{32,17... | collective-permute-start | bytes 12296 | tf_op jit(solution)/shard_map/ppermute | solution.py:44
  102.8 0.8 collective-permute-done.30
  103.7 3.3 %collective-permute-done.29 = f32[8,128]{1,0:T(8,128)S(1)} collective-permute-done((f32[8,128]{1,0:T(8,128)S(1)}, f32[8,128]{1,0:T(8,128)S(1)}, u32[]{:S(2)}, u32[]{:S(2)}) %collective-permute-start.29) | collective-permute-done | bytes 4128 | tf_op jit(solution)/shard_map/ppermute | solution.py:44
  107.0 11.6 %all_to_all.5.grams = f32[16,8,128]{2,1,0:T(8,128)S(1)} all-to-all(f32[16,8,128]{2,1,0:T(8,128)S(1)} %broadcast_in_dim.2), channel_id=1, replica_groups=mesh['x'=4,'cube'=2,'level'=4,'y'=4,'core'=2] {'x','level'}, dimensions={0} | all-to-all | bytes 131072 | tf_op jit(solution)/shard_map/all_to_all | solution.py:313
  118.6 1.0 shard_map.61
  (39 shorter events, 8.4 us)
Async XLA Ops:
  4.3 4.5 %collective-permute-start = (f32[16,2048]{1,0:T(8,128)S(1)}, f32[16,2048]{1,0:T(8,128)S(1)}, u32[]{:S(2)}, u32[]{:S(2)}) collective-permute-start(f32[16,2048]{1,0:T(8,128)S(1)} %get-tuple-element.12), channel_id=1, source_target_pairs={{0,1},{1,0},{2,3},{3,2},{4,5},{5,4},{6,7},{7,6},{8,9},{9,8},{10,11... | collective-permute-start | bytes 393224 | tf_op jit(solution)/shard_map/ppermute | solution.py:44
  8.9 9.1 %collective-permute-start.3 = (f32[16,2048]{1,0:T(8,128)S(1)}, f32[16,2048]{1,0:T(8,128)S(1)}, u32[]{:S(2)}, u32[]{:S(2)}) collective-permute-start(f32[16,2048]{1,0:T(8,128)S(1)} %add.81), channel_id=1, source_target_pairs={{0,6},{2,4},{4,2},{6,0},{1,7},{3,5},{5,3},{7,1},{8,14},{10,12},{12... | collective-permute-start | bytes 393224 | tf_op jit(solution)/shard_map/ppermute | solution.py:44
  10.0 8.0 %collective-permute-start.2 = (f32[16,2048]{1,0:T(8,128)S(1)}, f32[16,2048]{1,0:T(8,128)S(1)}, u32[]{:S(2)}, u32[]{:S(2)}) collective-permute-start(f32[16,2048]{1,0:T(8,128)S(1)} %add.81), channel_id=1, source_target_pairs={{0,4},{2,6},{4,0},{6,2},{1,5},{3,7},{5,1},{7,3},{8,12},{10,14},{12... | collective-permute-start | bytes 393224 | tf_op jit(solution)/shard_map/ppermute | solution.py:44
  10.3 7.9 %collective-permute-start.1 = (f32[16,2048]{1,0:T(8,128)S(1)}, f32[16,2048]{1,0:T(8,128)S(1)}, u32[]{:S(2)}, u32[]{:S(2)}) collective-permute-start(f32[16,2048]{1,0:T(8,128)S(1)} %add.81), channel_id=1, source_target_pairs={{0,2},{2,0},{4,6},{6,4},{1,3},{3,1},{5,7},{7,5},{8,10},{10,8},{12,... | collective-permute-start | bytes 393224 | tf_op jit(solution)/shard_map/ppermute | solution.py:44
  18.3 2.4 %collective-permute-start.4 = (f32[16,2048]{1,0:T(8,128)S(1)}, f32[16,2048]{1,0:T(8,128)S(1)}, u32[]{:S(2)}, u32[]{:S(2)}) collective-permute-start(f32[16,2048]{1,0:T(8,128)S(1)} %add_add_fusion.2.half), channel_id=1, source_target_pairs={{0,1},{1,0},{2,3},{3,2},{4,5},{5,4},{6,7},{7,6},{8,9},{9,8},{10,11... | collective-permute-start | bytes 393224 | tf_op jit(solution)/shard_map/ppermute | solution.py:44
  21.6 4.4 %collective-permute-start.7 = (f32[136,128]{1,0:T(8,128)S(1)}, f32[136,128]{1,0:T(8,128)S(1)}, u32[]{:S(2)}, u32[]{:S(2)}) collective-permute-start(f32[136,128]{1,0:T(8,128)S(1)} %shard_map.53), channel_id=1, source_target_pairs={{0,192},{64,128},{128,64},{192,0},{1,193},{65,129},{129,65},{193,1... | collective-permute-start | bytes 208904 | tf_op jit(solution)/shard_map/ppermute | solution.py:44
  22.8 4.7 %collective-permute-start.6 = (f32[136,128]{1,0:T(8,128)S(1)}, f32[136,128]{1,0:T(8,128)S(1)}, u32[]{:S(2)}, u32[]{:S(2)}) collective-permute-start(f32[136,128]{1,0:T(8,128)S(1)} %shard_map.53), channel_id=1, source_target_pairs={{0,128},{64,192},{128,0},{192,64},{1,129},{65,193},{129,1},{193,65... | collective-permute-start | bytes 208904 | tf_op jit(solution)/shard_map/ppermute | solution.py:44
  23.3 4.3 %collective-permute-start.5 = (f32[136,128]{1,0:T(8,128)S(1)}, f32[136,128]{1,0:T(8,128)S(1)}, u32[]{:S(2)}, u32[]{:S(2)}) collective-permute-start(f32[136,128]{1,0:T(8,128)S(1)} %shard_map.53), channel_id=1, source_target_pairs={{0,64},{64,0},{128,192},{192,128},{1,65},{65,1},{129,193},{193,129... | collective-permute-start | bytes 208904 | tf_op jit(solution)/shard_map/ppermute | solution.py:44
  27.7 5.9 %collective-permute-start.10 = (f32[136,128]{1,0:T(8,128)S(1)}, f32[136,128]{1,0:T(8,128)S(1)}, u32[]{:S(2)}, u32[]{:S(2)}) collective-permute-start(f32[136,128]{1,0:T(8,128)S(1)} %add_add_fusion.6), channel_id=1, source_target_pairs={{0,24},{8,16},{16,8},{24,0},{32,56},{40,48},{48,40},{56,32},{1,25}... | collective-permute-start | bytes 208904 | tf_op jit(solution)/shard_map/ppermute | solution.py:44
  31.9 5.0 %collective-permute-start.9 = (f32[136,128]{1,0:T(8,128)S(1)}, f32[136,128]{1,0:T(8,128)S(1)}, u32[]{:S(2)}, u32[]{:S(2)}) collective-permute-start(f32[136,128]{1,0:T(8,128)S(1)} %add_add_fusion.6), channel_id=1, source_target_pairs={{0,16},{8,24},{16,0},{24,8},{32,48},{40,56},{48,32},{56,40},{1,17}... | collective-permute-start | bytes 208904 | tf_op jit(solution)/shard_map/ppermute | solution.py:44
  31.9 5.0 %collective-permute-start.8 = (f32[136,128]{1,0:T(8,128)S(1)}, f32[136,128]{1,0:T(8,128)S(1)}, u32[]{:S(2)}, u32[]{:S(2)}) collective-permute-start(f32[136,128]{1,0:T(8,128)S(1)} %add_add_fusion.6), channel_id=1, source_target_pairs={{0,8},{8,0},{16,24},{24,16},{32,40},{40,32},{48,56},{56,48},{1,9},... | collective-permute-start | bytes 208904 | tf_op jit(solution)/shard_map/ppermute | solution.py:44
  36.9 6.1 %collective-permute-start.11 = (f32[136,128]{1,0:T(8,128)S(1)}, f32[136,128]{1,0:T(8,128)S(1)}, u32[]{:S(2)}, u32[]{:S(2)}) collective-permute-start(f32[136,128]{1,0:T(8,128)S(1)} %add_add_fusion.5.mine), channel_id=1, source_target_pairs={{0,48},{8,56},{16,32},{24,40},{32,16},{40,24},{48,0},{56,8},{1,49}... | collective-permute-start | bytes 208904 | tf_op jit(solution)/shard_map/ppermute | solution.py:44
  44.4 4.6 %collective-permute-start.12 = (f32[16,2048]{1,0:T(8,128)S(1)}, f32[16,2048]{1,0:T(8,128)S(1)}, u32[]{:S(2)}, u32[]{:S(2)}) collective-permute-start(f32[16,2048]{1,0:T(8,128)S(1)} %get-tuple-element.15), channel_id=1, source_target_pairs={{0,1},{1,0},{2,3},{3,2},{4,5},{5,4},{6,7},{7,6},{8,9},{9,8},{10,11... | collective-permute-start | bytes 393224 | tf_op jit(solution)/shard_map/ppermute | solution.py:44
  49.0 7.7 %collective-permute-start.15 = (f32[16,2048]{1,0:T(8,128)S(1)}, f32[16,2048]{1,0:T(8,128)S(1)}, u32[]{:S(2)}, u32[]{:S(2)}) collective-permute-start(f32[16,2048]{1,0:T(8,128)S(1)} %add.91), channel_id=1, source_target_pairs={{0,6},{2,4},{4,2},{6,0},{1,7},{3,5},{5,3},{7,1},{8,14},{10,12},{12... | collective-permute-start | bytes 393224 | tf_op jit(solution)/shard_map/ppermute | solution.py:44
  51.3 6.2 %collective-permute-start.14 = (f32[16,2048]{1,0:T(8,128)S(1)}, f32[16,2048]{1,0:T(8,128)S(1)}, u32[]{:S(2)}, u32[]{:S(2)}) collective-permute-start(f32[16,2048]{1,0:T(8,128)S(1)} %add.91), channel_id=1, source_target_pairs={{0,4},{2,6},{4,0},{6,2},{1,5},{3,7},{5,1},{7,3},{8,12},{10,14},{12... | collective-permute-start | bytes 393224 | tf_op jit(solution)/shard_map/ppermute | solution.py:44
  51.7 6.7 %collective-permute-start.13 = (f32[16,2048]{1,0:T(8,128)S(1)}, f32[16,2048]{1,0:T(8,128)S(1)}, u32[]{:S(2)}, u32[]{:S(2)}) collective-permute-start(f32[16,2048]{1,0:T(8,128)S(1)} %add.91), channel_id=1, source_target_pairs={{0,2},{2,0},{4,6},{6,4},{1,3},{3,1},{5,7},{7,5},{8,10},{10,8},{12,... | collective-permute-start | bytes 393224 | tf_op jit(solution)/shard_map/ppermute | solution.py:44
  58.4 2.4 %collective-permute-start.16 = (f32[16,2048]{1,0:T(8,128)S(1)}, f32[16,2048]{1,0:T(8,128)S(1)}, u32[]{:S(2)}, u32[]{:S(2)}) collective-permute-start(f32[16,2048]{1,0:T(8,128)S(1)} %add_add_fusion.1.half), channel_id=1, source_target_pairs={{0,1},{1,0},{2,3},{3,2},{4,5},{5,4},{6,7},{7,6},{8,9},{9,8},{10,11... | collective-permute-start | bytes 393224 | tf_op jit(solution)/shard_map/ppermute | solution.py:44
  61.7 4.4 %collective-permute-start.19 = (f32[136,128]{1,0:T(8,128)S(1)}, f32[136,128]{1,0:T(8,128)S(1)}, u32[]{:S(2)}, u32[]{:S(2)}) collective-permute-start(f32[136,128]{1,0:T(8,128)S(1)} %shard_map.57), channel_id=1, source_target_pairs={{0,192},{64,128},{128,64},{192,0},{1,193},{65,129},{129,65},{193,1... | collective-permute-start | bytes 208904 | tf_op jit(solution)/shard_map/ppermute | solution.py:44
  62.9 4.8 %collective-permute-start.18 = (f32[136,128]{1,0:T(8,128)S(1)}, f32[136,128]{1,0:T(8,128)S(1)}, u32[]{:S(2)}, u32[]{:S(2)}) collective-permute-start(f32[136,128]{1,0:T(8,128)S(1)} %shard_map.57), channel_id=1, source_target_pairs={{0,128},{64,192},{128,0},{192,64},{1,129},{65,193},{129,1},{193,65... | collective-permute-start | bytes 208904 | tf_op jit(solution)/shard_map/ppermute | solution.py:44
  63.7 4.3 %collective-permute-start.17 = (f32[136,128]{1,0:T(8,128)S(1)}, f32[136,128]{1,0:T(8,128)S(1)}, u32[]{:S(2)}, u32[]{:S(2)}) collective-permute-start(f32[136,128]{1,0:T(8,128)S(1)} %shard_map.57), channel_id=1, source_target_pairs={{0,64},{64,0},{128,192},{192,128},{1,65},{65,1},{129,193},{193,129... | collective-permute-start | bytes 208904 | tf_op jit(solution)/shard_map/ppermute | solution.py:44
  68.0 5.2 %collective-permute-start.22 = (f32[136,128]{1,0:T(8,128)S(1)}, f32[136,128]{1,0:T(8,128)S(1)}, u32[]{:S(2)}, u32[]{:S(2)}) collective-permute-start(f32[136,128]{1,0:T(8,128)S(1)} %add_add_fusion.4), channel_id=1, source_target_pairs={{0,24},{8,16},{16,8},{24,0},{32,56},{40,48},{48,40},{56,32},{1,25}... | collective-permute-start | bytes 208904 | tf_op jit(solution)/shard_map/ppermute | solution.py:44
  69.9 5.9 %collective-permute-start.21 = (f32[136,128]{1,0:T(8,128)S(1)}, f32[136,128]{1,0:T(8,128)S(1)}, u32[]{:S(2)}, u32[]{:S(2)}) collective-permute-start(f32[136,128]{1,0:T(8,128)S(1)} %add_add_fusion.4), channel_id=1, source_target_pairs={{0,16},{8,24},{16,0},{24,8},{32,48},{40,56},{48,32},{56,40},{1,17}... | collective-permute-start | bytes 208904 | tf_op jit(solution)/shard_map/ppermute | solution.py:44
  70.9 4.9 %collective-permute-start.20 = (f32[136,128]{1,0:T(8,128)S(1)}, f32[136,128]{1,0:T(8,128)S(1)}, u32[]{:S(2)}, u32[]{:S(2)}) collective-permute-start(f32[136,128]{1,0:T(8,128)S(1)} %add_add_fusion.4), channel_id=1, source_target_pairs={{0,8},{8,0},{16,24},{24,16},{32,40},{40,32},{48,56},{56,48},{1,9},... | collective-permute-start | bytes 208904 | tf_op jit(solution)/shard_map/ppermute | solution.py:44
  75.8 6.0 %collective-permute-start.23 = (f32[136,128]{1,0:T(8,128)S(1)}, f32[136,128]{1,0:T(8,128)S(1)}, u32[]{:S(2)}, u32[]{:S(2)}) collective-permute-start(f32[136,128]{1,0:T(8,128)S(1)} %add_add_fusion.3.mine), channel_id=1, source_target_pairs={{0,48},{8,56},{16,32},{24,40},{32,16},{40,24},{48,0},{56,8},{1,49}... | collective-permute-start | bytes 208904 | tf_op jit(solution)/shard_map/ppermute | solution.py:44
  83.1 4.6 %collective-permute-start.24 = (f32[16,2048]{1,0:T(8,128)S(1)}, f32[16,2048]{1,0:T(8,128)S(1)}, u32[]{:S(2)}, u32[]{:S(2)}) collective-permute-start(f32[16,2048]{1,0:T(8,128)S(1)} %get-tuple-element.17), channel_id=1, source_target_pairs={{0,1},{1,0},{2,3},{3,2},{4,5},{5,4},{6,7},{7,6},{8,9},{9,8},{10,11... | collective-permute-start | bytes 393224 | tf_op jit(solution)/shard_map/ppermute | solution.py:44
  87.7 7.7 %collective-permute-start.27 = (f32[16,2048]{1,0:T(8,128)S(1)}, f32[16,2048]{1,0:T(8,128)S(1)}, u32[]{:S(2)}, u32[]{:S(2)}) collective-permute-start(f32[16,2048]{1,0:T(8,128)S(1)} %add.101), channel_id=1, source_target_pairs={{0,6},{2,4},{4,2},{6,0},{1,7},{3,5},{5,3},{7,1},{8,14},{10,12},{12... | collective-permute-start | bytes 393224 | tf_op jit(solution)/shard_map/ppermute | solution.py:44
  90.0 6.2 %collective-permute-start.26 = (f32[16,2048]{1,0:T(8,128)S(1)}, f32[16,2048]{1,0:T(8,128)S(1)}, u32[]{:S(2)}, u32[]{:S(2)}) collective-permute-start(f32[16,2048]{1,0:T(8,128)S(1)} %add.101), channel_id=1, source_target_pairs={{0,4},{2,6},{4,0},{6,2},{1,5},{3,7},{5,1},{7,3},{8,12},{10,14},{12... | collective-permute-start | bytes 393224 | tf_op jit(solution)/shard_map/ppermute | solution.py:44
  90.4 6.7 %collective-permute-start.25 = (f32[16,2048]{1,0:T(8,128)S(1)}, f32[16,2048]{1,0:T(8,128)S(1)}, u32[]{:S(2)}, u32[]{:S(2)}) collective-permute-start(f32[16,2048]{1,0:T(8,128)S(1)} %add.101), channel_id=1, source_target_pairs={{0,2},{2,0},{4,6},{6,4},{1,3},{3,1},{5,7},{7,5},{8,10},{10,8},{12,... | collective-permute-start | bytes 393224 | tf_op jit(solution)/shard_map/ppermute | solution.py:44
  97.5 6.2 %collective-permute-start.30 = (f32[8,128]{1,0:T(8,128)S(1)}, f32[8,128]{1,0:T(8,128)S(1)}, u32[]{:S(2)}, u32[]{:S(2)}) collective-permute-start(f32[8,128]{1,0:T(8,128)S(1)} %shard_map.60), channel_id=1, source_target_pairs={{0,49},{1,48},{8,57},{9,56},{16,33},{17,32},{24,41},{25,40},{32,17... | collective-permute-start | bytes 12296 | tf_op jit(solution)/shard_map/ppermute | solution.py:44
  102.4 4.6 %collective-permute-start.29 = (f32[8,128]{1,0:T(8,128)S(1)}, f32[8,128]{1,0:T(8,128)S(1)}, u32[]{:S(2)}, u32[]{:S(2)}) collective-permute-start(f32[8,128]{1,0:T(8,128)S(1)} %shard_map.60), channel_id=1, source_target_pairs={{0,48},{1,49},{8,56},{9,57},{16,32},{17,33},{24,40},{25,41},{32,16... | collective-permute-start | bytes 12296 | tf_op jit(solution)/shard_map/ppermute | solution.py:44
  102.4 4.6 %collective-permute-start.28 = (f32[8,128]{1,0:T(8,128)S(1)}, f32[8,128]{1,0:T(8,128)S(1)}, u32[]{:S(2)}, u32[]{:S(2)}) collective-permute-start(f32[8,128]{1,0:T(8,128)S(1)} %shard_map.60), channel_id=1, source_target_pairs={{0,1},{1,0},{8,9},{9,8},{16,17},{17,16},{24,25},{25,24},{32,33},{3... | collective-permute-start | bytes 12296 | tf_op jit(solution)/shard_map/ppermute | solution.py:44

commit v11 on v10

--- a/solution.py
+++ b/solution.py
@@ -152,9 +152,10 @@
     for k in range(K):
         seeds = jnp.where(row == k, seeds_here[k], seeds)
     for start in range(0, ids_here.shape[1], 128):
+        if start == ids_here.shape[1] // 2:
+            later = load_half(affinity, held_own, own_arrived, core)
         ids = jnp.broadcast_to(ids_here[:, start : start + 128], (K, 128))
         left[:, start : start + 128] = test_matrix(seeds, ids, columns)
-    later = load_half(affinity, held_own, own_arrived, core)
     project_half(left, held_other, other, None, copies)
     for copy in later:
         copy.wait()

time: 120 us -> 120 us (level)
  no operation moved by 1% of the time
where the time goes in v11:
time: 120 us
  starting transfers between devices  49.1 us (41%)
  waiting for transfers between devices  42.8 us (36%)
  Pallas kernels  15.1 us (13%)
  blocking collectives  11.6 us (10%)
    ppermute x31, starting transfers between devices, swap(): return lax.ppermute(value, axis, [(i, i ^ offset) for i in range(count)])  49.1 us
    ppermute x31, waiting for transfers between devices, swap(): return lax.ppermute(value, axis, [(i, i ^ offset) for i in range(count)])  42.8 us
    pallas_call x12, Pallas kernels, call(): pl.pallas_call(kernel, in_specs=spaces or [whole] * len(args), out_specs=...  15.1 us
    all_to_all x1, blocking collectives, body(): grams = lax.all_to_all(spread, ('x', 'level'), 0, 0)  11.6 us
  transfers between devices with their start and end apart: 31, of which 24 were waited for; matrix products, arithmetic and copies ran while one was open for 0% of the time, Pallas kernels for 5%

profile of v11, /device:TPU:1, one launch (start us, length us, event | category | flops | bytes accessed | tf_op | source)
XLA Modules:
  0.0 119.6 jit_solution(15258476522608276821)
XLA Ops:
  0.6 3.7 %shard_map.50 = (bf16[16,1024]{1,0:T(8,128)(2,1)S(1)}, bf16[2048,1024]{1,0:T(8,128)(2,1)S(1)}, bf16[2048,1024]{1,0:T(8,128)(2,1)S(1)}, f32[16,2048]{1,0:T(8,128)S(1)}) custom-call(s32[16]{0:T(128)} %seed_values.1, s32[1,1024]{1,0:T(1,128)} %bitcast.1, bf16[4096,1024]{1,0:T(8,128)(2,1)} %affinity.1), custom_call_target="tpu_custom_call" | custom-call | flops 67108864 | bytes 4194304 | tf_op jit(solution)/shard_map/pallas_call | solution.py:235
  4.3 3.3 %collective-permute-start = (f32[16,2048]{1,0:T(8,128)S(1)}, f32[16,2048]{1,0:T(8,128)S(1)}, u32[]{:S(2)}, u32[]{:S(2)}) collective-permute-start(f32[16,2048]{1,0:T(8,128)S(1)} %get-tuple-element.12), channel_id=1, source_target_pairs={{0,1},{1,0},{2,3},{3,2},{4,5},{5,4},{6,7},{7,6},{8,9},{9,8},{10,11... | collective-permute-start | bytes 393224 | tf_op jit(solution)/shard_map/ppermute | solution.py:44
  7.6 1.2 shard_map.51
  8.9 1.1 collective-permute-start.3
  10.3 1.9 %collective-permute-start.1 = (f32[16,2048]{1,0:T(8,128)S(1)}, f32[16,2048]{1,0:T(8,128)S(1)}, u32[]{:S(2)}, u32[]{:S(2)}) collective-permute-start(f32[16,2048]{1,0:T(8,128)S(1)} %add.81), channel_id=1, source_target_pairs={{0,2},{2,0},{4,6},{6,4},{1,3},{3,1},{5,7},{7,5},{8,10},{10,8},{12,... | collective-permute-start | bytes 393224 | tf_op jit(solution)/shard_map/ppermute | solution.py:44
  12.2 5.7 %collective-permute-done.3 = f32[16,2048]{1,0:T(8,128)S(1)} collective-permute-done((f32[16,2048]{1,0:T(8,128)S(1)}, f32[16,2048]{1,0:T(8,128)S(1)}, u32[]{:S(2)}, u32[]{:S(2)}) %collective-permute-start.3) | collective-permute-done | bytes 131104 | tf_op jit(solution)/shard_map/ppermute | solution.py:44
  18.3 1.4 %collective-permute-start.4 = (f32[16,2048]{1,0:T(8,128)S(1)}, f32[16,2048]{1,0:T(8,128)S(1)}, u32[]{:S(2)}, u32[]{:S(2)}) collective-permute-start(f32[16,2048]{1,0:T(8,128)S(1)} %add_add_fusion.2.half), channel_id=1, source_target_pairs={{0,1},{1,0},{2,3},{3,2},{4,5},{5,4},{6,7},{7,6},{8,9},{9,8},{10,11... | collective-permute-start | bytes 393224 | tf_op jit(solution)/shard_map/ppermute | solution.py:44
  19.6 0.9 shard_map.52.before
  20.6 0.9 shard_map.53
  21.6 1.2 %collective-permute-start.7 = (f32[136,128]{1,0:T(8,128)S(1)}, f32[136,128]{1,0:T(8,128)S(1)}, u32[]{:S(2)}, u32[]{:S(2)}) collective-permute-start(f32[136,128]{1,0:T(8,128)S(1)} %shard_map.53), channel_id=1, source_target_pairs={{0,192},{64,128},{128,64},{192,0},{1,193},{65,129},{129,65},{193,1... | collective-permute-start | bytes 208904 | tf_op jit(solution)/shard_map/ppermute | solution.py:44
  23.3 1.5 %collective-permute-start.5 = (f32[136,128]{1,0:T(8,128)S(1)}, f32[136,128]{1,0:T(8,128)S(1)}, u32[]{:S(2)}, u32[]{:S(2)}) collective-permute-start(f32[136,128]{1,0:T(8,128)S(1)} %shard_map.53), channel_id=1, source_target_pairs={{0,64},{64,0},{128,192},{192,128},{1,65},{65,1},{129,193},{193,129... | collective-permute-start | bytes 208904 | tf_op jit(solution)/shard_map/ppermute | solution.py:44
  24.8 1.1 collective-permute-done.7
  26.0 1.6 %collective-permute-done.6 = f32[136,128]{1,0:T(8,128)S(1)} collective-permute-done((f32[136,128]{1,0:T(8,128)S(1)}, f32[136,128]{1,0:T(8,128)S(1)}, u32[]{:S(2)}, u32[]{:S(2)}) %collective-permute-start.6) | collective-permute-done | bytes 69664 | tf_op jit(solution)/shard_map/ppermute | solution.py:44
  27.7 4.2 %collective-permute-start.10 = (f32[136,128]{1,0:T(8,128)S(1)}, f32[136,128]{1,0:T(8,128)S(1)}, u32[]{:S(2)}, u32[]{:S(2)}) collective-permute-start(f32[136,128]{1,0:T(8,128)S(1)} %add_add_fusion.6), channel_id=1, source_target_pairs={{0,24},{8,16},{16,8},{24,0},{32,56},{40,48},{48,40},{56,32},{1,25}... | collective-permute-start | bytes 208904 | tf_op jit(solution)/shard_map/ppermute | solution.py:44
  32.3 1.3 %collective-permute-done.10 = f32[136,128]{1,0:T(8,128)S(1)} collective-permute-done((f32[136,128]{1,0:T(8,128)S(1)}, f32[136,128]{1,0:T(8,128)S(1)}, u32[]{:S(2)}, u32[]{:S(2)}) %collective-permute-start.10) | collective-permute-done | bytes 69664 | tf_op jit(solution)/shard_map/ppermute | solution.py:44
  33.6 3.3 %collective-permute-done.9 = f32[136,128]{1,0:T(8,128)S(1)} collective-permute-done((f32[136,128]{1,0:T(8,128)S(1)}, f32[136,128]{1,0:T(8,128)S(1)}, u32[]{:S(2)}, u32[]{:S(2)}) %collective-permute-start.9) | collective-permute-done | bytes 69664 | tf_op jit(solution)/shard_map/ppermute | solution.py:44
  36.9 3.1 %collective-permute-start.11 = (f32[136,128]{1,0:T(8,128)S(1)}, f32[136,128]{1,0:T(8,128)S(1)}, u32[]{:S(2)}, u32[]{:S(2)}) collective-permute-start(f32[136,128]{1,0:T(8,128)S(1)} %add_add_fusion.5.mine), channel_id=1, source_target_pairs={{0,48},{8,56},{16,32},{24,40},{32,16},{40,24},{48,0},{56,8},{1,49}... | collective-permute-start | bytes 208904 | tf_op jit(solution)/shard_map/ppermute | solution.py:44
  40.1 3.0 %collective-permute-done.11.theirs = f32[136,128]{1,0:T(8,128)S(1)} collective-permute-done((f32[136,128]{1,0:T(8,128)S(1)}, f32[136,128]{1,0:T(8,128)S(1)}, u32[]{:S(2)}, u32[]{:S(2)}) %collective-permute-start.11) | collective-permute-done | bytes 69664 | tf_op jit(solution)/shard_map/ppermute | solution.py:44
  43.0 1.4 %shard_map.54 = (bf16[16,1024]{1,0:T(8,128)(2,1)S(1)}, f32[16,2048]{1,0:T(8,128)S(1)}) custom-call(f32[136,128]{1,0:T(8,128)S(1)} %add_add_fusion.5.mine, f32[136,128]{1,0:T(8,128)S(1)} %collective-permute-done.11.theirs, bf16[2048,1024]{1,0:T(8,128)(2,1)S(1)} %get-tuple-element.13.held), custom_call_target="tpu_custom_call" | custom-call | flops 67108864 | bytes 4194304 | tf_op jit(solution)/shard_map/pallas_call | solution.py:235
  44.4 3.4 %collective-permute-start.12 = (f32[16,2048]{1,0:T(8,128)S(1)}, f32[16,2048]{1,0:T(8,128)S(1)}, u32[]{:S(2)}, u32[]{:S(2)}) collective-permute-start(f32[16,2048]{1,0:T(8,128)S(1)} %get-tuple-element.15), channel_id=1, source_target_pairs={{0,1},{1,0},{2,3},{3,2},{4,5},{5,4},{6,7},{7,6},{8,9},{9,8},{10,11... | collective-permute-start | bytes 393224 | tf_op jit(solution)/shard_map/ppermute | solution.py:44
  47.8 1.2 shard_map.55
  49.0 2.3 %collective-permute-start.15 = (f32[16,2048]{1,0:T(8,128)S(1)}, f32[16,2048]{1,0:T(8,128)S(1)}, u32[]{:S(2)}, u32[]{:S(2)}) collective-permute-start(f32[16,2048]{1,0:T(8,128)S(1)} %add.91), channel_id=1, source_target_pairs={{0,6},{2,4},{4,2},{6,0},{1,7},{3,5},{5,3},{7,1},{8,14},{10,12},{12... | collective-permute-start | bytes 393224 | tf_op jit(solution)/shard_map/ppermute | solution.py:44
  52.4 4.4 %collective-permute-done.15 = f32[16,2048]{1,0:T(8,128)S(1)} collective-permute-done((f32[16,2048]{1,0:T(8,128)S(1)}, f32[16,2048]{1,0:T(8,128)S(1)}, u32[]{:S(2)}, u32[]{:S(2)}) %collective-permute-start.15) | collective-permute-done | bytes 131104 | tf_op jit(solution)/shard_map/ppermute | solution.py:44
  57.5 0.9 collective-permute-done.13
  58.4 1.4 %collective-permute-start.16 = (f32[16,2048]{1,0:T(8,128)S(1)}, f32[16,2048]{1,0:T(8,128)S(1)}, u32[]{:S(2)}, u32[]{:S(2)}) collective-permute-start(f32[16,2048]{1,0:T(8,128)S(1)} %add_add_fusion.1.half), channel_id=1, source_target_pairs={{0,1},{1,0},{2,3},{3,2},{4,5},{5,4},{6,7},{7,6},{8,9},{9,8},{10,11... | collective-permute-start | bytes 393224 | tf_op jit(solution)/shard_map/ppermute | solution.py:44
  59.8 0.9 shard_map.56.before
  60.8 0.9 shard_map.57
  61.7 1.2 collective-permute-start.19
  63.7 1.4 %collective-permute-start.17 = (f32[136,128]{1,0:T(8,128)S(1)}, f32[136,128]{1,0:T(8,128)S(1)}, u32[]{:S(2)}, u32[]{:S(2)}) collective-permute-start(f32[136,128]{1,0:T(8,128)S(1)} %shard_map.57), channel_id=1, source_target_pairs={{0,64},{64,0},{128,192},{192,128},{1,65},{65,1},{129,193},{193,129... | collective-permute-start | bytes 208904 | tf_op jit(solution)/shard_map/ppermute | solution.py:44
  65.0 1.1 collective-permute-done.19
  66.1 1.5 %collective-permute-done.18 = f32[136,128]{1,0:T(8,128)S(1)} collective-permute-done((f32[136,128]{1,0:T(8,128)S(1)}, f32[136,128]{1,0:T(8,128)S(1)}, u32[]{:S(2)}, u32[]{:S(2)}) %collective-permute-start.18) | collective-permute-done | bytes 69664 | tf_op jit(solution)/shard_map/ppermute | solution.py:44
  68.0 1.8 %collective-permute-start.22 = (f32[136,128]{1,0:T(8,128)S(1)}, f32[136,128]{1,0:T(8,128)S(1)}, u32[]{:S(2)}, u32[]{:S(2)}) collective-permute-start(f32[136,128]{1,0:T(8,128)S(1)} %add_add_fusion.4), channel_id=1, source_target_pairs={{0,24},{8,16},{16,8},{24,0},{32,56},{40,48},{48,40},{56,32},{1,25}... | collective-permute-start | bytes 208904 | tf_op jit(solution)/shard_map/ppermute | solution.py:44
  69.9 1.0 collective-permute-start.21
  71.7 1.5 %collective-permute-done.22 = f32[136,128]{1,0:T(8,128)S(1)} collective-permute-done((f32[136,128]{1,0:T(8,128)S(1)}, f32[136,128]{1,0:T(8,128)S(1)}, u32[]{:S(2)}, u32[]{:S(2)}) %collective-permute-start.22) | collective-permute-done | bytes 69664 | tf_op jit(solution)/shard_map/ppermute | solution.py:44
  73.2 2.6 %collective-permute-done.21 = f32[136,128]{1,0:T(8,128)S(1)} collective-permute-done((f32[136,128]{1,0:T(8,128)S(1)}, f32[136,128]{1,0:T(8,128)S(1)}, u32[]{:S(2)}, u32[]{:S(2)}) %collective-permute-start.21) | collective-permute-done | bytes 69664 | tf_op jit(solution)/shard_map/ppermute | solution.py:44
  75.8 2.9 %collective-permute-start.23 = (f32[136,128]{1,0:T(8,128)S(1)}, f32[136,128]{1,0:T(8,128)S(1)}, u32[]{:S(2)}, u32[]{:S(2)}) collective-permute-start(f32[136,128]{1,0:T(8,128)S(1)} %add_add_fusion.3.mine), channel_id=1, source_target_pairs={{0,48},{8,56},{16,32},{24,40},{32,16},{40,24},{48,0},{56,8},{1,49}... | collective-permute-start | bytes 208904 | tf_op jit(solution)/shard_map/ppermute | solution.py:44
  78.7 3.1 %collective-permute-done.23.theirs = f32[136,128]{1,0:T(8,128)S(1)} collective-permute-done((f32[136,128]{1,0:T(8,128)S(1)}, f32[136,128]{1,0:T(8,128)S(1)}, u32[]{:S(2)}, u32[]{:S(2)}) %collective-permute-start.23) | collective-permute-done | bytes 69664 | tf_op jit(solution)/shard_map/ppermute | solution.py:44
  81.7 1.4 %shard_map.58 = (bf16[16,1024]{1,0:T(8,128)(2,1)S(1)}, f32[16,2048]{1,0:T(8,128)S(1)}) custom-call(f32[136,128]{1,0:T(8,128)S(1)} %add_add_fusion.3.mine, f32[136,128]{1,0:T(8,128)S(1)} %collective-permute-done.23.theirs, bf16[2048,1024]{1,0:T(8,128)(2,1)S(1)} %get-tuple-element.13.held), custom_call_target="tpu_custom_call" | custom-call | flops 67108864 | bytes 4194304 | tf_op jit(solution)/shard_map/pallas_call | solution.py:235
  83.1 3.4 %collective-permute-start.24 = (f32[16,2048]{1,0:T(8,128)S(1)}, f32[16,2048]{1,0:T(8,128)S(1)}, u32[]{:S(2)}, u32[]{:S(2)}) collective-permute-start(f32[16,2048]{1,0:T(8,128)S(1)} %get-tuple-element.17), channel_id=1, source_target_pairs={{0,1},{1,0},{2,3},{3,2},{4,5},{5,4},{6,7},{7,6},{8,9},{9,8},{10,11... | collective-permute-start | bytes 393224 | tf_op jit(solution)/shard_map/ppermute | solution.py:44
  86.5 1.2 shard_map.59
  87.8 2.3 %collective-permute-start.27 = (f32[16,2048]{1,0:T(8,128)S(1)}, f32[16,2048]{1,0:T(8,128)S(1)}, u32[]{:S(2)}, u32[]{:S(2)}) collective-permute-start(f32[16,2048]{1,0:T(8,128)S(1)} %add.101), channel_id=1, source_target_pairs={{0,6},{2,4},{4,2},{6,0},{1,7},{3,5},{5,3},{7,1},{8,14},{10,12},{12... | collective-permute-start | bytes 393224 | tf_op jit(solution)/shard_map/ppermute | solution.py:44
  91.1 4.4 %collective-permute-done.27 = f32[16,2048]{1,0:T(8,128)S(1)} collective-permute-done((f32[16,2048]{1,0:T(8,128)S(1)}, f32[16,2048]{1,0:T(8,128)S(1)}, u32[]{:S(2)}, u32[]{:S(2)}) %collective-permute-start.27) | collective-permute-done | bytes 131104 | tf_op jit(solution)/shard_map/ppermute | solution.py:44
  96.2 0.9 collective-permute-done.25
  97.5 4.9 %collective-permute-start.30 = (f32[8,128]{1,0:T(8,128)S(1)}, f32[8,128]{1,0:T(8,128)S(1)}, u32[]{:S(2)}, u32[]{:S(2)}) collective-permute-start(f32[8,128]{1,0:T(8,128)S(1)} %shard_map.60), channel_id=1, source_target_pairs={{0,49},{1,48},{8,57},{9,56},{16,33},{17,32},{24,41},{25,40},{32,17... | collective-permute-start | bytes 12296 | tf_op jit(solution)/shard_map/ppermute | solution.py:44
  102.8 0.8 collective-permute-done.30
  103.7 3.3 %collective-permute-done.29 = f32[8,128]{1,0:T(8,128)S(1)} collective-permute-done((f32[8,128]{1,0:T(8,128)S(1)}, f32[8,128]{1,0:T(8,128)S(1)}, u32[]{:S(2)}, u32[]{:S(2)}) %collective-permute-start.29) | collective-permute-done | bytes 4128 | tf_op jit(solution)/shard_map/ppermute | solution.py:44
  107.0 11.6 %all_to_all.5.grams = f32[16,8,128]{2,1,0:T(8,128)S(1)} all-to-all(f32[16,8,128]{2,1,0:T(8,128)S(1)} %broadcast_in_dim.2), channel_id=1, replica_groups=mesh['x'=4,'cube'=2,'level'=4,'y'=4,'core'=2] {'x','level'}, dimensions={0} | all-to-all | bytes 131072 | tf_op jit(solution)/shard_map/all_to_all | solution.py:314
  118.6 1.0 shard_map.61
  (39 shorter events, 8.4 us)
Async XLA Ops:
  4.3 4.5 %collective-permute-start = (f32[16,2048]{1,0:T(8,128)S(1)}, f32[16,2048]{1,0:T(8,128)S(1)}, u32[]{:S(2)}, u32[]{:S(2)}) collective-permute-start(f32[16,2048]{1,0:T(8,128)S(1)} %get-tuple-element.12), channel_id=1, source_target_pairs={{0,1},{1,0},{2,3},{3,2},{4,5},{5,4},{6,7},{7,6},{8,9},{9,8},{10,11... | collective-permute-start | bytes 393224 | tf_op jit(solution)/shard_map/ppermute | solution.py:44
  8.9 9.1 %collective-permute-start.3 = (f32[16,2048]{1,0:T(8,128)S(1)}, f32[16,2048]{1,0:T(8,128)S(1)}, u32[]{:S(2)}, u32[]{:S(2)}) collective-permute-start(f32[16,2048]{1,0:T(8,128)S(1)} %add.81), channel_id=1, source_target_pairs={{0,6},{2,4},{4,2},{6,0},{1,7},{3,5},{5,3},{7,1},{8,14},{10,12},{12... | collective-permute-start | bytes 393224 | tf_op jit(solution)/shard_map/ppermute | solution.py:44
  10.0 8.0 %collective-permute-start.2 = (f32[16,2048]{1,0:T(8,128)S(1)}, f32[16,2048]{1,0:T(8,128)S(1)}, u32[]{:S(2)}, u32[]{:S(2)}) collective-permute-start(f32[16,2048]{1,0:T(8,128)S(1)} %add.81), channel_id=1, source_target_pairs={{0,4},{2,6},{4,0},{6,2},{1,5},{3,7},{5,1},{7,3},{8,12},{10,14},{12... | collective-permute-start | bytes 393224 | tf_op jit(solution)/shard_map/ppermute | solution.py:44
  10.3 7.9 %collective-permute-start.1 = (f32[16,2048]{1,0:T(8,128)S(1)}, f32[16,2048]{1,0:T(8,128)S(1)}, u32[]{:S(2)}, u32[]{:S(2)}) collective-permute-start(f32[16,2048]{1,0:T(8,128)S(1)} %add.81), channel_id=1, source_target_pairs={{0,2},{2,0},{4,6},{6,4},{1,3},{3,1},{5,7},{7,5},{8,10},{10,8},{12,... | collective-permute-start | bytes 393224 | tf_op jit(solution)/shard_map/ppermute | solution.py:44
  18.3 2.4 %collective-permute-start.4 = (f32[16,2048]{1,0:T(8,128)S(1)}, f32[16,2048]{1,0:T(8,128)S(1)}, u32[]{:S(2)}, u32[]{:S(2)}) collective-permute-start(f32[16,2048]{1,0:T(8,128)S(1)} %add_add_fusion.2.half), channel_id=1, source_target_pairs={{0,1},{1,0},{2,3},{3,2},{4,5},{5,4},{6,7},{7,6},{8,9},{9,8},{10,11... | collective-permute-start | bytes 393224 | tf_op jit(solution)/shard_map/ppermute | solution.py:44
  21.6 4.4 %collective-permute-start.7 = (f32[136,128]{1,0:T(8,128)S(1)}, f32[136,128]{1,0:T(8,128)S(1)}, u32[]{:S(2)}, u32[]{:S(2)}) collective-permute-start(f32[136,128]{1,0:T(8,128)S(1)} %shard_map.53), channel_id=1, source_target_pairs={{0,192},{64,128},{128,64},{192,0},{1,193},{65,129},{129,65},{193,1... | collective-permute-start | bytes 208904 | tf_op jit(solution)/shard_map/ppermute | solution.py:44
  22.8 4.7 %collective-permute-start.6 = (f32[136,128]{1,0:T(8,128)S(1)}, f32[136,128]{1,0:T(8,128)S(1)}, u32[]{:S(2)}, u32[]{:S(2)}) collective-permute-start(f32[136,128]{1,0:T(8,128)S(1)} %shard_map.53), channel_id=1, source_target_pairs={{0,128},{64,192},{128,0},{192,64},{1,129},{65,193},{129,1},{193,65... | collective-permute-start | bytes 208904 | tf_op jit(solution)/shard_map/ppermute | solution.py:44
  23.3 4.3 %collective-permute-start.5 = (f32[136,128]{1,0:T(8,128)S(1)}, f32[136,128]{1,0:T(8,128)S(1)}, u32[]{:S(2)}, u32[]{:S(2)}) collective-permute-start(f32[136,128]{1,0:T(8,128)S(1)} %shard_map.53), channel_id=1, source_target_pairs={{0,64},{64,0},{128,192},{192,128},{1,65},{65,1},{129,193},{193,129... | collective-permute-start | bytes 208904 | tf_op jit(solution)/shard_map/ppermute | solution.py:44
  27.7 5.9 %collective-permute-start.10 = (f32[136,128]{1,0:T(8,128)S(1)}, f32[136,128]{1,0:T(8,128)S(1)}, u32[]{:S(2)}, u32[]{:S(2)}) collective-permute-start(f32[136,128]{1,0:T(8,128)S(1)} %add_add_fusion.6), channel_id=1, source_target_pairs={{0,24},{8,16},{16,8},{24,0},{32,56},{40,48},{48,40},{56,32},{1,25}... | collective-permute-start | bytes 208904 | tf_op jit(solution)/shard_map/ppermute | solution.py:44
  31.9 5.0 %collective-permute-start.9 = (f32[136,128]{1,0:T(8,128)S(1)}, f32[136,128]{1,0:T(8,128)S(1)}, u32[]{:S(2)}, u32[]{:S(2)}) collective-permute-start(f32[136,128]{1,0:T(8,128)S(1)} %add_add_fusion.6), channel_id=1, source_target_pairs={{0,16},{8,24},{16,0},{24,8},{32,48},{40,56},{48,32},{56,40},{1,17}... | collective-permute-start | bytes 208904 | tf_op jit(solution)/shard_map/ppermute | solution.py:44
  31.9 5.0 %collective-permute-start.8 = (f32[136,128]{1,0:T(8,128)S(1)}, f32[136,128]{1,0:T(8,128)S(1)}, u32[]{:S(2)}, u32[]{:S(2)}) collective-permute-start(f32[136,128]{1,0:T(8,128)S(1)} %add_add_fusion.6), channel_id=1, source_target_pairs={{0,8},{8,0},{16,24},{24,16},{32,40},{40,32},{48,56},{56,48},{1,9},... | collective-permute-start | bytes 208904 | tf_op jit(solution)/shard_map/ppermute | solution.py:44
  36.9 6.1 %collective-permute-start.11 = (f32[136,128]{1,0:T(8,128)S(1)}, f32[136,128]{1,0:T(8,128)S(1)}, u32[]{:S(2)}, u32[]{:S(2)}) collective-permute-start(f32[136,128]{1,0:T(8,128)S(1)} %add_add_fusion.5.mine), channel_id=1, source_target_pairs={{0,48},{8,56},{16,32},{24,40},{32,16},{40,24},{48,0},{56,8},{1,49}... | collective-permute-start | bytes 208904 | tf_op jit(solution)/shard_map/ppermute | solution.py:44
  44.4 4.6 %collective-permute-start.12 = (f32[16,2048]{1,0:T(8,128)S(1)}, f32[16,2048]{1,0:T(8,128)S(1)}, u32[]{:S(2)}, u32[]{:S(2)}) collective-permute-start(f32[16,2048]{1,0:T(8,128)S(1)} %get-tuple-element.15), channel_id=1, source_target_pairs={{0,1},{1,0},{2,3},{3,2},{4,5},{5,4},{6,7},{7,6},{8,9},{9,8},{10,11... | collective-permute-start | bytes 393224 | tf_op jit(solution)/shard_map/ppermute | solution.py:44
  49.0 7.7 %collective-permute-start.15 = (f32[16,2048]{1,0:T(8,128)S(1)}, f32[16,2048]{1,0:T(8,128)S(1)}, u32[]{:S(2)}, u32[]{:S(2)}) collective-permute-start(f32[16,2048]{1,0:T(8,128)S(1)} %add.91), channel_id=1, source_target_pairs={{0,6},{2,4},{4,2},{6,0},{1,7},{3,5},{5,3},{7,1},{8,14},{10,12},{12... | collective-permute-start | bytes 393224 | tf_op jit(solution)/shard_map/ppermute | solution.py:44
  51.3 6.2 %collective-permute-start.14 = (f32[16,2048]{1,0:T(8,128)S(1)}, f32[16,2048]{1,0:T(8,128)S(1)}, u32[]{:S(2)}, u32[]{:S(2)}) collective-permute-start(f32[16,2048]{1,0:T(8,128)S(1)} %add.91), channel_id=1, source_target_pairs={{0,4},{2,6},{4,0},{6,2},{1,5},{3,7},{5,1},{7,3},{8,12},{10,14},{12... | collective-permute-start | bytes 393224 | tf_op jit(solution)/shard_map/ppermute | solution.py:44
  51.7 6.7 %collective-permute-start.13 = (f32[16,2048]{1,0:T(8,128)S(1)}, f32[16,2048]{1,0:T(8,128)S(1)}, u32[]{:S(2)}, u32[]{:S(2)}) collective-permute-start(f32[16,2048]{1,0:T(8,128)S(1)} %add.91), channel_id=1, source_target_pairs={{0,2},{2,0},{4,6},{6,4},{1,3},{3,1},{5,7},{7,5},{8,10},{10,8},{12,... | collective-permute-start | bytes 393224 | tf_op jit(solution)/shard_map/ppermute | solution.py:44
  58.4 2.4 %collective-permute-start.16 = (f32[16,2048]{1,0:T(8,128)S(1)}, f32[16,2048]{1,0:T(8,128)S(1)}, u32[]{:S(2)}, u32[]{:S(2)}) collective-permute-start(f32[16,2048]{1,0:T(8,128)S(1)} %add_add_fusion.1.half), channel_id=1, source_target_pairs={{0,1},{1,0},{2,3},{3,2},{4,5},{5,4},{6,7},{7,6},{8,9},{9,8},{10,11... | collective-permute-start | bytes 393224 | tf_op jit(solution)/shard_map/ppermute | solution.py:44
  61.7 4.4 %collective-permute-start.19 = (f32[136,128]{1,0:T(8,128)S(1)}, f32[136,128]{1,0:T(8,128)S(1)}, u32[]{:S(2)}, u32[]{:S(2)}) collective-permute-start(f32[136,128]{1,0:T(8,128)S(1)} %shard_map.57), channel_id=1, source_target_pairs={{0,192},{64,128},{128,64},{192,0},{1,193},{65,129},{129,65},{193,1... | collective-permute-start | bytes 208904 | tf_op jit(solution)/shard_map/ppermute | solution.py:44
  62.9 4.8 %collective-permute-start.18 = (f32[136,128]{1,0:T(8,128)S(1)}, f32[136,128]{1,0:T(8,128)S(1)}, u32[]{:S(2)}, u32[]{:S(2)}) collective-permute-start(f32[136,128]{1,0:T(8,128)S(1)} %shard_map.57), channel_id=1, source_target_pairs={{0,128},{64,192},{128,0},{192,64},{1,129},{65,193},{129,1},{193,65... | collective-permute-start | bytes 208904 | tf_op jit(solution)/shard_map/ppermute | solution.py:44
  63.7 4.3 %collective-permute-start.17 = (f32[136,128]{1,0:T(8,128)S(1)}, f32[136,128]{1,0:T(8,128)S(1)}, u32[]{:S(2)}, u32[]{:S(2)}) collective-permute-start(f32[136,128]{1,0:T(8,128)S(1)} %shard_map.57), channel_id=1, source_target_pairs={{0,64},{64,0},{128,192},{192,128},{1,65},{65,1},{129,193},{193,129... | collective-permute-start | bytes 208904 | tf_op jit(solution)/shard_map/ppermute | solution.py:44
  68.0 5.2 %collective-permute-start.22 = (f32[136,128]{1,0:T(8,128)S(1)}, f32[136,128]{1,0:T(8,128)S(1)}, u32[]{:S(2)}, u32[]{:S(2)}) collective-permute-start(f32[136,128]{1,0:T(8,128)S(1)} %add_add_fusion.4), channel_id=1, source_target_pairs={{0,24},{8,16},{16,8},{24,0},{32,56},{40,48},{48,40},{56,32},{1,25}... | collective-permute-start | bytes 208904 | tf_op jit(solution)/shard_map/ppermute | solution.py:44
  69.9 5.9 %collective-permute-start.21 = (f32[136,128]{1,0:T(8,128)S(1)}, f32[136,128]{1,0:T(8,128)S(1)}, u32[]{:S(2)}, u32[]{:S(2)}) collective-permute-start(f32[136,128]{1,0:T(8,128)S(1)} %add_add_fusion.4), channel_id=1, source_target_pairs={{0,16},{8,24},{16,0},{24,8},{32,48},{40,56},{48,32},{56,40},{1,17}... | collective-permute-start | bytes 208904 | tf_op jit(solution)/shard_map/ppermute | solution.py:44
  70.9 4.9 %collective-permute-start.20 = (f32[136,128]{1,0:T(8,128)S(1)}, f32[136,128]{1,0:T(8,128)S(1)}, u32[]{:S(2)}, u32[]{:S(2)}) collective-permute-start(f32[136,128]{1,0:T(8,128)S(1)} %add_add_fusion.4), channel_id=1, source_target_pairs={{0,8},{8,0},{16,24},{24,16},{32,40},{40,32},{48,56},{56,48},{1,9},... | collective-permute-start | bytes 208904 | tf_op jit(solution)/shard_map/ppermute | solution.py:44
  75.8 6.0 %collective-permute-start.23 = (f32[136,128]{1,0:T(8,128)S(1)}, f32[136,128]{1,0:T(8,128)S(1)}, u32[]{:S(2)}, u32[]{:S(2)}) collective-permute-start(f32[136,128]{1,0:T(8,128)S(1)} %add_add_fusion.3.mine), channel_id=1, source_target_pairs={{0,48},{8,56},{16,32},{24,40},{32,16},{40,24},{48,0},{56,8},{1,49}... | collective-permute-start | bytes 208904 | tf_op jit(solution)/shard_map/ppermute | solution.py:44
  83.1 4.6 %collective-permute-start.24 = (f32[16,2048]{1,0:T(8,128)S(1)}, f32[16,2048]{1,0:T(8,128)S(1)}, u32[]{:S(2)}, u32[]{:S(2)}) collective-permute-start(f32[16,2048]{1,0:T(8,128)S(1)} %get-tuple-element.17), channel_id=1, source_target_pairs={{0,1},{1,0},{2,3},{3,2},{4,5},{5,4},{6,7},{7,6},{8,9},{9,8},{10,11... | collective-permute-start | bytes 393224 | tf_op jit(solution)/shard_map/ppermute | solution.py:44
  87.8 7.7 %collective-permute-start.27 = (f32[16,2048]{1,0:T(8,128)S(1)}, f32[16,2048]{1,0:T(8,128)S(1)}, u32[]{:S(2)}, u32[]{:S(2)}) collective-permute-start(f32[16,2048]{1,0:T(8,128)S(1)} %add.101), channel_id=1, source_target_pairs={{0,6},{2,4},{4,2},{6,0},{1,7},{3,5},{5,3},{7,1},{8,14},{10,12},{12... | collective-permute-start | bytes 393224 | tf_op jit(solution)/shard_map/ppermute | solution.py:44
  90.0 6.2 %collective-permute-start.26 = (f32[16,2048]{1,0:T(8,128)S(1)}, f32[16,2048]{1,0:T(8,128)S(1)}, u32[]{:S(2)}, u32[]{:S(2)}) collective-permute-start(f32[16,2048]{1,0:T(8,128)S(1)} %add.101), channel_id=1, source_target_pairs={{0,4},{2,6},{4,0},{6,2},{1,5},{3,7},{5,1},{7,3},{8,12},{10,14},{12... | collective-permute-start | bytes 393224 | tf_op jit(solution)/shard_map/ppermute | solution.py:44
  90.4 6.7 %collective-permute-start.25 = (f32[16,2048]{1,0:T(8,128)S(1)}, f32[16,2048]{1,0:T(8,128)S(1)}, u32[]{:S(2)}, u32[]{:S(2)}) collective-permute-start(f32[16,2048]{1,0:T(8,128)S(1)} %add.101), channel_id=1, source_target_pairs={{0,2},{2,0},{4,6},{6,4},{1,3},{3,1},{5,7},{7,5},{8,10},{10,8},{12,... | collective-permute-start | bytes 393224 | tf_op jit(solution)/shard_map/ppermute | solution.py:44
  97.5 6.2 %collective-permute-start.30 = (f32[8,128]{1,0:T(8,128)S(1)}, f32[8,128]{1,0:T(8,128)S(1)}, u32[]{:S(2)}, u32[]{:S(2)}) collective-permute-start(f32[8,128]{1,0:T(8,128)S(1)} %shard_map.60), channel_id=1, source_target_pairs={{0,49},{1,48},{8,57},{9,56},{16,33},{17,32},{24,41},{25,40},{32,17... | collective-permute-start | bytes 12296 | tf_op jit(solution)/shard_map/ppermute | solution.py:44
  102.4 4.6 %collective-permute-start.29 = (f32[8,128]{1,0:T(8,128)S(1)}, f32[8,128]{1,0:T(8,128)S(1)}, u32[]{:S(2)}, u32[]{:S(2)}) collective-permute-start(f32[8,128]{1,0:T(8,128)S(1)} %shard_map.60), channel_id=1, source_target_pairs={{0,48},{1,49},{8,56},{9,57},{16,32},{17,33},{24,40},{25,41},{32,16... | collective-permute-start | bytes 12296 | tf_op jit(solution)/shard_map/ppermute | solution.py:44
  102.4 4.6 %collective-permute-start.28 = (f32[8,128]{1,0:T(8,128)S(1)}, f32[8,128]{1,0:T(8,128)S(1)}, u32[]{:S(2)}, u32[]{:S(2)}) collective-permute-start(f32[8,128]{1,0:T(8,128)S(1)} %shard_map.60), channel_id=1, source_target_pairs={{0,1},{1,0},{8,9},{9,8},{16,17},{17,16},{24,25},{25,24},{32,33},{3... | collective-permute-start | bytes 12296 | tf_op jit(solution)/shard_map/ppermute | solution.py:44
